TPU v7x, 32 devices: a whole 2x2x4 slice. The times are simulated.
32 devices in a mesh: groups: 2 (over y), req: 4 (over x, core), tp: 4 (over z).
Axes of the slice: x: 2, y: 2, z: 4, core: 2. Of those that a mesh axis runs over, the one named last changes fastest.
Arguments:
- tokens: bfloat16 [4096, 8192], P(('groups', 'req'), 'tp'), parts along dimension 0, may hold values from -6 to 6
- norm_gain: bfloat16 [8192], replicated, may hold values from 0.25 to 1.75
- w_query: bfloat16 [8192, 4096], P(None, 'tp'), may hold values from -0.0625 to 0.0625
- key_weight: bfloat16 [8192, 1024], P(None, 'tp'), may hold values from -0.0625 to 0.0625
- value_weight: bfloat16 [8192, 1024], P(None, 'tp'), may hold values from -0.0625 to 0.0625
- lengths: int32 [8], P('groups'), parts along dimension 0, may hold values from 1 to 512, 1024 in all
- plan: int32 [32], P('groups'), parts along dimension 0, may hold values from 0 to 15, as said below
Outputs:
- attended: bfloat16 [4096, 4096], P(('groups', 'req'), 'tp'), parts along dimension 0
- cache: bfloat16 [2, 4096, 1024], P(None, ('groups', 'req'), 'tp'), parts along dimension 1
There are 2 independent parts, one for each index of `groups`. A program takes and returns all parts, laid end to end along the dimension named above; an argument that names none is the same for every part. Nothing has to cross between parts.
Inputs may be any that keep to these rules, and one draw needn't show every extreme that they name: lengths: the longest request is exactly 512. plan is a permutation of the spans 0 to 15; span g is request g // 4 at positions (g % 4) * 128 onward; slot k belongs to worker k // 4; the 4 spans of one request go to 4 different workers.
All inputs are finite; a program needn't handle non-finite values.
Results may differ from a plain program's by a relative error of at most 0.008.
Values may be sent and summed in bfloat16 or wider, within the bound.
No kernel may reach another device: no remote copies, remote signals or barrier semaphores. Data moves between devices by JAX's collectives and lax.ppermute only.
A program may use at most 128 MiB of HBM per device.

v0:
```python
import functools
import math

import jax
import jax.numpy as jnp
import numpy as np
from jax import lax
from jax.experimental import pallas as pl
from jax.experimental.pallas import tpu as pltpu
from jax.sharding import PartitionSpec as P

HEAD_SIZE = 128
SPAN = 128
ALIGN = 16
TILE = 2 * SPAN
SHARES = (3, 5, 5, 3)
DEPTH = 1024
MEBI = 1024 * 1024
F32, BF16 = jnp.float32, jnp.bfloat16


def run_of(lengths_ref, request, count):
    start = jnp.int32(0)
    length = jnp.int32(0)
    for other in range(count):
        amount = lengths_ref[other]
        start = start + jnp.where(other < request, amount, 0)
        length = jnp.where(other == request, amount, length)
    return start, length


def iota(shape, dimension):
    return lax.broadcasted_iota(jnp.int32, shape, dimension)


def deal_kernel(chips, bases, sizes, twins, lengths_ref, *refs):
    me = lax.axis_index("req")
    chip, core = lax.div(me, 2), lax.rem(me, 2)
    sources, refs = refs[: len(twins)], refs[len(twins) :]
    count = 2 * len(sizes)
    priors, out_refs = refs[:-count], refs[-count:]
    requests = [me + 1 - 2 * core if twin else me for twin in twins]
    runs = [run_of(lengths_ref, request, 2 * chips) for request in requests]
    slots = sources[0].shape[0]
    for chunk, (base, rows) in enumerate(zip(bases, sizes)):
        home_ref, away_ref = out_refs[2 * chunk : 2 * chunk + 2]
        for hop in range(chips):
            target = lax.rem(chip + hop, chips) * 2 + core
            number = base + target * rows + iota((rows, slots), 0)
            slot = iota((rows, slots), 1)
            total = None
            for (start, length), source in zip(runs, sources):
                hot = ((number - start == slot) & (slot < length)).astype(BF16)
                part = jnp.dot(hot, source[...], preferred_element_type=F32)
                total = part if total is None else total + part
            total = total.astype(BF16)
            if hop == 0:
                home_ref[...] = total + priors[2 * chunk][...] if priors else total
            elif priors:
                away_ref[hop - 1] = total + priors[2 * chunk + 1][hop - 1]
            else:
                away_ref[hop - 1] = total


def deal(chips, bases, sizes, lengths, sources, twins, priors=()):
    slots, width = sources[0].shape
    block = min(1024, width)
    out_specs, out_shape = [], []
    for rows in sizes:
        out_specs += [
            pl.BlockSpec((rows, block), lambda i: (0, i)),
            pl.BlockSpec((chips - 1, rows, block), lambda i: (0, 0, i)),
        ]
        out_shape += [
            jax.ShapeDtypeStruct((rows, width), BF16),
            jax.ShapeDtypeStruct((chips - 1, rows, width), BF16),
        ]
    return pl.pallas_call(
        functools.partial(deal_kernel, chips, bases, sizes, twins),
        grid=(width // block,),
        in_specs=[pl.BlockSpec(memory_space=pltpu.SMEM)]
        + [pl.BlockSpec((slots, block), lambda i: (0, i)) for _ in sources]
        + (out_specs if priors else []),
        out_specs=out_specs,
        out_shape=out_shape,
        compiler_params=pltpu.CompilerParams(vmem_limit_bytes=10 * MEBI),
        name="deal",
    )(lengths, *sources, *priors)


def merge_kernel(count, passed, home_ref, *refs):
    total = home_ref[...]
    for ref in refs[:count]:
        total = total + ref[...]
    refs[len(refs) - 1 - passed][...] = total


def merge(home, arrived, later):
    count = len(arrived)
    vmem, anywhere = pl.BlockSpec(memory_space=pltpu.VMEM), pl.BlockSpec(memory_space=pl.ANY)
    block, *later = pl.pallas_call(
        functools.partial(merge_kernel, count, len(later)),
        in_specs=[vmem] * (count + 1) + [anywhere] * len(later),
        out_specs=[vmem] + [anywhere] * len(later),
        out_shape=[jax.ShapeDtypeStruct(leaf.shape, leaf.dtype) for leaf in (home, *later)],
        input_output_aliases={count + 1 + at: 1 + at for at in range(len(later))},
        compiler_params=pltpu.CompilerParams(vmem_limit_bytes=4 * MEBI),
        name="merge",
    )(home, *arrived, *later)
    return block, later


def after(arrays, anchors):
    def kernel(*refs):
        pass

    anywhere = pl.BlockSpec(memory_space=pl.ANY)
    return pl.pallas_call(
        kernel,
        in_specs=[anywhere] * (len(arrays) + len(anchors)),
        out_specs=[anywhere] * len(arrays),
        out_shape=[jax.ShapeDtypeStruct(leaf.shape, leaf.dtype) for leaf in arrays],
        input_output_aliases={at: at for at in range(len(arrays))},
        compiler_params=pltpu.CompilerParams(vmem_limit_bytes=MEBI),
        name="after",
    )(*arrays, *anchors)


def routes_of(shards):
    routes, masks, distance = [], [0], shards // 2
    while distance:
        for source in range(len(masks)):
            routes.append((source, distance))
            masks.append(masks[source] ^ distance)
        distance //= 2
    return routes, masks


def angles_kernel(groups, members, lengths_ref, frequency_ref, anchor_ref, *out_refs):
    me = lax.axis_index("req")
    for group, (bases, sizes) in enumerate(groups):
        first = 0
        for base, rows in zip(bases, sizes):
            number = base + me * rows + iota((rows, HEAD_SIZE), 0)
            start = jnp.zeros((rows, HEAD_SIZE), jnp.int32)
            before = jnp.int32(0)
            for other in range(members):
                before = before + lengths_ref[other]
                start = jnp.where(number >= before, before, start)
            angle = (number - start).astype(F32) * frequency_ref[...]
            sine = jnp.sin(angle)
            lower = iota((rows, HEAD_SIZE), 1) < HEAD_SIZE // 2
            out_refs[2 * group][first : first + rows, :] = jnp.cos(angle)
            out_refs[2 * group + 1][first : first + rows, :] = jnp.where(lower, -sine, sine)
            first += rows


def angles(groups, lengths, frequency, anchor):
    shapes = [
        jax.ShapeDtypeStruct((sum(sizes), HEAD_SIZE), F32) for _, sizes in groups for _ in range(2)
    ]
    vmem = pl.BlockSpec(memory_space=pltpu.VMEM)
    tables = pl.pallas_call(
        functools.partial(angles_kernel, groups, lengths.shape[0]),
        in_specs=[
            pl.BlockSpec(memory_space=pltpu.SMEM),
            vmem,
            pl.BlockSpec(memory_space=pl.ANY),
        ],
        out_specs=[vmem] * len(shapes),
        out_shape=shapes,
        compiler_params=pltpu.CompilerParams(vmem_limit_bytes=4 * MEBI),
        name="angles",
    )(lengths, frequency, anchor)
    return [tables[at : at + 2] for at in range(0, len(tables), 2)]


def load(weight, anchor):
    parts = 8
    depth = weight.shape[0] // parts

    def kernel(weight_ref, anchor_ref, out_ref, token_ref, sems):
        copies = [
            pltpu.make_async_copy(
                weight_ref.at[pl.ds(part * depth, depth), :],
                out_ref.at[pl.ds(part * depth, depth), :],
                sems.at[part],
            )
            for part in range(parts)
        ]
        for copy in copies:
            copy.start()
        token_ref[...] = jnp.zeros_like(token_ref)
        for copy in copies:
            copy.wait()

    vmem, anywhere = pl.BlockSpec(memory_space=pltpu.VMEM), pl.BlockSpec(memory_space=pl.ANY)
    return pl.pallas_call(
        kernel,
        in_specs=[anywhere, anywhere],
        out_specs=[vmem, vmem],
        out_shape=[
            jax.ShapeDtypeStruct(weight.shape, weight.dtype),
            jax.ShapeDtypeStruct((8, 128), F32),
        ],
        scratch_shapes=[pltpu.SemaphoreType.DMA((parts,))],
        compiler_params=pltpu.CompilerParams(vmem_limit_bytes=2 * MEBI),
        name="load",
    )(pltpu.with_memory_space_constraint(weight, pltpu.HBM), anchor)


def project_kernel(masks, carries, final, shards, *refs):
    pieces, refs = refs[: len(masks)], refs[len(masks) :]
    (gain_ref, *weights), refs = refs[:4], refs[4:]
    if carries:
        sums_in, squares_in, *refs = refs
    if final:
        cosine_ref, sine_ref, out_ref, *refs = refs
    sums, squares = refs
    width = pieces[0].shape[1]
    depth = min(DEPTH, width)
    sums[...] = sums_in[...] if carries else jnp.zeros_like(sums)
    squares[...] = squares_in[...] if carries else jnp.zeros_like(squares)
    for piece, mask in zip(pieces, masks):
        shard = lax.bitwise_xor(lax.axis_index("tp"), jnp.int32(mask))

        def add_part(part, carry):
            at = pl.multiple_of(part * depth, depth)
            deep = pl.ds(pl.multiple_of(shard * width + at, depth), depth)
            wide = piece[:, pl.ds(at, depth)].astype(F32)
            square = wide * wide
            lanes = square[:, :128]
            for left in range(128, depth, 128):
                lanes = lanes + square[:, left : left + 128]
            squares[...] += lanes
            scaled = (wide * gain_ref[:, deep]).astype(BF16)
            left = 0
            for weight in weights:
                columns = slice(left, left + weight.shape[1])
                sums[:, columns] += jnp.dot(
                    scaled, weight[deep, :], preferred_element_type=F32
                )
                left += weight.shape[1]
            return carry

        lax.fori_loop(0, width // depth, add_part, 0)
    if final:
        mean = jnp.sum(squares[...], axis=1, keepdims=True) / (shards * width)
        scale = lax.rsqrt(mean + 1e-05)
        turned = sums.shape[1] - weights[-1].shape[1]
        for left in range(0, sums.shape[1], HEAD_SIZE):
            columns = slice(left, left + HEAD_SIZE)
            head = sums[:, columns] * scale
            if left < turned:
                head = head * cosine_ref[...] + pltpu.roll(
                    head, HEAD_SIZE // 2, 1
                ) * sine_ref[...]
            out_ref[:, columns] = head.astype(BF16)


def project(final, shards, masks, pieces, gain, weights, carried, tables):
    rows = pieces[0].shape[0]
    columns = sum(weight.shape[1] for weight in weights)
    operands = [*pieces, gain, *weights, *carried, *tables]
    sums = (rows, columns), (rows, 128)
    if final:
        out_shape = [jax.ShapeDtypeStruct((rows, columns), BF16)]
        scratch = [pltpu.VMEM(shape, F32) for shape in sums]
    else:
        out_shape = [jax.ShapeDtypeStruct(shape, F32) for shape in sums]
        scratch = []
    vmem = pl.BlockSpec(memory_space=pltpu.VMEM)
    return pl.pallas_call(
        functools.partial(project_kernel, masks, bool(carried), final, shards),
        in_specs=[vmem] * len(operands),
        out_specs=[vmem] * len(out_shape),
        out_shape=out_shape,
        scratch_shapes=scratch,
        compiler_params=pltpu.CompilerParams(vmem_limit_bytes=6 * MEBI),
        name="project",
    )(*operands)


def attend_kernel(
    chips, groups, known, prior, query_width, key_width, lengths_ref, plan_ref, *refs
):
    blocks, refs = refs[: -13 if prior else -11], refs[-11:]
    attended_out, cache_out, token_ref, attended_ref, cache_ref, rows_ref, queries_ref = refs[:7]
    scores_ref, top_ref, sems, out_sems = refs[7:]
    token_ref[...] = jnp.zeros_like(token_ref)
    workers = 2 * chips
    me = lax.axis_index("req")
    chip, core = lax.div(me, 2), lax.rem(me, 2)
    slots = cache_ref.shape[1]
    spans = slots // SPAN
    total = workers * sum(sum(sizes) for _, sizes in groups)
    end = needed = jnp.int32(0)
    for other in range(workers):
        end = end + lengths_ref[other]
        needed = jnp.where(end <= prior, end, needed)
    copies = []
    for group, (bases, sizes) in enumerate(groups):
        for hop in range(chips):
            source = lax.rem(chip - hop + chips, chips) * 2
            for twin in range(2):
                owner = source + (core if twin == 0 else 1 - core)
                block = blocks[(group * chips + hop) * 2 + twin]
                first = 0
                for base, rows in zip(bases, sizes):
                    at = pl.multiple_of(base + owner * rows, ALIGN)
                    copy = pltpu.make_async_copy(
                        block.at[pl.ds(first, rows), :],
                        rows_ref.at[pl.ds(at, rows), :],
                        sems.at[len(copies)],
                    )
                    copies.append((at + rows > needed, copy))
                    first += rows
    for wanted, copy in copies:

        @pl.when(wanted)
        def _():
            copy.start()

    rows_ref[total:, :] = jnp.zeros((rows_ref.shape[0] - total, rows_ref.shape[1]), BF16)
    for wanted, copy in copies:

        @pl.when(wanted)
        def _():
            copy.wait()

    def window(row, columns):
        first = pl.multiple_of(lax.div(row, ALIGN) * ALIGN, ALIGN)
        shape = (SPAN, 2 * SPAN)
        hot = (iota(shape, 1) == iota(shape, 0) + (row - first)).astype(BF16)
        return jnp.dot(
            hot, rows_ref[pl.ds(first, 2 * SPAN), columns], preferred_element_type=F32
        )

    own_start, own_length = run_of(lengths_ref, me, workers)
    mine = (own_start + own_length <= known) & (own_start + own_length > prior)
    cache_copy = pltpu.make_async_copy(cache_ref, cache_out, out_sems.at[spans])

    @pl.when(mine)
    def _():
        def step(part, carry):
            at = pl.multiple_of(part * SPAN, SPAN)

            @pl.when(at < own_length)
            def _():
                picked = window(own_start + at, slice(query_width, query_width + 2 * key_width))
                live = at + iota(picked.shape, 0) < own_length
                picked = jnp.where(live, picked, 0.0).astype(BF16)
                cache_ref[0, pl.ds(at, SPAN), :] = picked[:, :key_width]
                cache_ref[1, pl.ds(at, SPAN), :] = picked[:, key_width:]

            @pl.when(at >= own_length)
            def _():
                empty = jnp.zeros((SPAN, key_width), BF16)
                cache_ref[0, pl.ds(at, SPAN), :] = empty
                cache_ref[1, pl.ds(at, SPAN), :] = empty

            return carry

        lax.fori_loop(0, spans, step, 0)
        cache_copy.start()

    heads, key_heads = query_width // HEAD_SIZE, key_width // HEAD_SIZE
    group = heads // key_heads
    factor = math.log2(math.e) / math.sqrt(HEAD_SIZE)
    tall = group * SPAN

    def span_of(slot):
        span = plan_ref[me * spans + slot]
        start, length = run_of(lengths_ref, lax.div(span, spans), workers)
        offset = lax.rem(span, spans) * SPAN
        dead = offset >= length
        needed = start + jnp.minimum(offset + SPAN, length)
        due = jnp.logical_not(dead) & (needed <= known) & (needed > prior)
        return start, length, offset, dead, due

    def result(slot):
        rows = pl.ds(pl.multiple_of(slot * SPAN, SPAN), SPAN)
        return pltpu.make_async_copy(
            attended_ref.at[rows, :], attended_out.at[rows, :], out_sems.at[slot]
        )

    def attend_slot(slot, carry):
        start, length, offset, dead, due = span_of(slot)
        out_rows = pl.ds(pl.multiple_of(slot * SPAN, SPAN), SPAN)

        if not prior:

            @pl.when(dead)
            def _():
                attended_ref[out_rows, :] = jnp.zeros((SPAN, query_width), BF16)
                result(slot).start()

        @pl.when(due)
        def _():
            queries = window(start + offset, slice(0, query_width)).astype(BF16)
            for head in range(heads):
                at = head % group * SPAN
                queries_ref[head // group, at : at + SPAN, :] = queries[
                    :, head * HEAD_SIZE : (head + 1) * HEAD_SIZE
                ]
            first = pl.multiple_of(lax.div(start, ALIGN) * ALIGN, ALIGN)
            shift = start - first
            reach = shift + jnp.minimum(offset + SPAN, length)
            tiles = lax.div(reach + TILE - 1, TILE)

            def columns(at, head):
                return slice(at + head * HEAD_SIZE, at + (head + 1) * HEAD_SIZE)

            def tile_rows(tile):
                return pl.ds(pl.multiple_of(first + tile * TILE, ALIGN), TILE)

            top_ref[...] = jnp.full(top_ref.shape, -1e30, F32)

            def score(tile, carry):
                key_pos = tile * TILE + iota((SPAN, TILE), 1) - shift
                query_pos = offset + iota((SPAN, TILE), 0)
                allowed = (key_pos >= 0) & (key_pos <= query_pos) & (key_pos < length)
                bias = jnp.where(allowed, 0.0, -1e30)
                bias = jnp.concatenate([bias] * group, axis=0)
                for head in range(key_heads):
                    scores = lax.dot_general(
                        queries_ref[head],
                        rows_ref[tile_rows(tile), columns(query_width, head)],
                        (((1,), (1,)), ((), ())),
                        preferred_element_type=F32,
                    )
                    scores = scores + bias
                    scores_ref[head, tile] = scores
                    top_ref[head] = jnp.maximum(top_ref[head], scores)
                return carry

            lax.fori_loop(0, tiles, score, 0)
            tops = [jnp.max(top_ref[head], axis=1, keepdims=True) for head in range(key_heads)]

            def mix(tile, carry):
                ones = jnp.ones((TILE, HEAD_SIZE), BF16)
                totals = []
                for head in range(key_heads):
                    weights = jnp.exp2((scores_ref[head, tile] - tops[head]) * factor)
                    values = rows_ref[tile_rows(tile), columns(query_width + key_width, head)]
                    values = jnp.concatenate([values, ones], axis=1)
                    totals.append(
                        carry[head]
                        + jnp.dot(weights.astype(BF16), values, preferred_element_type=F32)
                    )
                return tuple(totals)

            empty = jnp.zeros((tall, 2 * HEAD_SIZE), F32)
            mixed = lax.fori_loop(0, tiles, mix, (empty,) * key_heads)
            live = offset + iota((SPAN, HEAD_SIZE), 0) < length
            for head in range(heads):
                at = head % group * SPAN
                part = mixed[head // group][at : at + SPAN]
                part = part[:, :HEAD_SIZE] / part[:, HEAD_SIZE:]
                attended_ref[out_rows, columns(0, head)] = jnp.where(live, part, 0.0).astype(BF16)

            result(slot).start()

        return carry

    lax.fori_loop(0, spans, attend_slot, 0)

    def finish(slot, carry):
        _, _, _, dead, due = span_of(slot)

        @pl.when(due if prior else due | dead)
        def _():
            result(slot).wait()

        return carry

    lax.fori_loop(0, spans, finish, 0)

    @pl.when(mine)
    def _():
        cache_copy.wait()


def attend(chips, groups, known, prior, widths, slots, lengths, plan, blocks, outputs):
    query_width, key_width = widths
    width = query_width + 2 * key_width
    total = 2 * chips * sum(sum(sizes) for _, sizes in groups)
    copies = 2 * chips * sum(len(sizes) for _, sizes in groups)
    key_heads, tall = key_width // HEAD_SIZE, query_width // key_width * SPAN
    at = 2 + len(blocks)
    return pl.pallas_call(
        functools.partial(attend_kernel, chips, groups, known, prior, query_width, key_width),
        in_specs=[pl.BlockSpec(memory_space=pltpu.SMEM)] * 2
        + [pl.BlockSpec(memory_space=pl.ANY)] * (len(blocks) + len(outputs)),
        out_specs=[pl.BlockSpec(memory_space=pl.ANY)] * 2
        + [pl.BlockSpec(memory_space=pltpu.VMEM)],
        out_shape=[
            jax.ShapeDtypeStruct((slots, query_width), BF16),
            jax.ShapeDtypeStruct((2, slots, key_width), BF16),
            jax.ShapeDtypeStruct((8, 128), F32),
        ],
        input_output_aliases={at + index: index for index in range(len(outputs))},
        scratch_shapes=[
            pltpu.VMEM((slots, query_width), BF16),
            pltpu.VMEM((2, slots, key_width), BF16),
            pltpu.VMEM((total + TILE + ALIGN, width), BF16),
            pltpu.VMEM((key_heads, tall, HEAD_SIZE), BF16),
            pltpu.VMEM((key_heads, slots // TILE + 1, tall, TILE), F32),
            pltpu.VMEM((key_heads, tall, TILE), F32),
            pltpu.SemaphoreType.DMA((copies,)),
            pltpu.SemaphoreType.DMA((slots // SPAN + 1,)),
        ],
        compiler_params=pltpu.CompilerParams(vmem_limit_bytes=16 * MEBI),
        name="attend",
    )(lengths, plan, *blocks, *outputs)


def shift_chips(value, hop, chips):
    pairs = [(2 * x + c, 2 * ((x + hop) % chips) + c) for x in range(chips) for c in range(2)]
    return lax.ppermute(value, "req", pairs)


def swap_cores(value, chips):
    return lax.ppermute(value, "req", [(d, d ^ 1) for d in range(2 * chips)])


def local(
    chips, shards, tokens, norm_gain, w_query, key_weight, value_weight, lengths, plan
):
    workers = 2 * chips
    slots = tokens.shape[0]
    live = slots // 2
    sizes = [live * share // sum(SHARES) // ALIGN * ALIGN for share in SHARES]
    sizes[-1] = live - sum(sizes[:-1])
    bases = [workers * sum(sizes[:chunk]) for chunk in range(len(sizes))]
    weights = [w_query, key_weight, value_weight]
    gain = norm_gain.astype(F32).reshape(1, -1)
    halfway = HEAD_SIZE // 2
    frequency = np.exp(-np.arange(halfway) * 2.0 / HEAD_SIZE * math.log(500000.0))
    frequency = jnp.asarray(np.tile(frequency, 2)[None, :], F32)

    twin = swap_cores(tokens, chips)
    first = deal(chips, bases[:1], sizes[:1], lengths, [tokens], [False])
    dealt = [
        *deal(chips, bases[:1], sizes[:1], lengths, [twin], [True], first),
        *deal(chips, bases[1:], sizes[1:], lengths, [tokens, twin], [False, True]),
    ]
    homes, aways = dealt[::2], dealt[1::2]
    routes, masks = routes_of(shards)
    direct = [at + 1 for at, (source, _) in enumerate(routes) if source == 0]
    kinds = {"first": [0, *direct]}
    kinds["late"] = [piece for piece in range(len(masks)) if piece not in kinds["first"]]
    relayed = [piece for piece in direct if piece in {source for source, _ in routes}]

    groups = [([base], [rows]) for base, rows in zip(bases, sizes)]
    widths = w_query.shape[1], key_weight.shape[1]

    def add(kind, chunk, carried=()):
        pieces = [lines[chunk][piece] for piece in kinds[kind]]
        final = kind == "late"
        turned = turns[chunk] if final else ()
        offsets = [masks[piece] for piece in kinds[kind]]
        return project(final, shards, offsets, pieces, gain, weights, carried, turned)

    def from_chips(block):
        return [shift_chips(block, hop, chips) for hop in range(1, chips)]

    def all_blocks(block, arrived):
        return [leaf for piece in (block, *arrived) for leaf in (piece, swap_cores(piece, chips))]

    def start(line, group):
        for index, (source, distance) in enumerate(routes):
            if index + 1 in group:
                pairs = [(at, at ^ distance) for at in range(shards)]
                line[index + 1] = lax.ppermute(line[source], "tp", pairs)

    lines, own, sent = [], [], []
    last = len(sizes) - 1

    def finish(chunk):
        own.append(add("late", chunk, add("first", chunk))[0])
        sent.append(from_chips(own[-1]))

    def fence(chunk, block):
        passed, anchors = [], []
        if chunk:
            before = lines[chunk - 1]
            passed = [before[piece] for piece in relayed]
            anchors += [before[piece] for piece in direct if piece not in relayed]
        if chunk == 1:
            weights[0], token = load(w_query, lines[0][0])
            anchors.append(token)
        if 1 < chunk <= last:
            finish(chunk - 2)
            anchors.append(own[-1])
        if chunk > 2:
            anchors += sent[chunk - 3]
        if passed:
            passed = after([*passed, *block], anchors)
            before.update(zip(relayed, passed))
            block = passed[len(relayed) :]
        return block

    for chunk in range(last + 1):
        arrived = [shift_chips(aways[chunk][hop - 1], hop, chips) for hop in range(1, chips)]
        later = aways[chunk + 1 : chunk + 2]
        block, aways[chunk + 1 : chunk + 2] = merge(homes[chunk], arrived, later)
        lines.append({0: fence(chunk, [block])[0]})
        if chunk:
            start(lines[-2], kinds["late"])
        start(lines[-1], direct)
        if chunk == 1:
            turns = angles(groups, lengths, frequency, lines[1][0])
    fence(last + 1, [])
    start(lines[-1], kinds["late"])
    for chunk in (last - 1, last):
        finish(chunk)
    blocks = []
    for at in range(last):
        blocks += all_blocks(own[at], after(sent[at], own[at + 1 : at + 2]))
    sent.append(from_chips(own[last]))
    known = workers * sum(sizes[:-1])
    common = widths, slots, lengths, plan
    *outputs, token = attend(chips, groups[:-1], known, 0, *common, blocks, ())
    blocks += all_blocks(own[last], after(sent[last], [token]))
    return tuple(attend(chips, groups, workers * live, known, *common, blocks, outputs)[:2])


def solution(mesh):
    placed = (
        P(("groups", "req"), "tp"),
        P(),
        P(None, "tp"),
        P(None, "tp"),
        P(None, "tp"),
        P("groups"),
        P("groups"),
    )
    return jax.shard_map(
        functools.partial(local, mesh.shape["req"] // 2, mesh.shape["tp"]),
        mesh=mesh,
        in_specs=placed,
        out_specs=(P(("groups", "req"), "tp"), P(None, ("groups", "req"), "tp")),
        check_vma=False,
    )
```

profile of v0, /device:TPU:0, one launch (start us, length us, event | category | flops | bytes accessed | tf_op | source)
XLA Modules:
  0.0 113.0 jit_solution(16999428270193005432)
XLA Ops:
  0.6 0.5 collective-permute-start
  1.1 1.6 %copy-done.2 = bf16[512,2048]{1,0:T(8,128)(2,1)S(1)} copy-done((bf16[512,2048]{1,0:T(8,128)(2,1)S(1)}, bf16[512,2048]{1,0:T(8,128)(2,1)}, u32[]{:S(2)}) %copy-start.2) | copy-done | bytes 2097176
  2.7 0.7 copy-done.4
  3.4 1.6 %deal.3 = (bf16[48,2048]{1,0:T(8,128)(2,1)S(1)}, bf16[1,48,2048]{2,1,0:T(8,128)(2,1)S(1)}) custom-call(s32[4]{0:T(128)S(1)} %copy-done.4, bf16[512,2048]{1,0:T(8,128)(2,1)S(1)} %copy-done.2), custom_call_target="tpu_custom_call" | custom-call | tf_op jit(solution)/shard_map/deal/pallas_call | solution.py:78
  5.0 0.1 collective-permute-done.refs_0_.refs_1_
  5.1 1.7 %deal.4 = (bf16[48,2048]{1,0:T(8,128)(2,1)S(1)}, bf16[1,48,2048]{2,1,0:T(8,128)(2,1)S(1)}) custom-call(s32[4]{0:T(128)S(1)} %copy-done.4, bf16[512,2048]{1,0:T(8,128)(2,1)S(1)} %collective-permute-done.refs_0_.refs_1_, bf16[48,2048]{1,0:T(8,128)(2,1)S(1)} %get-tuple-element.47.refs_1_, bf16[1,48,2048]{2,1,0:T(8,128)(2,1)S(1)} %get-tuple-element.48.refs_2_), custom_call_target="tpu_custom_call" | custom-call | tf_op jit(solution)/shard_map/deal/pallas_call | solution.py:78
  6.8 2.9 %collective-permute-start.1 = (bf16[48,2048]{1,0:T(8,128)(2,1)S(1)}, bf16[48,2048]{1,0:T(8,128)(2,1)S(1)}, u32[]{:S(2)}, u32[]{:S(2)}) collective-permute-start(bf16[48,2048]{1,0:T(8,128)(2,1)S(1)} %bitcast.16), channel_id=1, source_target_pairs={{0,8},{4,12},{8,0},{12,4},{1,9},{5,13},{9,1},{13,5},{2,10},{6,14},... | collective-permute-start | bytes 589832 | tf_op jit(solution)/shard_map/ppermute | solution.py:520
  9.7 5.4 %deal.5 = (bf16[80,2048]{1,0:T(8,128)(2,1)S(1)}, bf16[1,80,2048]{2,1,0:T(8,128)(2,1)S(1)}, bf16[80,2048]{1,0:T(8,128)(2,1)S(1)}, bf16[1,80,2048]{2,1,0:T(8,128)(...) custom-call(s32[4]{0:T(128)S(1)} %copy-done.4, bf16[512,2048]{1,0:T(8,128)(2,1)S(1)} %copy-done.3, ...), custom_call_target="tpu_custom_call" | custom-call | tf_op jit(solution)/shard_map/deal/pallas_call | solution.py:78
  15.1 0.0 collective-permute-done.1.refs_0_
  15.2 1.6 %collective-permute-start.3 = (bf16[80,2048]{1,0:T(8,128)(2,1)S(1)}, bf16[80,2048]{1,0:T(8,128)(2,1)S(1)}, u32[]{:S(2)}, u32[]{:S(2)}) collective-permute-start(bf16[80,2048]{1,0:T(8,128)(2,1)S(1)} %bitcast.13), channel_id=1, source_target_pairs={{0,8},{4,12},{8,0},{12,4},{1,9},{5,13},{9,1},{13,5},{2,10},{6,14},... | collective-permute-start | bytes 983048 | tf_op jit(solution)/shard_map/ppermute | solution.py:520
  16.8 1.6 %collective-permute-start.4 = (bf16[48,2048]{1,0:T(8,128)(2,1)S(1)}, bf16[48,2048]{1,0:T(8,128)(2,1)S(1)}, u32[]{:S(2)}, u32[]{:S(2)}) collective-permute-start(bf16[48,2048]{1,0:T(8,128)(2,1)S(1)} %get-tuple-element.52.anchor_ref.refs_0_), channel_id=1, source_target_pairs={{0,1},{1,0},{2,3},{3,2},{4,5},{5,4},{6,7},{7,6},{8,9},{9,8},{10,11... | collective-permute-start | bytes 589832 | tf_op jit(solution)/shard_map/ppermute | solution.py:575
  18.3 2.6 %collective-permute-start.2 = (bf16[48,2048]{1,0:T(8,128)(2,1)S(1)}, bf16[48,2048]{1,0:T(8,128)(2,1)S(1)}, u32[]{:S(2)}, u32[]{:S(2)}) collective-permute-start(bf16[48,2048]{1,0:T(8,128)(2,1)S(1)} %get-tuple-element.52.anchor_ref.refs_0_), channel_id=1, source_target_pairs={{0,2},{1,3},{2,0},{3,1},{4,6},{5,7},{6,4},{7,5},{8,10},{9,11},{10,... | collective-permute-start | bytes 589832 | tf_op jit(solution)/shard_map/ppermute | solution.py:575
  20.9 6.1 %load.1 = (bf16[8192,1024]{1,0:T(8,128)(2,1)S(1)}, f32[8,128]{1,0:T(8,128)S(1)}) custom-call(bf16[8192,1024]{1,0:T(8,128)(2,1)} %weight_ref.1, bf16[48,2048]{1,0:T(8,128)(2,1)S(1)} %get-tuple-element.52.anchor_ref.refs_0_), custom_call_target="tpu_custom_call" | custom-call | tf_op jit(solution)/shard_map/load/pallas_call | solution.py:198
  27.1 0.6 collective-permute-start.9
  27.7 0.0 collective-permute-done.4.refs_2_
  27.7 1.4 %collective-permute-done.2.refs_0_ = bf16[48,2048]{1,0:T(8,128)(2,1)S(1)} collective-permute-done((bf16[48,2048]{1,0:T(8,128)(2,1)S(1)}, bf16[48,2048]{1,0:T(8,128)(2,1)S(1)}, u32[]{:S(2)}, u32[]{:S(2)}) %collective-permute-start.2) | collective-permute-done | bytes 196640 | tf_op jit(solution)/shard_map/ppermute | solution.py:575
  29.1 0.4 collective-permute-start.10
  29.5 2.7 %collective-permute-start.8 = (bf16[80,2048]{1,0:T(8,128)(2,1)S(1)}, bf16[80,2048]{1,0:T(8,128)(2,1)S(1)}, u32[]{:S(2)}, u32[]{:S(2)}) collective-permute-start(bf16[80,2048]{1,0:T(8,128)(2,1)S(1)} %get-tuple-element.62.anchor_ref.refs_0_), channel_id=1, source_target_pairs={{0,2},{1,3},{2,0},{3,1},{4,6},{5,7},{6,4},{7,5},{8,10},{9,11},{10,... | collective-permute-start | bytes 983048 | tf_op jit(solution)/shard_map/ppermute | solution.py:575
  32.2 0.0 collective-permute-start.5
  32.2 1.1 angles.1
  33.3 4.0 %project.8 = (f32[48,1536]{1,0:T(8,128)S(1)}, f32[48,128]{1,0:T(8,128)S(1)}) custom-call(bf16[48,2048]{1,0:T(8,128)(2,1)S(1)} %get-tuple-element.52.anchor_ref.refs_0_, bf16[48,2048]{1,0:T(8,128)(2,1)S(1)} %get-tuple-element.58.refs_1_, bf16[48,2048]{1,0:T(8,128)(2,1)S(1)} %collective-permute-done.4.refs_2_, f32[1,8192]{1,0:T(1,128)S(1)} %bitcast.5, ...), custom_call_target="tpu_custom_call" | custom-call | tf_op jit(solution)/shard_map/project/pallas_call | solution.py:273
  37.4 9.9 %collective-permute-done.5.refs_0_ = bf16[48,2048]{1,0:T(8,128)(2,1)S(1)} collective-permute-done((bf16[48,2048]{1,0:T(8,128)(2,1)S(1)}, bf16[48,2048]{1,0:T(8,128)(2,1)S(1)}, u32[]{:S(2)}, u32[]{:S(2)}) %collective-permute-start.5) | collective-permute-done | bytes 196640 | tf_op jit(solution)/shard_map/ppermute | solution.py:575
  47.3 1.6 %project.9.refs_3_.refs_0_ = bf16[48,1536]{1,0:T(8,128)(2,1)S(1)} custom-call(bf16[48,2048]{1,0:T(8,128)(2,1)S(1)} %collective-permute-done.5.refs_0_, f32[1,8192]{1,0:T(1,128)S(1)} %bitcast.6, bf16[8192,1024]{1,0:T(8,128)(2,1)S(1)} %get-tuple-element.59.refs_4_.refs_2_, bf16[8192,256]{1,0:T(8,128)(2,1)S(1)} %copy-done, bf16[8192,256]{1,0:T(8,128)(2,1)S(1)} %copy-done.1, ...), custom_call_target="tpu_custom_call" | custom-call | tf_op jit(solution)/shard_map/project/pallas_call | solution.py:273
  48.9 0.0 collective-permute-done.9.refs_0_
  49.0 1.1 %collective-permute-start.11 = (bf16[80,2048]{1,0:T(8,128)(2,1)S(1)}, bf16[80,2048]{1,0:T(8,128)(2,1)S(1)}, u32[]{:S(2)}, u32[]{:S(2)}) collective-permute-start(bf16[80,2048]{1,0:T(8,128)(2,1)S(1)} %get-tuple-element.69.refs_1_), channel_id=1, source_target_pairs={{0,1},{1,0},{2,3},{3,2},{4,5},{5,4},{6,7},{7,6},{8,9},{9,8},{10,11... | collective-permute-start | bytes 983048 | tf_op jit(solution)/shard_map/ppermute | solution.py:575
  50.1 2.0 %collective-permute-start.15 = (bf16[80,2048]{1,0:T(8,128)(2,1)S(1)}, bf16[80,2048]{1,0:T(8,128)(2,1)S(1)}, u32[]{:S(2)}, u32[]{:S(2)}) collective-permute-start(bf16[80,2048]{1,0:T(8,128)(2,1)S(1)} %get-tuple-element.74.refs_0_), channel_id=1, source_target_pairs={{0,2},{1,3},{2,0},{3,1},{4,6},{5,7},{6,4},{7,5},{8,10},{9,11},{10,... | collective-permute-start | bytes 983048 | tf_op jit(solution)/shard_map/ppermute | solution.py:575
  52.1 0.1 collective-permute-start.17
  52.1 1.5 %collective-permute-start.16 = (bf16[48,2048]{1,0:T(8,128)(2,1)S(1)}, bf16[48,2048]{1,0:T(8,128)(2,1)S(1)}, u32[]{:S(2)}, u32[]{:S(2)}) collective-permute-start(bf16[48,2048]{1,0:T(8,128)(2,1)S(1)} %bitcast.15), channel_id=1, source_target_pairs={{0,8},{4,12},{8,0},{12,4},{1,9},{5,13},{9,1},{13,5},{2,10},{6,14},... | collective-permute-start | bytes 589832 | tf_op jit(solution)/shard_map/ppermute | solution.py:520
  53.6 0.6 collective-permute-start.7
  54.2 4.3 %project.10 = (f32[80,1536]{1,0:T(8,128)S(1)}, f32[80,128]{1,0:T(8,128)S(1)}) custom-call(bf16[80,2048]{1,0:T(8,128)(2,1)S(1)} %get-tuple-element.62.anchor_ref.refs_0_, bf16[80,2048]{1,0:T(8,128)(2,1)S(1)} %get-tuple-element.69.refs_1_, bf16[80,2048]{1,0:T(8,128)(2,1)S(1)} %collective-permute-done.10.refs_2_, f32[1,8192]{1,0:T(1,128)S(1)} %bitcast.7, ...), custom_call_target="tpu_custom_call" | custom-call | tf_op jit(solution)/shard_map/project/pallas_call | solution.py:273
  58.4 0.8 collective-permute-done.16.refs_0_
  59.3 6.8 %collective-permute-done.11.refs_0_ = bf16[80,2048]{1,0:T(8,128)(2,1)S(1)} collective-permute-done((bf16[80,2048]{1,0:T(8,128)(2,1)S(1)}, bf16[80,2048]{1,0:T(8,128)(2,1)S(1)}, u32[]{:S(2)}, u32[]{:S(2)}) %collective-permute-start.11) | collective-permute-done | bytes 327712 | tf_op jit(solution)/shard_map/ppermute | solution.py:575
  66.1 1.7 %project.11.refs_1_.refs_3_.refs_4_ = bf16[80,1536]{1,0:T(8,128)(2,1)S(1)} custom-call(bf16[80,2048]{1,0:T(8,128)(2,1)S(1)} %collective-permute-done.11.refs_0_, f32[1,8192]{1,0:T(1,128)S(1)} %bitcast.8, bf16[8192,1024]{1,0:T(8,128)(2,1)S(1)} %get-tuple-element.59.refs_4_.refs_2_, bf16[8192,256]{1,0:T(8,128)(2,1)S(1)} %copy-done, ...), custom_call_target="tpu_custom_call" | custom-call | tf_op jit(solution)/shard_map/project/pallas_call | solution.py:273
  67.8 0.0 collective-permute-done.7.refs_0_.refs_4_
  67.8 0.0 collective-permute-done.15.refs_0_
  67.9 3.1 %collective-permute-done.17.refs_2_ = bf16[80,2048]{1,0:T(8,128)(2,1)S(1)} collective-permute-done((bf16[80,2048]{1,0:T(8,128)(2,1)S(1)}, bf16[80,2048]{1,0:T(8,128)(2,1)S(1)}, u32[]{:S(2)}, u32[]{:S(2)}) %collective-permute-start.17) | collective-permute-done | bytes 327712 | tf_op jit(solution)/shard_map/ppermute | solution.py:575
  71.0 0.3 collective-permute-start.18
  71.3 2.4 %collective-permute-start.14 = (bf16[80,1536]{1,0:T(8,128)(2,1)S(1)}, bf16[80,1536]{1,0:T(8,128)(2,1)S(1)}, u32[]{:S(2)}, u32[]{:S(2)}) collective-permute-start(bf16[80,1536]{1,0:T(8,128)(2,1)S(1)} %project.11.refs_1_.refs_3_.refs_4_), channel_id=1, source_target_pairs={{0,8},{4,12},{8,0},{12,4},{1,9},{5,13},{9,1},{13,5},{2,10},{6,14},... | collective-permute-start | bytes 737288 | tf_op jit(solution)/shard_map/ppermute | solution.py:520
  73.7 2.0 %collective-permute-start.22 = (bf16[48,2048]{1,0:T(8,128)(2,1)S(1)}, bf16[48,2048]{1,0:T(8,128)(2,1)S(1)}, u32[]{:S(2)}, u32[]{:S(2)}) collective-permute-start(bf16[48,2048]{1,0:T(8,128)(2,1)S(1)} %get-tuple-element.82.refs_0_), channel_id=1, source_target_pairs={{0,2},{1,3},{2,0},{3,1},{4,6},{5,7},{6,4},{7,5},{8,10},{9,11},{10,... | collective-permute-start | bytes 589832 | tf_op jit(solution)/shard_map/ppermute | solution.py:575
  75.6 0.3 collective-permute-start.23
  75.9 4.3 %project.12 = (f32[80,1536]{1,0:T(8,128)S(1)}, f32[80,128]{1,0:T(8,128)S(1)}) custom-call(bf16[80,2048]{1,0:T(8,128)(2,1)S(1)} %get-tuple-element.74.refs_0_, bf16[80,2048]{1,0:T(8,128)(2,1)S(1)} %get-tuple-element.77.refs_1_, bf16[80,2048]{1,0:T(8,128)(2,1)S(1)} %collective-permute-done.17.refs_2_, f32[1,8192]{1,0:T(1,128)S(1)} %bitcast.9, ...), custom_call_target="tpu_custom_call" | custom-call | tf_op jit(solution)/shard_map/project/pallas_call | solution.py:273
  80.2 4.6 %collective-permute-done.18.refs_0_ = bf16[80,2048]{1,0:T(8,128)(2,1)S(1)} collective-permute-done((bf16[80,2048]{1,0:T(8,128)(2,1)S(1)}, bf16[80,2048]{1,0:T(8,128)(2,1)S(1)}, u32[]{:S(2)}, u32[]{:S(2)}) %collective-permute-start.18) | collective-permute-done | bytes 327712 | tf_op jit(solution)/shard_map/ppermute | solution.py:575
  84.8 1.7 %project.13.refs_1_.refs_8_ = bf16[80,1536]{1,0:T(8,128)(2,1)S(1)} custom-call(bf16[80,2048]{1,0:T(8,128)(2,1)S(1)} %collective-permute-done.18.refs_0_, f32[1,8192]{1,0:T(1,128)S(1)} %bitcast.10, bf16[8192,1024]{1,0:T(8,128)(2,1)S(1)} %get-tuple-element.59.refs_4_.refs_2_, bf16[8192,256]{1,0:T(8,128)(2,1)S(1)} %copy-done, bf16[8192,256]{1,0:T(8,128)(2,1)S(1)} %copy-done.1, ...), custom_call_target="tpu_custom_call" | custom-call | tf_op jit(solution)/shard_map/project/pallas_call | solution.py:273
  86.5 0.3 collective-permute-start.21
  86.8 0.4 collective-permute-done.23.refs_1_.refs_2_
  87.3 0.0 collective-permute-done.14.refs_0_.refs_2_
  87.3 1.0 collective-permute-start.24
  88.3 0.5 collective-permute-start.12
  88.8 4.2 %project.14 = (f32[48,1536]{1,0:T(8,128)S(1)}, f32[48,128]{1,0:T(8,128)S(1)}) custom-call(bf16[48,2048]{1,0:T(8,128)(2,1)S(1)} %get-tuple-element.82.refs_0_, bf16[48,2048]{1,0:T(8,128)(2,1)S(1)} %after.13.refs_1_, bf16[48,2048]{1,0:T(8,128)(2,1)S(1)} %collective-permute-done.23.refs_1_.refs_2_, f32[1,8192]{1,0:T(1,128)S(1)} %bitcast.11, ...), custom_call_target="tpu_custom_call" | custom-call | tf_op jit(solution)/shard_map/project/pallas_call | solution.py:273
  93.0 0.0 collective-permute-done.24.refs_0_
  93.0 0.6 collective-permute-start.20
  93.6 1.6 %project.15.refs_1_.refs_12_ = bf16[48,1536]{1,0:T(8,128)(2,1)S(1)} custom-call(bf16[48,2048]{1,0:T(8,128)(2,1)S(1)} %collective-permute-done.24.refs_0_, f32[1,8192]{1,0:T(1,128)S(1)} %bitcast.12, bf16[8192,1024]{1,0:T(8,128)(2,1)S(1)} %get-tuple-element.59.refs_4_.refs_2_, bf16[8192,256]{1,0:T(8,128)(2,1)S(1)} %copy-done, bf16[8192,256]{1,0:T(8,128)(2,1)S(1)} %copy-done.1, ...), custom_call_target="tpu_custom_call" | custom-call | tf_op jit(solution)/shard_map/project/pallas_call | solution.py:273
  95.2 0.0 collective-permute-done.21.refs_0_
  95.2 0.1 collective-permute-start.19
  95.3 0.0 collective-permute-done.6.refs_1_
  95.3 0.5 collective-permute-start.25
  95.8 0.0 collective-permute-done.12.refs_3_
  95.8 0.9 collective-permute-start.27
  96.7 0.1 collective-permute-start.26
  96.8 0.3 collective-permute-done.25.refs_11_
  97.1 8.6 %attend.2 = (bf16[512,1024]{1,0:T(8,128)(2,1)}, bf16[2,512,256]{2,1,0:T(8,128)(2,1)}, f32[8,128]{1,0:T(8,128)S(1)}) custom-call(s32[4]{0:T(128)S(1)} %copy-done.5, s32[16]{0:T(128)S(1)} %copy-done.6, bf16[48,1536]{1,0:T(8,128)(2,1)S(1)} %project.9.refs_3_.refs_0_, bf16[48,1536]{1,0:T(8,128)(2,1)S(1)} %collective-permute-done.6.refs_1_, ...), custom_call_target="tpu_custom_call" | custom-call | tf_op jit(solution)/shard_map/attend/pallas_call | solution.py:491
  105.7 1.2 %collective-permute-start.28 = (bf16[48,1536]{1,0:T(8,128)(2,1)S(1)}, bf16[48,1536]{1,0:T(8,128)(2,1)S(1)}, u32[]{:S(2)}, u32[]{:S(2)}) collective-permute-start(bf16[48,1536]{1,0:T(8,128)(2,1)S(1)} %after.15.refs_14_), channel_id=1, source_target_pairs={{0,4},{4,0},{8,12},{12,8},{1,5},{5,1},{9,13},{13,9},{2,6},{6,2},{1... | collective-permute-start | bytes 442376 | tf_op jit(solution)/shard_map/ppermute | solution.py:524
  106.9 1.0 collective-permute-done.28.refs_15_
  107.9 5.0 %attend.3 = (bf16[512,1024]{1,0:T(8,128)(2,1)}, bf16[2,512,256]{2,1,0:T(8,128)(2,1)}, f32[8,128]{1,0:T(8,128)}) custom-call(s32[4]{0:T(128)S(1)} %copy-done.5, s32[16]{0:T(128)S(1)} %copy-done.6, bf16[48,1536]{1,0:T(8,128)(2,1)S(1)} %project.9.refs_3_.refs_0_, ...), custom_call_target="tpu_custom_call", output_to_operand_aliasing={{0}: (18, {}), {1}: (19, {})} | custom-call | tf_op jit(solution)/shard_map/attend/pallas_call | solution.py:491
  (40 shorter events, 0.2 us)
Async XLA Ops:
  0.6 4.5 %collective-permute-start = (bf16[512,2048]{1,0:T(8,128)(2,1)}, bf16[512,2048]{1,0:T(8,128)(2,1)S(1)}, u32[]{:S(2)}, u32[]{:S(2)}) collective-permute-start(bf16[512,2048]{1,0:T(8,128)(2,1)} %refs_0_.3), channel_id=1, source_target_pairs={{0,4},{4,0},{8,12},{12,8},{1,5},{5,1},{9,13},{13,9},{2,6},{6,2},{1... | collective-permute-start | bytes 6291464 | tf_op jit(solution)/shard_map/ppermute | solution.py:524
  1.1 1.6 %copy-start.2 = (bf16[512,2048]{1,0:T(8,128)(2,1)S(1)}, bf16[512,2048]{1,0:T(8,128)(2,1)}, u32[]{:S(2)}) copy-start(bf16[512,2048]{1,0:T(8,128)(2,1)} %refs_0_.3) | copy-start | bytes 6291460
  2.7 0.7 copy-start.4
  3.4 6.3 %copy-start.3 = (bf16[512,2048]{1,0:T(8,128)(2,1)S(1)}, bf16[512,2048]{1,0:T(8,128)(2,1)}, u32[]{:S(2)}) copy-start(bf16[512,2048]{1,0:T(8,128)(2,1)} %refs_0_.3) | copy-start | bytes 6291460
  6.8 8.3 %collective-permute-start.1 = (bf16[48,2048]{1,0:T(8,128)(2,1)S(1)}, bf16[48,2048]{1,0:T(8,128)(2,1)S(1)}, u32[]{:S(2)}, u32[]{:S(2)}) collective-permute-start(bf16[48,2048]{1,0:T(8,128)(2,1)S(1)} %bitcast.16), channel_id=1, source_target_pairs={{0,8},{4,12},{8,0},{12,4},{1,9},{5,13},{9,1},{13,5},{2,10},{6,14},... | collective-permute-start | bytes 589832 | tf_op jit(solution)/shard_map/ppermute | solution.py:520
  15.2 11.8 %collective-permute-start.3 = (bf16[80,2048]{1,0:T(8,128)(2,1)S(1)}, bf16[80,2048]{1,0:T(8,128)(2,1)S(1)}, u32[]{:S(2)}, u32[]{:S(2)}) collective-permute-start(bf16[80,2048]{1,0:T(8,128)(2,1)S(1)} %bitcast.13), channel_id=1, source_target_pairs={{0,8},{4,12},{8,0},{12,4},{1,9},{5,13},{9,1},{13,5},{2,10},{6,14},... | collective-permute-start | bytes 983048 | tf_op jit(solution)/shard_map/ppermute | solution.py:520
  16.8 15.4 %copy-start.8 = (bf16[8192]{0:T(1024)(128)(2,1)S(1)}, bf16[8192]{0:T(1024)(128)(2,1)}, u32[]{:S(2)}) copy-start(bf16[8192]{0:T(1024)(128)(2,1)} %param.9) | copy-start | bytes 49156
  16.8 15.5 %copy-start.5 = (s32[4]{0:T(128)S(1)}, s32[4]{0:T(128)}, u32[]{:S(2)}) copy-start(s32[4]{0:T(128)} %lengths_ref.11) | copy-start | bytes 52
  16.8 15.5 %copy-start.7 = (f32[1,128]{1,0:T(1,128)S(1)}, f32[1,128]{1,0:T(1,128)}, u32[]{:S(2)}) copy-start(f32[1,128]{1,0:T(1,128)} %constant.2.clone.frequency_ref) | copy-start | bytes 1540
  16.8 10.9 %collective-permute-start.4 = (bf16[48,2048]{1,0:T(8,128)(2,1)S(1)}, bf16[48,2048]{1,0:T(8,128)(2,1)S(1)}, u32[]{:S(2)}, u32[]{:S(2)}) collective-permute-start(bf16[48,2048]{1,0:T(8,128)(2,1)S(1)} %get-tuple-element.52.anchor_ref.refs_0_), channel_id=1, source_target_pairs={{0,1},{1,0},{2,3},{3,2},{4,5},{5,4},{6,7},{7,6},{8,9},{9,8},{10,11... | collective-permute-start | bytes 589832 | tf_op jit(solution)/shard_map/ppermute | solution.py:575
  18.3 10.7 %collective-permute-start.2 = (bf16[48,2048]{1,0:T(8,128)(2,1)S(1)}, bf16[48,2048]{1,0:T(8,128)(2,1)S(1)}, u32[]{:S(2)}, u32[]{:S(2)}) collective-permute-start(bf16[48,2048]{1,0:T(8,128)(2,1)S(1)} %get-tuple-element.52.anchor_ref.refs_0_), channel_id=1, source_target_pairs={{0,2},{1,3},{2,0},{3,1},{4,6},{5,7},{6,4},{7,5},{8,10},{9,11},{10,... | collective-permute-start | bytes 589832 | tf_op jit(solution)/shard_map/ppermute | solution.py:575
  20.9 12.4 %copy-start = (bf16[8192,256]{1,0:T(8,128)(2,1)S(1)}, bf16[8192,256]{1,0:T(8,128)(2,1)}, u32[]{:S(2)}) copy-start(bf16[8192,256]{1,0:T(8,128)(2,1)} %refs_3_.7) | copy-start | bytes 12582916
  20.9 12.4 %copy-start.1 = (bf16[8192,256]{1,0:T(8,128)(2,1)S(1)}, bf16[8192,256]{1,0:T(8,128)(2,1)}, u32[]{:S(2)}) copy-start(bf16[8192,256]{1,0:T(8,128)(2,1)} %refs_4_.7) | copy-start | bytes 12582916
  27.1 21.8 %collective-permute-start.9 = (bf16[80,2048]{1,0:T(8,128)(2,1)S(1)}, bf16[80,2048]{1,0:T(8,128)(2,1)S(1)}, u32[]{:S(2)}, u32[]{:S(2)}) collective-permute-start(bf16[80,2048]{1,0:T(8,128)(2,1)S(1)} %bitcast.14), channel_id=1, source_target_pairs={{0,8},{4,12},{8,0},{12,4},{1,9},{5,13},{9,1},{13,5},{2,10},{6,14},... | collective-permute-start | bytes 983048 | tf_op jit(solution)/shard_map/ppermute | solution.py:520
  29.1 19.9 %collective-permute-start.10 = (bf16[80,2048]{1,0:T(8,128)(2,1)S(1)}, bf16[80,2048]{1,0:T(8,128)(2,1)S(1)}, u32[]{:S(2)}, u32[]{:S(2)}) collective-permute-start(bf16[80,2048]{1,0:T(8,128)(2,1)S(1)} %get-tuple-element.62.anchor_ref.refs_0_), channel_id=1, source_target_pairs={{0,1},{1,0},{2,3},{3,2},{4,5},{5,4},{6,7},{7,6},{8,9},{9,8},{10,11... | collective-permute-start | bytes 983048 | tf_op jit(solution)/shard_map/ppermute | solution.py:575
  29.5 19.4 %collective-permute-start.8 = (bf16[80,2048]{1,0:T(8,128)(2,1)S(1)}, bf16[80,2048]{1,0:T(8,128)(2,1)S(1)}, u32[]{:S(2)}, u32[]{:S(2)}) collective-permute-start(bf16[80,2048]{1,0:T(8,128)(2,1)S(1)} %get-tuple-element.62.anchor_ref.refs_0_), channel_id=1, source_target_pairs={{0,2},{1,3},{2,0},{3,1},{4,6},{5,7},{6,4},{7,5},{8,10},{9,11},{10,... | collective-permute-start | bytes 983048 | tf_op jit(solution)/shard_map/ppermute | solution.py:575
  32.2 15.1 %collective-permute-start.5 = (bf16[48,2048]{1,0:T(8,128)(2,1)S(1)}, bf16[48,2048]{1,0:T(8,128)(2,1)S(1)}, u32[]{:S(2)}, u32[]{:S(2)}) collective-permute-start(bf16[48,2048]{1,0:T(8,128)(2,1)S(1)} %get-tuple-element.58.refs_1_), channel_id=1, source_target_pairs={{0,1},{1,0},{2,3},{3,2},{4,5},{5,4},{6,7},{7,6},{8,9},{9,8},{10,11... | collective-permute-start | bytes 589832 | tf_op jit(solution)/shard_map/ppermute | solution.py:575
  49.0 17.2 %collective-permute-start.11 = (bf16[80,2048]{1,0:T(8,128)(2,1)S(1)}, bf16[80,2048]{1,0:T(8,128)(2,1)S(1)}, u32[]{:S(2)}, u32[]{:S(2)}) collective-permute-start(bf16[80,2048]{1,0:T(8,128)(2,1)S(1)} %get-tuple-element.69.refs_1_), channel_id=1, source_target_pairs={{0,1},{1,0},{2,3},{3,2},{4,5},{5,4},{6,7},{7,6},{8,9},{9,8},{10,11... | collective-permute-start | bytes 983048 | tf_op jit(solution)/shard_map/ppermute | solution.py:575
  50.1 17.7 %collective-permute-start.15 = (bf16[80,2048]{1,0:T(8,128)(2,1)S(1)}, bf16[80,2048]{1,0:T(8,128)(2,1)S(1)}, u32[]{:S(2)}, u32[]{:S(2)}) collective-permute-start(bf16[80,2048]{1,0:T(8,128)(2,1)S(1)} %get-tuple-element.74.refs_0_), channel_id=1, source_target_pairs={{0,2},{1,3},{2,0},{3,1},{4,6},{5,7},{6,4},{7,5},{8,10},{9,11},{10,... | collective-permute-start | bytes 983048 | tf_op jit(solution)/shard_map/ppermute | solution.py:575
  52.1 18.9 %collective-permute-start.17 = (bf16[80,2048]{1,0:T(8,128)(2,1)S(1)}, bf16[80,2048]{1,0:T(8,128)(2,1)S(1)}, u32[]{:S(2)}, u32[]{:S(2)}) collective-permute-start(bf16[80,2048]{1,0:T(8,128)(2,1)S(1)} %get-tuple-element.74.refs_0_), channel_id=1, source_target_pairs={{0,1},{1,0},{2,3},{3,2},{4,5},{5,4},{6,7},{7,6},{8,9},{9,8},{10,11... | collective-permute-start | bytes 983048 | tf_op jit(solution)/shard_map/ppermute | solution.py:575
  52.1 7.1 %collective-permute-start.16 = (bf16[48,2048]{1,0:T(8,128)(2,1)S(1)}, bf16[48,2048]{1,0:T(8,128)(2,1)S(1)}, u32[]{:S(2)}, u32[]{:S(2)}) collective-permute-start(bf16[48,2048]{1,0:T(8,128)(2,1)S(1)} %bitcast.15), channel_id=1, source_target_pairs={{0,8},{4,12},{8,0},{12,4},{1,9},{5,13},{9,1},{13,5},{2,10},{6,14},... | collective-permute-start | bytes 589832 | tf_op jit(solution)/shard_map/ppermute | solution.py:520
  53.6 14.2 %collective-permute-start.7 = (bf16[48,1536]{1,0:T(8,128)(2,1)S(1)}, bf16[48,1536]{1,0:T(8,128)(2,1)S(1)}, u32[]{:S(2)}, u32[]{:S(2)}) collective-permute-start(bf16[48,1536]{1,0:T(8,128)(2,1)S(1)} %project.9.refs_3_.refs_0_), channel_id=1, source_target_pairs={{0,8},{4,12},{8,0},{12,4},{1,9},{5,13},{9,1},{13,5},{2,10},{6,14},... | collective-permute-start | bytes 442376 | tf_op jit(solution)/shard_map/ppermute | solution.py:520
  71.0 13.9 %collective-permute-start.18 = (bf16[80,2048]{1,0:T(8,128)(2,1)S(1)}, bf16[80,2048]{1,0:T(8,128)(2,1)S(1)}, u32[]{:S(2)}, u32[]{:S(2)}) collective-permute-start(bf16[80,2048]{1,0:T(8,128)(2,1)S(1)} %get-tuple-element.77.refs_1_), channel_id=1, source_target_pairs={{0,1},{1,0},{2,3},{3,2},{4,5},{5,4},{6,7},{7,6},{8,9},{9,8},{10,11... | collective-permute-start | bytes 983048 | tf_op jit(solution)/shard_map/ppermute | solution.py:575
  71.3 16.0 %collective-permute-start.14 = (bf16[80,1536]{1,0:T(8,128)(2,1)S(1)}, bf16[80,1536]{1,0:T(8,128)(2,1)S(1)}, u32[]{:S(2)}, u32[]{:S(2)}) collective-permute-start(bf16[80,1536]{1,0:T(8,128)(2,1)S(1)} %project.11.refs_1_.refs_3_.refs_4_), channel_id=1, source_target_pairs={{0,8},{4,12},{8,0},{12,4},{1,9},{5,13},{9,1},{13,5},{2,10},{6,14},... | collective-permute-start | bytes 737288 | tf_op jit(solution)/shard_map/ppermute | solution.py:520
  73.7 13.2 %collective-permute-start.22 = (bf16[48,2048]{1,0:T(8,128)(2,1)S(1)}, bf16[48,2048]{1,0:T(8,128)(2,1)S(1)}, u32[]{:S(2)}, u32[]{:S(2)}) collective-permute-start(bf16[48,2048]{1,0:T(8,128)(2,1)S(1)} %get-tuple-element.82.refs_0_), channel_id=1, source_target_pairs={{0,2},{1,3},{2,0},{3,1},{4,6},{5,7},{6,4},{7,5},{8,10},{9,11},{10,... | collective-permute-start | bytes 589832 | tf_op jit(solution)/shard_map/ppermute | solution.py:575
  75.6 11.7 %collective-permute-start.23 = (bf16[48,2048]{1,0:T(8,128)(2,1)S(1)}, bf16[48,2048]{1,0:T(8,128)(2,1)S(1)}, u32[]{:S(2)}, u32[]{:S(2)}) collective-permute-start(bf16[48,2048]{1,0:T(8,128)(2,1)S(1)} %get-tuple-element.82.refs_0_), channel_id=1, source_target_pairs={{0,1},{1,0},{2,3},{3,2},{4,5},{5,4},{6,7},{7,6},{8,9},{9,8},{10,11... | collective-permute-start | bytes 589832 | tf_op jit(solution)/shard_map/ppermute | solution.py:575
  86.5 8.7 %collective-permute-start.21 = (bf16[80,1536]{1,0:T(8,128)(2,1)S(1)}, bf16[80,1536]{1,0:T(8,128)(2,1)S(1)}, u32[]{:S(2)}, u32[]{:S(2)}) collective-permute-start(bf16[80,1536]{1,0:T(8,128)(2,1)S(1)} %project.13.refs_1_.refs_8_), channel_id=1, source_target_pairs={{0,8},{4,12},{8,0},{12,4},{1,9},{5,13},{9,1},{13,5},{2,10},{6,14},... | collective-permute-start | bytes 737288 | tf_op jit(solution)/shard_map/ppermute | solution.py:520
  87.3 5.7 %collective-permute-start.24 = (bf16[48,2048]{1,0:T(8,128)(2,1)S(1)}, bf16[48,2048]{1,0:T(8,128)(2,1)S(1)}, u32[]{:S(2)}, u32[]{:S(2)}) collective-permute-start(bf16[48,2048]{1,0:T(8,128)(2,1)S(1)} %after.13.refs_1_), channel_id=1, source_target_pairs={{0,1},{1,0},{2,3},{3,2},{4,5},{5,4},{6,7},{7,6},{8,9},{9,8},{10,11... | collective-permute-start | bytes 589832 | tf_op jit(solution)/shard_map/ppermute | solution.py:575
  88.3 7.0 %collective-permute-start.6 = (bf16[48,1536]{1,0:T(8,128)(2,1)S(1)}, bf16[48,1536]{1,0:T(8,128)(2,1)S(1)}, u32[]{:S(2)}, u32[]{:S(2)}) collective-permute-start(bf16[48,1536]{1,0:T(8,128)(2,1)S(1)} %project.9.refs_3_.refs_0_), channel_id=1, source_target_pairs={{0,4},{4,0},{8,12},{12,8},{1,5},{5,1},{9,13},{13,9},{2,6},{6,2},{1... | collective-permute-start | bytes 442376 | tf_op jit(solution)/shard_map/ppermute | solution.py:524
  88.3 7.5 %collective-permute-start.12 = (bf16[48,1536]{1,0:T(8,128)(2,1)S(1)}, bf16[48,1536]{1,0:T(8,128)(2,1)S(1)}, u32[]{:S(2)}, u32[]{:S(2)}) collective-permute-start(bf16[48,1536]{1,0:T(8,128)(2,1)S(1)} %after.10.refs_2_), channel_id=1, source_target_pairs={{0,4},{4,0},{8,12},{12,8},{1,5},{5,1},{9,13},{13,9},{2,6},{6,2},{1... | collective-permute-start | bytes 442376 | tf_op jit(solution)/shard_map/ppermute | solution.py:524
  88.8 7.9 %collective-permute-start.13 = (bf16[80,1536]{1,0:T(8,128)(2,1)S(1)}, bf16[80,1536]{1,0:T(8,128)(2,1)S(1)}, u32[]{:S(2)}, u32[]{:S(2)}) collective-permute-start(bf16[80,1536]{1,0:T(8,128)(2,1)S(1)} %project.11.refs_1_.refs_3_.refs_4_), channel_id=1, source_target_pairs={{0,4},{4,0},{8,12},{12,8},{1,5},{5,1},{9,13},{13,9},{2,6},{6,2},{1... | collective-permute-start | bytes 737288 | tf_op jit(solution)/shard_map/ppermute | solution.py:524
  93.0 3.7 %collective-permute-start.20 = (bf16[80,1536]{1,0:T(8,128)(2,1)S(1)}, bf16[80,1536]{1,0:T(8,128)(2,1)S(1)}, u32[]{:S(2)}, u32[]{:S(2)}) collective-permute-start(bf16[80,1536]{1,0:T(8,128)(2,1)S(1)} %project.13.refs_1_.refs_8_), channel_id=1, source_target_pairs={{0,4},{4,0},{8,12},{12,8},{1,5},{5,1},{9,13},{13,9},{2,6},{6,2},{1... | collective-permute-start | bytes 737288 | tf_op jit(solution)/shard_map/ppermute | solution.py:524
  93.6 3.5 %copy-start.6 = (s32[16]{0:T(128)S(1)}, s32[16]{0:T(128)}, u32[]{:S(2)}) copy-start(s32[16]{0:T(128)} %plan_ref.3) | copy-start | bytes 196
  95.2 1.6 %collective-permute-start.19 = (bf16[80,1536]{1,0:T(8,128)(2,1)S(1)}, bf16[80,1536]{1,0:T(8,128)(2,1)S(1)}, u32[]{:S(2)}, u32[]{:S(2)}) collective-permute-start(bf16[80,1536]{1,0:T(8,128)(2,1)S(1)} %after.12.refs_6_), channel_id=1, source_target_pairs={{0,4},{4,0},{8,12},{12,8},{1,5},{5,1},{9,13},{13,9},{2,6},{6,2},{1... | collective-permute-start | bytes 737288 | tf_op jit(solution)/shard_map/ppermute | solution.py:524
  95.3 1.8 %collective-permute-start.25 = (bf16[80,1536]{1,0:T(8,128)(2,1)S(1)}, bf16[80,1536]{1,0:T(8,128)(2,1)S(1)}, u32[]{:S(2)}, u32[]{:S(2)}) collective-permute-start(bf16[80,1536]{1,0:T(8,128)(2,1)S(1)} %after.14.refs_10_), channel_id=1, source_target_pairs={{0,4},{4,0},{8,12},{12,8},{1,5},{5,1},{9,13},{13,9},{2,6},{6,2},{1... | collective-permute-start | bytes 737288 | tf_op jit(solution)/shard_map/ppermute | solution.py:524
  95.8 9.9 %collective-permute-start.27 = (bf16[48,1536]{1,0:T(8,128)(2,1)S(1)}, bf16[48,1536]{1,0:T(8,128)(2,1)S(1)}, u32[]{:S(2)}, u32[]{:S(2)}) collective-permute-start(bf16[48,1536]{1,0:T(8,128)(2,1)S(1)} %project.15.refs_1_.refs_12_), channel_id=1, source_target_pairs={{0,8},{4,12},{8,0},{12,4},{1,9},{5,13},{9,1},{13,5},{2,10},{6,14},... | collective-permute-start | bytes 442376 | tf_op jit(solution)/shard_map/ppermute | solution.py:520
  96.7 10.2 %collective-permute-start.26 = (bf16[48,1536]{1,0:T(8,128)(2,1)S(1)}, bf16[48,1536]{1,0:T(8,128)(2,1)S(1)}, u32[]{:S(2)}, u32[]{:S(2)}) collective-permute-start(bf16[48,1536]{1,0:T(8,128)(2,1)S(1)} %project.15.refs_1_.refs_12_), channel_id=1, source_target_pairs={{0,4},{4,0},{8,12},{12,8},{1,5},{5,1},{9,13},{13,9},{2,6},{6,2},{1... | collective-permute-start | bytes 442376 | tf_op jit(solution)/shard_map/ppermute | solution.py:524
  105.7 2.2 %collective-permute-start.28 = (bf16[48,1536]{1,0:T(8,128)(2,1)S(1)}, bf16[48,1536]{1,0:T(8,128)(2,1)S(1)}, u32[]{:S(2)}, u32[]{:S(2)}) collective-permute-start(bf16[48,1536]{1,0:T(8,128)(2,1)S(1)} %after.15.refs_14_), channel_id=1, source_target_pairs={{0,4},{4,0},{8,12},{12,8},{1,5},{5,1},{9,13},{13,9},{2,6},{6,2},{1... | collective-permute-start | bytes 442376 | tf_op jit(solution)/shard_map/ppermute | solution.py:524
where the time goes:
time: 115 us; the launch traced here: 113 us
  Pallas kernels  52.8 us (46%)
  waiting for transfers between devices  28.7 us (25%)
  starting transfers between devices  28.2 us (25%)
  local copies, waits for them, and re-layouts  2.27 us (2%)
    ppermute x12, waiting for transfers between devices, start(): line[index + 1] = lax.ppermute(line[source], 'tp', pairs)  26.4 us
    pallas_call x8, Pallas kernels, project(): pl.pallas_call(functools.partial(project_kernel, masks, bool(carried), fi...  23.3 us
    ppermute x12, starting transfers between devices, start(): line[index + 1] = lax.ppermute(line[source], 'tp', pairs)  14 us
    pallas_call x2, Pallas kernels, attend(): pl.pallas_call(functools.partial(attend_kernel, chips, groups, known, pri...  13.6 us
    ppermute x8, starting transfers between devices, shift_chips(): return lax.ppermute(value, 'req', pairs)  10.8 us
    pallas_call x3, Pallas kernels, deal(): pl.pallas_call(functools.partial(deal_kernel, chips, bases, sizes, twins)...  8.67 us
    pallas_call x1, Pallas kernels, load(): pl.pallas_call(kernel, in_specs=[anywhere, anywhere], out_specs=[vmem, vm...  6.06 us
    ppermute x9, starting transfers between devices, swap_cores(): return lax.ppermute(value, 'req', [(d, d ^ 1) for d in range(2 * chips)])  3.41 us
  transfers between devices with their start and end apart: 29, of which 10 were waited for; matrix products, arithmetic and copies ran while one was open for 0% of the time, Pallas kernels for 41%

commit v1 on v0

--- a/solution.py
+++ b/solution.py
@@ -42,24 +42,32 @@
     requests = [me + 1 - 2 * core if twin else me for twin in twins]
     runs = [run_of(lengths_ref, request, 2 * chips) for request in requests]
     slots = sources[0].shape[0]
-    for chunk, (base, rows) in enumerate(zip(bases, sizes)):
-        home_ref, away_ref = out_refs[2 * chunk : 2 * chunk + 2]
+    total = None
+    for (start, length), source in zip(runs, sources):
+        hots = []
+        for base, rows in zip(bases, sizes):
+            for hop in range(chips):
+                target = lax.rem(chip + hop, chips) * 2 + core
+                number = base + target * rows + iota((rows, slots), 0)
+                slot = iota((rows, slots), 1)
+                hot = (number - start == slot) & (slot < length)
+                hots.append(hot.astype(F32).astype(BF16))
+        hot = jnp.concatenate(hots, axis=0) if len(hots) > 1 else hots[0]
+        part = jnp.dot(hot, source[...], preferred_element_type=F32)
+        total = part if total is None else total + part
+    total = total.astype(BF16)
+    at = 0
+    for chunk, rows in enumerate(sizes):
         for hop in range(chips):
-            target = lax.rem(chip + hop, chips) * 2 + core
-            number = base + target * rows + iota((rows, slots), 0)
-            slot = iota((rows, slots), 1)
-            total = None
-            for (start, length), source in zip(runs, sources):
-                hot = ((number - start == slot) & (slot < length)).astype(BF16)
-                part = jnp.dot(hot, source[...], preferred_element_type=F32)
-                total = part if total is None else total + part
-            total = total.astype(BF16)
-            if hop == 0:
-                home_ref[...] = total + priors[2 * chunk][...] if priors else total
-            elif priors:
-                away_ref[hop - 1] = total + priors[2 * chunk + 1][hop - 1]
+            picked = total[at : at + rows]
+            at += rows
+            if priors:
+                prior = priors[2 * chunk + 1][hop - 1] if hop else priors[2 * chunk][...]
+                picked = picked + prior
+            if hop:
+                out_refs[2 * chunk + 1][hop - 1] = picked
             else:
-                away_ref[hop - 1] = total
+                out_refs[2 * chunk][...] = picked
 
 
 def deal(chips, bases, sizes, lengths, sources, twins, priors=()):

time: 115 us -> 116 us (level)
  Pallas kernels: 52.8 us -> 47.6 us
  starting transfers between devices: 28.2 us -> 32.9 us
  waiting for transfers between devices: 28.7 us -> 30.4 us
    pallas_call x3, Pallas kernels: 8.67 us -> 5.53 us  [deal(): pl.pallas_call(functools.partial(deal_kernel, chips, bases, sizes, twins)...]
    ppermute x9, starting transfers between devices: 3.41 us -> 5.78 us  [swap_cores(): return lax.ppermute(value, 'req', [(d, d ^ 1) for d in range(2 * chips)])]
    ppermute x8, waiting for transfers between devices: 0.86 us -> 3.13 us  [shift_chips(): return lax.ppermute(value, 'req', pairs)]
    pallas_call x2, Pallas kernels: 13.6 us -> 11.6 us  [attend(): pl.pallas_call(functools.partial(attend_kernel, chips, groups, known, pri...]
    ppermute x12, starting transfers between devices: 14 us -> 15.8 us  [start(): line[index + 1] = lax.ppermute(line[source], 'tp', pairs)]
    ppermute x12, waiting for transfers between devices: 26.4 us -> 24.9 us  [start(): line[index + 1] = lax.ppermute(line[source], 'tp', pairs)]
  transfers between devices with their start and end apart: 29 -> 29, of which waited for: 10 -> 12; matrix products, arithmetic and copies ran while one was open for 0% -> 0% of each run, Pallas kernels for 41% -> 37%
where the time goes in v1:
time: 116 us; the launch traced here: 114 us
  Pallas kernels  47.6 us (41%)
  starting transfers between devices  32.9 us (28%)
  waiting for transfers between devices  30.4 us (26%)
  local copies, waits for them, and re-layouts  2.27 us (2%)
    ppermute x12, waiting for transfers between devices, start(): line[index + 1] = lax.ppermute(line[source], 'tp', pairs)  24.9 us
    pallas_call x8, Pallas kernels, project(): pl.pallas_call(functools.partial(project_kernel, masks, bool(carried), fi...  23.2 us
    ppermute x12, starting transfers between devices, start(): line[index + 1] = lax.ppermute(line[source], 'tp', pairs)  15.8 us
    pallas_call x2, Pallas kernels, attend(): pl.pallas_call(functools.partial(attend_kernel, chips, groups, known, pri...  11.6 us
    ppermute x8, starting transfers between devices, shift_chips(): return lax.ppermute(value, 'req', pairs)  11.2 us
    pallas_call x1, Pallas kernels, load(): pl.pallas_call(kernel, in_specs=[anywhere, anywhere], out_specs=[vmem, vm...  6.06 us
    ppermute x9, starting transfers between devices, swap_cores(): return lax.ppermute(value, 'req', [(d, d ^ 1) for d in range(2 * chips)])  5.78 us
    pallas_call x3, Pallas kernels, deal(): pl.pallas_call(functools.partial(deal_kernel, chips, bases, sizes, twins)...  5.53 us
  transfers between devices with their start and end apart: 29, of which 12 were waited for; matrix products, arithmetic and copies ran while one was open for 0% of the time, Pallas kernels for 37%

profile of v1, /device:TPU:0, one launch (start us, length us, event | category | flops | bytes accessed | tf_op | source)
XLA Modules:
  0.0 114.3 jit_solution(13731385656109466266)
XLA Ops:
  0.6 0.5 collective-permute-start
  1.1 1.6 %copy-done.2 = bf16[512,2048]{1,0:T(8,128)(2,1)S(1)} copy-done((bf16[512,2048]{1,0:T(8,128)(2,1)S(1)}, bf16[512,2048]{1,0:T(8,128)(2,1)}, u32[]{:S(2)}) %copy-start.2) | copy-done | bytes 2097176
  2.7 0.7 copy-done.4
  3.4 1.3 %deal.3 = (bf16[48,2048]{1,0:T(8,128)(2,1)S(1)}, bf16[1,48,2048]{2,1,0:T(8,128)(2,1)S(1)}) custom-call(s32[4]{0:T(128)S(1)} %copy-done.4, bf16[512,2048]{1,0:T(8,128)(2,1)S(1)} %copy-done.2), custom_call_target="tpu_custom_call" | custom-call | tf_op jit(solution)/shard_map/deal/pallas_call | solution.py:86
  4.7 0.4 collective-permute-done.refs_0_.refs_1_
  5.1 1.3 %deal.4 = (bf16[48,2048]{1,0:T(8,128)(2,1)S(1)}, bf16[1,48,2048]{2,1,0:T(8,128)(2,1)S(1)}) custom-call(s32[4]{0:T(128)S(1)} %copy-done.4, bf16[512,2048]{1,0:T(8,128)(2,1)S(1)} %collective-permute-done.refs_0_.refs_1_, bf16[48,2048]{1,0:T(8,128)(2,1)S(1)} %get-tuple-element.47.refs_1_, bf16[1,48,2048]{2,1,0:T(8,128)(2,1)S(1)} %get-tuple-element.48.refs_2_), custom_call_target="tpu_custom_call" | custom-call | tf_op jit(solution)/shard_map/deal/pallas_call | solution.py:86
  6.5 2.9 %collective-permute-start.1 = (bf16[48,2048]{1,0:T(8,128)(2,1)S(1)}, bf16[48,2048]{1,0:T(8,128)(2,1)S(1)}, u32[]{:S(2)}, u32[]{:S(2)}) collective-permute-start(bf16[48,2048]{1,0:T(8,128)(2,1)S(1)} %bitcast.16), channel_id=1, source_target_pairs={{0,8},{4,12},{8,0},{12,4},{1,9},{5,13},{9,1},{13,5},{2,10},{6,14},... | collective-permute-start | bytes 589832 | tf_op jit(solution)/shard_map/ppermute | solution.py:528
  9.4 2.9 %deal.5 = (bf16[80,2048]{1,0:T(8,128)(2,1)S(1)}, bf16[1,80,2048]{2,1,0:T(8,128)(2,1)S(1)}, bf16[80,2048]{1,0:T(8,128)(2,1)S(1)}, bf16[1,80,2048]{2,1,0:T(8,128)(...) custom-call(s32[4]{0:T(128)S(1)} %copy-done.4, bf16[512,2048]{1,0:T(8,128)(2,1)S(1)} %copy-done.3, ...), custom_call_target="tpu_custom_call" | custom-call | tf_op jit(solution)/shard_map/deal/pallas_call | solution.py:86
  12.3 2.3 %collective-permute-done.1.refs_0_ = bf16[48,2048]{1,0:T(8,128)(2,1)S(1)} collective-permute-done((bf16[48,2048]{1,0:T(8,128)(2,1)S(1)}, bf16[48,2048]{1,0:T(8,128)(2,1)S(1)}, u32[]{:S(2)}, u32[]{:S(2)}) %collective-permute-start.1) | collective-permute-done | bytes 196640 | tf_op jit(solution)/shard_map/ppermute | solution.py:528
  14.6 1.8 %collective-permute-start.3 = (bf16[80,2048]{1,0:T(8,128)(2,1)S(1)}, bf16[80,2048]{1,0:T(8,128)(2,1)S(1)}, u32[]{:S(2)}, u32[]{:S(2)}) collective-permute-start(bf16[80,2048]{1,0:T(8,128)(2,1)S(1)} %bitcast.13), channel_id=1, source_target_pairs={{0,8},{4,12},{8,0},{12,4},{1,9},{5,13},{9,1},{13,5},{2,10},{6,14},... | collective-permute-start | bytes 983048 | tf_op jit(solution)/shard_map/ppermute | solution.py:528
  16.4 1.6 %collective-permute-start.4 = (bf16[48,2048]{1,0:T(8,128)(2,1)S(1)}, bf16[48,2048]{1,0:T(8,128)(2,1)S(1)}, u32[]{:S(2)}, u32[]{:S(2)}) collective-permute-start(bf16[48,2048]{1,0:T(8,128)(2,1)S(1)} %get-tuple-element.52.anchor_ref.refs_0_), channel_id=1, source_target_pairs={{0,1},{1,0},{2,3},{3,2},{4,5},{5,4},{6,7},{7,6},{8,9},{9,8},{10,11... | collective-permute-start | bytes 589832 | tf_op jit(solution)/shard_map/ppermute | solution.py:583
  18.0 2.6 %collective-permute-start.2 = (bf16[48,2048]{1,0:T(8,128)(2,1)S(1)}, bf16[48,2048]{1,0:T(8,128)(2,1)S(1)}, u32[]{:S(2)}, u32[]{:S(2)}) collective-permute-start(bf16[48,2048]{1,0:T(8,128)(2,1)S(1)} %get-tuple-element.52.anchor_ref.refs_0_), channel_id=1, source_target_pairs={{0,2},{1,3},{2,0},{3,1},{4,6},{5,7},{6,4},{7,5},{8,10},{9,11},{10,... | collective-permute-start | bytes 589832 | tf_op jit(solution)/shard_map/ppermute | solution.py:583
  20.6 6.1 %load.1 = (bf16[8192,1024]{1,0:T(8,128)(2,1)S(1)}, f32[8,128]{1,0:T(8,128)S(1)}) custom-call(bf16[8192,1024]{1,0:T(8,128)(2,1)} %weight_ref.1, bf16[48,2048]{1,0:T(8,128)(2,1)S(1)} %get-tuple-element.52.anchor_ref.refs_0_), custom_call_target="tpu_custom_call" | custom-call | tf_op jit(solution)/shard_map/load/pallas_call | solution.py:206
  26.7 0.0 collective-permute-done.3.refs_0_
  26.7 0.6 collective-permute-start.9
  27.3 0.0 collective-permute-done.4.refs_2_
  27.3 1.5 %collective-permute-done.2.refs_0_ = bf16[48,2048]{1,0:T(8,128)(2,1)S(1)} collective-permute-done((bf16[48,2048]{1,0:T(8,128)(2,1)S(1)}, bf16[48,2048]{1,0:T(8,128)(2,1)S(1)}, u32[]{:S(2)}, u32[]{:S(2)}) %collective-permute-start.2) | collective-permute-done | bytes 196640 | tf_op jit(solution)/shard_map/ppermute | solution.py:583
  28.8 0.3 collective-permute-start.10
  29.2 2.7 %collective-permute-start.8 = (bf16[80,2048]{1,0:T(8,128)(2,1)S(1)}, bf16[80,2048]{1,0:T(8,128)(2,1)S(1)}, u32[]{:S(2)}, u32[]{:S(2)}) collective-permute-start(bf16[80,2048]{1,0:T(8,128)(2,1)S(1)} %get-tuple-element.62.anchor_ref.refs_0_), channel_id=1, source_target_pairs={{0,2},{1,3},{2,0},{3,1},{4,6},{5,7},{6,4},{7,5},{8,10},{9,11},{10,... | collective-permute-start | bytes 983048 | tf_op jit(solution)/shard_map/ppermute | solution.py:583
  31.9 0.0 collective-permute-start.5
  31.9 1.1 angles.1
  33.0 4.0 %project.8 = (f32[48,1536]{1,0:T(8,128)S(1)}, f32[48,128]{1,0:T(8,128)S(1)}) custom-call(bf16[48,2048]{1,0:T(8,128)(2,1)S(1)} %get-tuple-element.52.anchor_ref.refs_0_, bf16[48,2048]{1,0:T(8,128)(2,1)S(1)} %get-tuple-element.58.refs_1_, bf16[48,2048]{1,0:T(8,128)(2,1)S(1)} %collective-permute-done.4.refs_2_, f32[1,8192]{1,0:T(1,128)S(1)} %bitcast.5, ...), custom_call_target="tpu_custom_call" | custom-call | tf_op jit(solution)/shard_map/project/pallas_call | solution.py:281
  37.0 9.4 %collective-permute-done.5.refs_0_ = bf16[48,2048]{1,0:T(8,128)(2,1)S(1)} collective-permute-done((bf16[48,2048]{1,0:T(8,128)(2,1)S(1)}, bf16[48,2048]{1,0:T(8,128)(2,1)S(1)}, u32[]{:S(2)}, u32[]{:S(2)}) %collective-permute-start.5) | collective-permute-done | bytes 196640 | tf_op jit(solution)/shard_map/ppermute | solution.py:583
  46.5 1.6 %project.9.refs_3_.refs_0_ = bf16[48,1536]{1,0:T(8,128)(2,1)S(1)} custom-call(bf16[48,2048]{1,0:T(8,128)(2,1)S(1)} %collective-permute-done.5.refs_0_, f32[1,8192]{1,0:T(1,128)S(1)} %bitcast.6, bf16[8192,1024]{1,0:T(8,128)(2,1)S(1)} %get-tuple-element.59.refs_4_.refs_2_, bf16[8192,256]{1,0:T(8,128)(2,1)S(1)} %copy-done, bf16[8192,256]{1,0:T(8,128)(2,1)S(1)} %copy-done.1, ...), custom_call_target="tpu_custom_call" | custom-call | tf_op jit(solution)/shard_map/project/pallas_call | solution.py:281
  48.1 0.0 collective-permute-done.8.refs_0_
  48.1 1.6 %collective-permute-start.11 = (bf16[80,2048]{1,0:T(8,128)(2,1)S(1)}, bf16[80,2048]{1,0:T(8,128)(2,1)S(1)}, u32[]{:S(2)}, u32[]{:S(2)}) collective-permute-start(bf16[80,2048]{1,0:T(8,128)(2,1)S(1)} %get-tuple-element.69.refs_1_), channel_id=1, source_target_pairs={{0,1},{1,0},{2,3},{3,2},{4,5},{5,4},{6,7},{7,6},{8,9},{9,8},{10,11... | collective-permute-start | bytes 983048 | tf_op jit(solution)/shard_map/ppermute | solution.py:583
  49.8 1.9 %collective-permute-start.15 = (bf16[80,2048]{1,0:T(8,128)(2,1)S(1)}, bf16[80,2048]{1,0:T(8,128)(2,1)S(1)}, u32[]{:S(2)}, u32[]{:S(2)}) collective-permute-start(bf16[80,2048]{1,0:T(8,128)(2,1)S(1)} %get-tuple-element.74.refs_0_), channel_id=1, source_target_pairs={{0,2},{1,3},{2,0},{3,1},{4,6},{5,7},{6,4},{7,5},{8,10},{9,11},{10,... | collective-permute-start | bytes 983048 | tf_op jit(solution)/shard_map/ppermute | solution.py:583
  51.7 0.1 collective-permute-start.17
  51.8 0.5 collective-permute-start.16
  52.3 1.5 %collective-permute-start.7 = (bf16[48,1536]{1,0:T(8,128)(2,1)S(1)}, bf16[48,1536]{1,0:T(8,128)(2,1)S(1)}, u32[]{:S(2)}, u32[]{:S(2)}) collective-permute-start(bf16[48,1536]{1,0:T(8,128)(2,1)S(1)} %project.9.refs_3_.refs_0_), channel_id=1, source_target_pairs={{0,8},{4,12},{8,0},{12,4},{1,9},{5,13},{9,1},{13,5},{2,10},{6,14},... | collective-permute-start | bytes 442376 | tf_op jit(solution)/shard_map/ppermute | solution.py:528
  53.8 4.3 %project.10 = (f32[80,1536]{1,0:T(8,128)S(1)}, f32[80,128]{1,0:T(8,128)S(1)}) custom-call(bf16[80,2048]{1,0:T(8,128)(2,1)S(1)} %get-tuple-element.62.anchor_ref.refs_0_, bf16[80,2048]{1,0:T(8,128)(2,1)S(1)} %get-tuple-element.69.refs_1_, bf16[80,2048]{1,0:T(8,128)(2,1)S(1)} %collective-permute-done.10.refs_2_, f32[1,8192]{1,0:T(1,128)S(1)} %bitcast.7, ...), custom_call_target="tpu_custom_call" | custom-call | tf_op jit(solution)/shard_map/project/pallas_call | solution.py:281
  58.1 0.9 collective-permute-done.16.refs_0_
  59.0 6.8 %collective-permute-done.11.refs_0_ = bf16[80,2048]{1,0:T(8,128)(2,1)S(1)} collective-permute-done((bf16[80,2048]{1,0:T(8,128)(2,1)S(1)}, bf16[80,2048]{1,0:T(8,128)(2,1)S(1)}, u32[]{:S(2)}, u32[]{:S(2)}) %collective-permute-start.11) | collective-permute-done | bytes 327712 | tf_op jit(solution)/shard_map/ppermute | solution.py:583
  65.8 1.7 %project.11.refs_1_.refs_3_.refs_4_ = bf16[80,1536]{1,0:T(8,128)(2,1)S(1)} custom-call(bf16[80,2048]{1,0:T(8,128)(2,1)S(1)} %collective-permute-done.11.refs_0_, f32[1,8192]{1,0:T(1,128)S(1)} %bitcast.8, bf16[8192,1024]{1,0:T(8,128)(2,1)S(1)} %get-tuple-element.59.refs_4_.refs_2_, bf16[8192,256]{1,0:T(8,128)(2,1)S(1)} %copy-done, ...), custom_call_target="tpu_custom_call" | custom-call | tf_op jit(solution)/shard_map/project/pallas_call | solution.py:281
  67.5 0.0 collective-permute-done.7.refs_0_.refs_4_
  67.5 0.0 collective-permute-done.15.refs_0_
  67.5 2.5 %collective-permute-done.17.refs_2_ = bf16[80,2048]{1,0:T(8,128)(2,1)S(1)} collective-permute-done((bf16[80,2048]{1,0:T(8,128)(2,1)S(1)}, bf16[80,2048]{1,0:T(8,128)(2,1)S(1)}, u32[]{:S(2)}, u32[]{:S(2)}) %collective-permute-start.17) | collective-permute-done | bytes 327712 | tf_op jit(solution)/shard_map/ppermute | solution.py:583
  70.1 1.6 %collective-permute-start.18 = (bf16[80,2048]{1,0:T(8,128)(2,1)S(1)}, bf16[80,2048]{1,0:T(8,128)(2,1)S(1)}, u32[]{:S(2)}, u32[]{:S(2)}) collective-permute-start(bf16[80,2048]{1,0:T(8,128)(2,1)S(1)} %get-tuple-element.77.refs_1_), channel_id=1, source_target_pairs={{0,1},{1,0},{2,3},{3,2},{4,5},{5,4},{6,7},{7,6},{8,9},{9,8},{10,11... | collective-permute-start | bytes 983048 | tf_op jit(solution)/shard_map/ppermute | solution.py:583
  71.6 0.6 collective-permute-start.14
  72.2 3.0 %collective-permute-start.22 = (bf16[48,2048]{1,0:T(8,128)(2,1)S(1)}, bf16[48,2048]{1,0:T(8,128)(2,1)S(1)}, u32[]{:S(2)}, u32[]{:S(2)}) collective-permute-start(bf16[48,2048]{1,0:T(8,128)(2,1)S(1)} %get-tuple-element.82.refs_0_), channel_id=1, source_target_pairs={{0,2},{1,3},{2,0},{3,1},{4,6},{5,7},{6,4},{7,5},{8,10},{9,11},{10,... | collective-permute-start | bytes 589832 | tf_op jit(solution)/shard_map/ppermute | solution.py:583
  75.2 0.3 collective-permute-start.23
  75.6 4.3 %project.12 = (f32[80,1536]{1,0:T(8,128)S(1)}, f32[80,128]{1,0:T(8,128)S(1)}) custom-call(bf16[80,2048]{1,0:T(8,128)(2,1)S(1)} %get-tuple-element.74.refs_0_, bf16[80,2048]{1,0:T(8,128)(2,1)S(1)} %get-tuple-element.77.refs_1_, bf16[80,2048]{1,0:T(8,128)(2,1)S(1)} %collective-permute-done.17.refs_2_, f32[1,8192]{1,0:T(1,128)S(1)} %bitcast.9, ...), custom_call_target="tpu_custom_call" | custom-call | tf_op jit(solution)/shard_map/project/pallas_call | solution.py:281
  79.8 3.7 %collective-permute-done.18.refs_0_ = bf16[80,2048]{1,0:T(8,128)(2,1)S(1)} collective-permute-done((bf16[80,2048]{1,0:T(8,128)(2,1)S(1)}, bf16[80,2048]{1,0:T(8,128)(2,1)S(1)}, u32[]{:S(2)}, u32[]{:S(2)}) %collective-permute-start.18) | collective-permute-done | bytes 327712 | tf_op jit(solution)/shard_map/ppermute | solution.py:583
  83.5 1.7 %project.13.refs_1_.refs_8_ = bf16[80,1536]{1,0:T(8,128)(2,1)S(1)} custom-call(bf16[80,2048]{1,0:T(8,128)(2,1)S(1)} %collective-permute-done.18.refs_0_, f32[1,8192]{1,0:T(1,128)S(1)} %bitcast.10, bf16[8192,1024]{1,0:T(8,128)(2,1)S(1)} %get-tuple-element.59.refs_4_.refs_2_, bf16[8192,256]{1,0:T(8,128)(2,1)S(1)} %copy-done, bf16[8192,256]{1,0:T(8,128)(2,1)S(1)} %copy-done.1, ...), custom_call_target="tpu_custom_call" | custom-call | tf_op jit(solution)/shard_map/project/pallas_call | solution.py:281
  85.2 3.0 %collective-permute-start.21 = (bf16[80,1536]{1,0:T(8,128)(2,1)S(1)}, bf16[80,1536]{1,0:T(8,128)(2,1)S(1)}, u32[]{:S(2)}, u32[]{:S(2)}) collective-permute-start(bf16[80,1536]{1,0:T(8,128)(2,1)S(1)} %project.13.refs_1_.refs_8_), channel_id=1, source_target_pairs={{0,8},{4,12},{8,0},{12,4},{1,9},{5,13},{9,1},{13,5},{2,10},{6,14},... | collective-permute-start | bytes 737288 | tf_op jit(solution)/shard_map/ppermute | solution.py:528
  88.2 0.0 collective-permute-done.22.refs_0_
  88.2 0.0 collective-permute-done.23.refs_1_.refs_2_
  88.2 0.1 collective-permute-start.24
  88.3 0.1 collective-permute-start.6
  88.4 0.5 collective-permute-start.12
  88.9 0.1 collective-permute-start.13
  89.0 4.1 %project.14 = (f32[48,1536]{1,0:T(8,128)S(1)}, f32[48,128]{1,0:T(8,128)S(1)}) custom-call(bf16[48,2048]{1,0:T(8,128)(2,1)S(1)} %get-tuple-element.82.refs_0_, bf16[48,2048]{1,0:T(8,128)(2,1)S(1)} %after.13.refs_1_, bf16[48,2048]{1,0:T(8,128)(2,1)S(1)} %collective-permute-done.23.refs_1_.refs_2_, f32[1,8192]{1,0:T(1,128)S(1)} %bitcast.11, ...), custom_call_target="tpu_custom_call" | custom-call | tf_op jit(solution)/shard_map/project/pallas_call | solution.py:281
  93.0 0.9 collective-permute-done.24.refs_0_
  94.0 1.7 %project.15.refs_1_.refs_12_ = bf16[48,1536]{1,0:T(8,128)(2,1)S(1)} custom-call(bf16[48,2048]{1,0:T(8,128)(2,1)S(1)} %collective-permute-done.24.refs_0_, f32[1,8192]{1,0:T(1,128)S(1)} %bitcast.12, bf16[8192,1024]{1,0:T(8,128)(2,1)S(1)} %get-tuple-element.59.refs_4_.refs_2_, bf16[8192,256]{1,0:T(8,128)(2,1)S(1)} %copy-done, bf16[8192,256]{1,0:T(8,128)(2,1)S(1)} %copy-done.1, ...), custom_call_target="tpu_custom_call" | custom-call | tf_op jit(solution)/shard_map/project/pallas_call | solution.py:281
  95.6 0.6 collective-permute-start.19
  96.2 0.1 collective-permute-start.25
  96.3 0.3 collective-permute-start.27
  96.6 0.2 collective-permute-start.26
  96.8 0.5 collective-permute-done.19.refs_7_
  97.4 0.4 collective-permute-done.25.refs_11_
  97.7 7.9 %attend.2 = (bf16[512,1024]{1,0:T(8,128)(2,1)}, bf16[2,512,256]{2,1,0:T(8,128)(2,1)}, f32[8,128]{1,0:T(8,128)S(1)}) custom-call(s32[4]{0:T(128)S(1)} %copy-done.5, s32[16]{0:T(128)S(1)} %copy-done.6, bf16[48,1536]{1,0:T(8,128)(2,1)S(1)} %project.9.refs_3_.refs_0_, bf16[48,1536]{1,0:T(8,128)(2,1)S(1)} %collective-permute-done.6.refs_1_, ...), custom_call_target="tpu_custom_call" | custom-call | tf_op jit(solution)/shard_map/attend/pallas_call | solution.py:499
  105.7 3.7 %collective-permute-start.28 = (bf16[48,1536]{1,0:T(8,128)(2,1)S(1)}, bf16[48,1536]{1,0:T(8,128)(2,1)S(1)}, u32[]{:S(2)}, u32[]{:S(2)}) collective-permute-start(bf16[48,1536]{1,0:T(8,128)(2,1)S(1)} %after.15.refs_14_), channel_id=1, source_target_pairs={{0,4},{4,0},{8,12},{12,8},{1,5},{5,1},{9,13},{13,9},{2,6},{6,2},{1... | collective-permute-start | bytes 442376 | tf_op jit(solution)/shard_map/ppermute | solution.py:532
  109.4 1.0 collective-permute-done.28.refs_15_
  110.4 3.7 %attend.3 = (bf16[512,1024]{1,0:T(8,128)(2,1)}, bf16[2,512,256]{2,1,0:T(8,128)(2,1)}, f32[8,128]{1,0:T(8,128)}) custom-call(s32[4]{0:T(128)S(1)} %copy-done.5, s32[16]{0:T(128)S(1)} %copy-done.6, bf16[48,1536]{1,0:T(8,128)(2,1)S(1)} %project.9.refs_3_.refs_0_, ...), custom_call_target="tpu_custom_call", output_to_operand_aliasing={{0}: (18, {}), {1}: (19, {})} | custom-call | tf_op jit(solution)/shard_map/attend/pallas_call | solution.py:499
  (40 shorter events, 0.2 us)
Async XLA Ops:
  0.6 4.5 %collective-permute-start = (bf16[512,2048]{1,0:T(8,128)(2,1)}, bf16[512,2048]{1,0:T(8,128)(2,1)S(1)}, u32[]{:S(2)}, u32[]{:S(2)}) collective-permute-start(bf16[512,2048]{1,0:T(8,128)(2,1)} %refs_0_.3), channel_id=1, source_target_pairs={{0,4},{4,0},{8,12},{12,8},{1,5},{5,1},{9,13},{13,9},{2,6},{6,2},{1... | collective-permute-start | bytes 6291464 | tf_op jit(solution)/shard_map/ppermute | solution.py:532
  1.1 1.6 %copy-start.2 = (bf16[512,2048]{1,0:T(8,128)(2,1)S(1)}, bf16[512,2048]{1,0:T(8,128)(2,1)}, u32[]{:S(2)}) copy-start(bf16[512,2048]{1,0:T(8,128)(2,1)} %refs_0_.3) | copy-start | bytes 6291460
  2.7 0.7 copy-start.4
  3.4 6.0 %copy-start.3 = (bf16[512,2048]{1,0:T(8,128)(2,1)S(1)}, bf16[512,2048]{1,0:T(8,128)(2,1)}, u32[]{:S(2)}) copy-start(bf16[512,2048]{1,0:T(8,128)(2,1)} %refs_0_.3) | copy-start | bytes 6291460
  6.5 8.1 %collective-permute-start.1 = (bf16[48,2048]{1,0:T(8,128)(2,1)S(1)}, bf16[48,2048]{1,0:T(8,128)(2,1)S(1)}, u32[]{:S(2)}, u32[]{:S(2)}) collective-permute-start(bf16[48,2048]{1,0:T(8,128)(2,1)S(1)} %bitcast.16), channel_id=1, source_target_pairs={{0,8},{4,12},{8,0},{12,4},{1,9},{5,13},{9,1},{13,5},{2,10},{6,14},... | collective-permute-start | bytes 589832 | tf_op jit(solution)/shard_map/ppermute | solution.py:528
  14.6 12.1 %collective-permute-start.3 = (bf16[80,2048]{1,0:T(8,128)(2,1)S(1)}, bf16[80,2048]{1,0:T(8,128)(2,1)S(1)}, u32[]{:S(2)}, u32[]{:S(2)}) collective-permute-start(bf16[80,2048]{1,0:T(8,128)(2,1)S(1)} %bitcast.13), channel_id=1, source_target_pairs={{0,8},{4,12},{8,0},{12,4},{1,9},{5,13},{9,1},{13,5},{2,10},{6,14},... | collective-permute-start | bytes 983048 | tf_op jit(solution)/shard_map/ppermute | solution.py:528
  16.4 15.4 %copy-start.8 = (bf16[8192]{0:T(1024)(128)(2,1)S(1)}, bf16[8192]{0:T(1024)(128)(2,1)}, u32[]{:S(2)}) copy-start(bf16[8192]{0:T(1024)(128)(2,1)} %param.9) | copy-start | bytes 49156
  16.4 15.5 %copy-start.5 = (s32[4]{0:T(128)S(1)}, s32[4]{0:T(128)}, u32[]{:S(2)}) copy-start(s32[4]{0:T(128)} %lengths_ref.11) | copy-start | bytes 52
  16.4 15.5 %copy-start.7 = (f32[1,128]{1,0:T(1,128)S(1)}, f32[1,128]{1,0:T(1,128)}, u32[]{:S(2)}) copy-start(f32[1,128]{1,0:T(1,128)} %constant.2.clone.frequency_ref) | copy-start | bytes 1540
  16.4 10.9 %collective-permute-start.4 = (bf16[48,2048]{1,0:T(8,128)(2,1)S(1)}, bf16[48,2048]{1,0:T(8,128)(2,1)S(1)}, u32[]{:S(2)}, u32[]{:S(2)}) collective-permute-start(bf16[48,2048]{1,0:T(8,128)(2,1)S(1)} %get-tuple-element.52.anchor_ref.refs_0_), channel_id=1, source_target_pairs={{0,1},{1,0},{2,3},{3,2},{4,5},{5,4},{6,7},{7,6},{8,9},{9,8},{10,11... | collective-permute-start | bytes 589832 | tf_op jit(solution)/shard_map/ppermute | solution.py:583
  18.0 10.8 %collective-permute-start.2 = (bf16[48,2048]{1,0:T(8,128)(2,1)S(1)}, bf16[48,2048]{1,0:T(8,128)(2,1)S(1)}, u32[]{:S(2)}, u32[]{:S(2)}) collective-permute-start(bf16[48,2048]{1,0:T(8,128)(2,1)S(1)} %get-tuple-element.52.anchor_ref.refs_0_), channel_id=1, source_target_pairs={{0,2},{1,3},{2,0},{3,1},{4,6},{5,7},{6,4},{7,5},{8,10},{9,11},{10,... | collective-permute-start | bytes 589832 | tf_op jit(solution)/shard_map/ppermute | solution.py:583
  20.6 12.4 %copy-start = (bf16[8192,256]{1,0:T(8,128)(2,1)S(1)}, bf16[8192,256]{1,0:T(8,128)(2,1)}, u32[]{:S(2)}) copy-start(bf16[8192,256]{1,0:T(8,128)(2,1)} %refs_3_.7) | copy-start | bytes 12582916
  20.6 12.4 %copy-start.1 = (bf16[8192,256]{1,0:T(8,128)(2,1)S(1)}, bf16[8192,256]{1,0:T(8,128)(2,1)}, u32[]{:S(2)}) copy-start(bf16[8192,256]{1,0:T(8,128)(2,1)} %refs_4_.7) | copy-start | bytes 12582916
  26.7 21.3 %collective-permute-start.9 = (bf16[80,2048]{1,0:T(8,128)(2,1)S(1)}, bf16[80,2048]{1,0:T(8,128)(2,1)S(1)}, u32[]{:S(2)}, u32[]{:S(2)}) collective-permute-start(bf16[80,2048]{1,0:T(8,128)(2,1)S(1)} %bitcast.14), channel_id=1, source_target_pairs={{0,8},{4,12},{8,0},{12,4},{1,9},{5,13},{9,1},{13,5},{2,10},{6,14},... | collective-permute-start | bytes 983048 | tf_op jit(solution)/shard_map/ppermute | solution.py:528
  28.8 19.3 %collective-permute-start.10 = (bf16[80,2048]{1,0:T(8,128)(2,1)S(1)}, bf16[80,2048]{1,0:T(8,128)(2,1)S(1)}, u32[]{:S(2)}, u32[]{:S(2)}) collective-permute-start(bf16[80,2048]{1,0:T(8,128)(2,1)S(1)} %get-tuple-element.62.anchor_ref.refs_0_), channel_id=1, source_target_pairs={{0,1},{1,0},{2,3},{3,2},{4,5},{5,4},{6,7},{7,6},{8,9},{9,8},{10,11... | collective-permute-start | bytes 983048 | tf_op jit(solution)/shard_map/ppermute | solution.py:583
  29.2 18.9 %collective-permute-start.8 = (bf16[80,2048]{1,0:T(8,128)(2,1)S(1)}, bf16[80,2048]{1,0:T(8,128)(2,1)S(1)}, u32[]{:S(2)}, u32[]{:S(2)}) collective-permute-start(bf16[80,2048]{1,0:T(8,128)(2,1)S(1)} %get-tuple-element.62.anchor_ref.refs_0_), channel_id=1, source_target_pairs={{0,2},{1,3},{2,0},{3,1},{4,6},{5,7},{6,4},{7,5},{8,10},{9,11},{10,... | collective-permute-start | bytes 983048 | tf_op jit(solution)/shard_map/ppermute | solution.py:583
  31.9 14.6 %collective-permute-start.5 = (bf16[48,2048]{1,0:T(8,128)(2,1)S(1)}, bf16[48,2048]{1,0:T(8,128)(2,1)S(1)}, u32[]{:S(2)}, u32[]{:S(2)}) collective-permute-start(bf16[48,2048]{1,0:T(8,128)(2,1)S(1)} %get-tuple-element.58.refs_1_), channel_id=1, source_target_pairs={{0,1},{1,0},{2,3},{3,2},{4,5},{5,4},{6,7},{7,6},{8,9},{9,8},{10,11... | collective-permute-start | bytes 589832 | tf_op jit(solution)/shard_map/ppermute | solution.py:583
  48.1 17.7 %collective-permute-start.11 = (bf16[80,2048]{1,0:T(8,128)(2,1)S(1)}, bf16[80,2048]{1,0:T(8,128)(2,1)S(1)}, u32[]{:S(2)}, u32[]{:S(2)}) collective-permute-start(bf16[80,2048]{1,0:T(8,128)(2,1)S(1)} %get-tuple-element.69.refs_1_), channel_id=1, source_target_pairs={{0,1},{1,0},{2,3},{3,2},{4,5},{5,4},{6,7},{7,6},{8,9},{9,8},{10,11... | collective-permute-start | bytes 983048 | tf_op jit(solution)/shard_map/ppermute | solution.py:583
  49.8 17.7 %collective-permute-start.15 = (bf16[80,2048]{1,0:T(8,128)(2,1)S(1)}, bf16[80,2048]{1,0:T(8,128)(2,1)S(1)}, u32[]{:S(2)}, u32[]{:S(2)}) collective-permute-start(bf16[80,2048]{1,0:T(8,128)(2,1)S(1)} %get-tuple-element.74.refs_0_), channel_id=1, source_target_pairs={{0,2},{1,3},{2,0},{3,1},{4,6},{5,7},{6,4},{7,5},{8,10},{9,11},{10,... | collective-permute-start | bytes 983048 | tf_op jit(solution)/shard_map/ppermute | solution.py:583
  51.7 18.3 %collective-permute-start.17 = (bf16[80,2048]{1,0:T(8,128)(2,1)S(1)}, bf16[80,2048]{1,0:T(8,128)(2,1)S(1)}, u32[]{:S(2)}, u32[]{:S(2)}) collective-permute-start(bf16[80,2048]{1,0:T(8,128)(2,1)S(1)} %get-tuple-element.74.refs_0_), channel_id=1, source_target_pairs={{0,1},{1,0},{2,3},{3,2},{4,5},{5,4},{6,7},{7,6},{8,9},{9,8},{10,11... | collective-permute-start | bytes 983048 | tf_op jit(solution)/shard_map/ppermute | solution.py:583
  51.8 7.1 %collective-permute-start.16 = (bf16[48,2048]{1,0:T(8,128)(2,1)S(1)}, bf16[48,2048]{1,0:T(8,128)(2,1)S(1)}, u32[]{:S(2)}, u32[]{:S(2)}) collective-permute-start(bf16[48,2048]{1,0:T(8,128)(2,1)S(1)} %bitcast.15), channel_id=1, source_target_pairs={{0,8},{4,12},{8,0},{12,4},{1,9},{5,13},{9,1},{13,5},{2,10},{6,14},... | collective-permute-start | bytes 589832 | tf_op jit(solution)/shard_map/ppermute | solution.py:528
  52.3 15.2 %collective-permute-start.7 = (bf16[48,1536]{1,0:T(8,128)(2,1)S(1)}, bf16[48,1536]{1,0:T(8,128)(2,1)S(1)}, u32[]{:S(2)}, u32[]{:S(2)}) collective-permute-start(bf16[48,1536]{1,0:T(8,128)(2,1)S(1)} %project.9.refs_3_.refs_0_), channel_id=1, source_target_pairs={{0,8},{4,12},{8,0},{12,4},{1,9},{5,13},{9,1},{13,5},{2,10},{6,14},... | collective-permute-start | bytes 442376 | tf_op jit(solution)/shard_map/ppermute | solution.py:528
  70.1 13.4 %collective-permute-start.18 = (bf16[80,2048]{1,0:T(8,128)(2,1)S(1)}, bf16[80,2048]{1,0:T(8,128)(2,1)S(1)}, u32[]{:S(2)}, u32[]{:S(2)}) collective-permute-start(bf16[80,2048]{1,0:T(8,128)(2,1)S(1)} %get-tuple-element.77.refs_1_), channel_id=1, source_target_pairs={{0,1},{1,0},{2,3},{3,2},{4,5},{5,4},{6,7},{7,6},{8,9},{9,8},{10,11... | collective-permute-start | bytes 983048 | tf_op jit(solution)/shard_map/ppermute | solution.py:583
  71.6 16.6 %collective-permute-start.14 = (bf16[80,1536]{1,0:T(8,128)(2,1)S(1)}, bf16[80,1536]{1,0:T(8,128)(2,1)S(1)}, u32[]{:S(2)}, u32[]{:S(2)}) collective-permute-start(bf16[80,1536]{1,0:T(8,128)(2,1)S(1)} %project.11.refs_1_.refs_3_.refs_4_), channel_id=1, source_target_pairs={{0,8},{4,12},{8,0},{12,4},{1,9},{5,13},{9,1},{13,5},{2,10},{6,14},... | collective-permute-start | bytes 737288 | tf_op jit(solution)/shard_map/ppermute | solution.py:528
  72.2 16.0 %collective-permute-start.22 = (bf16[48,2048]{1,0:T(8,128)(2,1)S(1)}, bf16[48,2048]{1,0:T(8,128)(2,1)S(1)}, u32[]{:S(2)}, u32[]{:S(2)}) collective-permute-start(bf16[48,2048]{1,0:T(8,128)(2,1)S(1)} %get-tuple-element.82.refs_0_), channel_id=1, source_target_pairs={{0,2},{1,3},{2,0},{3,1},{4,6},{5,7},{6,4},{7,5},{8,10},{9,11},{10,... | collective-permute-start | bytes 589832 | tf_op jit(solution)/shard_map/ppermute | solution.py:583
  75.2 13.0 %collective-permute-start.23 = (bf16[48,2048]{1,0:T(8,128)(2,1)S(1)}, bf16[48,2048]{1,0:T(8,128)(2,1)S(1)}, u32[]{:S(2)}, u32[]{:S(2)}) collective-permute-start(bf16[48,2048]{1,0:T(8,128)(2,1)S(1)} %get-tuple-element.82.refs_0_), channel_id=1, source_target_pairs={{0,1},{1,0},{2,3},{3,2},{4,5},{5,4},{6,7},{7,6},{8,9},{9,8},{10,11... | collective-permute-start | bytes 589832 | tf_op jit(solution)/shard_map/ppermute | solution.py:583
  85.2 10.5 %collective-permute-start.21 = (bf16[80,1536]{1,0:T(8,128)(2,1)S(1)}, bf16[80,1536]{1,0:T(8,128)(2,1)S(1)}, u32[]{:S(2)}, u32[]{:S(2)}) collective-permute-start(bf16[80,1536]{1,0:T(8,128)(2,1)S(1)} %project.13.refs_1_.refs_8_), channel_id=1, source_target_pairs={{0,8},{4,12},{8,0},{12,4},{1,9},{5,13},{9,1},{13,5},{2,10},{6,14},... | collective-permute-start | bytes 737288 | tf_op jit(solution)/shard_map/ppermute | solution.py:528
  88.2 5.7 %collective-permute-start.24 = (bf16[48,2048]{1,0:T(8,128)(2,1)S(1)}, bf16[48,2048]{1,0:T(8,128)(2,1)S(1)}, u32[]{:S(2)}, u32[]{:S(2)}) collective-permute-start(bf16[48,2048]{1,0:T(8,128)(2,1)S(1)} %after.13.refs_1_), channel_id=1, source_target_pairs={{0,1},{1,0},{2,3},{3,2},{4,5},{5,4},{6,7},{7,6},{8,9},{9,8},{10,11... | collective-permute-start | bytes 589832 | tf_op jit(solution)/shard_map/ppermute | solution.py:583
  88.3 7.9 %collective-permute-start.6 = (bf16[48,1536]{1,0:T(8,128)(2,1)S(1)}, bf16[48,1536]{1,0:T(8,128)(2,1)S(1)}, u32[]{:S(2)}, u32[]{:S(2)}) collective-permute-start(bf16[48,1536]{1,0:T(8,128)(2,1)S(1)} %project.9.refs_3_.refs_0_), channel_id=1, source_target_pairs={{0,4},{4,0},{8,12},{12,8},{1,5},{5,1},{9,13},{13,9},{2,6},{6,2},{1... | collective-permute-start | bytes 442376 | tf_op jit(solution)/shard_map/ppermute | solution.py:532
  88.4 7.9 %collective-permute-start.12 = (bf16[48,1536]{1,0:T(8,128)(2,1)S(1)}, bf16[48,1536]{1,0:T(8,128)(2,1)S(1)}, u32[]{:S(2)}, u32[]{:S(2)}) collective-permute-start(bf16[48,1536]{1,0:T(8,128)(2,1)S(1)} %after.10.refs_2_), channel_id=1, source_target_pairs={{0,4},{4,0},{8,12},{12,8},{1,5},{5,1},{9,13},{13,9},{2,6},{6,2},{1... | collective-permute-start | bytes 442376 | tf_op jit(solution)/shard_map/ppermute | solution.py:532
  88.9 7.7 %collective-permute-start.13 = (bf16[80,1536]{1,0:T(8,128)(2,1)S(1)}, bf16[80,1536]{1,0:T(8,128)(2,1)S(1)}, u32[]{:S(2)}, u32[]{:S(2)}) collective-permute-start(bf16[80,1536]{1,0:T(8,128)(2,1)S(1)} %project.11.refs_1_.refs_3_.refs_4_), channel_id=1, source_target_pairs={{0,4},{4,0},{8,12},{12,8},{1,5},{5,1},{9,13},{13,9},{2,6},{6,2},{1... | collective-permute-start | bytes 737288 | tf_op jit(solution)/shard_map/ppermute | solution.py:532
  93.9 3.4 %collective-permute-start.20 = (bf16[80,1536]{1,0:T(8,128)(2,1)S(1)}, bf16[80,1536]{1,0:T(8,128)(2,1)S(1)}, u32[]{:S(2)}, u32[]{:S(2)}) collective-permute-start(bf16[80,1536]{1,0:T(8,128)(2,1)S(1)} %project.13.refs_1_.refs_8_), channel_id=1, source_target_pairs={{0,4},{4,0},{8,12},{12,8},{1,5},{5,1},{9,13},{13,9},{2,6},{6,2},{1... | collective-permute-start | bytes 737288 | tf_op jit(solution)/shard_map/ppermute | solution.py:532
  94.0 3.8 %copy-start.6 = (s32[16]{0:T(128)S(1)}, s32[16]{0:T(128)}, u32[]{:S(2)}) copy-start(s32[16]{0:T(128)} %plan_ref.3) | copy-start | bytes 196
  95.6 1.7 %collective-permute-start.19 = (bf16[80,1536]{1,0:T(8,128)(2,1)S(1)}, bf16[80,1536]{1,0:T(8,128)(2,1)S(1)}, u32[]{:S(2)}, u32[]{:S(2)}) collective-permute-start(bf16[80,1536]{1,0:T(8,128)(2,1)S(1)} %after.12.refs_6_), channel_id=1, source_target_pairs={{0,4},{4,0},{8,12},{12,8},{1,5},{5,1},{9,13},{13,9},{2,6},{6,2},{1... | collective-permute-start | bytes 737288 | tf_op jit(solution)/shard_map/ppermute | solution.py:532
  96.2 1.5 %collective-permute-start.25 = (bf16[80,1536]{1,0:T(8,128)(2,1)S(1)}, bf16[80,1536]{1,0:T(8,128)(2,1)S(1)}, u32[]{:S(2)}, u32[]{:S(2)}) collective-permute-start(bf16[80,1536]{1,0:T(8,128)(2,1)S(1)} %after.14.refs_10_), channel_id=1, source_target_pairs={{0,4},{4,0},{8,12},{12,8},{1,5},{5,1},{9,13},{13,9},{2,6},{6,2},{1... | collective-permute-start | bytes 737288 | tf_op jit(solution)/shard_map/ppermute | solution.py:532
  96.3 9.4 %collective-permute-start.27 = (bf16[48,1536]{1,0:T(8,128)(2,1)S(1)}, bf16[48,1536]{1,0:T(8,128)(2,1)S(1)}, u32[]{:S(2)}, u32[]{:S(2)}) collective-permute-start(bf16[48,1536]{1,0:T(8,128)(2,1)S(1)} %project.15.refs_1_.refs_12_), channel_id=1, source_target_pairs={{0,8},{4,12},{8,0},{12,4},{1,9},{5,13},{9,1},{13,5},{2,10},{6,14},... | collective-permute-start | bytes 442376 | tf_op jit(solution)/shard_map/ppermute | solution.py:528
  96.6 12.8 %collective-permute-start.26 = (bf16[48,1536]{1,0:T(8,128)(2,1)S(1)}, bf16[48,1536]{1,0:T(8,128)(2,1)S(1)}, u32[]{:S(2)}, u32[]{:S(2)}) collective-permute-start(bf16[48,1536]{1,0:T(8,128)(2,1)S(1)} %project.15.refs_1_.refs_12_), channel_id=1, source_target_pairs={{0,4},{4,0},{8,12},{12,8},{1,5},{5,1},{9,13},{13,9},{2,6},{6,2},{1... | collective-permute-start | bytes 442376 | tf_op jit(solution)/shard_map/ppermute | solution.py:532
  105.7 4.7 %collective-permute-start.28 = (bf16[48,1536]{1,0:T(8,128)(2,1)S(1)}, bf16[48,1536]{1,0:T(8,128)(2,1)S(1)}, u32[]{:S(2)}, u32[]{:S(2)}) collective-permute-start(bf16[48,1536]{1,0:T(8,128)(2,1)S(1)} %after.15.refs_14_), channel_id=1, source_target_pairs={{0,4},{4,0},{8,12},{12,8},{1,5},{5,1},{9,13},{13,9},{2,6},{6,2},{1... | collective-permute-start | bytes 442376 | tf_op jit(solution)/shard_map/ppermute | solution.py:532

commit v2 on v1

--- a/solution.py
+++ b/solution.py
@@ -582,15 +582,15 @@
                 pairs = [(at, at ^ distance) for at in range(shards)]
                 line[index + 1] = lax.ppermute(line[source], "tp", pairs)
 
-    lines, own, sent = [], [], []
+    lines, own, sent, blocks = [], [], [], []
     last = len(sizes) - 1
 
     def finish(chunk):
         own.append(add("late", chunk, add("first", chunk))[0])
         sent.append(from_chips(own[-1]))
 
-    def fence(chunk, block):
-        passed, anchors = [], []
+    def fence(chunk, block, *anchors):
+        passed, anchors = [], list(anchors)
         if chunk:
             before = lines[chunk - 1]
             passed = [before[piece] for piece in relayed]
@@ -601,8 +601,10 @@
         if 1 < chunk <= last:
             finish(chunk - 2)
             anchors.append(own[-1])
-        if chunk > 2:
-            anchors += sent[chunk - 3]
+        if 2 < chunk <= last:
+            arrived = after(sent[chunk - 3], own[-1:])
+            blocks.extend(all_blocks(own[chunk - 3], arrived))
+            anchors += blocks[-2 * chips :]
         if passed:
             passed = after([*passed, *block], anchors)
             before.update(zip(relayed, passed))
@@ -619,19 +621,28 @@
         start(lines[-1], direct)
         if chunk == 1:
             turns = angles(groups, lengths, frequency, lines[1][0])
+    common = widths, slots, lengths, plan
+
+    def attended(at, prior, blocks, outputs):
+        known = workers * sum(sizes[: at + 1])
+        return attend(chips, groups[: at + 1], known, prior, *common, blocks, outputs)
+
+    sums = list(add("first", last - 1))
+    for at in range(last - 2, last - 1):
+        blocks += all_blocks(own[at], after(sent[at], own[at + 1 : at + 2] or [sums[1]]))
+    *outputs, token = attended(last - 2, 0, blocks, ())
+    sums[1:] = after(sums[1:], [token])
     fence(last + 1, [])
     start(lines[-1], kinds["late"])
-    for chunk in (last - 1, last):
-        finish(chunk)
-    blocks = []
-    for at in range(last):
-        blocks += all_blocks(own[at], after(sent[at], own[at + 1 : at + 2]))
-    sent.append(from_chips(own[last]))
-    known = workers * sum(sizes[:-1])
-    common = widths, slots, lengths, plan
-    *outputs, token = attend(chips, groups[:-1], known, 0, *common, blocks, ())
+    own.append(add("late", last - 1, sums)[0])
+    sent.append(from_chips(own[-1]))
+    finish(last)
+    blocks += all_blocks(own[last - 1], after(sent[last - 1], own[last:]))
+    prior = workers * sum(sizes[:-2])
+    *outputs, token = attended(last - 1, prior, blocks, outputs)
     blocks += all_blocks(own[last], after(sent[last], [token]))
-    return tuple(attend(chips, groups, workers * live, known, *common, blocks, outputs)[:2])
+    prior = workers * sum(sizes[:-1])
+    return tuple(attended(last, prior, blocks, outputs)[:2])
 
 
 def solution(mesh):

time: 116 us -> 116 us (level)
  the two profiles are of different devices: /device:TPU:0 before, /device:TPU:15 now
where the time goes in v2:
time: 116 us
  Pallas kernels  57 us (49%)
  starting transfers between devices  35.8 us (31%)
  waiting for transfers between devices  19.5 us (17%)
  local copies, waits for them, and re-layouts  2.27 us (2%)
    pallas_call x8, Pallas kernels, project(): pl.pallas_call(functools.partial(project_kernel, masks, bool(carried), fi...  22.9 us
    pallas_call x3, Pallas kernels, attend(): pl.pallas_call(functools.partial(attend_kernel, chips, groups, known, pri...  21.3 us
    ppermute x9, starting transfers between devices, swap_cores(): return lax.ppermute(value, 'req', [(d, d ^ 1) for d in range(2 * chips)])  16.1 us
    ppermute x12, starting transfers between devices, start(): line[index + 1] = lax.ppermute(line[source], 'tp', pairs)  16 us
    ppermute x12, waiting for transfers between devices, start(): line[index + 1] = lax.ppermute(line[source], 'tp', pairs)  13.8 us
    pallas_call x1, Pallas kernels, load(): pl.pallas_call(kernel, in_specs=[anywhere, anywhere], out_specs=[vmem, vm...  6.06 us
    pallas_call x3, Pallas kernels, deal(): pl.pallas_call(functools.partial(deal_kernel, chips, bases, sizes, twins)...  5.54 us
    ppermute x8, starting transfers between devices, shift_chips(): return lax.ppermute(value, 'req', pairs)  3.7 us
  transfers between devices with their start and end apart: 29, of which 9 were waited for; matrix products, arithmetic and copies ran while one was open for 0% of the time, Pallas kernels for 42%

profile of v2, /device:TPU:15, one launch (start us, length us, event | category | flops | bytes accessed | tf_op | source)
XLA Modules:
  0.0 115.7 jit_solution(2868797310570892076)
XLA Ops:
  0.6 0.7 collective-permute-start
  1.4 1.6 %copy-done.2 = bf16[512,2048]{1,0:T(8,128)(2,1)S(1)} copy-done((bf16[512,2048]{1,0:T(8,128)(2,1)S(1)}, bf16[512,2048]{1,0:T(8,128)(2,1)}, u32[]{:S(2)}) %copy-start.2) | copy-done | bytes 2097176
  3.0 0.7 copy-done.4
  3.6 1.3 %deal.3 = (bf16[48,2048]{1,0:T(8,128)(2,1)S(1)}, bf16[1,48,2048]{2,1,0:T(8,128)(2,1)S(1)}) custom-call(s32[4]{0:T(128)S(1)} %copy-done.4, bf16[512,2048]{1,0:T(8,128)(2,1)S(1)} %copy-done.2), custom_call_target="tpu_custom_call" | custom-call | tf_op jit(solution)/shard_map/deal/pallas_call | solution.py:86
  4.9 0.5 collective-permute-done.refs_0_.refs_1_
  5.4 1.3 %deal.4 = (bf16[48,2048]{1,0:T(8,128)(2,1)S(1)}, bf16[1,48,2048]{2,1,0:T(8,128)(2,1)S(1)}) custom-call(s32[4]{0:T(128)S(1)} %copy-done.4, bf16[512,2048]{1,0:T(8,128)(2,1)S(1)} %collective-permute-done.refs_0_.refs_1_, bf16[48,2048]{1,0:T(8,128)(2,1)S(1)} %get-tuple-element.50.refs_1_, bf16[1,48,2048]{2,1,0:T(8,128)(2,1)S(1)} %get-tuple-element.51.refs_2_), custom_call_target="tpu_custom_call" | custom-call | tf_op jit(solution)/shard_map/deal/pallas_call | solution.py:86
  6.7 0.3 collective-permute-start.1
  7.0 2.9 %deal.5 = (bf16[80,2048]{1,0:T(8,128)(2,1)S(1)}, bf16[1,80,2048]{2,1,0:T(8,128)(2,1)S(1)}, bf16[80,2048]{1,0:T(8,128)(2,1)S(1)}, bf16[1,80,2048]{2,1,0:T(8,128)(...) custom-call(s32[4]{0:T(128)S(1)} %copy-done.4, bf16[512,2048]{1,0:T(8,128)(2,1)S(1)} %copy-done.3, ...), custom_call_target="tpu_custom_call" | custom-call | tf_op jit(solution)/shard_map/deal/pallas_call | solution.py:86
  10.0 2.9 %collective-permute-done.1.refs_0_ = bf16[48,2048]{1,0:T(8,128)(2,1)S(1)} collective-permute-done((bf16[48,2048]{1,0:T(8,128)(2,1)S(1)}, bf16[48,2048]{1,0:T(8,128)(2,1)S(1)}, u32[]{:S(2)}, u32[]{:S(2)}) %collective-permute-start.1) | collective-permute-done | bytes 196640 | tf_op jit(solution)/shard_map/ppermute | solution.py:528
  12.9 0.3 collective-permute-start.3
  13.2 0.2 collective-permute-start.4
  13.4 2.3 %collective-permute-start.2 = (bf16[48,2048]{1,0:T(8,128)(2,1)S(1)}, bf16[48,2048]{1,0:T(8,128)(2,1)S(1)}, u32[]{:S(2)}, u32[]{:S(2)}) collective-permute-start(bf16[48,2048]{1,0:T(8,128)(2,1)S(1)} %get-tuple-element.55.anchor_ref.refs_0_), channel_id=1, source_target_pairs={{0,2},{1,3},{2,0},{3,1},{4,6},{5,7},{6,4},{7,5},{8,10},{9,11},{10,... | collective-permute-start | bytes 589832 | tf_op jit(solution)/shard_map/ppermute | solution.py:583
  15.7 6.1 %load.1 = (bf16[8192,1024]{1,0:T(8,128)(2,1)S(1)}, f32[8,128]{1,0:T(8,128)S(1)}) custom-call(bf16[8192,1024]{1,0:T(8,128)(2,1)} %weight_ref.1, bf16[48,2048]{1,0:T(8,128)(2,1)S(1)} %get-tuple-element.55.anchor_ref.refs_0_), custom_call_target="tpu_custom_call" | custom-call | tf_op jit(solution)/shard_map/load/pallas_call | solution.py:206
  21.8 1.3 %collective-permute-start.9 = (bf16[80,2048]{1,0:T(8,128)(2,1)S(1)}, bf16[80,2048]{1,0:T(8,128)(2,1)S(1)}, u32[]{:S(2)}, u32[]{:S(2)}) collective-permute-start(bf16[80,2048]{1,0:T(8,128)(2,1)S(1)} %bitcast.14), channel_id=1, source_target_pairs={{0,8},{4,12},{8,0},{12,4},{1,9},{5,13},{9,1},{13,5},{2,10},{6,14},... | collective-permute-start | bytes 983048 | tf_op jit(solution)/shard_map/ppermute | solution.py:528
  23.1 0.0 collective-permute-done.4.refs_2_
  23.1 0.2 collective-permute-done.2.refs_0_
  23.3 1.1 collective-permute-start.10
  24.4 0.4 collective-permute-start.8
  24.8 0.7 collective-permute-start.5
  25.5 1.1 angles.1
  26.6 4.0 %project.8 = (f32[48,1536]{1,0:T(8,128)S(1)}, f32[48,128]{1,0:T(8,128)S(1)}) custom-call(bf16[48,2048]{1,0:T(8,128)(2,1)S(1)} %get-tuple-element.55.anchor_ref.refs_0_, bf16[48,2048]{1,0:T(8,128)(2,1)S(1)} %get-tuple-element.61.refs_1_, bf16[48,2048]{1,0:T(8,128)(2,1)S(1)} %collective-permute-done.4.refs_2_, f32[1,8192]{1,0:T(1,128)S(1)} %bitcast.5, ...), custom_call_target="tpu_custom_call" | custom-call | tf_op jit(solution)/shard_map/project/pallas_call | solution.py:281
  30.7 11.1 %collective-permute-done.5.refs_0_ = bf16[48,2048]{1,0:T(8,128)(2,1)S(1)} collective-permute-done((bf16[48,2048]{1,0:T(8,128)(2,1)S(1)}, bf16[48,2048]{1,0:T(8,128)(2,1)S(1)}, u32[]{:S(2)}, u32[]{:S(2)}) %collective-permute-start.5) | collective-permute-done | bytes 196640 | tf_op jit(solution)/shard_map/ppermute | solution.py:583
  41.7 1.6 %project.9.refs_3_.refs_4_.refs_0_ = bf16[48,1536]{1,0:T(8,128)(2,1)S(1)} custom-call(bf16[48,2048]{1,0:T(8,128)(2,1)S(1)} %collective-permute-done.5.refs_0_, f32[1,8192]{1,0:T(1,128)S(1)} %bitcast.6, bf16[8192,1024]{1,0:T(8,128)(2,1)S(1)} %get-tuple-element.62.refs_4_.refs_2_, bf16[8192,256]{1,0:T(8,128)(2,1)S(1)} %copy-done, ...), custom_call_target="tpu_custom_call" | custom-call | tf_op jit(solution)/shard_map/project/pallas_call | solution.py:281
  43.3 0.0 collective-permute-done.10.refs_2_
  43.3 0.0 collective-permute-done.8.refs_0_
  43.4 2.3 %collective-permute-start.11 = (bf16[80,2048]{1,0:T(8,128)(2,1)S(1)}, bf16[80,2048]{1,0:T(8,128)(2,1)S(1)}, u32[]{:S(2)}, u32[]{:S(2)}) collective-permute-start(bf16[80,2048]{1,0:T(8,128)(2,1)S(1)} %get-tuple-element.72.refs_1_), channel_id=1, source_target_pairs={{0,1},{1,0},{2,3},{3,2},{4,5},{5,4},{6,7},{7,6},{8,9},{9,8},{10,11... | collective-permute-start | bytes 983048 | tf_op jit(solution)/shard_map/ppermute | solution.py:583
  45.6 2.6 %collective-permute-start.15 = (bf16[80,2048]{1,0:T(8,128)(2,1)S(1)}, bf16[80,2048]{1,0:T(8,128)(2,1)S(1)}, u32[]{:S(2)}, u32[]{:S(2)}) collective-permute-start(bf16[80,2048]{1,0:T(8,128)(2,1)S(1)} %get-tuple-element.77.refs_0_), channel_id=1, source_target_pairs={{0,2},{1,3},{2,0},{3,1},{4,6},{5,7},{6,4},{7,5},{8,10},{9,11},{10,... | collective-permute-start | bytes 983048 | tf_op jit(solution)/shard_map/ppermute | solution.py:583
  48.2 1.4 %collective-permute-start.17 = (bf16[80,2048]{1,0:T(8,128)(2,1)S(1)}, bf16[80,2048]{1,0:T(8,128)(2,1)S(1)}, u32[]{:S(2)}, u32[]{:S(2)}) collective-permute-start(bf16[80,2048]{1,0:T(8,128)(2,1)S(1)} %get-tuple-element.77.refs_0_), channel_id=1, source_target_pairs={{0,1},{1,0},{2,3},{3,2},{4,5},{5,4},{6,7},{7,6},{8,9},{9,8},{10,11... | collective-permute-start | bytes 983048 | tf_op jit(solution)/shard_map/ppermute | solution.py:583
  49.6 0.2 collective-permute-start.7
  49.9 4.2 %project.10 = (f32[80,1536]{1,0:T(8,128)S(1)}, f32[80,128]{1,0:T(8,128)S(1)}) custom-call(bf16[80,2048]{1,0:T(8,128)(2,1)S(1)} %get-tuple-element.65.anchor_ref.refs_0_, bf16[80,2048]{1,0:T(8,128)(2,1)S(1)} %get-tuple-element.72.refs_1_, bf16[80,2048]{1,0:T(8,128)(2,1)S(1)} %collective-permute-done.10.refs_2_, f32[1,8192]{1,0:T(1,128)S(1)} %bitcast.7, ...), custom_call_target="tpu_custom_call" | custom-call | tf_op jit(solution)/shard_map/project/pallas_call | solution.py:281
  54.1 2.1 %collective-permute-done.11.refs_0_ = bf16[80,2048]{1,0:T(8,128)(2,1)S(1)} collective-permute-done((bf16[80,2048]{1,0:T(8,128)(2,1)S(1)}, bf16[80,2048]{1,0:T(8,128)(2,1)S(1)}, u32[]{:S(2)}, u32[]{:S(2)}) %collective-permute-start.11) | collective-permute-done | bytes 327712 | tf_op jit(solution)/shard_map/ppermute | solution.py:583
  56.2 1.7 %project.11.refs_1_.refs_3_.refs_4_ = bf16[80,1536]{1,0:T(8,128)(2,1)S(1)} custom-call(bf16[80,2048]{1,0:T(8,128)(2,1)S(1)} %collective-permute-done.11.refs_0_, f32[1,8192]{1,0:T(1,128)S(1)} %bitcast.8, bf16[8192,1024]{1,0:T(8,128)(2,1)S(1)} %get-tuple-element.62.refs_4_.refs_2_, bf16[8192,256]{1,0:T(8,128)(2,1)S(1)} %copy-done, ...), custom_call_target="tpu_custom_call" | custom-call | tf_op jit(solution)/shard_map/project/pallas_call | solution.py:281
  57.9 0.1 collective-permute-start.14
  58.0 0.0 collective-permute-done.7.refs_0_
  58.0 7.4 %collective-permute-start.6 = (bf16[48,1536]{1,0:T(8,128)(2,1)S(1)}, bf16[48,1536]{1,0:T(8,128)(2,1)S(1)}, u32[]{:S(2)}, u32[]{:S(2)}) collective-permute-start(bf16[48,1536]{1,0:T(8,128)(2,1)S(1)} %project.9.refs_3_.refs_4_.refs_0_), channel_id=1, source_target_pairs={{0,4},{4,0},{8,12},{12,8},{1,5},{5,1},{9,13},{13,9},{2,6},{6,2},{1... | collective-permute-start | bytes 442376 | tf_op jit(solution)/shard_map/ppermute | solution.py:532
  65.4 0.1 collective-permute-start.12
  65.5 0.9 collective-permute-done.6.refs_5_.refs_1_
  66.4 0.0 collective-permute-done.15.refs_0_
  66.4 0.4 collective-permute-done.12.refs_7_.refs_3_
  66.7 2.2 %collective-permute-start.19 = (bf16[80,2048]{1,0:T(8,128)(2,1)S(1)}, bf16[80,2048]{1,0:T(8,128)(2,1)S(1)}, u32[]{:S(2)}, u32[]{:S(2)}) collective-permute-start(bf16[80,2048]{1,0:T(8,128)(2,1)S(1)} %get-tuple-element.80.refs_1_), channel_id=1, source_target_pairs={{0,1},{1,0},{2,3},{3,2},{4,5},{5,4},{6,7},{7,6},{8,9},{9,8},{10,11... | collective-permute-start | bytes 983048 | tf_op jit(solution)/shard_map/ppermute | solution.py:583
  69.0 1.1 collective-permute-start.13
  70.1 4.2 %project.12 = (f32[80,1536]{1,0:T(8,128)S(1)}, f32[80,128]{1,0:T(8,128)S(1)}) custom-call(bf16[80,2048]{1,0:T(8,128)(2,1)S(1)} %get-tuple-element.77.refs_0_, bf16[80,2048]{1,0:T(8,128)(2,1)S(1)} %get-tuple-element.80.refs_1_, bf16[80,2048]{1,0:T(8,128)(2,1)S(1)} %collective-permute-done.17.refs_2_, f32[1,8192]{1,0:T(1,128)S(1)} %bitcast.9, ...), custom_call_target="tpu_custom_call" | custom-call | tf_op jit(solution)/shard_map/project/pallas_call | solution.py:281
  74.3 0.0 collective-permute-done.14.refs_0_
  74.3 0.1 collective-permute-start.18
  74.4 1.4 %collective-permute-start.22 = (bf16[48,2048]{1,0:T(8,128)(2,1)S(1)}, bf16[48,2048]{1,0:T(8,128)(2,1)S(1)}, u32[]{:S(2)}, u32[]{:S(2)}) collective-permute-start(bf16[48,2048]{1,0:T(8,128)(2,1)S(1)} %get-tuple-element.86.refs_0_), channel_id=1, source_target_pairs={{0,2},{1,3},{2,0},{3,1},{4,6},{5,7},{6,4},{7,5},{8,10},{9,11},{10,... | collective-permute-start | bytes 589832 | tf_op jit(solution)/shard_map/ppermute | solution.py:583
  75.8 1.4 %collective-permute-start.23 = (bf16[48,2048]{1,0:T(8,128)(2,1)S(1)}, bf16[48,2048]{1,0:T(8,128)(2,1)S(1)}, u32[]{:S(2)}, u32[]{:S(2)}) collective-permute-start(bf16[48,2048]{1,0:T(8,128)(2,1)S(1)} %get-tuple-element.86.refs_0_), channel_id=1, source_target_pairs={{0,1},{1,0},{2,3},{3,2},{4,5},{5,4},{6,7},{7,6},{8,9},{9,8},{10,11... | collective-permute-start | bytes 589832 | tf_op jit(solution)/shard_map/ppermute | solution.py:583
  77.2 0.0 collective-permute-done.13.refs_5_
  77.2 0.0 collective-permute-done.18.refs_7_
  77.2 7.5 %attend.3 = (bf16[512,1024]{1,0:T(8,128)(2,1)}, bf16[2,512,256]{2,1,0:T(8,128)(2,1)}, f32[8,128]{1,0:T(8,128)S(1)}) custom-call(s32[4]{0:T(128)S(1)} %copy-done.5, s32[16]{0:T(128)S(1)} %copy-done.6, bf16[48,1536]{1,0:T(8,128)(2,1)S(1)} %project.9.refs_3_.refs_4_.refs_0_, bf16[48,1536]{1,0:T(8,128)(2,1)S(1)} %collective-permute-done.6.refs_5_.refs_1_, ...), custom_call_target="tpu_custom_call" | custom-call | tf_op jit(solution)/shard_map/attend/pallas_call | solution.py:499
  84.7 0.0 collective-permute-done.19.refs_0_
  84.8 1.7 %project.13.refs_8_ = bf16[80,1536]{1,0:T(8,128)(2,1)S(1)} custom-call(bf16[80,2048]{1,0:T(8,128)(2,1)S(1)} %collective-permute-done.19.refs_0_, f32[1,8192]{1,0:T(1,128)S(1)} %bitcast.10, bf16[8192,1024]{1,0:T(8,128)(2,1)S(1)} %get-tuple-element.62.refs_4_.refs_2_, bf16[8192,256]{1,0:T(8,128)(2,1)S(1)} %copy-done, bf16[8192,256]{1,0:T(8,128)(2,1)S(1)} %copy-done.1, ...), custom_call_target="tpu_custom_call" | custom-call | tf_op jit(solution)/shard_map/project/pallas_call | solution.py:281
  86.5 0.1 collective-permute-start.21
  86.6 0.1 collective-permute-start.24
  86.7 4.0 %project.14 = (f32[48,1536]{1,0:T(8,128)S(1)}, f32[48,128]{1,0:T(8,128)S(1)}) custom-call(bf16[48,2048]{1,0:T(8,128)(2,1)S(1)} %get-tuple-element.86.refs_0_, bf16[48,2048]{1,0:T(8,128)(2,1)S(1)} %after.15.refs_1_, bf16[48,2048]{1,0:T(8,128)(2,1)S(1)} %collective-permute-done.23.refs_1_.refs_2_, f32[1,8192]{1,0:T(1,128)S(1)} %bitcast.11, ...), custom_call_target="tpu_custom_call" | custom-call | tf_op jit(solution)/shard_map/project/pallas_call | solution.py:281
  90.7 1.3 %collective-permute-start.20 = (bf16[80,1536]{1,0:T(8,128)(2,1)S(1)}, bf16[80,1536]{1,0:T(8,128)(2,1)S(1)}, u32[]{:S(2)}, u32[]{:S(2)}) collective-permute-start(bf16[80,1536]{1,0:T(8,128)(2,1)S(1)} %project.13.refs_8_), channel_id=1, source_target_pairs={{0,4},{4,0},{8,12},{12,8},{1,5},{5,1},{9,13},{13,9},{2,6},{6,2},{1... | collective-permute-start | bytes 737288 | tf_op jit(solution)/shard_map/ppermute | solution.py:532
  92.0 0.4 collective-permute-done.24.refs_0_
  92.4 1.6 %project.15.refs_1_.refs_12_ = bf16[48,1536]{1,0:T(8,128)(2,1)S(1)} custom-call(bf16[48,2048]{1,0:T(8,128)(2,1)S(1)} %collective-permute-done.24.refs_0_, f32[1,8192]{1,0:T(1,128)S(1)} %bitcast.12, bf16[8192,1024]{1,0:T(8,128)(2,1)S(1)} %get-tuple-element.62.refs_4_.refs_2_, bf16[8192,256]{1,0:T(8,128)(2,1)S(1)} %copy-done, bf16[8192,256]{1,0:T(8,128)(2,1)S(1)} %copy-done.1, ...), custom_call_target="tpu_custom_call" | custom-call | tf_op jit(solution)/shard_map/project/pallas_call | solution.py:281
  93.9 1.7 %collective-permute-start.25 = (bf16[80,1536]{1,0:T(8,128)(2,1)S(1)}, bf16[80,1536]{1,0:T(8,128)(2,1)S(1)}, u32[]{:S(2)}, u32[]{:S(2)}) collective-permute-start(bf16[80,1536]{1,0:T(8,128)(2,1)S(1)} %after.16.refs_10_), channel_id=1, source_target_pairs={{0,4},{4,0},{8,12},{12,8},{1,5},{5,1},{9,13},{13,9},{2,6},{6,2},{1... | collective-permute-start | bytes 737288 | tf_op jit(solution)/shard_map/ppermute | solution.py:532
  95.6 1.4 %collective-permute-start.27 = (bf16[48,1536]{1,0:T(8,128)(2,1)S(1)}, bf16[48,1536]{1,0:T(8,128)(2,1)S(1)}, u32[]{:S(2)}, u32[]{:S(2)}) collective-permute-start(bf16[48,1536]{1,0:T(8,128)(2,1)S(1)} %project.15.refs_1_.refs_12_), channel_id=1, source_target_pairs={{0,8},{4,12},{8,0},{12,4},{1,9},{5,13},{9,1},{13,5},{2,10},{6,14},... | collective-permute-start | bytes 442376 | tf_op jit(solution)/shard_map/ppermute | solution.py:528
  97.0 0.3 collective-permute-start.26
  97.3 6.9 %attend.4 = (bf16[512,1024]{1,0:T(8,128)(2,1)}, bf16[2,512,256]{2,1,0:T(8,128)(2,1)}, f32[8,128]{1,0:T(8,128)S(1)}) custom-call(s32[4]{0:T(128)S(1)} %copy-done.5, s32[16]{0:T(128)S(1)} %copy-done.6, bf16[48,1536]{1,0:T(8,128)(2,1)S(1)} %project.9.refs_3_.refs_4_.refs_0_, ...), custom_call_target="tpu_custom_call", output_to_operand_aliasing={{0}: (14, {}), {1}: (15, {})} | custom-call | tf_op jit(solution)/shard_map/attend/pallas_call | solution.py:499
  104.2 3.4 %collective-permute-start.28 = (bf16[48,1536]{1,0:T(8,128)(2,1)S(1)}, bf16[48,1536]{1,0:T(8,128)(2,1)S(1)}, u32[]{:S(2)}, u32[]{:S(2)}) collective-permute-start(bf16[48,1536]{1,0:T(8,128)(2,1)S(1)} %after.17.refs_14_), channel_id=1, source_target_pairs={{0,4},{4,0},{8,12},{12,8},{1,5},{5,1},{9,13},{13,9},{2,6},{6,2},{1... | collective-permute-start | bytes 442376 | tf_op jit(solution)/shard_map/ppermute | solution.py:532
  107.6 1.0 collective-permute-done.28.refs_15_
  108.6 7.0 %attend.5 = (bf16[512,1024]{1,0:T(8,128)(2,1)}, bf16[2,512,256]{2,1,0:T(8,128)(2,1)}, f32[8,128]{1,0:T(8,128)}) custom-call(s32[4]{0:T(128)S(1)} %copy-done.5, s32[16]{0:T(128)S(1)} %copy-done.6, bf16[48,1536]{1,0:T(8,128)(2,1)S(1)} %project.9.refs_3_.refs_4_.refs_0_, ...), custom_call_target="tpu_custom_call", output_to_operand_aliasing={{0}: (18, {}), {1}: (19, {})} | custom-call | tf_op jit(solution)/shard_map/attend/pallas_call | solution.py:499
  (42 shorter events, 0.2 us)
Async XLA Ops:
  0.6 4.7 %collective-permute-start = (bf16[512,2048]{1,0:T(8,128)(2,1)}, bf16[512,2048]{1,0:T(8,128)(2,1)S(1)}, u32[]{:S(2)}, u32[]{:S(2)}) collective-permute-start(bf16[512,2048]{1,0:T(8,128)(2,1)} %refs_0_.3), channel_id=1, source_target_pairs={{0,4},{4,0},{8,12},{12,8},{1,5},{5,1},{9,13},{13,9},{2,6},{6,2},{1... | collective-permute-start | bytes 6291464 | tf_op jit(solution)/shard_map/ppermute | solution.py:532
  1.4 1.6 %copy-start.2 = (bf16[512,2048]{1,0:T(8,128)(2,1)S(1)}, bf16[512,2048]{1,0:T(8,128)(2,1)}, u32[]{:S(2)}) copy-start(bf16[512,2048]{1,0:T(8,128)(2,1)} %refs_0_.3) | copy-start | bytes 6291460
  3.0 0.7 copy-start.4
  3.6 3.4 %copy-start.3 = (bf16[512,2048]{1,0:T(8,128)(2,1)S(1)}, bf16[512,2048]{1,0:T(8,128)(2,1)}, u32[]{:S(2)}) copy-start(bf16[512,2048]{1,0:T(8,128)(2,1)} %refs_0_.3) | copy-start | bytes 6291460
  6.7 6.2 %collective-permute-start.1 = (bf16[48,2048]{1,0:T(8,128)(2,1)S(1)}, bf16[48,2048]{1,0:T(8,128)(2,1)S(1)}, u32[]{:S(2)}, u32[]{:S(2)}) collective-permute-start(bf16[48,2048]{1,0:T(8,128)(2,1)S(1)} %bitcast.16), channel_id=1, source_target_pairs={{0,8},{4,12},{8,0},{12,4},{1,9},{5,13},{9,1},{13,5},{2,10},{6,14},... | collective-permute-start | bytes 589832 | tf_op jit(solution)/shard_map/ppermute | solution.py:528
  12.9 8.9 %collective-permute-start.3 = (bf16[80,2048]{1,0:T(8,128)(2,1)S(1)}, bf16[80,2048]{1,0:T(8,128)(2,1)S(1)}, u32[]{:S(2)}, u32[]{:S(2)}) collective-permute-start(bf16[80,2048]{1,0:T(8,128)(2,1)S(1)} %bitcast.13), channel_id=1, source_target_pairs={{0,8},{4,12},{8,0},{12,4},{1,9},{5,13},{9,1},{13,5},{2,10},{6,14},... | collective-permute-start | bytes 983048 | tf_op jit(solution)/shard_map/ppermute | solution.py:528
  13.2 12.3 %copy-start.8 = (bf16[8192]{0:T(1024)(128)(2,1)S(1)}, bf16[8192]{0:T(1024)(128)(2,1)}, u32[]{:S(2)}) copy-start(bf16[8192]{0:T(1024)(128)(2,1)} %param.9) | copy-start | bytes 49156
  13.2 12.3 %copy-start.5 = (s32[4]{0:T(128)S(1)}, s32[4]{0:T(128)}, u32[]{:S(2)}) copy-start(s32[4]{0:T(128)} %lengths_ref.13) | copy-start | bytes 52
  13.2 12.3 %copy-start.7 = (f32[1,128]{1,0:T(1,128)S(1)}, f32[1,128]{1,0:T(1,128)}, u32[]{:S(2)}) copy-start(f32[1,128]{1,0:T(1,128)} %constant.2.clone.frequency_ref) | copy-start | bytes 1540
  13.2 9.9 %collective-permute-start.4 = (bf16[48,2048]{1,0:T(8,128)(2,1)S(1)}, bf16[48,2048]{1,0:T(8,128)(2,1)S(1)}, u32[]{:S(2)}, u32[]{:S(2)}) collective-permute-start(bf16[48,2048]{1,0:T(8,128)(2,1)S(1)} %get-tuple-element.55.anchor_ref.refs_0_), channel_id=1, source_target_pairs={{0,1},{1,0},{2,3},{3,2},{4,5},{5,4},{6,7},{7,6},{8,9},{9,8},{10,11... | collective-permute-start | bytes 589832 | tf_op jit(solution)/shard_map/ppermute | solution.py:583
  13.4 10.0 %collective-permute-start.2 = (bf16[48,2048]{1,0:T(8,128)(2,1)S(1)}, bf16[48,2048]{1,0:T(8,128)(2,1)S(1)}, u32[]{:S(2)}, u32[]{:S(2)}) collective-permute-start(bf16[48,2048]{1,0:T(8,128)(2,1)S(1)} %get-tuple-element.55.anchor_ref.refs_0_), channel_id=1, source_target_pairs={{0,2},{1,3},{2,0},{3,1},{4,6},{5,7},{6,4},{7,5},{8,10},{9,11},{10,... | collective-permute-start | bytes 589832 | tf_op jit(solution)/shard_map/ppermute | solution.py:583
  15.7 10.9 %copy-start = (bf16[8192,256]{1,0:T(8,128)(2,1)S(1)}, bf16[8192,256]{1,0:T(8,128)(2,1)}, u32[]{:S(2)}) copy-start(bf16[8192,256]{1,0:T(8,128)(2,1)} %refs_3_.7) | copy-start | bytes 12582916
  15.7 10.9 %copy-start.1 = (bf16[8192,256]{1,0:T(8,128)(2,1)S(1)}, bf16[8192,256]{1,0:T(8,128)(2,1)}, u32[]{:S(2)}) copy-start(bf16[8192,256]{1,0:T(8,128)(2,1)} %refs_4_.7) | copy-start | bytes 12582916
  21.8 21.5 %collective-permute-start.9 = (bf16[80,2048]{1,0:T(8,128)(2,1)S(1)}, bf16[80,2048]{1,0:T(8,128)(2,1)S(1)}, u32[]{:S(2)}, u32[]{:S(2)}) collective-permute-start(bf16[80,2048]{1,0:T(8,128)(2,1)S(1)} %bitcast.14), channel_id=1, source_target_pairs={{0,8},{4,12},{8,0},{12,4},{1,9},{5,13},{9,1},{13,5},{2,10},{6,14},... | collective-permute-start | bytes 983048 | tf_op jit(solution)/shard_map/ppermute | solution.py:528
  23.3 20.0 %collective-permute-start.10 = (bf16[80,2048]{1,0:T(8,128)(2,1)S(1)}, bf16[80,2048]{1,0:T(8,128)(2,1)S(1)}, u32[]{:S(2)}, u32[]{:S(2)}) collective-permute-start(bf16[80,2048]{1,0:T(8,128)(2,1)S(1)} %get-tuple-element.65.anchor_ref.refs_0_), channel_id=1, source_target_pairs={{0,1},{1,0},{2,3},{3,2},{4,5},{5,4},{6,7},{7,6},{8,9},{9,8},{10,11... | collective-permute-start | bytes 983048 | tf_op jit(solution)/shard_map/ppermute | solution.py:583
  24.4 18.9 %collective-permute-start.8 = (bf16[80,2048]{1,0:T(8,128)(2,1)S(1)}, bf16[80,2048]{1,0:T(8,128)(2,1)S(1)}, u32[]{:S(2)}, u32[]{:S(2)}) collective-permute-start(bf16[80,2048]{1,0:T(8,128)(2,1)S(1)} %get-tuple-element.65.anchor_ref.refs_0_), channel_id=1, source_target_pairs={{0,2},{1,3},{2,0},{3,1},{4,6},{5,7},{6,4},{7,5},{8,10},{9,11},{10,... | collective-permute-start | bytes 983048 | tf_op jit(solution)/shard_map/ppermute | solution.py:583
  24.8 16.9 %collective-permute-start.5 = (bf16[48,2048]{1,0:T(8,128)(2,1)S(1)}, bf16[48,2048]{1,0:T(8,128)(2,1)S(1)}, u32[]{:S(2)}, u32[]{:S(2)}) collective-permute-start(bf16[48,2048]{1,0:T(8,128)(2,1)S(1)} %get-tuple-element.61.refs_1_), channel_id=1, source_target_pairs={{0,1},{1,0},{2,3},{3,2},{4,5},{5,4},{6,7},{7,6},{8,9},{9,8},{10,11... | collective-permute-start | bytes 589832 | tf_op jit(solution)/shard_map/ppermute | solution.py:583
  43.4 12.8 %collective-permute-start.11 = (bf16[80,2048]{1,0:T(8,128)(2,1)S(1)}, bf16[80,2048]{1,0:T(8,128)(2,1)S(1)}, u32[]{:S(2)}, u32[]{:S(2)}) collective-permute-start(bf16[80,2048]{1,0:T(8,128)(2,1)S(1)} %get-tuple-element.72.refs_1_), channel_id=1, source_target_pairs={{0,1},{1,0},{2,3},{3,2},{4,5},{5,4},{6,7},{7,6},{8,9},{9,8},{10,11... | collective-permute-start | bytes 983048 | tf_op jit(solution)/shard_map/ppermute | solution.py:583
  45.6 19.7 %collective-permute-start.16 = (bf16[48,2048]{1,0:T(8,128)(2,1)S(1)}, bf16[48,2048]{1,0:T(8,128)(2,1)S(1)}, u32[]{:S(2)}, u32[]{:S(2)}) collective-permute-start(bf16[48,2048]{1,0:T(8,128)(2,1)S(1)} %bitcast.15), channel_id=1, source_target_pairs={{0,8},{4,12},{8,0},{12,4},{1,9},{5,13},{9,1},{13,5},{2,10},{6,14},... | collective-permute-start | bytes 589832 | tf_op jit(solution)/shard_map/ppermute | solution.py:528
  45.6 20.7 %collective-permute-start.15 = (bf16[80,2048]{1,0:T(8,128)(2,1)S(1)}, bf16[80,2048]{1,0:T(8,128)(2,1)S(1)}, u32[]{:S(2)}, u32[]{:S(2)}) collective-permute-start(bf16[80,2048]{1,0:T(8,128)(2,1)S(1)} %get-tuple-element.77.refs_0_), channel_id=1, source_target_pairs={{0,2},{1,3},{2,0},{3,1},{4,6},{5,7},{6,4},{7,5},{8,10},{9,11},{10,... | collective-permute-start | bytes 983048 | tf_op jit(solution)/shard_map/ppermute | solution.py:583
  48.2 18.1 %collective-permute-start.17 = (bf16[80,2048]{1,0:T(8,128)(2,1)S(1)}, bf16[80,2048]{1,0:T(8,128)(2,1)S(1)}, u32[]{:S(2)}, u32[]{:S(2)}) collective-permute-start(bf16[80,2048]{1,0:T(8,128)(2,1)S(1)} %get-tuple-element.77.refs_0_), channel_id=1, source_target_pairs={{0,1},{1,0},{2,3},{3,2},{4,5},{5,4},{6,7},{7,6},{8,9},{9,8},{10,11... | collective-permute-start | bytes 983048 | tf_op jit(solution)/shard_map/ppermute | solution.py:583
  49.6 8.4 %collective-permute-start.7 = (bf16[48,1536]{1,0:T(8,128)(2,1)S(1)}, bf16[48,1536]{1,0:T(8,128)(2,1)S(1)}, u32[]{:S(2)}, u32[]{:S(2)}) collective-permute-start(bf16[48,1536]{1,0:T(8,128)(2,1)S(1)} %project.9.refs_3_.refs_4_.refs_0_), channel_id=1, source_target_pairs={{0,8},{4,12},{8,0},{12,4},{1,9},{5,13},{9,1},{13,5},{2,10},{6,14},... | collective-permute-start | bytes 442376 | tf_op jit(solution)/shard_map/ppermute | solution.py:528
  57.9 16.4 %collective-permute-start.14 = (bf16[80,1536]{1,0:T(8,128)(2,1)S(1)}, bf16[80,1536]{1,0:T(8,128)(2,1)S(1)}, u32[]{:S(2)}, u32[]{:S(2)}) collective-permute-start(bf16[80,1536]{1,0:T(8,128)(2,1)S(1)} %project.11.refs_1_.refs_3_.refs_4_), channel_id=1, source_target_pairs={{0,8},{4,12},{8,0},{12,4},{1,9},{5,13},{9,1},{13,5},{2,10},{6,14},... | collective-permute-start | bytes 737288 | tf_op jit(solution)/shard_map/ppermute | solution.py:528
  58.0 8.4 %collective-permute-start.6 = (bf16[48,1536]{1,0:T(8,128)(2,1)S(1)}, bf16[48,1536]{1,0:T(8,128)(2,1)S(1)}, u32[]{:S(2)}, u32[]{:S(2)}) collective-permute-start(bf16[48,1536]{1,0:T(8,128)(2,1)S(1)} %project.9.refs_3_.refs_4_.refs_0_), channel_id=1, source_target_pairs={{0,4},{4,0},{8,12},{12,8},{1,5},{5,1},{9,13},{13,9},{2,6},{6,2},{1... | collective-permute-start | bytes 442376 | tf_op jit(solution)/shard_map/ppermute | solution.py:532
  65.4 1.4 %collective-permute-start.12 = (bf16[48,1536]{1,0:T(8,128)(2,1)S(1)}, bf16[48,1536]{1,0:T(8,128)(2,1)S(1)}, u32[]{:S(2)}, u32[]{:S(2)}) collective-permute-start(bf16[48,1536]{1,0:T(8,128)(2,1)S(1)} %after.11.refs_6_.refs_2_), channel_id=1, source_target_pairs={{0,4},{4,0},{8,12},{12,8},{1,5},{5,1},{9,13},{13,9},{2,6},{6,2},{1... | collective-permute-start | bytes 442376 | tf_op jit(solution)/shard_map/ppermute | solution.py:532
  66.7 10.5 %copy-start.6 = (s32[16]{0:T(128)S(1)}, s32[16]{0:T(128)}, u32[]{:S(2)}) copy-start(s32[16]{0:T(128)} %plan_ref.5) | copy-start | bytes 196
  66.7 18.0 %collective-permute-start.19 = (bf16[80,2048]{1,0:T(8,128)(2,1)S(1)}, bf16[80,2048]{1,0:T(8,128)(2,1)S(1)}, u32[]{:S(2)}, u32[]{:S(2)}) collective-permute-start(bf16[80,2048]{1,0:T(8,128)(2,1)S(1)} %get-tuple-element.80.refs_1_), channel_id=1, source_target_pairs={{0,1},{1,0},{2,3},{3,2},{4,5},{5,4},{6,7},{7,6},{8,9},{9,8},{10,11... | collective-permute-start | bytes 983048 | tf_op jit(solution)/shard_map/ppermute | solution.py:583
  69.0 8.3 %collective-permute-start.13 = (bf16[80,1536]{1,0:T(8,128)(2,1)S(1)}, bf16[80,1536]{1,0:T(8,128)(2,1)S(1)}, u32[]{:S(2)}, u32[]{:S(2)}) collective-permute-start(bf16[80,1536]{1,0:T(8,128)(2,1)S(1)} %project.11.refs_1_.refs_3_.refs_4_), channel_id=1, source_target_pairs={{0,4},{4,0},{8,12},{12,8},{1,5},{5,1},{9,13},{13,9},{2,6},{6,2},{1... | collective-permute-start | bytes 737288 | tf_op jit(solution)/shard_map/ppermute | solution.py:532
  74.3 2.9 %collective-permute-start.18 = (bf16[80,1536]{1,0:T(8,128)(2,1)S(1)}, bf16[80,1536]{1,0:T(8,128)(2,1)S(1)}, u32[]{:S(2)}, u32[]{:S(2)}) collective-permute-start(bf16[80,1536]{1,0:T(8,128)(2,1)S(1)} %after.13.refs_6_), channel_id=1, source_target_pairs={{0,4},{4,0},{8,12},{12,8},{1,5},{5,1},{9,13},{13,9},{2,6},{6,2},{1... | collective-permute-start | bytes 737288 | tf_op jit(solution)/shard_map/ppermute | solution.py:532
  74.4 12.1 %collective-permute-start.22 = (bf16[48,2048]{1,0:T(8,128)(2,1)S(1)}, bf16[48,2048]{1,0:T(8,128)(2,1)S(1)}, u32[]{:S(2)}, u32[]{:S(2)}) collective-permute-start(bf16[48,2048]{1,0:T(8,128)(2,1)S(1)} %get-tuple-element.86.refs_0_), channel_id=1, source_target_pairs={{0,2},{1,3},{2,0},{3,1},{4,6},{5,7},{6,4},{7,5},{8,10},{9,11},{10,... | collective-permute-start | bytes 589832 | tf_op jit(solution)/shard_map/ppermute | solution.py:583
  75.8 10.7 %collective-permute-start.23 = (bf16[48,2048]{1,0:T(8,128)(2,1)S(1)}, bf16[48,2048]{1,0:T(8,128)(2,1)S(1)}, u32[]{:S(2)}, u32[]{:S(2)}) collective-permute-start(bf16[48,2048]{1,0:T(8,128)(2,1)S(1)} %get-tuple-element.86.refs_0_), channel_id=1, source_target_pairs={{0,1},{1,0},{2,3},{3,2},{4,5},{5,4},{6,7},{7,6},{8,9},{9,8},{10,11... | collective-permute-start | bytes 589832 | tf_op jit(solution)/shard_map/ppermute | solution.py:583
  86.5 7.5 %collective-permute-start.21 = (bf16[80,1536]{1,0:T(8,128)(2,1)S(1)}, bf16[80,1536]{1,0:T(8,128)(2,1)S(1)}, u32[]{:S(2)}, u32[]{:S(2)}) collective-permute-start(bf16[80,1536]{1,0:T(8,128)(2,1)S(1)} %project.13.refs_8_), channel_id=1, source_target_pairs={{0,8},{4,12},{8,0},{12,4},{1,9},{5,13},{9,1},{13,5},{2,10},{6,14},... | collective-permute-start | bytes 737288 | tf_op jit(solution)/shard_map/ppermute | solution.py:528
  86.6 5.8 %collective-permute-start.24 = (bf16[48,2048]{1,0:T(8,128)(2,1)S(1)}, bf16[48,2048]{1,0:T(8,128)(2,1)S(1)}, u32[]{:S(2)}, u32[]{:S(2)}) collective-permute-start(bf16[48,2048]{1,0:T(8,128)(2,1)S(1)} %after.15.refs_1_), channel_id=1, source_target_pairs={{0,1},{1,0},{2,3},{3,2},{4,5},{5,4},{6,7},{7,6},{8,9},{9,8},{10,11... | collective-permute-start | bytes 589832 | tf_op jit(solution)/shard_map/ppermute | solution.py:583
  90.7 6.6 %collective-permute-start.20 = (bf16[80,1536]{1,0:T(8,128)(2,1)S(1)}, bf16[80,1536]{1,0:T(8,128)(2,1)S(1)}, u32[]{:S(2)}, u32[]{:S(2)}) collective-permute-start(bf16[80,1536]{1,0:T(8,128)(2,1)S(1)} %project.13.refs_8_), channel_id=1, source_target_pairs={{0,4},{4,0},{8,12},{12,8},{1,5},{5,1},{9,13},{13,9},{2,6},{6,2},{1... | collective-permute-start | bytes 737288 | tf_op jit(solution)/shard_map/ppermute | solution.py:532
  93.9 3.4 %collective-permute-start.25 = (bf16[80,1536]{1,0:T(8,128)(2,1)S(1)}, bf16[80,1536]{1,0:T(8,128)(2,1)S(1)}, u32[]{:S(2)}, u32[]{:S(2)}) collective-permute-start(bf16[80,1536]{1,0:T(8,128)(2,1)S(1)} %after.16.refs_10_), channel_id=1, source_target_pairs={{0,4},{4,0},{8,12},{12,8},{1,5},{5,1},{9,13},{13,9},{2,6},{6,2},{1... | collective-permute-start | bytes 737288 | tf_op jit(solution)/shard_map/ppermute | solution.py:532
  95.6 8.6 %collective-permute-start.27 = (bf16[48,1536]{1,0:T(8,128)(2,1)S(1)}, bf16[48,1536]{1,0:T(8,128)(2,1)S(1)}, u32[]{:S(2)}, u32[]{:S(2)}) collective-permute-start(bf16[48,1536]{1,0:T(8,128)(2,1)S(1)} %project.15.refs_1_.refs_12_), channel_id=1, source_target_pairs={{0,8},{4,12},{8,0},{12,4},{1,9},{5,13},{9,1},{13,5},{2,10},{6,14},... | collective-permute-start | bytes 442376 | tf_op jit(solution)/shard_map/ppermute | solution.py:528
  97.0 10.6 %collective-permute-start.26 = (bf16[48,1536]{1,0:T(8,128)(2,1)S(1)}, bf16[48,1536]{1,0:T(8,128)(2,1)S(1)}, u32[]{:S(2)}, u32[]{:S(2)}) collective-permute-start(bf16[48,1536]{1,0:T(8,128)(2,1)S(1)} %project.15.refs_1_.refs_12_), channel_id=1, source_target_pairs={{0,4},{4,0},{8,12},{12,8},{1,5},{5,1},{9,13},{13,9},{2,6},{6,2},{1... | collective-permute-start | bytes 442376 | tf_op jit(solution)/shard_map/ppermute | solution.py:532
  104.2 4.4 %collective-permute-start.28 = (bf16[48,1536]{1,0:T(8,128)(2,1)S(1)}, bf16[48,1536]{1,0:T(8,128)(2,1)S(1)}, u32[]{:S(2)}, u32[]{:S(2)}) collective-permute-start(bf16[48,1536]{1,0:T(8,128)(2,1)S(1)} %after.17.refs_14_), channel_id=1, source_target_pairs={{0,4},{4,0},{8,12},{12,8},{1,5},{5,1},{9,13},{13,9},{2,6},{6,2},{1... | collective-permute-start | bytes 442376 | tf_op jit(solution)/shard_map/ppermute | solution.py:532

commit v3 on v2

--- a/solution.py
+++ b/solution.py
@@ -316,12 +316,16 @@
                 first = 0
                 for base, rows in zip(bases, sizes):
                     at = pl.multiple_of(base + owner * rows, ALIGN)
-                    copy = pltpu.make_async_copy(
-                        block.at[pl.ds(first, rows), :],
-                        rows_ref.at[pl.ds(at, rows), :],
-                        sems.at[len(copies)],
-                    )
-                    copies.append((at + rows > needed, copy))
+                    for columns, least in (
+                        (slice(query_width, None), needed),
+                        (slice(0, query_width), prior - SPAN - ALIGN),
+                    ):
+                        copy = pltpu.make_async_copy(
+                            block.at[pl.ds(first, rows), columns],
+                            rows_ref.at[pl.ds(at, rows), columns],
+                            sems.at[len(copies)],
+                        )
+                        copies.append((at + rows > least, copy))
                     first += rows
     for wanted, copy in copies:
 
@@ -493,7 +497,7 @@
     query_width, key_width = widths
     width = query_width + 2 * key_width
     total = 2 * chips * sum(sum(sizes) for _, sizes in groups)
-    copies = 2 * chips * sum(len(sizes) for _, sizes in groups)
+    copies = 4 * chips * sum(len(sizes) for _, sizes in groups)
     key_heads, tall = key_width // HEAD_SIZE, query_width // key_width * SPAN
     at = 2 + len(blocks)
     return pl.pallas_call(

time: 116 us -> 110 us (0.948)
  the two profiles are of different devices: /device:TPU:15 before, /device:TPU:0 now
where the time goes in v3:
time: 110 us; the launch traced here: 109 us
  Pallas kernels  48.6 us (44%)
  waiting for transfers between devices  30.1 us (27%)
  starting transfers between devices  27.3 us (25%)
  local copies, waits for them, and re-layouts  2.27 us (2%)
    pallas_call x8, Pallas kernels, project(): pl.pallas_call(functools.partial(project_kernel, masks, bool(carried), fi...  22.9 us
    ppermute x12, waiting for transfers between devices, start(): line[index + 1] = lax.ppermute(line[source], 'tp', pairs)  22.7 us
    ppermute x12, starting transfers between devices, start(): line[index + 1] = lax.ppermute(line[source], 'tp', pairs)  16.4 us
    pallas_call x3, Pallas kernels, attend(): pl.pallas_call(functools.partial(attend_kernel, chips, groups, known, pri...  12.8 us
    ppermute x8, starting transfers between devices, shift_chips(): return lax.ppermute(value, 'req', pairs)  8.95 us
    pallas_call x1, Pallas kernels, load(): pl.pallas_call(kernel, in_specs=[anywhere, anywhere], out_specs=[vmem, vm...  6.06 us
    pallas_call x3, Pallas kernels, deal(): pl.pallas_call(functools.partial(deal_kernel, chips, bases, sizes, twins)...  5.53 us
    ppermute x9, waiting for transfers between devices, swap_cores(): return lax.ppermute(value, 'req', [(d, d ^ 1) for d in range(2 * chips)])  3.84 us
  transfers between devices with their start and end apart: 29, of which 13 were waited for; matrix products, arithmetic and copies ran while one was open for 0% of the time, Pallas kernels for 39%

profile of v3, /device:TPU:0, one launch (start us, length us, event | category | flops | bytes accessed | tf_op | source)
XLA Modules:
  0.0 109.3 jit_solution(2985979547615030076)
XLA Ops:
  0.6 0.5 collective-permute-start
  1.1 1.6 %copy-done.2 = bf16[512,2048]{1,0:T(8,128)(2,1)S(1)} copy-done((bf16[512,2048]{1,0:T(8,128)(2,1)S(1)}, bf16[512,2048]{1,0:T(8,128)(2,1)}, u32[]{:S(2)}) %copy-start.2) | copy-done | bytes 2097176
  2.7 0.7 copy-done.4
  3.4 1.3 %deal.3 = (bf16[48,2048]{1,0:T(8,128)(2,1)S(1)}, bf16[1,48,2048]{2,1,0:T(8,128)(2,1)S(1)}) custom-call(s32[4]{0:T(128)S(1)} %copy-done.4, bf16[512,2048]{1,0:T(8,128)(2,1)S(1)} %copy-done.2), custom_call_target="tpu_custom_call" | custom-call | tf_op jit(solution)/shard_map/deal/pallas_call | solution.py:86
  4.7 0.4 collective-permute-done.refs_0_.refs_1_
  5.1 1.3 %deal.4 = (bf16[48,2048]{1,0:T(8,128)(2,1)S(1)}, bf16[1,48,2048]{2,1,0:T(8,128)(2,1)S(1)}) custom-call(s32[4]{0:T(128)S(1)} %copy-done.4, bf16[512,2048]{1,0:T(8,128)(2,1)S(1)} %collective-permute-done.refs_0_.refs_1_, bf16[48,2048]{1,0:T(8,128)(2,1)S(1)} %get-tuple-element.50.refs_1_, bf16[1,48,2048]{2,1,0:T(8,128)(2,1)S(1)} %get-tuple-element.51.refs_2_), custom_call_target="tpu_custom_call" | custom-call | tf_op jit(solution)/shard_map/deal/pallas_call | solution.py:86
  6.5 2.9 %collective-permute-start.1 = (bf16[48,2048]{1,0:T(8,128)(2,1)S(1)}, bf16[48,2048]{1,0:T(8,128)(2,1)S(1)}, u32[]{:S(2)}, u32[]{:S(2)}) collective-permute-start(bf16[48,2048]{1,0:T(8,128)(2,1)S(1)} %bitcast.16), channel_id=1, source_target_pairs={{0,8},{4,12},{8,0},{12,4},{1,9},{5,13},{9,1},{13,5},{2,10},{6,14},... | collective-permute-start | bytes 589832 | tf_op jit(solution)/shard_map/ppermute | solution.py:532
  9.4 2.9 %deal.5 = (bf16[80,2048]{1,0:T(8,128)(2,1)S(1)}, bf16[1,80,2048]{2,1,0:T(8,128)(2,1)S(1)}, bf16[80,2048]{1,0:T(8,128)(2,1)S(1)}, bf16[1,80,2048]{2,1,0:T(8,128)(...) custom-call(s32[4]{0:T(128)S(1)} %copy-done.4, bf16[512,2048]{1,0:T(8,128)(2,1)S(1)} %copy-done.3, ...), custom_call_target="tpu_custom_call" | custom-call | tf_op jit(solution)/shard_map/deal/pallas_call | solution.py:86
  12.3 2.3 %collective-permute-done.1.refs_0_ = bf16[48,2048]{1,0:T(8,128)(2,1)S(1)} collective-permute-done((bf16[48,2048]{1,0:T(8,128)(2,1)S(1)}, bf16[48,2048]{1,0:T(8,128)(2,1)S(1)}, u32[]{:S(2)}, u32[]{:S(2)}) %collective-permute-start.1) | collective-permute-done | bytes 196640 | tf_op jit(solution)/shard_map/ppermute | solution.py:532
  14.6 1.8 %collective-permute-start.3 = (bf16[80,2048]{1,0:T(8,128)(2,1)S(1)}, bf16[80,2048]{1,0:T(8,128)(2,1)S(1)}, u32[]{:S(2)}, u32[]{:S(2)}) collective-permute-start(bf16[80,2048]{1,0:T(8,128)(2,1)S(1)} %bitcast.13), channel_id=1, source_target_pairs={{0,8},{4,12},{8,0},{12,4},{1,9},{5,13},{9,1},{13,5},{2,10},{6,14},... | collective-permute-start | bytes 983048 | tf_op jit(solution)/shard_map/ppermute | solution.py:532
  16.4 1.6 %collective-permute-start.4 = (bf16[48,2048]{1,0:T(8,128)(2,1)S(1)}, bf16[48,2048]{1,0:T(8,128)(2,1)S(1)}, u32[]{:S(2)}, u32[]{:S(2)}) collective-permute-start(bf16[48,2048]{1,0:T(8,128)(2,1)S(1)} %get-tuple-element.55.anchor_ref.refs_0_), channel_id=1, source_target_pairs={{0,1},{1,0},{2,3},{3,2},{4,5},{5,4},{6,7},{7,6},{8,9},{9,8},{10,11... | collective-permute-start | bytes 589832 | tf_op jit(solution)/shard_map/ppermute | solution.py:587
  18.0 2.6 %collective-permute-start.2 = (bf16[48,2048]{1,0:T(8,128)(2,1)S(1)}, bf16[48,2048]{1,0:T(8,128)(2,1)S(1)}, u32[]{:S(2)}, u32[]{:S(2)}) collective-permute-start(bf16[48,2048]{1,0:T(8,128)(2,1)S(1)} %get-tuple-element.55.anchor_ref.refs_0_), channel_id=1, source_target_pairs={{0,2},{1,3},{2,0},{3,1},{4,6},{5,7},{6,4},{7,5},{8,10},{9,11},{10,... | collective-permute-start | bytes 589832 | tf_op jit(solution)/shard_map/ppermute | solution.py:587
  20.6 6.1 %load.1 = (bf16[8192,1024]{1,0:T(8,128)(2,1)S(1)}, f32[8,128]{1,0:T(8,128)S(1)}) custom-call(bf16[8192,1024]{1,0:T(8,128)(2,1)} %weight_ref.1, bf16[48,2048]{1,0:T(8,128)(2,1)S(1)} %get-tuple-element.55.anchor_ref.refs_0_), custom_call_target="tpu_custom_call" | custom-call | tf_op jit(solution)/shard_map/load/pallas_call | solution.py:206
  26.7 0.0 collective-permute-done.3.refs_0_
  26.7 0.6 collective-permute-start.9
  27.3 0.0 collective-permute-done.4.refs_2_
  27.3 1.5 %collective-permute-done.2.refs_0_ = bf16[48,2048]{1,0:T(8,128)(2,1)S(1)} collective-permute-done((bf16[48,2048]{1,0:T(8,128)(2,1)S(1)}, bf16[48,2048]{1,0:T(8,128)(2,1)S(1)}, u32[]{:S(2)}, u32[]{:S(2)}) %collective-permute-start.2) | collective-permute-done | bytes 196640 | tf_op jit(solution)/shard_map/ppermute | solution.py:587
  28.8 0.3 collective-permute-start.10
  29.2 2.7 %collective-permute-start.8 = (bf16[80,2048]{1,0:T(8,128)(2,1)S(1)}, bf16[80,2048]{1,0:T(8,128)(2,1)S(1)}, u32[]{:S(2)}, u32[]{:S(2)}) collective-permute-start(bf16[80,2048]{1,0:T(8,128)(2,1)S(1)} %get-tuple-element.65.anchor_ref.refs_0_), channel_id=1, source_target_pairs={{0,2},{1,3},{2,0},{3,1},{4,6},{5,7},{6,4},{7,5},{8,10},{9,11},{10,... | collective-permute-start | bytes 983048 | tf_op jit(solution)/shard_map/ppermute | solution.py:587
  31.9 0.0 collective-permute-start.5
  31.9 1.1 angles.1
  33.0 4.0 %project.8 = (f32[48,1536]{1,0:T(8,128)S(1)}, f32[48,128]{1,0:T(8,128)S(1)}) custom-call(bf16[48,2048]{1,0:T(8,128)(2,1)S(1)} %get-tuple-element.55.anchor_ref.refs_0_, bf16[48,2048]{1,0:T(8,128)(2,1)S(1)} %get-tuple-element.61.refs_1_, bf16[48,2048]{1,0:T(8,128)(2,1)S(1)} %collective-permute-done.4.refs_2_, f32[1,8192]{1,0:T(1,128)S(1)} %bitcast.5, ...), custom_call_target="tpu_custom_call" | custom-call | tf_op jit(solution)/shard_map/project/pallas_call | solution.py:281
  37.0 9.5 %collective-permute-done.5.refs_0_ = bf16[48,2048]{1,0:T(8,128)(2,1)S(1)} collective-permute-done((bf16[48,2048]{1,0:T(8,128)(2,1)S(1)}, bf16[48,2048]{1,0:T(8,128)(2,1)S(1)}, u32[]{:S(2)}, u32[]{:S(2)}) %collective-permute-start.5) | collective-permute-done | bytes 196640 | tf_op jit(solution)/shard_map/ppermute | solution.py:587
  46.5 1.6 %project.9.refs_3_.refs_4_.refs_0_ = bf16[48,1536]{1,0:T(8,128)(2,1)S(1)} custom-call(bf16[48,2048]{1,0:T(8,128)(2,1)S(1)} %collective-permute-done.5.refs_0_, f32[1,8192]{1,0:T(1,128)S(1)} %bitcast.6, bf16[8192,1024]{1,0:T(8,128)(2,1)S(1)} %get-tuple-element.62.refs_4_.refs_2_, bf16[8192,256]{1,0:T(8,128)(2,1)S(1)} %copy-done, ...), custom_call_target="tpu_custom_call" | custom-call | tf_op jit(solution)/shard_map/project/pallas_call | solution.py:281
  48.1 0.0 collective-permute-done.10.refs_2_
  48.1 0.0 collective-permute-done.8.refs_0_
  48.1 1.6 %collective-permute-start.11 = (bf16[80,2048]{1,0:T(8,128)(2,1)S(1)}, bf16[80,2048]{1,0:T(8,128)(2,1)S(1)}, u32[]{:S(2)}, u32[]{:S(2)}) collective-permute-start(bf16[80,2048]{1,0:T(8,128)(2,1)S(1)} %get-tuple-element.72.refs_1_), channel_id=1, source_target_pairs={{0,1},{1,0},{2,3},{3,2},{4,5},{5,4},{6,7},{7,6},{8,9},{9,8},{10,11... | collective-permute-start | bytes 983048 | tf_op jit(solution)/shard_map/ppermute | solution.py:587
  49.8 0.5 collective-permute-start.16
  50.3 2.0 %collective-permute-start.15 = (bf16[80,2048]{1,0:T(8,128)(2,1)S(1)}, bf16[80,2048]{1,0:T(8,128)(2,1)S(1)}, u32[]{:S(2)}, u32[]{:S(2)}) collective-permute-start(bf16[80,2048]{1,0:T(8,128)(2,1)S(1)} %get-tuple-element.77.refs_0_), channel_id=1, source_target_pairs={{0,2},{1,3},{2,0},{3,1},{4,6},{5,7},{6,4},{7,5},{8,10},{9,11},{10,... | collective-permute-start | bytes 983048 | tf_op jit(solution)/shard_map/ppermute | solution.py:587
  52.3 0.1 collective-permute-start.17
  52.3 1.5 %collective-permute-start.7 = (bf16[48,1536]{1,0:T(8,128)(2,1)S(1)}, bf16[48,1536]{1,0:T(8,128)(2,1)S(1)}, u32[]{:S(2)}, u32[]{:S(2)}) collective-permute-start(bf16[48,1536]{1,0:T(8,128)(2,1)S(1)} %project.9.refs_3_.refs_4_.refs_0_), channel_id=1, source_target_pairs={{0,8},{4,12},{8,0},{12,4},{1,9},{5,13},{9,1},{13,5},{2,10},{6,14},... | collective-permute-start | bytes 442376 | tf_op jit(solution)/shard_map/ppermute | solution.py:532
  53.8 4.2 %project.10 = (f32[80,1536]{1,0:T(8,128)S(1)}, f32[80,128]{1,0:T(8,128)S(1)}) custom-call(bf16[80,2048]{1,0:T(8,128)(2,1)S(1)} %get-tuple-element.65.anchor_ref.refs_0_, bf16[80,2048]{1,0:T(8,128)(2,1)S(1)} %get-tuple-element.72.refs_1_, bf16[80,2048]{1,0:T(8,128)(2,1)S(1)} %collective-permute-done.10.refs_2_, f32[1,8192]{1,0:T(1,128)S(1)} %bitcast.7, ...), custom_call_target="tpu_custom_call" | custom-call | tf_op jit(solution)/shard_map/project/pallas_call | solution.py:281
  58.1 7.8 %collective-permute-done.11.refs_0_ = bf16[80,2048]{1,0:T(8,128)(2,1)S(1)} collective-permute-done((bf16[80,2048]{1,0:T(8,128)(2,1)S(1)}, bf16[80,2048]{1,0:T(8,128)(2,1)S(1)}, u32[]{:S(2)}, u32[]{:S(2)}) %collective-permute-start.11) | collective-permute-done | bytes 327712 | tf_op jit(solution)/shard_map/ppermute | solution.py:587
  65.9 1.7 %project.11.refs_1_.refs_3_.refs_4_ = bf16[80,1536]{1,0:T(8,128)(2,1)S(1)} custom-call(bf16[80,2048]{1,0:T(8,128)(2,1)S(1)} %collective-permute-done.11.refs_0_, f32[1,8192]{1,0:T(1,128)S(1)} %bitcast.8, bf16[8192,1024]{1,0:T(8,128)(2,1)S(1)} %get-tuple-element.62.refs_4_.refs_2_, bf16[8192,256]{1,0:T(8,128)(2,1)S(1)} %copy-done, ...), custom_call_target="tpu_custom_call" | custom-call | tf_op jit(solution)/shard_map/project/pallas_call | solution.py:281
  67.6 1.2 %collective-permute-start.14 = (bf16[80,1536]{1,0:T(8,128)(2,1)S(1)}, bf16[80,1536]{1,0:T(8,128)(2,1)S(1)}, u32[]{:S(2)}, u32[]{:S(2)}) collective-permute-start(bf16[80,1536]{1,0:T(8,128)(2,1)S(1)} %project.11.refs_1_.refs_3_.refs_4_), channel_id=1, source_target_pairs={{0,8},{4,12},{8,0},{12,4},{1,9},{5,13},{9,1},{13,5},{2,10},{6,14},... | collective-permute-start | bytes 737288 | tf_op jit(solution)/shard_map/ppermute | solution.py:532
  68.7 0.0 collective-permute-done.7.refs_0_
  68.7 0.0 collective-permute-done.16.refs_0_
  68.8 0.5 collective-permute-start.12
  69.3 0.8 collective-permute-done.6.refs_5_.refs_1_
  70.1 0.0 collective-permute-done.15.refs_0_
  70.1 0.2 collective-permute-done.12.refs_7_.refs_3_
  70.3 0.6 collective-permute-start.19
  70.9 4.2 %project.12 = (f32[80,1536]{1,0:T(8,128)S(1)}, f32[80,128]{1,0:T(8,128)S(1)}) custom-call(bf16[80,2048]{1,0:T(8,128)(2,1)S(1)} %get-tuple-element.77.refs_0_, bf16[80,2048]{1,0:T(8,128)(2,1)S(1)} %get-tuple-element.80.refs_1_, bf16[80,2048]{1,0:T(8,128)(2,1)S(1)} %collective-permute-done.17.refs_2_, f32[1,8192]{1,0:T(1,128)S(1)} %bitcast.9, ...), custom_call_target="tpu_custom_call" | custom-call | tf_op jit(solution)/shard_map/project/pallas_call | solution.py:281
  75.1 0.6 collective-permute-start.18
  75.7 3.8 %collective-permute-start.22 = (bf16[48,2048]{1,0:T(8,128)(2,1)S(1)}, bf16[48,2048]{1,0:T(8,128)(2,1)S(1)}, u32[]{:S(2)}, u32[]{:S(2)}) collective-permute-start(bf16[48,2048]{1,0:T(8,128)(2,1)S(1)} %get-tuple-element.86.refs_0_), channel_id=1, source_target_pairs={{0,2},{1,3},{2,0},{3,1},{4,6},{5,7},{6,4},{7,5},{8,10},{9,11},{10,... | collective-permute-start | bytes 589832 | tf_op jit(solution)/shard_map/ppermute | solution.py:587
  79.5 0.3 collective-permute-start.23
  79.9 5.1 %attend.3 = (bf16[512,1024]{1,0:T(8,128)(2,1)}, bf16[2,512,256]{2,1,0:T(8,128)(2,1)}, f32[8,128]{1,0:T(8,128)S(1)}) custom-call(s32[4]{0:T(128)S(1)} %copy-done.5, s32[16]{0:T(128)S(1)} %copy-done.6, bf16[48,1536]{1,0:T(8,128)(2,1)S(1)} %project.9.refs_3_.refs_4_.refs_0_, bf16[48,1536]{1,0:T(8,128)(2,1)S(1)} %collective-permute-done.6.refs_5_.refs_1_, ...), custom_call_target="tpu_custom_call" | custom-call | tf_op jit(solution)/shard_map/attend/pallas_call | solution.py:503
  85.0 1.7 %project.13.refs_8_ = bf16[80,1536]{1,0:T(8,128)(2,1)S(1)} custom-call(bf16[80,2048]{1,0:T(8,128)(2,1)S(1)} %collective-permute-done.19.refs_0_, f32[1,8192]{1,0:T(1,128)S(1)} %bitcast.10, bf16[8192,1024]{1,0:T(8,128)(2,1)S(1)} %get-tuple-element.62.refs_4_.refs_2_, bf16[8192,256]{1,0:T(8,128)(2,1)S(1)} %copy-done, bf16[8192,256]{1,0:T(8,128)(2,1)S(1)} %copy-done.1, ...), custom_call_target="tpu_custom_call" | custom-call | tf_op jit(solution)/shard_map/project/pallas_call | solution.py:281
  86.7 0.1 collective-permute-start.21
  86.7 2.2 %collective-permute-done.22.refs_0_ = bf16[48,2048]{1,0:T(8,128)(2,1)S(1)} collective-permute-done((bf16[48,2048]{1,0:T(8,128)(2,1)S(1)}, bf16[48,2048]{1,0:T(8,128)(2,1)S(1)}, u32[]{:S(2)}, u32[]{:S(2)}) %collective-permute-start.22) | collective-permute-done | bytes 196640 | tf_op jit(solution)/shard_map/ppermute | solution.py:587
  88.9 1.0 collective-permute-done.23.refs_1_.refs_2_
  89.9 0.8 collective-permute-start.24
  90.7 4.0 %project.14 = (f32[48,1536]{1,0:T(8,128)S(1)}, f32[48,128]{1,0:T(8,128)S(1)}) custom-call(bf16[48,2048]{1,0:T(8,128)(2,1)S(1)} %get-tuple-element.86.refs_0_, bf16[48,2048]{1,0:T(8,128)(2,1)S(1)} %after.15.refs_1_, bf16[48,2048]{1,0:T(8,128)(2,1)S(1)} %collective-permute-done.23.refs_1_.refs_2_, f32[1,8192]{1,0:T(1,128)S(1)} %bitcast.11, ...), custom_call_target="tpu_custom_call" | custom-call | tf_op jit(solution)/shard_map/project/pallas_call | solution.py:281
  94.7 0.1 collective-permute-start.20
  94.8 0.8 collective-permute-done.24.refs_0_
  95.5 1.6 %project.15.refs_1_.refs_12_ = bf16[48,1536]{1,0:T(8,128)(2,1)S(1)} custom-call(bf16[48,2048]{1,0:T(8,128)(2,1)S(1)} %collective-permute-done.24.refs_0_, f32[1,8192]{1,0:T(1,128)S(1)} %bitcast.12, bf16[8192,1024]{1,0:T(8,128)(2,1)S(1)} %get-tuple-element.62.refs_4_.refs_2_, bf16[8192,256]{1,0:T(8,128)(2,1)S(1)} %copy-done, bf16[8192,256]{1,0:T(8,128)(2,1)S(1)} %copy-done.1, ...), custom_call_target="tpu_custom_call" | custom-call | tf_op jit(solution)/shard_map/project/pallas_call | solution.py:281
  97.1 0.1 collective-permute-start.25
  97.2 0.3 collective-permute-start.27
  97.5 0.2 collective-permute-start.26
  97.7 1.0 collective-permute-done.25.refs_11_
  98.7 3.5 %attend.4 = (bf16[512,1024]{1,0:T(8,128)(2,1)}, bf16[2,512,256]{2,1,0:T(8,128)(2,1)}, f32[8,128]{1,0:T(8,128)S(1)}) custom-call(s32[4]{0:T(128)S(1)} %copy-done.5, s32[16]{0:T(128)S(1)} %copy-done.6, bf16[48,1536]{1,0:T(8,128)(2,1)S(1)} %project.9.refs_3_.refs_4_.refs_0_, ...), custom_call_target="tpu_custom_call", output_to_operand_aliasing={{0}: (14, {}), {1}: (15, {})} | custom-call | tf_op jit(solution)/shard_map/attend/pallas_call | solution.py:503
  102.2 1.3 %collective-permute-done.27.refs_0_ = bf16[48,1536]{1,0:T(8,128)(2,1)S(1)} collective-permute-done((bf16[48,1536]{1,0:T(8,128)(2,1)S(1)}, bf16[48,1536]{1,0:T(8,128)(2,1)S(1)}, u32[]{:S(2)}, u32[]{:S(2)}) %collective-permute-start.27) | collective-permute-done | bytes 147488 | tf_op jit(solution)/shard_map/ppermute | solution.py:532
  103.5 1.4 %collective-permute-done.28.refs_15_ = bf16[48,1536]{1,0:T(8,128)(2,1)S(1)} collective-permute-done((bf16[48,1536]{1,0:T(8,128)(2,1)S(1)}, bf16[48,1536]{1,0:T(8,128)(2,1)S(1)}, u32[]{:S(2)}, u32[]{:S(2)}) %collective-permute-start.28) | collective-permute-done | bytes 147488 | tf_op jit(solution)/shard_map/ppermute | solution.py:536
  104.8 4.3 %attend.5 = (bf16[512,1024]{1,0:T(8,128)(2,1)}, bf16[2,512,256]{2,1,0:T(8,128)(2,1)}, f32[8,128]{1,0:T(8,128)}) custom-call(s32[4]{0:T(128)S(1)} %copy-done.5, s32[16]{0:T(128)S(1)} %copy-done.6, bf16[48,1536]{1,0:T(8,128)(2,1)S(1)} %project.9.refs_3_.refs_4_.refs_0_, ...), custom_call_target="tpu_custom_call", output_to_operand_aliasing={{0}: (18, {}), {1}: (19, {})} | custom-call | tf_op jit(solution)/shard_map/attend/pallas_call | solution.py:503
  (42 shorter events, 0.2 us)
Async XLA Ops:
  0.6 4.5 %collective-permute-start = (bf16[512,2048]{1,0:T(8,128)(2,1)}, bf16[512,2048]{1,0:T(8,128)(2,1)S(1)}, u32[]{:S(2)}, u32[]{:S(2)}) collective-permute-start(bf16[512,2048]{1,0:T(8,128)(2,1)} %refs_0_.3), channel_id=1, source_target_pairs={{0,4},{4,0},{8,12},{12,8},{1,5},{5,1},{9,13},{13,9},{2,6},{6,2},{1... | collective-permute-start | bytes 6291464 | tf_op jit(solution)/shard_map/ppermute | solution.py:536
  1.1 1.6 %copy-start.2 = (bf16[512,2048]{1,0:T(8,128)(2,1)S(1)}, bf16[512,2048]{1,0:T(8,128)(2,1)}, u32[]{:S(2)}) copy-start(bf16[512,2048]{1,0:T(8,128)(2,1)} %refs_0_.3) | copy-start | bytes 6291460
  2.7 0.7 copy-start.4
  3.4 6.0 %copy-start.3 = (bf16[512,2048]{1,0:T(8,128)(2,1)S(1)}, bf16[512,2048]{1,0:T(8,128)(2,1)}, u32[]{:S(2)}) copy-start(bf16[512,2048]{1,0:T(8,128)(2,1)} %refs_0_.3) | copy-start | bytes 6291460
  6.5 8.1 %collective-permute-start.1 = (bf16[48,2048]{1,0:T(8,128)(2,1)S(1)}, bf16[48,2048]{1,0:T(8,128)(2,1)S(1)}, u32[]{:S(2)}, u32[]{:S(2)}) collective-permute-start(bf16[48,2048]{1,0:T(8,128)(2,1)S(1)} %bitcast.16), channel_id=1, source_target_pairs={{0,8},{4,12},{8,0},{12,4},{1,9},{5,13},{9,1},{13,5},{2,10},{6,14},... | collective-permute-start | bytes 589832 | tf_op jit(solution)/shard_map/ppermute | solution.py:532
  14.6 12.1 %collective-permute-start.3 = (bf16[80,2048]{1,0:T(8,128)(2,1)S(1)}, bf16[80,2048]{1,0:T(8,128)(2,1)S(1)}, u32[]{:S(2)}, u32[]{:S(2)}) collective-permute-start(bf16[80,2048]{1,0:T(8,128)(2,1)S(1)} %bitcast.13), channel_id=1, source_target_pairs={{0,8},{4,12},{8,0},{12,4},{1,9},{5,13},{9,1},{13,5},{2,10},{6,14},... | collective-permute-start | bytes 983048 | tf_op jit(solution)/shard_map/ppermute | solution.py:532
  16.4 15.4 %copy-start.8 = (bf16[8192]{0:T(1024)(128)(2,1)S(1)}, bf16[8192]{0:T(1024)(128)(2,1)}, u32[]{:S(2)}) copy-start(bf16[8192]{0:T(1024)(128)(2,1)} %param.9) | copy-start | bytes 49156
  16.4 15.5 %copy-start.5 = (s32[4]{0:T(128)S(1)}, s32[4]{0:T(128)}, u32[]{:S(2)}) copy-start(s32[4]{0:T(128)} %lengths_ref.13) | copy-start | bytes 52
  16.4 15.5 %copy-start.7 = (f32[1,128]{1,0:T(1,128)S(1)}, f32[1,128]{1,0:T(1,128)}, u32[]{:S(2)}) copy-start(f32[1,128]{1,0:T(1,128)} %constant.2.clone.frequency_ref) | copy-start | bytes 1540
  16.4 10.9 %collective-permute-start.4 = (bf16[48,2048]{1,0:T(8,128)(2,1)S(1)}, bf16[48,2048]{1,0:T(8,128)(2,1)S(1)}, u32[]{:S(2)}, u32[]{:S(2)}) collective-permute-start(bf16[48,2048]{1,0:T(8,128)(2,1)S(1)} %get-tuple-element.55.anchor_ref.refs_0_), channel_id=1, source_target_pairs={{0,1},{1,0},{2,3},{3,2},{4,5},{5,4},{6,7},{7,6},{8,9},{9,8},{10,11... | collective-permute-start | bytes 589832 | tf_op jit(solution)/shard_map/ppermute | solution.py:587
  18.0 10.8 %collective-permute-start.2 = (bf16[48,2048]{1,0:T(8,128)(2,1)S(1)}, bf16[48,2048]{1,0:T(8,128)(2,1)S(1)}, u32[]{:S(2)}, u32[]{:S(2)}) collective-permute-start(bf16[48,2048]{1,0:T(8,128)(2,1)S(1)} %get-tuple-element.55.anchor_ref.refs_0_), channel_id=1, source_target_pairs={{0,2},{1,3},{2,0},{3,1},{4,6},{5,7},{6,4},{7,5},{8,10},{9,11},{10,... | collective-permute-start | bytes 589832 | tf_op jit(solution)/shard_map/ppermute | solution.py:587
  20.6 12.4 %copy-start = (bf16[8192,256]{1,0:T(8,128)(2,1)S(1)}, bf16[8192,256]{1,0:T(8,128)(2,1)}, u32[]{:S(2)}) copy-start(bf16[8192,256]{1,0:T(8,128)(2,1)} %refs_3_.7) | copy-start | bytes 12582916
  20.6 12.4 %copy-start.1 = (bf16[8192,256]{1,0:T(8,128)(2,1)S(1)}, bf16[8192,256]{1,0:T(8,128)(2,1)}, u32[]{:S(2)}) copy-start(bf16[8192,256]{1,0:T(8,128)(2,1)} %refs_4_.7) | copy-start | bytes 12582916
  26.7 21.3 %collective-permute-start.9 = (bf16[80,2048]{1,0:T(8,128)(2,1)S(1)}, bf16[80,2048]{1,0:T(8,128)(2,1)S(1)}, u32[]{:S(2)}, u32[]{:S(2)}) collective-permute-start(bf16[80,2048]{1,0:T(8,128)(2,1)S(1)} %bitcast.14), channel_id=1, source_target_pairs={{0,8},{4,12},{8,0},{12,4},{1,9},{5,13},{9,1},{13,5},{2,10},{6,14},... | collective-permute-start | bytes 983048 | tf_op jit(solution)/shard_map/ppermute | solution.py:532
  28.8 19.3 %collective-permute-start.10 = (bf16[80,2048]{1,0:T(8,128)(2,1)S(1)}, bf16[80,2048]{1,0:T(8,128)(2,1)S(1)}, u32[]{:S(2)}, u32[]{:S(2)}) collective-permute-start(bf16[80,2048]{1,0:T(8,128)(2,1)S(1)} %get-tuple-element.65.anchor_ref.refs_0_), channel_id=1, source_target_pairs={{0,1},{1,0},{2,3},{3,2},{4,5},{5,4},{6,7},{7,6},{8,9},{9,8},{10,11... | collective-permute-start | bytes 983048 | tf_op jit(solution)/shard_map/ppermute | solution.py:587
  29.2 19.0 %collective-permute-start.8 = (bf16[80,2048]{1,0:T(8,128)(2,1)S(1)}, bf16[80,2048]{1,0:T(8,128)(2,1)S(1)}, u32[]{:S(2)}, u32[]{:S(2)}) collective-permute-start(bf16[80,2048]{1,0:T(8,128)(2,1)S(1)} %get-tuple-element.65.anchor_ref.refs_0_), channel_id=1, source_target_pairs={{0,2},{1,3},{2,0},{3,1},{4,6},{5,7},{6,4},{7,5},{8,10},{9,11},{10,... | collective-permute-start | bytes 983048 | tf_op jit(solution)/shard_map/ppermute | solution.py:587
  31.9 14.6 %collective-permute-start.5 = (bf16[48,2048]{1,0:T(8,128)(2,1)S(1)}, bf16[48,2048]{1,0:T(8,128)(2,1)S(1)}, u32[]{:S(2)}, u32[]{:S(2)}) collective-permute-start(bf16[48,2048]{1,0:T(8,128)(2,1)S(1)} %get-tuple-element.61.refs_1_), channel_id=1, source_target_pairs={{0,1},{1,0},{2,3},{3,2},{4,5},{5,4},{6,7},{7,6},{8,9},{9,8},{10,11... | collective-permute-start | bytes 589832 | tf_op jit(solution)/shard_map/ppermute | solution.py:587
  48.1 17.7 %collective-permute-start.11 = (bf16[80,2048]{1,0:T(8,128)(2,1)S(1)}, bf16[80,2048]{1,0:T(8,128)(2,1)S(1)}, u32[]{:S(2)}, u32[]{:S(2)}) collective-permute-start(bf16[80,2048]{1,0:T(8,128)(2,1)S(1)} %get-tuple-element.72.refs_1_), channel_id=1, source_target_pairs={{0,1},{1,0},{2,3},{3,2},{4,5},{5,4},{6,7},{7,6},{8,9},{9,8},{10,11... | collective-permute-start | bytes 983048 | tf_op jit(solution)/shard_map/ppermute | solution.py:587
  49.8 19.0 %collective-permute-start.16 = (bf16[48,2048]{1,0:T(8,128)(2,1)S(1)}, bf16[48,2048]{1,0:T(8,128)(2,1)S(1)}, u32[]{:S(2)}, u32[]{:S(2)}) collective-permute-start(bf16[48,2048]{1,0:T(8,128)(2,1)S(1)} %bitcast.15), channel_id=1, source_target_pairs={{0,8},{4,12},{8,0},{12,4},{1,9},{5,13},{9,1},{13,5},{2,10},{6,14},... | collective-permute-start | bytes 589832 | tf_op jit(solution)/shard_map/ppermute | solution.py:532
  50.3 19.8 %collective-permute-start.15 = (bf16[80,2048]{1,0:T(8,128)(2,1)S(1)}, bf16[80,2048]{1,0:T(8,128)(2,1)S(1)}, u32[]{:S(2)}, u32[]{:S(2)}) collective-permute-start(bf16[80,2048]{1,0:T(8,128)(2,1)S(1)} %get-tuple-element.77.refs_0_), channel_id=1, source_target_pairs={{0,2},{1,3},{2,0},{3,1},{4,6},{5,7},{6,4},{7,5},{8,10},{9,11},{10,... | collective-permute-start | bytes 983048 | tf_op jit(solution)/shard_map/ppermute | solution.py:587
  52.3 17.9 %collective-permute-start.17 = (bf16[80,2048]{1,0:T(8,128)(2,1)S(1)}, bf16[80,2048]{1,0:T(8,128)(2,1)S(1)}, u32[]{:S(2)}, u32[]{:S(2)}) collective-permute-start(bf16[80,2048]{1,0:T(8,128)(2,1)S(1)} %get-tuple-element.77.refs_0_), channel_id=1, source_target_pairs={{0,1},{1,0},{2,3},{3,2},{4,5},{5,4},{6,7},{7,6},{8,9},{9,8},{10,11... | collective-permute-start | bytes 983048 | tf_op jit(solution)/shard_map/ppermute | solution.py:587
  52.3 16.4 %collective-permute-start.7 = (bf16[48,1536]{1,0:T(8,128)(2,1)S(1)}, bf16[48,1536]{1,0:T(8,128)(2,1)S(1)}, u32[]{:S(2)}, u32[]{:S(2)}) collective-permute-start(bf16[48,1536]{1,0:T(8,128)(2,1)S(1)} %project.9.refs_3_.refs_4_.refs_0_), channel_id=1, source_target_pairs={{0,8},{4,12},{8,0},{12,4},{1,9},{5,13},{9,1},{13,5},{2,10},{6,14},... | collective-permute-start | bytes 442376 | tf_op jit(solution)/shard_map/ppermute | solution.py:532
  67.6 7.6 %collective-permute-start.14 = (bf16[80,1536]{1,0:T(8,128)(2,1)S(1)}, bf16[80,1536]{1,0:T(8,128)(2,1)S(1)}, u32[]{:S(2)}, u32[]{:S(2)}) collective-permute-start(bf16[80,1536]{1,0:T(8,128)(2,1)S(1)} %project.11.refs_1_.refs_3_.refs_4_), channel_id=1, source_target_pairs={{0,8},{4,12},{8,0},{12,4},{1,9},{5,13},{9,1},{13,5},{2,10},{6,14},... | collective-permute-start | bytes 737288 | tf_op jit(solution)/shard_map/ppermute | solution.py:532
  68.7 1.4 %collective-permute-start.6 = (bf16[48,1536]{1,0:T(8,128)(2,1)S(1)}, bf16[48,1536]{1,0:T(8,128)(2,1)S(1)}, u32[]{:S(2)}, u32[]{:S(2)}) collective-permute-start(bf16[48,1536]{1,0:T(8,128)(2,1)S(1)} %project.9.refs_3_.refs_4_.refs_0_), channel_id=1, source_target_pairs={{0,4},{4,0},{8,12},{12,8},{1,5},{5,1},{9,13},{13,9},{2,6},{6,2},{1... | collective-permute-start | bytes 442376 | tf_op jit(solution)/shard_map/ppermute | solution.py:536
  68.8 1.6 %collective-permute-start.12 = (bf16[48,1536]{1,0:T(8,128)(2,1)S(1)}, bf16[48,1536]{1,0:T(8,128)(2,1)S(1)}, u32[]{:S(2)}, u32[]{:S(2)}) collective-permute-start(bf16[48,1536]{1,0:T(8,128)(2,1)S(1)} %after.11.refs_6_.refs_2_), channel_id=1, source_target_pairs={{0,4},{4,0},{8,12},{12,8},{1,5},{5,1},{9,13},{13,9},{2,6},{6,2},{1... | collective-permute-start | bytes 442376 | tf_op jit(solution)/shard_map/ppermute | solution.py:536
  70.3 9.5 %copy-start.6 = (s32[16]{0:T(128)S(1)}, s32[16]{0:T(128)}, u32[]{:S(2)}) copy-start(s32[16]{0:T(128)} %plan_ref.5) | copy-start | bytes 196
  70.3 14.6 %collective-permute-start.19 = (bf16[80,2048]{1,0:T(8,128)(2,1)S(1)}, bf16[80,2048]{1,0:T(8,128)(2,1)S(1)}, u32[]{:S(2)}, u32[]{:S(2)}) collective-permute-start(bf16[80,2048]{1,0:T(8,128)(2,1)S(1)} %get-tuple-element.80.refs_1_), channel_id=1, source_target_pairs={{0,1},{1,0},{2,3},{3,2},{4,5},{5,4},{6,7},{7,6},{8,9},{9,8},{10,11... | collective-permute-start | bytes 983048 | tf_op jit(solution)/shard_map/ppermute | solution.py:587
  70.9 8.9 %collective-permute-start.13 = (bf16[80,1536]{1,0:T(8,128)(2,1)S(1)}, bf16[80,1536]{1,0:T(8,128)(2,1)S(1)}, u32[]{:S(2)}, u32[]{:S(2)}) collective-permute-start(bf16[80,1536]{1,0:T(8,128)(2,1)S(1)} %project.11.refs_1_.refs_3_.refs_4_), channel_id=1, source_target_pairs={{0,4},{4,0},{8,12},{12,8},{1,5},{5,1},{9,13},{13,9},{2,6},{6,2},{1... | collective-permute-start | bytes 737288 | tf_op jit(solution)/shard_map/ppermute | solution.py:536
  75.1 4.7 %collective-permute-start.18 = (bf16[80,1536]{1,0:T(8,128)(2,1)S(1)}, bf16[80,1536]{1,0:T(8,128)(2,1)S(1)}, u32[]{:S(2)}, u32[]{:S(2)}) collective-permute-start(bf16[80,1536]{1,0:T(8,128)(2,1)S(1)} %after.13.refs_6_), channel_id=1, source_target_pairs={{0,4},{4,0},{8,12},{12,8},{1,5},{5,1},{9,13},{13,9},{2,6},{6,2},{1... | collective-permute-start | bytes 737288 | tf_op jit(solution)/shard_map/ppermute | solution.py:536
  75.7 13.2 %collective-permute-start.22 = (bf16[48,2048]{1,0:T(8,128)(2,1)S(1)}, bf16[48,2048]{1,0:T(8,128)(2,1)S(1)}, u32[]{:S(2)}, u32[]{:S(2)}) collective-permute-start(bf16[48,2048]{1,0:T(8,128)(2,1)S(1)} %get-tuple-element.86.refs_0_), channel_id=1, source_target_pairs={{0,2},{1,3},{2,0},{3,1},{4,6},{5,7},{6,4},{7,5},{8,10},{9,11},{10,... | collective-permute-start | bytes 589832 | tf_op jit(solution)/shard_map/ppermute | solution.py:587
  79.5 10.3 %collective-permute-start.23 = (bf16[48,2048]{1,0:T(8,128)(2,1)S(1)}, bf16[48,2048]{1,0:T(8,128)(2,1)S(1)}, u32[]{:S(2)}, u32[]{:S(2)}) collective-permute-start(bf16[48,2048]{1,0:T(8,128)(2,1)S(1)} %get-tuple-element.86.refs_0_), channel_id=1, source_target_pairs={{0,1},{1,0},{2,3},{3,2},{4,5},{5,4},{6,7},{7,6},{8,9},{9,8},{10,11... | collective-permute-start | bytes 589832 | tf_op jit(solution)/shard_map/ppermute | solution.py:587
  86.7 10.4 %collective-permute-start.21 = (bf16[80,1536]{1,0:T(8,128)(2,1)S(1)}, bf16[80,1536]{1,0:T(8,128)(2,1)S(1)}, u32[]{:S(2)}, u32[]{:S(2)}) collective-permute-start(bf16[80,1536]{1,0:T(8,128)(2,1)S(1)} %project.13.refs_8_), channel_id=1, source_target_pairs={{0,8},{4,12},{8,0},{12,4},{1,9},{5,13},{9,1},{13,5},{2,10},{6,14},... | collective-permute-start | bytes 737288 | tf_op jit(solution)/shard_map/ppermute | solution.py:532
  89.9 5.7 %collective-permute-start.24 = (bf16[48,2048]{1,0:T(8,128)(2,1)S(1)}, bf16[48,2048]{1,0:T(8,128)(2,1)S(1)}, u32[]{:S(2)}, u32[]{:S(2)}) collective-permute-start(bf16[48,2048]{1,0:T(8,128)(2,1)S(1)} %after.15.refs_1_), channel_id=1, source_target_pairs={{0,1},{1,0},{2,3},{3,2},{4,5},{5,4},{6,7},{7,6},{8,9},{9,8},{10,11... | collective-permute-start | bytes 589832 | tf_op jit(solution)/shard_map/ppermute | solution.py:587
  94.7 3.0 %collective-permute-start.20 = (bf16[80,1536]{1,0:T(8,128)(2,1)S(1)}, bf16[80,1536]{1,0:T(8,128)(2,1)S(1)}, u32[]{:S(2)}, u32[]{:S(2)}) collective-permute-start(bf16[80,1536]{1,0:T(8,128)(2,1)S(1)} %project.13.refs_8_), channel_id=1, source_target_pairs={{0,4},{4,0},{8,12},{12,8},{1,5},{5,1},{9,13},{13,9},{2,6},{6,2},{1... | collective-permute-start | bytes 737288 | tf_op jit(solution)/shard_map/ppermute | solution.py:536
  97.1 1.6 %collective-permute-start.25 = (bf16[80,1536]{1,0:T(8,128)(2,1)S(1)}, bf16[80,1536]{1,0:T(8,128)(2,1)S(1)}, u32[]{:S(2)}, u32[]{:S(2)}) collective-permute-start(bf16[80,1536]{1,0:T(8,128)(2,1)S(1)} %after.16.refs_10_), channel_id=1, source_target_pairs={{0,4},{4,0},{8,12},{12,8},{1,5},{5,1},{9,13},{13,9},{2,6},{6,2},{1... | collective-permute-start | bytes 737288 | tf_op jit(solution)/shard_map/ppermute | solution.py:536
  97.2 6.3 %collective-permute-start.27 = (bf16[48,1536]{1,0:T(8,128)(2,1)S(1)}, bf16[48,1536]{1,0:T(8,128)(2,1)S(1)}, u32[]{:S(2)}, u32[]{:S(2)}) collective-permute-start(bf16[48,1536]{1,0:T(8,128)(2,1)S(1)} %project.15.refs_1_.refs_12_), channel_id=1, source_target_pairs={{0,8},{4,12},{8,0},{12,4},{1,9},{5,13},{9,1},{13,5},{2,10},{6,14},... | collective-permute-start | bytes 442376 | tf_op jit(solution)/shard_map/ppermute | solution.py:532
  97.5 5.9 %collective-permute-start.26 = (bf16[48,1536]{1,0:T(8,128)(2,1)S(1)}, bf16[48,1536]{1,0:T(8,128)(2,1)S(1)}, u32[]{:S(2)}, u32[]{:S(2)}) collective-permute-start(bf16[48,1536]{1,0:T(8,128)(2,1)S(1)} %project.15.refs_1_.refs_12_), channel_id=1, source_target_pairs={{0,4},{4,0},{8,12},{12,8},{1,5},{5,1},{9,13},{13,9},{2,6},{6,2},{1... | collective-permute-start | bytes 442376 | tf_op jit(solution)/shard_map/ppermute | solution.py:536
  103.5 1.4 %collective-permute-start.28 = (bf16[48,1536]{1,0:T(8,128)(2,1)S(1)}, bf16[48,1536]{1,0:T(8,128)(2,1)S(1)}, u32[]{:S(2)}, u32[]{:S(2)}) collective-permute-start(bf16[48,1536]{1,0:T(8,128)(2,1)S(1)} %after.17.refs_14_), channel_id=1, source_target_pairs={{0,4},{4,0},{8,12},{12,8},{1,5},{5,1},{9,13},{13,9},{2,6},{6,2},{1... | collective-permute-start | bytes 442376 | tf_op jit(solution)/shard_map/ppermute | solution.py:536

commit v4 on v1

--- a/solution.py
+++ b/solution.py
@@ -316,12 +316,16 @@
                 first = 0
                 for base, rows in zip(bases, sizes):
                     at = pl.multiple_of(base + owner * rows, ALIGN)
-                    copy = pltpu.make_async_copy(
-                        block.at[pl.ds(first, rows), :],
-                        rows_ref.at[pl.ds(at, rows), :],
-                        sems.at[len(copies)],
-                    )
-                    copies.append((at + rows > needed, copy))
+                    for columns, least in (
+                        (slice(query_width, None), needed),
+                        (slice(0, query_width), prior - SPAN - ALIGN),
+                    ):
+                        copy = pltpu.make_async_copy(
+                            block.at[pl.ds(first, rows), columns],
+                            rows_ref.at[pl.ds(at, rows), columns],
+                            sems.at[len(copies)],
+                        )
+                        copies.append((at + rows > least, copy))
                     first += rows
     for wanted, copy in copies:
 
@@ -493,7 +497,7 @@
     query_width, key_width = widths
     width = query_width + 2 * key_width
     total = 2 * chips * sum(sum(sizes) for _, sizes in groups)
-    copies = 2 * chips * sum(len(sizes) for _, sizes in groups)
+    copies = 4 * chips * sum(len(sizes) for _, sizes in groups)
     key_heads, tall = key_width // HEAD_SIZE, query_width // key_width * SPAN
     at = 2 + len(blocks)
     return pl.pallas_call(

time: 116 us -> 111 us (0.957)
  the two profiles are of different devices: /device:TPU:0 before, /device:TPU:1 now
where the time goes in v4:
time: 111 us; the launch traced here: 110 us
  Pallas kernels  45 us (41%)
  starting transfers between devices  37.7 us (34%)
  waiting for transfers between devices  24.2 us (22%)
  local copies, waits for them, and re-layouts  2.27 us (2%)
    pallas_call x8, Pallas kernels, project(): pl.pallas_call(functools.partial(project_kernel, masks, bool(carried), fi...  23.2 us
    ppermute x12, waiting for transfers between devices, start(): line[index + 1] = lax.ppermute(line[source], 'tp', pairs)  19.3 us
    ppermute x12, starting transfers between devices, start(): line[index + 1] = lax.ppermute(line[source], 'tp', pairs)  15.8 us
    ppermute x8, starting transfers between devices, shift_chips(): return lax.ppermute(value, 'req', pairs)  12.6 us
    ppermute x9, starting transfers between devices, swap_cores(): return lax.ppermute(value, 'req', [(d, d ^ 1) for d in range(2 * chips)])  9.33 us
    pallas_call x2, Pallas kernels, attend(): pl.pallas_call(functools.partial(attend_kernel, chips, groups, known, pri...  8.96 us
    pallas_call x1, Pallas kernels, load(): pl.pallas_call(kernel, in_specs=[anywhere, anywhere], out_specs=[vmem, vm...  6.06 us
    pallas_call x3, Pallas kernels, deal(): pl.pallas_call(functools.partial(deal_kernel, chips, bases, sizes, twins)...  5.54 us
  transfers between devices with their start and end apart: 29, of which 9 were waited for; matrix products, arithmetic and copies ran while one was open for 0% of the time, Pallas kernels for 35%

profile of v4, /device:TPU:1, one launch (start us, length us, event | category | flops | bytes accessed | tf_op | source)
XLA Modules:
  0.0 110.2 jit_solution(11618840454968789600)
XLA Ops:
  0.6 0.1 collective-permute-start
  0.8 1.6 %copy-done.2 = bf16[512,2048]{1,0:T(8,128)(2,1)S(1)} copy-done((bf16[512,2048]{1,0:T(8,128)(2,1)S(1)}, bf16[512,2048]{1,0:T(8,128)(2,1)}, u32[]{:S(2)}) %copy-start.2) | copy-done | bytes 2097176
  2.3 0.7 copy-done.4
  3.0 1.3 %deal.3 = (bf16[48,2048]{1,0:T(8,128)(2,1)S(1)}, bf16[1,48,2048]{2,1,0:T(8,128)(2,1)S(1)}) custom-call(s32[4]{0:T(128)S(1)} %copy-done.4, bf16[512,2048]{1,0:T(8,128)(2,1)S(1)} %copy-done.2), custom_call_target="tpu_custom_call" | custom-call | tf_op jit(solution)/shard_map/deal/pallas_call | solution.py:86
  4.3 0.8 collective-permute-done.refs_0_.refs_1_
  5.1 1.3 %deal.4 = (bf16[48,2048]{1,0:T(8,128)(2,1)S(1)}, bf16[1,48,2048]{2,1,0:T(8,128)(2,1)S(1)}) custom-call(s32[4]{0:T(128)S(1)} %copy-done.4, bf16[512,2048]{1,0:T(8,128)(2,1)S(1)} %collective-permute-done.refs_0_.refs_1_, bf16[48,2048]{1,0:T(8,128)(2,1)S(1)} %get-tuple-element.47.refs_1_, bf16[1,48,2048]{2,1,0:T(8,128)(2,1)S(1)} %get-tuple-element.48.refs_2_), custom_call_target="tpu_custom_call" | custom-call | tf_op jit(solution)/shard_map/deal/pallas_call | solution.py:86
  6.4 2.4 %collective-permute-start.1 = (bf16[48,2048]{1,0:T(8,128)(2,1)S(1)}, bf16[48,2048]{1,0:T(8,128)(2,1)S(1)}, u32[]{:S(2)}, u32[]{:S(2)}) collective-permute-start(bf16[48,2048]{1,0:T(8,128)(2,1)S(1)} %bitcast.16), channel_id=1, source_target_pairs={{0,8},{4,12},{8,0},{12,4},{1,9},{5,13},{9,1},{13,5},{2,10},{6,14},... | collective-permute-start | bytes 589832 | tf_op jit(solution)/shard_map/ppermute | solution.py:532
  8.8 2.9 %deal.5 = (bf16[80,2048]{1,0:T(8,128)(2,1)S(1)}, bf16[1,80,2048]{2,1,0:T(8,128)(2,1)S(1)}, bf16[80,2048]{1,0:T(8,128)(2,1)S(1)}, bf16[1,80,2048]{2,1,0:T(8,128)(...) custom-call(s32[4]{0:T(128)S(1)} %copy-done.4, bf16[512,2048]{1,0:T(8,128)(2,1)S(1)} %copy-done.3, ...), custom_call_target="tpu_custom_call" | custom-call | tf_op jit(solution)/shard_map/deal/pallas_call | solution.py:86
  11.7 2.0 %collective-permute-done.1.refs_0_ = bf16[48,2048]{1,0:T(8,128)(2,1)S(1)} collective-permute-done((bf16[48,2048]{1,0:T(8,128)(2,1)S(1)}, bf16[48,2048]{1,0:T(8,128)(2,1)S(1)}, u32[]{:S(2)}, u32[]{:S(2)}) %collective-permute-start.1) | collective-permute-done | bytes 196640 | tf_op jit(solution)/shard_map/ppermute | solution.py:532
  13.8 1.2 %collective-permute-start.3 = (bf16[80,2048]{1,0:T(8,128)(2,1)S(1)}, bf16[80,2048]{1,0:T(8,128)(2,1)S(1)}, u32[]{:S(2)}, u32[]{:S(2)}) collective-permute-start(bf16[80,2048]{1,0:T(8,128)(2,1)S(1)} %bitcast.13), channel_id=1, source_target_pairs={{0,8},{4,12},{8,0},{12,4},{1,9},{5,13},{9,1},{13,5},{2,10},{6,14},... | collective-permute-start | bytes 983048 | tf_op jit(solution)/shard_map/ppermute | solution.py:532
  15.0 1.3 %collective-permute-start.4 = (bf16[48,2048]{1,0:T(8,128)(2,1)S(1)}, bf16[48,2048]{1,0:T(8,128)(2,1)S(1)}, u32[]{:S(2)}, u32[]{:S(2)}) collective-permute-start(bf16[48,2048]{1,0:T(8,128)(2,1)S(1)} %get-tuple-element.52.anchor_ref.refs_0_), channel_id=1, source_target_pairs={{0,1},{1,0},{2,3},{3,2},{4,5},{5,4},{6,7},{7,6},{8,9},{9,8},{10,11... | collective-permute-start | bytes 589832 | tf_op jit(solution)/shard_map/ppermute | solution.py:587
  16.3 2.3 %collective-permute-start.2 = (bf16[48,2048]{1,0:T(8,128)(2,1)S(1)}, bf16[48,2048]{1,0:T(8,128)(2,1)S(1)}, u32[]{:S(2)}, u32[]{:S(2)}) collective-permute-start(bf16[48,2048]{1,0:T(8,128)(2,1)S(1)} %get-tuple-element.52.anchor_ref.refs_0_), channel_id=1, source_target_pairs={{0,2},{1,3},{2,0},{3,1},{4,6},{5,7},{6,4},{7,5},{8,10},{9,11},{10,... | collective-permute-start | bytes 589832 | tf_op jit(solution)/shard_map/ppermute | solution.py:587
  18.6 6.1 %load.1 = (bf16[8192,1024]{1,0:T(8,128)(2,1)S(1)}, f32[8,128]{1,0:T(8,128)S(1)}) custom-call(bf16[8192,1024]{1,0:T(8,128)(2,1)} %weight_ref.1, bf16[48,2048]{1,0:T(8,128)(2,1)S(1)} %get-tuple-element.52.anchor_ref.refs_0_), custom_call_target="tpu_custom_call" | custom-call | tf_op jit(solution)/shard_map/load/pallas_call | solution.py:206
  24.7 0.0 collective-permute-done.3.refs_0_
  24.7 0.3 collective-permute-start.9
  25.1 1.4 %collective-permute-start.10 = (bf16[80,2048]{1,0:T(8,128)(2,1)S(1)}, bf16[80,2048]{1,0:T(8,128)(2,1)S(1)}, u32[]{:S(2)}, u32[]{:S(2)}) collective-permute-start(bf16[80,2048]{1,0:T(8,128)(2,1)S(1)} %get-tuple-element.62.anchor_ref.refs_0_), channel_id=1, source_target_pairs={{0,1},{1,0},{2,3},{3,2},{4,5},{5,4},{6,7},{7,6},{8,9},{9,8},{10,11... | collective-permute-start | bytes 983048 | tf_op jit(solution)/shard_map/ppermute | solution.py:587
  26.4 0.6 collective-permute-start.8
  27.1 0.8 collective-permute-start.5
  27.9 1.1 angles.1
  29.0 4.0 %project.8 = (f32[48,1536]{1,0:T(8,128)S(1)}, f32[48,128]{1,0:T(8,128)S(1)}) custom-call(bf16[48,2048]{1,0:T(8,128)(2,1)S(1)} %get-tuple-element.52.anchor_ref.refs_0_, bf16[48,2048]{1,0:T(8,128)(2,1)S(1)} %get-tuple-element.58.refs_1_, bf16[48,2048]{1,0:T(8,128)(2,1)S(1)} %collective-permute-done.4.refs_2_, f32[1,8192]{1,0:T(1,128)S(1)} %bitcast.5, ...), custom_call_target="tpu_custom_call" | custom-call | tf_op jit(solution)/shard_map/project/pallas_call | solution.py:281
  33.1 10.8 %collective-permute-done.5.refs_0_ = bf16[48,2048]{1,0:T(8,128)(2,1)S(1)} collective-permute-done((bf16[48,2048]{1,0:T(8,128)(2,1)S(1)}, bf16[48,2048]{1,0:T(8,128)(2,1)S(1)}, u32[]{:S(2)}, u32[]{:S(2)}) %collective-permute-start.5) | collective-permute-done | bytes 196640 | tf_op jit(solution)/shard_map/ppermute | solution.py:587
  43.8 1.6 %project.9.refs_3_.refs_0_ = bf16[48,1536]{1,0:T(8,128)(2,1)S(1)} custom-call(bf16[48,2048]{1,0:T(8,128)(2,1)S(1)} %collective-permute-done.5.refs_0_, f32[1,8192]{1,0:T(1,128)S(1)} %bitcast.6, bf16[8192,1024]{1,0:T(8,128)(2,1)S(1)} %get-tuple-element.59.refs_4_.refs_2_, bf16[8192,256]{1,0:T(8,128)(2,1)S(1)} %copy-done, bf16[8192,256]{1,0:T(8,128)(2,1)S(1)} %copy-done.1, ...), custom_call_target="tpu_custom_call" | custom-call | tf_op jit(solution)/shard_map/project/pallas_call | solution.py:281
  45.4 0.0 collective-permute-done.10.refs_2_
  45.4 0.0 collective-permute-done.8.refs_0_
  45.5 0.7 collective-permute-start.11
  46.1 3.9 %collective-permute-start.15 = (bf16[80,2048]{1,0:T(8,128)(2,1)S(1)}, bf16[80,2048]{1,0:T(8,128)(2,1)S(1)}, u32[]{:S(2)}, u32[]{:S(2)}) collective-permute-start(bf16[80,2048]{1,0:T(8,128)(2,1)S(1)} %get-tuple-element.74.refs_0_), channel_id=1, source_target_pairs={{0,2},{1,3},{2,0},{3,1},{4,6},{5,7},{6,4},{7,5},{8,10},{9,11},{10,... | collective-permute-start | bytes 983048 | tf_op jit(solution)/shard_map/ppermute | solution.py:587
  50.0 0.1 collective-permute-start.17
  50.1 0.2 collective-permute-start.16
  50.3 1.2 %collective-permute-start.7 = (bf16[48,1536]{1,0:T(8,128)(2,1)S(1)}, bf16[48,1536]{1,0:T(8,128)(2,1)S(1)}, u32[]{:S(2)}, u32[]{:S(2)}) collective-permute-start(bf16[48,1536]{1,0:T(8,128)(2,1)S(1)} %project.9.refs_3_.refs_0_), channel_id=1, source_target_pairs={{0,8},{4,12},{8,0},{12,4},{1,9},{5,13},{9,1},{13,5},{2,10},{6,14},... | collective-permute-start | bytes 442376 | tf_op jit(solution)/shard_map/ppermute | solution.py:532
  51.6 4.3 %project.10 = (f32[80,1536]{1,0:T(8,128)S(1)}, f32[80,128]{1,0:T(8,128)S(1)}) custom-call(bf16[80,2048]{1,0:T(8,128)(2,1)S(1)} %get-tuple-element.62.anchor_ref.refs_0_, bf16[80,2048]{1,0:T(8,128)(2,1)S(1)} %get-tuple-element.69.refs_1_, bf16[80,2048]{1,0:T(8,128)(2,1)S(1)} %collective-permute-done.10.refs_2_, f32[1,8192]{1,0:T(1,128)S(1)} %bitcast.7, ...), custom_call_target="tpu_custom_call" | custom-call | tf_op jit(solution)/shard_map/project/pallas_call | solution.py:281
  55.9 2.2 %collective-permute-done.11.refs_0_ = bf16[80,2048]{1,0:T(8,128)(2,1)S(1)} collective-permute-done((bf16[80,2048]{1,0:T(8,128)(2,1)S(1)}, bf16[80,2048]{1,0:T(8,128)(2,1)S(1)}, u32[]{:S(2)}, u32[]{:S(2)}) %collective-permute-start.11) | collective-permute-done | bytes 327712 | tf_op jit(solution)/shard_map/ppermute | solution.py:587
  58.1 1.7 %project.11.refs_1_.refs_3_.refs_4_ = bf16[80,1536]{1,0:T(8,128)(2,1)S(1)} custom-call(bf16[80,2048]{1,0:T(8,128)(2,1)S(1)} %collective-permute-done.11.refs_0_, f32[1,8192]{1,0:T(1,128)S(1)} %bitcast.8, bf16[8192,1024]{1,0:T(8,128)(2,1)S(1)} %get-tuple-element.59.refs_4_.refs_2_, bf16[8192,256]{1,0:T(8,128)(2,1)S(1)} %copy-done, ...), custom_call_target="tpu_custom_call" | custom-call | tf_op jit(solution)/shard_map/project/pallas_call | solution.py:281
  59.8 0.0 collective-permute-done.15.refs_0_
  59.8 6.3 %collective-permute-done.17.refs_2_ = bf16[80,2048]{1,0:T(8,128)(2,1)S(1)} collective-permute-done((bf16[80,2048]{1,0:T(8,128)(2,1)S(1)}, bf16[80,2048]{1,0:T(8,128)(2,1)S(1)}, u32[]{:S(2)}, u32[]{:S(2)}) %collective-permute-start.17) | collective-permute-done | bytes 327712 | tf_op jit(solution)/shard_map/ppermute | solution.py:587
  66.1 0.7 collective-permute-start.18
  66.8 3.0 %collective-permute-start.14 = (bf16[80,1536]{1,0:T(8,128)(2,1)S(1)}, bf16[80,1536]{1,0:T(8,128)(2,1)S(1)}, u32[]{:S(2)}, u32[]{:S(2)}) collective-permute-start(bf16[80,1536]{1,0:T(8,128)(2,1)S(1)} %project.11.refs_1_.refs_3_.refs_4_), channel_id=1, source_target_pairs={{0,8},{4,12},{8,0},{12,4},{1,9},{5,13},{9,1},{13,5},{2,10},{6,14},... | collective-permute-start | bytes 737288 | tf_op jit(solution)/shard_map/ppermute | solution.py:532
  69.8 3.1 %collective-permute-start.22 = (bf16[48,2048]{1,0:T(8,128)(2,1)S(1)}, bf16[48,2048]{1,0:T(8,128)(2,1)S(1)}, u32[]{:S(2)}, u32[]{:S(2)}) collective-permute-start(bf16[48,2048]{1,0:T(8,128)(2,1)S(1)} %get-tuple-element.82.refs_0_), channel_id=1, source_target_pairs={{0,2},{1,3},{2,0},{3,1},{4,6},{5,7},{6,4},{7,5},{8,10},{9,11},{10,... | collective-permute-start | bytes 589832 | tf_op jit(solution)/shard_map/ppermute | solution.py:587
  72.9 0.0 collective-permute-start.23
  72.9 4.3 %project.12 = (f32[80,1536]{1,0:T(8,128)S(1)}, f32[80,128]{1,0:T(8,128)S(1)}) custom-call(bf16[80,2048]{1,0:T(8,128)(2,1)S(1)} %get-tuple-element.74.refs_0_, bf16[80,2048]{1,0:T(8,128)(2,1)S(1)} %get-tuple-element.77.refs_1_, bf16[80,2048]{1,0:T(8,128)(2,1)S(1)} %collective-permute-done.17.refs_2_, f32[1,8192]{1,0:T(1,128)S(1)} %bitcast.9, ...), custom_call_target="tpu_custom_call" | custom-call | tf_op jit(solution)/shard_map/project/pallas_call | solution.py:281
  77.2 0.0 collective-permute-done.18.refs_0_
  77.2 1.7 %project.13.refs_1_.refs_8_ = bf16[80,1536]{1,0:T(8,128)(2,1)S(1)} custom-call(bf16[80,2048]{1,0:T(8,128)(2,1)S(1)} %collective-permute-done.18.refs_0_, f32[1,8192]{1,0:T(1,128)S(1)} %bitcast.10, bf16[8192,1024]{1,0:T(8,128)(2,1)S(1)} %get-tuple-element.59.refs_4_.refs_2_, bf16[8192,256]{1,0:T(8,128)(2,1)S(1)} %copy-done, bf16[8192,256]{1,0:T(8,128)(2,1)S(1)} %copy-done.1, ...), custom_call_target="tpu_custom_call" | custom-call | tf_op jit(solution)/shard_map/project/pallas_call | solution.py:281
  78.9 4.2 %collective-permute-start.21 = (bf16[80,1536]{1,0:T(8,128)(2,1)S(1)}, bf16[80,1536]{1,0:T(8,128)(2,1)S(1)}, u32[]{:S(2)}, u32[]{:S(2)}) collective-permute-start(bf16[80,1536]{1,0:T(8,128)(2,1)S(1)} %project.13.refs_1_.refs_8_), channel_id=1, source_target_pairs={{0,8},{4,12},{8,0},{12,4},{1,9},{5,13},{9,1},{13,5},{2,10},{6,14},... | collective-permute-start | bytes 737288 | tf_op jit(solution)/shard_map/ppermute | solution.py:532
  83.1 0.0 collective-permute-done.22.refs_0_
  83.1 0.0 collective-permute-done.23.refs_1_.refs_2_
  83.1 0.0 collective-permute-done.14.refs_0_.refs_2_
  83.1 1.0 collective-permute-start.24
  84.0 4.4 %collective-permute-start.6 = (bf16[48,1536]{1,0:T(8,128)(2,1)S(1)}, bf16[48,1536]{1,0:T(8,128)(2,1)S(1)}, u32[]{:S(2)}, u32[]{:S(2)}) collective-permute-start(bf16[48,1536]{1,0:T(8,128)(2,1)S(1)} %project.9.refs_3_.refs_0_), channel_id=1, source_target_pairs={{0,4},{4,0},{8,12},{12,8},{1,5},{5,1},{9,13},{13,9},{2,6},{6,2},{1... | collective-permute-start | bytes 442376 | tf_op jit(solution)/shard_map/ppermute | solution.py:536
  88.4 0.1 collective-permute-start.12
  88.5 0.4 collective-permute-start.13
  88.9 4.1 %project.14 = (f32[48,1536]{1,0:T(8,128)S(1)}, f32[48,128]{1,0:T(8,128)S(1)}) custom-call(bf16[48,2048]{1,0:T(8,128)(2,1)S(1)} %get-tuple-element.82.refs_0_, bf16[48,2048]{1,0:T(8,128)(2,1)S(1)} %after.13.refs_1_, bf16[48,2048]{1,0:T(8,128)(2,1)S(1)} %collective-permute-done.23.refs_1_.refs_2_, f32[1,8192]{1,0:T(1,128)S(1)} %bitcast.11, ...), custom_call_target="tpu_custom_call" | custom-call | tf_op jit(solution)/shard_map/project/pallas_call | solution.py:281
  93.0 0.0 collective-permute-done.24.refs_0_
  93.0 1.0 collective-permute-start.20
  94.0 1.7 %project.15.refs_1_.refs_12_ = bf16[48,1536]{1,0:T(8,128)(2,1)S(1)} custom-call(bf16[48,2048]{1,0:T(8,128)(2,1)S(1)} %collective-permute-done.24.refs_0_, f32[1,8192]{1,0:T(1,128)S(1)} %bitcast.12, bf16[8192,1024]{1,0:T(8,128)(2,1)S(1)} %get-tuple-element.59.refs_4_.refs_2_, bf16[8192,256]{1,0:T(8,128)(2,1)S(1)} %copy-done, bf16[8192,256]{1,0:T(8,128)(2,1)S(1)} %copy-done.1, ...), custom_call_target="tpu_custom_call" | custom-call | tf_op jit(solution)/shard_map/project/pallas_call | solution.py:281
  95.7 0.1 collective-permute-start.19
  95.8 0.0 collective-permute-done.6.refs_1_
  95.8 0.5 collective-permute-start.25
  96.3 0.4 collective-permute-start.26
  96.7 0.6 collective-permute-done.19.refs_7_
  97.3 0.3 collective-permute-done.25.refs_11_
  97.6 4.0 %attend.2 = (bf16[512,1024]{1,0:T(8,128)(2,1)}, bf16[2,512,256]{2,1,0:T(8,128)(2,1)}, f32[8,128]{1,0:T(8,128)S(1)}) custom-call(s32[4]{0:T(128)S(1)} %copy-done.5, s32[16]{0:T(128)S(1)} %copy-done.6, bf16[48,1536]{1,0:T(8,128)(2,1)S(1)} %project.9.refs_3_.refs_0_, bf16[48,1536]{1,0:T(8,128)(2,1)S(1)} %collective-permute-done.6.refs_1_, ...), custom_call_target="tpu_custom_call" | custom-call | tf_op jit(solution)/shard_map/attend/pallas_call | solution.py:503
  101.6 0.1 collective-permute-done.27.refs_0_
  101.7 2.4 %collective-permute-start.28 = (bf16[48,1536]{1,0:T(8,128)(2,1)S(1)}, bf16[48,1536]{1,0:T(8,128)(2,1)S(1)}, u32[]{:S(2)}, u32[]{:S(2)}) collective-permute-start(bf16[48,1536]{1,0:T(8,128)(2,1)S(1)} %after.15.refs_14_), channel_id=1, source_target_pairs={{0,4},{4,0},{8,12},{12,8},{1,5},{5,1},{9,13},{13,9},{2,6},{6,2},{1... | collective-permute-start | bytes 442376 | tf_op jit(solution)/shard_map/ppermute | solution.py:536
  104.1 1.0 collective-permute-done.28.refs_15_
  105.1 5.0 %attend.3 = (bf16[512,1024]{1,0:T(8,128)(2,1)}, bf16[2,512,256]{2,1,0:T(8,128)(2,1)}, f32[8,128]{1,0:T(8,128)}) custom-call(s32[4]{0:T(128)S(1)} %copy-done.5, s32[16]{0:T(128)S(1)} %copy-done.6, bf16[48,1536]{1,0:T(8,128)(2,1)S(1)} %project.9.refs_3_.refs_0_, ...), custom_call_target="tpu_custom_call", output_to_operand_aliasing={{0}: (18, {}), {1}: (19, {})} | custom-call | tf_op jit(solution)/shard_map/attend/pallas_call | solution.py:503
  (40 shorter events, 0.2 us)
Async XLA Ops:
  0.6 4.4 %collective-permute-start = (bf16[512,2048]{1,0:T(8,128)(2,1)}, bf16[512,2048]{1,0:T(8,128)(2,1)S(1)}, u32[]{:S(2)}, u32[]{:S(2)}) collective-permute-start(bf16[512,2048]{1,0:T(8,128)(2,1)} %refs_0_.3), channel_id=1, source_target_pairs={{0,4},{4,0},{8,12},{12,8},{1,5},{5,1},{9,13},{13,9},{2,6},{6,2},{1... | collective-permute-start | bytes 6291464 | tf_op jit(solution)/shard_map/ppermute | solution.py:536
  0.8 1.6 %copy-start.2 = (bf16[512,2048]{1,0:T(8,128)(2,1)S(1)}, bf16[512,2048]{1,0:T(8,128)(2,1)}, u32[]{:S(2)}) copy-start(bf16[512,2048]{1,0:T(8,128)(2,1)} %refs_0_.3) | copy-start | bytes 6291460
  2.3 0.7 copy-start.4
  3.0 5.8 %copy-start.3 = (bf16[512,2048]{1,0:T(8,128)(2,1)S(1)}, bf16[512,2048]{1,0:T(8,128)(2,1)}, u32[]{:S(2)}) copy-start(bf16[512,2048]{1,0:T(8,128)(2,1)} %refs_0_.3) | copy-start | bytes 6291460
  6.4 7.4 %collective-permute-start.1 = (bf16[48,2048]{1,0:T(8,128)(2,1)S(1)}, bf16[48,2048]{1,0:T(8,128)(2,1)S(1)}, u32[]{:S(2)}, u32[]{:S(2)}) collective-permute-start(bf16[48,2048]{1,0:T(8,128)(2,1)S(1)} %bitcast.16), channel_id=1, source_target_pairs={{0,8},{4,12},{8,0},{12,4},{1,9},{5,13},{9,1},{13,5},{2,10},{6,14},... | collective-permute-start | bytes 589832 | tf_op jit(solution)/shard_map/ppermute | solution.py:532
  13.8 10.9 %collective-permute-start.3 = (bf16[80,2048]{1,0:T(8,128)(2,1)S(1)}, bf16[80,2048]{1,0:T(8,128)(2,1)S(1)}, u32[]{:S(2)}, u32[]{:S(2)}) collective-permute-start(bf16[80,2048]{1,0:T(8,128)(2,1)S(1)} %bitcast.13), channel_id=1, source_target_pairs={{0,8},{4,12},{8,0},{12,4},{1,9},{5,13},{9,1},{13,5},{2,10},{6,14},... | collective-permute-start | bytes 983048 | tf_op jit(solution)/shard_map/ppermute | solution.py:532
  15.0 12.9 %copy-start.8 = (bf16[8192]{0:T(1024)(128)(2,1)S(1)}, bf16[8192]{0:T(1024)(128)(2,1)}, u32[]{:S(2)}) copy-start(bf16[8192]{0:T(1024)(128)(2,1)} %param.9) | copy-start | bytes 49156
  15.0 12.9 %copy-start.5 = (s32[4]{0:T(128)S(1)}, s32[4]{0:T(128)}, u32[]{:S(2)}) copy-start(s32[4]{0:T(128)} %lengths_ref.11) | copy-start | bytes 52
  15.0 12.9 %copy-start.7 = (f32[1,128]{1,0:T(1,128)S(1)}, f32[1,128]{1,0:T(1,128)}, u32[]{:S(2)}) copy-start(f32[1,128]{1,0:T(1,128)} %constant.2.clone.frequency_ref) | copy-start | bytes 1540
  15.0 10.1 %collective-permute-start.4 = (bf16[48,2048]{1,0:T(8,128)(2,1)S(1)}, bf16[48,2048]{1,0:T(8,128)(2,1)S(1)}, u32[]{:S(2)}, u32[]{:S(2)}) collective-permute-start(bf16[48,2048]{1,0:T(8,128)(2,1)S(1)} %get-tuple-element.52.anchor_ref.refs_0_), channel_id=1, source_target_pairs={{0,1},{1,0},{2,3},{3,2},{4,5},{5,4},{6,7},{7,6},{8,9},{9,8},{10,11... | collective-permute-start | bytes 589832 | tf_op jit(solution)/shard_map/ppermute | solution.py:587
  16.3 8.8 %collective-permute-start.2 = (bf16[48,2048]{1,0:T(8,128)(2,1)S(1)}, bf16[48,2048]{1,0:T(8,128)(2,1)S(1)}, u32[]{:S(2)}, u32[]{:S(2)}) collective-permute-start(bf16[48,2048]{1,0:T(8,128)(2,1)S(1)} %get-tuple-element.52.anchor_ref.refs_0_), channel_id=1, source_target_pairs={{0,2},{1,3},{2,0},{3,1},{4,6},{5,7},{6,4},{7,5},{8,10},{9,11},{10,... | collective-permute-start | bytes 589832 | tf_op jit(solution)/shard_map/ppermute | solution.py:587
  18.6 10.4 %copy-start = (bf16[8192,256]{1,0:T(8,128)(2,1)S(1)}, bf16[8192,256]{1,0:T(8,128)(2,1)}, u32[]{:S(2)}) copy-start(bf16[8192,256]{1,0:T(8,128)(2,1)} %refs_3_.7) | copy-start | bytes 12582916
  18.6 10.4 %copy-start.1 = (bf16[8192,256]{1,0:T(8,128)(2,1)S(1)}, bf16[8192,256]{1,0:T(8,128)(2,1)}, u32[]{:S(2)}) copy-start(bf16[8192,256]{1,0:T(8,128)(2,1)} %refs_4_.7) | copy-start | bytes 12582916
  24.7 20.7 %collective-permute-start.9 = (bf16[80,2048]{1,0:T(8,128)(2,1)S(1)}, bf16[80,2048]{1,0:T(8,128)(2,1)S(1)}, u32[]{:S(2)}, u32[]{:S(2)}) collective-permute-start(bf16[80,2048]{1,0:T(8,128)(2,1)S(1)} %bitcast.14), channel_id=1, source_target_pairs={{0,8},{4,12},{8,0},{12,4},{1,9},{5,13},{9,1},{13,5},{2,10},{6,14},... | collective-permute-start | bytes 983048 | tf_op jit(solution)/shard_map/ppermute | solution.py:532
  25.1 20.4 %collective-permute-start.10 = (bf16[80,2048]{1,0:T(8,128)(2,1)S(1)}, bf16[80,2048]{1,0:T(8,128)(2,1)S(1)}, u32[]{:S(2)}, u32[]{:S(2)}) collective-permute-start(bf16[80,2048]{1,0:T(8,128)(2,1)S(1)} %get-tuple-element.62.anchor_ref.refs_0_), channel_id=1, source_target_pairs={{0,1},{1,0},{2,3},{3,2},{4,5},{5,4},{6,7},{7,6},{8,9},{9,8},{10,11... | collective-permute-start | bytes 983048 | tf_op jit(solution)/shard_map/ppermute | solution.py:587
  26.4 19.0 %collective-permute-start.8 = (bf16[80,2048]{1,0:T(8,128)(2,1)S(1)}, bf16[80,2048]{1,0:T(8,128)(2,1)S(1)}, u32[]{:S(2)}, u32[]{:S(2)}) collective-permute-start(bf16[80,2048]{1,0:T(8,128)(2,1)S(1)} %get-tuple-element.62.anchor_ref.refs_0_), channel_id=1, source_target_pairs={{0,2},{1,3},{2,0},{3,1},{4,6},{5,7},{6,4},{7,5},{8,10},{9,11},{10,... | collective-permute-start | bytes 983048 | tf_op jit(solution)/shard_map/ppermute | solution.py:587
  27.1 16.7 %collective-permute-start.5 = (bf16[48,2048]{1,0:T(8,128)(2,1)S(1)}, bf16[48,2048]{1,0:T(8,128)(2,1)S(1)}, u32[]{:S(2)}, u32[]{:S(2)}) collective-permute-start(bf16[48,2048]{1,0:T(8,128)(2,1)S(1)} %get-tuple-element.58.refs_1_), channel_id=1, source_target_pairs={{0,1},{1,0},{2,3},{3,2},{4,5},{5,4},{6,7},{7,6},{8,9},{9,8},{10,11... | collective-permute-start | bytes 589832 | tf_op jit(solution)/shard_map/ppermute | solution.py:587
  45.5 12.6 %collective-permute-start.11 = (bf16[80,2048]{1,0:T(8,128)(2,1)S(1)}, bf16[80,2048]{1,0:T(8,128)(2,1)S(1)}, u32[]{:S(2)}, u32[]{:S(2)}) collective-permute-start(bf16[80,2048]{1,0:T(8,128)(2,1)S(1)} %get-tuple-element.69.refs_1_), channel_id=1, source_target_pairs={{0,1},{1,0},{2,3},{3,2},{4,5},{5,4},{6,7},{7,6},{8,9},{9,8},{10,11... | collective-permute-start | bytes 983048 | tf_op jit(solution)/shard_map/ppermute | solution.py:587
  46.1 13.6 %collective-permute-start.15 = (bf16[80,2048]{1,0:T(8,128)(2,1)S(1)}, bf16[80,2048]{1,0:T(8,128)(2,1)S(1)}, u32[]{:S(2)}, u32[]{:S(2)}) collective-permute-start(bf16[80,2048]{1,0:T(8,128)(2,1)S(1)} %get-tuple-element.74.refs_0_), channel_id=1, source_target_pairs={{0,2},{1,3},{2,0},{3,1},{4,6},{5,7},{6,4},{7,5},{8,10},{9,11},{10,... | collective-permute-start | bytes 983048 | tf_op jit(solution)/shard_map/ppermute | solution.py:587
  50.0 16.1 %collective-permute-start.17 = (bf16[80,2048]{1,0:T(8,128)(2,1)S(1)}, bf16[80,2048]{1,0:T(8,128)(2,1)S(1)}, u32[]{:S(2)}, u32[]{:S(2)}) collective-permute-start(bf16[80,2048]{1,0:T(8,128)(2,1)S(1)} %get-tuple-element.74.refs_0_), channel_id=1, source_target_pairs={{0,1},{1,0},{2,3},{3,2},{4,5},{5,4},{6,7},{7,6},{8,9},{9,8},{10,11... | collective-permute-start | bytes 983048 | tf_op jit(solution)/shard_map/ppermute | solution.py:587
  50.1 5.7 %collective-permute-start.16 = (bf16[48,2048]{1,0:T(8,128)(2,1)S(1)}, bf16[48,2048]{1,0:T(8,128)(2,1)S(1)}, u32[]{:S(2)}, u32[]{:S(2)}) collective-permute-start(bf16[48,2048]{1,0:T(8,128)(2,1)S(1)} %bitcast.15), channel_id=1, source_target_pairs={{0,8},{4,12},{8,0},{12,4},{1,9},{5,13},{9,1},{13,5},{2,10},{6,14},... | collective-permute-start | bytes 589832 | tf_op jit(solution)/shard_map/ppermute | solution.py:532
  50.3 9.4 %collective-permute-start.7 = (bf16[48,1536]{1,0:T(8,128)(2,1)S(1)}, bf16[48,1536]{1,0:T(8,128)(2,1)S(1)}, u32[]{:S(2)}, u32[]{:S(2)}) collective-permute-start(bf16[48,1536]{1,0:T(8,128)(2,1)S(1)} %project.9.refs_3_.refs_0_), channel_id=1, source_target_pairs={{0,8},{4,12},{8,0},{12,4},{1,9},{5,13},{9,1},{13,5},{2,10},{6,14},... | collective-permute-start | bytes 442376 | tf_op jit(solution)/shard_map/ppermute | solution.py:532
  66.1 11.1 %collective-permute-start.18 = (bf16[80,2048]{1,0:T(8,128)(2,1)S(1)}, bf16[80,2048]{1,0:T(8,128)(2,1)S(1)}, u32[]{:S(2)}, u32[]{:S(2)}) collective-permute-start(bf16[80,2048]{1,0:T(8,128)(2,1)S(1)} %get-tuple-element.77.refs_1_), channel_id=1, source_target_pairs={{0,1},{1,0},{2,3},{3,2},{4,5},{5,4},{6,7},{7,6},{8,9},{9,8},{10,11... | collective-permute-start | bytes 983048 | tf_op jit(solution)/shard_map/ppermute | solution.py:587
  66.8 16.3 %collective-permute-start.14 = (bf16[80,1536]{1,0:T(8,128)(2,1)S(1)}, bf16[80,1536]{1,0:T(8,128)(2,1)S(1)}, u32[]{:S(2)}, u32[]{:S(2)}) collective-permute-start(bf16[80,1536]{1,0:T(8,128)(2,1)S(1)} %project.11.refs_1_.refs_3_.refs_4_), channel_id=1, source_target_pairs={{0,8},{4,12},{8,0},{12,4},{1,9},{5,13},{9,1},{13,5},{2,10},{6,14},... | collective-permute-start | bytes 737288 | tf_op jit(solution)/shard_map/ppermute | solution.py:532
  69.8 13.3 %collective-permute-start.22 = (bf16[48,2048]{1,0:T(8,128)(2,1)S(1)}, bf16[48,2048]{1,0:T(8,128)(2,1)S(1)}, u32[]{:S(2)}, u32[]{:S(2)}) collective-permute-start(bf16[48,2048]{1,0:T(8,128)(2,1)S(1)} %get-tuple-element.82.refs_0_), channel_id=1, source_target_pairs={{0,2},{1,3},{2,0},{3,1},{4,6},{5,7},{6,4},{7,5},{8,10},{9,11},{10,... | collective-permute-start | bytes 589832 | tf_op jit(solution)/shard_map/ppermute | solution.py:587
  72.9 10.2 %collective-permute-start.23 = (bf16[48,2048]{1,0:T(8,128)(2,1)S(1)}, bf16[48,2048]{1,0:T(8,128)(2,1)S(1)}, u32[]{:S(2)}, u32[]{:S(2)}) collective-permute-start(bf16[48,2048]{1,0:T(8,128)(2,1)S(1)} %get-tuple-element.82.refs_0_), channel_id=1, source_target_pairs={{0,1},{1,0},{2,3},{3,2},{4,5},{5,4},{6,7},{7,6},{8,9},{9,8},{10,11... | collective-permute-start | bytes 589832 | tf_op jit(solution)/shard_map/ppermute | solution.py:587
  78.9 16.8 %collective-permute-start.21 = (bf16[80,1536]{1,0:T(8,128)(2,1)S(1)}, bf16[80,1536]{1,0:T(8,128)(2,1)S(1)}, u32[]{:S(2)}, u32[]{:S(2)}) collective-permute-start(bf16[80,1536]{1,0:T(8,128)(2,1)S(1)} %project.13.refs_1_.refs_8_), channel_id=1, source_target_pairs={{0,8},{4,12},{8,0},{12,4},{1,9},{5,13},{9,1},{13,5},{2,10},{6,14},... | collective-permute-start | bytes 737288 | tf_op jit(solution)/shard_map/ppermute | solution.py:532
  83.1 9.9 %collective-permute-start.24 = (bf16[48,2048]{1,0:T(8,128)(2,1)S(1)}, bf16[48,2048]{1,0:T(8,128)(2,1)S(1)}, u32[]{:S(2)}, u32[]{:S(2)}) collective-permute-start(bf16[48,2048]{1,0:T(8,128)(2,1)S(1)} %after.13.refs_1_), channel_id=1, source_target_pairs={{0,1},{1,0},{2,3},{3,2},{4,5},{5,4},{6,7},{7,6},{8,9},{9,8},{10,11... | collective-permute-start | bytes 589832 | tf_op jit(solution)/shard_map/ppermute | solution.py:587
  84.0 11.8 %collective-permute-start.6 = (bf16[48,1536]{1,0:T(8,128)(2,1)S(1)}, bf16[48,1536]{1,0:T(8,128)(2,1)S(1)}, u32[]{:S(2)}, u32[]{:S(2)}) collective-permute-start(bf16[48,1536]{1,0:T(8,128)(2,1)S(1)} %project.9.refs_3_.refs_0_), channel_id=1, source_target_pairs={{0,4},{4,0},{8,12},{12,8},{1,5},{5,1},{9,13},{13,9},{2,6},{6,2},{1... | collective-permute-start | bytes 442376 | tf_op jit(solution)/shard_map/ppermute | solution.py:536
  88.4 7.9 %collective-permute-start.12 = (bf16[48,1536]{1,0:T(8,128)(2,1)S(1)}, bf16[48,1536]{1,0:T(8,128)(2,1)S(1)}, u32[]{:S(2)}, u32[]{:S(2)}) collective-permute-start(bf16[48,1536]{1,0:T(8,128)(2,1)S(1)} %after.10.refs_2_), channel_id=1, source_target_pairs={{0,4},{4,0},{8,12},{12,8},{1,5},{5,1},{9,13},{13,9},{2,6},{6,2},{1... | collective-permute-start | bytes 442376 | tf_op jit(solution)/shard_map/ppermute | solution.py:536
  88.5 7.8 %collective-permute-start.13 = (bf16[80,1536]{1,0:T(8,128)(2,1)S(1)}, bf16[80,1536]{1,0:T(8,128)(2,1)S(1)}, u32[]{:S(2)}, u32[]{:S(2)}) collective-permute-start(bf16[80,1536]{1,0:T(8,128)(2,1)S(1)} %project.11.refs_1_.refs_3_.refs_4_), channel_id=1, source_target_pairs={{0,4},{4,0},{8,12},{12,8},{1,5},{5,1},{9,13},{13,9},{2,6},{6,2},{1... | collective-permute-start | bytes 737288 | tf_op jit(solution)/shard_map/ppermute | solution.py:536
  93.0 4.3 %collective-permute-start.20 = (bf16[80,1536]{1,0:T(8,128)(2,1)S(1)}, bf16[80,1536]{1,0:T(8,128)(2,1)S(1)}, u32[]{:S(2)}, u32[]{:S(2)}) collective-permute-start(bf16[80,1536]{1,0:T(8,128)(2,1)S(1)} %project.13.refs_1_.refs_8_), channel_id=1, source_target_pairs={{0,4},{4,0},{8,12},{12,8},{1,5},{5,1},{9,13},{13,9},{2,6},{6,2},{1... | collective-permute-start | bytes 737288 | tf_op jit(solution)/shard_map/ppermute | solution.py:536
  94.0 3.6 %copy-start.6 = (s32[16]{0:T(128)S(1)}, s32[16]{0:T(128)}, u32[]{:S(2)}) copy-start(s32[16]{0:T(128)} %plan_ref.3) | copy-start | bytes 196
  95.7 1.6 %collective-permute-start.19 = (bf16[80,1536]{1,0:T(8,128)(2,1)S(1)}, bf16[80,1536]{1,0:T(8,128)(2,1)S(1)}, u32[]{:S(2)}, u32[]{:S(2)}) collective-permute-start(bf16[80,1536]{1,0:T(8,128)(2,1)S(1)} %after.12.refs_6_), channel_id=1, source_target_pairs={{0,4},{4,0},{8,12},{12,8},{1,5},{5,1},{9,13},{13,9},{2,6},{6,2},{1... | collective-permute-start | bytes 737288 | tf_op jit(solution)/shard_map/ppermute | solution.py:536
  95.8 1.8 %collective-permute-start.25 = (bf16[80,1536]{1,0:T(8,128)(2,1)S(1)}, bf16[80,1536]{1,0:T(8,128)(2,1)S(1)}, u32[]{:S(2)}, u32[]{:S(2)}) collective-permute-start(bf16[80,1536]{1,0:T(8,128)(2,1)S(1)} %after.14.refs_10_), channel_id=1, source_target_pairs={{0,4},{4,0},{8,12},{12,8},{1,5},{5,1},{9,13},{13,9},{2,6},{6,2},{1... | collective-permute-start | bytes 737288 | tf_op jit(solution)/shard_map/ppermute | solution.py:536
  96.3 5.4 %collective-permute-start.27 = (bf16[48,1536]{1,0:T(8,128)(2,1)S(1)}, bf16[48,1536]{1,0:T(8,128)(2,1)S(1)}, u32[]{:S(2)}, u32[]{:S(2)}) collective-permute-start(bf16[48,1536]{1,0:T(8,128)(2,1)S(1)} %project.15.refs_1_.refs_12_), channel_id=1, source_target_pairs={{0,8},{4,12},{8,0},{12,4},{1,9},{5,13},{9,1},{13,5},{2,10},{6,14},... | collective-permute-start | bytes 442376 | tf_op jit(solution)/shard_map/ppermute | solution.py:532
  96.3 7.8 %collective-permute-start.26 = (bf16[48,1536]{1,0:T(8,128)(2,1)S(1)}, bf16[48,1536]{1,0:T(8,128)(2,1)S(1)}, u32[]{:S(2)}, u32[]{:S(2)}) collective-permute-start(bf16[48,1536]{1,0:T(8,128)(2,1)S(1)} %project.15.refs_1_.refs_12_), channel_id=1, source_target_pairs={{0,4},{4,0},{8,12},{12,8},{1,5},{5,1},{9,13},{13,9},{2,6},{6,2},{1... | collective-permute-start | bytes 442376 | tf_op jit(solution)/shard_map/ppermute | solution.py:536
  101.7 3.4 %collective-permute-start.28 = (bf16[48,1536]{1,0:T(8,128)(2,1)S(1)}, bf16[48,1536]{1,0:T(8,128)(2,1)S(1)}, u32[]{:S(2)}, u32[]{:S(2)}) collective-permute-start(bf16[48,1536]{1,0:T(8,128)(2,1)S(1)} %after.15.refs_14_), channel_id=1, source_target_pairs={{0,4},{4,0},{8,12},{12,8},{1,5},{5,1},{9,13},{13,9},{2,6},{6,2},{1... | collective-permute-start | bytes 442376 | tf_op jit(solution)/shard_map/ppermute | solution.py:536

commit v5 on v4

--- a/solution.py
+++ b/solution.py
@@ -13,7 +13,7 @@
 SPAN = 128
 ALIGN = 16
 TILE = 2 * SPAN
-SHARES = (3, 5, 5, 3)
+SHARES = (2, 6, 5, 3)
 DEPTH = 1024
 MEBI = 1024 * 1024
 F32, BF16 = jnp.float32, jnp.bfloat16
@@ -625,11 +625,14 @@
             turns = angles(groups, lengths, frequency, lines[1][0])
     fence(last + 1, [])
     start(lines[-1], kinds["late"])
-    for chunk in (last - 1, last):
-        finish(chunk)
+    finish(last - 1)
+    sums = list(add("first", last))
     blocks = []
-    for at in range(last):
+    for at in range(last - 1):
         blocks += all_blocks(own[at], after(sent[at], own[at + 1 : at + 2]))
+    sums[1:] = after(sums[1:], blocks[: 2 * chips])
+    own.append(add("late", last, sums)[0])
+    blocks += all_blocks(own[last - 1], after(sent[last - 1], own[last:]))
     sent.append(from_chips(own[last]))
     known = workers * sum(sizes[:-1])
     common = widths, slots, lengths, plan

time: 111 us -> 111 us (level)
  the two profiles are of different devices: /device:TPU:1 before, /device:TPU:0 now
where the time goes in v5:
time: 111 us
  Pallas kernels  45.3 us (41%)
  waiting for transfers between devices  33.6 us (30%)
  starting transfers between devices  28.6 us (26%)
  local copies, waits for them, and re-layouts  2.27 us (2%)
  between operations  1.11 us (1%)
    ppermute x12, waiting for transfers between devices, start(): line[index + 1] = lax.ppermute(line[source], 'tp', pairs)  30.7 us
    pallas_call x8, Pallas kernels, project(): pl.pallas_call(functools.partial(project_kernel, masks, bool(carried), fi...  22.6 us
    ppermute x12, starting transfers between devices, start(): line[index + 1] = lax.ppermute(line[source], 'tp', pairs)  15.4 us
    ppermute x8, starting transfers between devices, shift_chips(): return lax.ppermute(value, 'req', pairs)  9.75 us
    pallas_call x2, Pallas kernels, attend(): pl.pallas_call(functools.partial(attend_kernel, chips, groups, known, pri...  9.72 us
    pallas_call x1, Pallas kernels, load(): pl.pallas_call(kernel, in_specs=[anywhere, anywhere], out_specs=[vmem, vm...  6.06 us
    pallas_call x3, Pallas kernels, deal(): pl.pallas_call(functools.partial(deal_kernel, chips, bases, sizes, twins)...  5.66 us
    ppermute x9, starting transfers between devices, swap_cores(): return lax.ppermute(value, 'req', [(d, d ^ 1) for d in range(2 * chips)])  3.46 us
  transfers between devices with their start and end apart: 29, of which 9 were waited for; matrix products, arithmetic and copies ran while one was open for 0% of the time, Pallas kernels for 35%

profile of v5, /device:TPU:0, one launch (start us, length us, event | category | flops | bytes accessed | tf_op | source)
XLA Modules:
  0.0 110.9 jit_solution(1752381897849901507)
XLA Ops:
  0.6 0.5 collective-permute-start
  1.1 1.6 %copy-done.2 = bf16[512,2048]{1,0:T(8,128)(2,1)S(1)} copy-done((bf16[512,2048]{1,0:T(8,128)(2,1)S(1)}, bf16[512,2048]{1,0:T(8,128)(2,1)}, u32[]{:S(2)}) %copy-start.2) | copy-done | bytes 2097176
  2.7 0.7 copy-done.4
  3.4 1.3 %deal.3 = (bf16[32,2048]{1,0:T(8,128)(2,1)S(1)}, bf16[1,32,2048]{2,1,0:T(8,128)(2,1)S(1)}) custom-call(s32[4]{0:T(128)S(1)} %copy-done.4, bf16[512,2048]{1,0:T(8,128)(2,1)S(1)} %copy-done.2), custom_call_target="tpu_custom_call" | custom-call | tf_op jit(solution)/shard_map/deal/pallas_call | solution.py:86
  4.7 0.5 collective-permute-done.refs_0_.refs_1_
  5.1 1.3 %deal.4 = (bf16[32,2048]{1,0:T(8,128)(2,1)S(1)}, bf16[1,32,2048]{2,1,0:T(8,128)(2,1)S(1)}) custom-call(s32[4]{0:T(128)S(1)} %copy-done.4, bf16[512,2048]{1,0:T(8,128)(2,1)S(1)} %collective-permute-done.refs_0_.refs_1_, bf16[32,2048]{1,0:T(8,128)(2,1)S(1)} %get-tuple-element.47.refs_1_, bf16[1,32,2048]{2,1,0:T(8,128)(2,1)S(1)} %get-tuple-element.48.refs_2_), custom_call_target="tpu_custom_call" | custom-call | tf_op jit(solution)/shard_map/deal/pallas_call | solution.py:86
  6.4 2.9 %collective-permute-start.1 = (bf16[32,2048]{1,0:T(8,128)(2,1)S(1)}, bf16[32,2048]{1,0:T(8,128)(2,1)S(1)}, u32[]{:S(2)}, u32[]{:S(2)}) collective-permute-start(bf16[32,2048]{1,0:T(8,128)(2,1)S(1)} %bitcast.16), channel_id=1, source_target_pairs={{0,8},{4,12},{8,0},{12,4},{1,9},{5,13},{9,1},{13,5},{2,10},{6,14},... | collective-permute-start | bytes 393224 | tf_op jit(solution)/shard_map/ppermute | solution.py:532
  9.4 3.1 %deal.5 = (bf16[96,2048]{1,0:T(8,128)(2,1)S(1)}, bf16[1,96,2048]{2,1,0:T(8,128)(2,1)S(1)}, bf16[80,2048]{1,0:T(8,128)(2,1)S(1)}, bf16[1,80,2048]{2,1,0:T(8,128)(...) custom-call(s32[4]{0:T(128)S(1)} %copy-done.4, bf16[512,2048]{1,0:T(8,128)(2,1)S(1)} %copy-done.3, ...), custom_call_target="tpu_custom_call" | custom-call | tf_op jit(solution)/shard_map/deal/pallas_call | solution.py:86
  12.5 0.7 collective-permute-done.1.refs_0_
  13.2 1.8 %collective-permute-start.3 = (bf16[96,2048]{1,0:T(8,128)(2,1)S(1)}, bf16[96,2048]{1,0:T(8,128)(2,1)S(1)}, u32[]{:S(2)}, u32[]{:S(2)}) collective-permute-start(bf16[96,2048]{1,0:T(8,128)(2,1)S(1)} %bitcast.13), channel_id=1, source_target_pairs={{0,8},{4,12},{8,0},{12,4},{1,9},{5,13},{9,1},{13,5},{2,10},{6,14},... | collective-permute-start | bytes 1179656 | tf_op jit(solution)/shard_map/ppermute | solution.py:532
  15.0 1.6 %collective-permute-start.4 = (bf16[32,2048]{1,0:T(8,128)(2,1)S(1)}, bf16[32,2048]{1,0:T(8,128)(2,1)S(1)}, u32[]{:S(2)}, u32[]{:S(2)}) collective-permute-start(bf16[32,2048]{1,0:T(8,128)(2,1)S(1)} %get-tuple-element.52.anchor_ref.refs_0_), channel_id=1, source_target_pairs={{0,1},{1,0},{2,3},{3,2},{4,5},{5,4},{6,7},{7,6},{8,9},{9,8},{10,11... | collective-permute-start | bytes 393224 | tf_op jit(solution)/shard_map/ppermute | solution.py:587
  16.6 2.6 %collective-permute-start.2 = (bf16[32,2048]{1,0:T(8,128)(2,1)S(1)}, bf16[32,2048]{1,0:T(8,128)(2,1)S(1)}, u32[]{:S(2)}, u32[]{:S(2)}) collective-permute-start(bf16[32,2048]{1,0:T(8,128)(2,1)S(1)} %get-tuple-element.52.anchor_ref.refs_0_), channel_id=1, source_target_pairs={{0,2},{1,3},{2,0},{3,1},{4,6},{5,7},{6,4},{7,5},{8,10},{9,11},{10,... | collective-permute-start | bytes 393224 | tf_op jit(solution)/shard_map/ppermute | solution.py:587
  19.2 6.1 %load.1 = (bf16[8192,1024]{1,0:T(8,128)(2,1)S(1)}, f32[8,128]{1,0:T(8,128)S(1)}) custom-call(bf16[8192,1024]{1,0:T(8,128)(2,1)} %weight_ref.1, bf16[32,2048]{1,0:T(8,128)(2,1)S(1)} %get-tuple-element.52.anchor_ref.refs_0_), custom_call_target="tpu_custom_call" | custom-call | tf_op jit(solution)/shard_map/load/pallas_call | solution.py:206
  25.2 0.0 collective-permute-done.3.refs_0_
  25.3 0.0 collective-permute-done.4.refs_2_
  25.3 0.5 collective-permute-start.10
  25.8 2.3 %collective-permute-start.8 = (bf16[96,2048]{1,0:T(8,128)(2,1)S(1)}, bf16[96,2048]{1,0:T(8,128)(2,1)S(1)}, u32[]{:S(2)}, u32[]{:S(2)}) collective-permute-start(bf16[96,2048]{1,0:T(8,128)(2,1)S(1)} %get-tuple-element.62.anchor_ref.refs_0_), channel_id=1, source_target_pairs={{0,2},{1,3},{2,0},{3,1},{4,6},{5,7},{6,4},{7,5},{8,10},{9,11},{10,... | collective-permute-start | bytes 1179656 | tf_op jit(solution)/shard_map/ppermute | solution.py:587
  28.2 1.5 %collective-permute-start.9 = (bf16[80,2048]{1,0:T(8,128)(2,1)S(1)}, bf16[80,2048]{1,0:T(8,128)(2,1)S(1)}, u32[]{:S(2)}, u32[]{:S(2)}) collective-permute-start(bf16[80,2048]{1,0:T(8,128)(2,1)S(1)} %bitcast.14), channel_id=1, source_target_pairs={{0,8},{4,12},{8,0},{12,4},{1,9},{5,13},{9,1},{13,5},{2,10},{6,14},... | collective-permute-start | bytes 983048 | tf_op jit(solution)/shard_map/ppermute | solution.py:532
  29.6 0.4 collective-permute-start.5
  30.1 1.1 angles.1
  31.2 4.0 %project.8 = (f32[32,1536]{1,0:T(8,128)S(1)}, f32[32,128]{1,0:T(8,128)S(1)}) custom-call(bf16[32,2048]{1,0:T(8,128)(2,1)S(1)} %get-tuple-element.52.anchor_ref.refs_0_, bf16[32,2048]{1,0:T(8,128)(2,1)S(1)} %get-tuple-element.58.refs_1_, bf16[32,2048]{1,0:T(8,128)(2,1)S(1)} %collective-permute-done.4.refs_2_, f32[1,8192]{1,0:T(1,128)S(1)} %bitcast.5, ...), custom_call_target="tpu_custom_call" | custom-call | tf_op jit(solution)/shard_map/project/pallas_call | solution.py:281
  35.2 10.9 %collective-permute-done.5.refs_0_ = bf16[32,2048]{1,0:T(8,128)(2,1)S(1)} collective-permute-done((bf16[32,2048]{1,0:T(8,128)(2,1)S(1)}, bf16[32,2048]{1,0:T(8,128)(2,1)S(1)}, u32[]{:S(2)}, u32[]{:S(2)}) %collective-permute-start.5) | collective-permute-done | bytes 131104 | tf_op jit(solution)/shard_map/ppermute | solution.py:587
  46.1 1.4 %project.9.refs_3_.refs_1_.refs_0_ = bf16[32,1536]{1,0:T(8,128)(2,1)S(1)} custom-call(bf16[32,2048]{1,0:T(8,128)(2,1)S(1)} %collective-permute-done.5.refs_0_, f32[1,8192]{1,0:T(1,128)S(1)} %bitcast.6, bf16[8192,1024]{1,0:T(8,128)(2,1)S(1)} %get-tuple-element.59.refs_4_.refs_2_, bf16[8192,256]{1,0:T(8,128)(2,1)S(1)} %copy-done, ...), custom_call_target="tpu_custom_call" | custom-call | tf_op jit(solution)/shard_map/project/pallas_call | solution.py:281
  47.6 0.0 collective-permute-done.8.refs_0_
  47.7 0.6 collective-permute-start.11
  48.2 2.2 %collective-permute-start.15 = (bf16[80,2048]{1,0:T(8,128)(2,1)S(1)}, bf16[80,2048]{1,0:T(8,128)(2,1)S(1)}, u32[]{:S(2)}, u32[]{:S(2)}) collective-permute-start(bf16[80,2048]{1,0:T(8,128)(2,1)S(1)} %get-tuple-element.74.refs_0_), channel_id=1, source_target_pairs={{0,2},{1,3},{2,0},{3,1},{4,6},{5,7},{6,4},{7,5},{8,10},{9,11},{10,... | collective-permute-start | bytes 983048 | tf_op jit(solution)/shard_map/ppermute | solution.py:587
  50.4 0.5 collective-permute-start.17
  50.9 1.5 %collective-permute-start.16 = (bf16[48,2048]{1,0:T(8,128)(2,1)S(1)}, bf16[48,2048]{1,0:T(8,128)(2,1)S(1)}, u32[]{:S(2)}, u32[]{:S(2)}) collective-permute-start(bf16[48,2048]{1,0:T(8,128)(2,1)S(1)} %bitcast.15), channel_id=1, source_target_pairs={{0,8},{4,12},{8,0},{12,4},{1,9},{5,13},{9,1},{13,5},{2,10},{6,14},... | collective-permute-start | bytes 589832 | tf_op jit(solution)/shard_map/ppermute | solution.py:532
  52.4 0.5 collective-permute-start.7
  52.9 4.0 %project.10 = (f32[96,1536]{1,0:T(8,128)S(1)}, f32[96,128]{1,0:T(8,128)S(1)}) custom-call(bf16[96,2048]{1,0:T(8,128)(2,1)S(1)} %get-tuple-element.62.anchor_ref.refs_0_, bf16[96,2048]{1,0:T(8,128)(2,1)S(1)} %get-tuple-element.69.refs_1_, bf16[96,2048]{1,0:T(8,128)(2,1)S(1)} %collective-permute-done.10.refs_2_, f32[1,8192]{1,0:T(1,128)S(1)} %bitcast.7, ...), custom_call_target="tpu_custom_call" | custom-call | tf_op jit(solution)/shard_map/project/pallas_call | solution.py:281
  57.0 8.8 %collective-permute-done.11.refs_0_ = bf16[96,2048]{1,0:T(8,128)(2,1)S(1)} collective-permute-done((bf16[96,2048]{1,0:T(8,128)(2,1)S(1)}, bf16[96,2048]{1,0:T(8,128)(2,1)S(1)}, u32[]{:S(2)}, u32[]{:S(2)}) %collective-permute-start.11) | collective-permute-done | bytes 393248 | tf_op jit(solution)/shard_map/ppermute | solution.py:587
  65.8 1.6 %project.11.refs_1_.refs_3_.refs_4_ = bf16[96,1536]{1,0:T(8,128)(2,1)S(1)} custom-call(bf16[96,2048]{1,0:T(8,128)(2,1)S(1)} %collective-permute-done.11.refs_0_, f32[1,8192]{1,0:T(1,128)S(1)} %bitcast.8, bf16[8192,1024]{1,0:T(8,128)(2,1)S(1)} %get-tuple-element.59.refs_4_.refs_2_, bf16[8192,256]{1,0:T(8,128)(2,1)S(1)} %copy-done, ...), custom_call_target="tpu_custom_call" | custom-call | tf_op jit(solution)/shard_map/project/pallas_call | solution.py:281
  67.4 0.0 collective-permute-done.15.refs_0_
  67.5 4.2 %collective-permute-done.17.refs_2_ = bf16[80,2048]{1,0:T(8,128)(2,1)S(1)} collective-permute-done((bf16[80,2048]{1,0:T(8,128)(2,1)S(1)}, bf16[80,2048]{1,0:T(8,128)(2,1)S(1)}, u32[]{:S(2)}, u32[]{:S(2)}) %collective-permute-start.17) | collective-permute-done | bytes 327712 | tf_op jit(solution)/shard_map/ppermute | solution.py:587
  71.7 0.3 collective-permute-start.18
  72.0 0.0 collective-permute-start.14
  72.0 3.9 %collective-permute-start.22 = (bf16[48,2048]{1,0:T(8,128)(2,1)S(1)}, bf16[48,2048]{1,0:T(8,128)(2,1)S(1)}, u32[]{:S(2)}, u32[]{:S(2)}) collective-permute-start(bf16[48,2048]{1,0:T(8,128)(2,1)S(1)} %get-tuple-element.82.refs_0_), channel_id=1, source_target_pairs={{0,2},{1,3},{2,0},{3,1},{4,6},{5,7},{6,4},{7,5},{8,10},{9,11},{10,... | collective-permute-start | bytes 589832 | tf_op jit(solution)/shard_map/ppermute | solution.py:587
  75.8 0.3 collective-permute-start.23
  76.1 4.2 %project.12 = (f32[80,1536]{1,0:T(8,128)S(1)}, f32[80,128]{1,0:T(8,128)S(1)}) custom-call(bf16[80,2048]{1,0:T(8,128)(2,1)S(1)} %get-tuple-element.74.refs_0_, bf16[80,2048]{1,0:T(8,128)(2,1)S(1)} %get-tuple-element.77.refs_1_, bf16[80,2048]{1,0:T(8,128)(2,1)S(1)} %collective-permute-done.17.refs_2_, f32[1,8192]{1,0:T(1,128)S(1)} %bitcast.9, ...), custom_call_target="tpu_custom_call" | custom-call | tf_op jit(solution)/shard_map/project/pallas_call | solution.py:281
  80.3 6.2 %collective-permute-done.18.refs_0_ = bf16[80,2048]{1,0:T(8,128)(2,1)S(1)} collective-permute-done((bf16[80,2048]{1,0:T(8,128)(2,1)S(1)}, bf16[80,2048]{1,0:T(8,128)(2,1)S(1)}, u32[]{:S(2)}, u32[]{:S(2)}) %collective-permute-start.18) | collective-permute-done | bytes 327712 | tf_op jit(solution)/shard_map/ppermute | solution.py:587
  86.5 1.7 %project.13.refs_1_.refs_8_ = bf16[80,1536]{1,0:T(8,128)(2,1)S(1)} custom-call(bf16[80,2048]{1,0:T(8,128)(2,1)S(1)} %collective-permute-done.18.refs_0_, f32[1,8192]{1,0:T(1,128)S(1)} %bitcast.10, bf16[8192,1024]{1,0:T(8,128)(2,1)S(1)} %get-tuple-element.59.refs_4_.refs_2_, bf16[8192,256]{1,0:T(8,128)(2,1)S(1)} %copy-done, bf16[8192,256]{1,0:T(8,128)(2,1)S(1)} %copy-done.1, ...), custom_call_target="tpu_custom_call" | custom-call | tf_op jit(solution)/shard_map/project/pallas_call | solution.py:281
  88.2 0.1 collective-permute-start.21
  88.2 0.0 collective-permute-done.22.refs_0_
  88.2 0.4 collective-permute-done.23.refs_1_.refs_2_
  88.7 0.3 collective-permute-start.24
  89.0 0.0 collective-permute-start.6
  89.0 0.5 collective-permute-start.12
  89.5 0.0 collective-permute-start.13
  89.5 0.8 collective-permute-done.6.refs_2_.refs_1_
  90.3 0.2 collective-permute-start.19
  90.4 4.0 %project.14 = (f32[48,1536]{1,0:T(8,128)S(1)}, f32[48,128]{1,0:T(8,128)S(1)}) custom-call(bf16[48,2048]{1,0:T(8,128)(2,1)S(1)} %get-tuple-element.82.refs_0_, bf16[48,2048]{1,0:T(8,128)(2,1)S(1)} %after.14.refs_1_, bf16[48,2048]{1,0:T(8,128)(2,1)S(1)} %collective-permute-done.23.refs_1_.refs_2_, f32[1,8192]{1,0:T(1,128)S(1)} %bitcast.11, ...), custom_call_target="tpu_custom_call" | custom-call | tf_op jit(solution)/shard_map/project/pallas_call | solution.py:281
  94.5 0.4 collective-permute-start.20
  94.9 0.0 collective-permute-done.24.refs_0_
  94.9 1.7 %project.15.refs_1_.refs_12_ = bf16[48,1536]{1,0:T(8,128)(2,1)S(1)} custom-call(bf16[48,2048]{1,0:T(8,128)(2,1)S(1)} %collective-permute-done.24.refs_0_, f32[1,8192]{1,0:T(1,128)S(1)} %bitcast.12, bf16[8192,1024]{1,0:T(8,128)(2,1)S(1)} %get-tuple-element.59.refs_4_.refs_2_, bf16[8192,256]{1,0:T(8,128)(2,1)S(1)} %copy-done, bf16[8192,256]{1,0:T(8,128)(2,1)S(1)} %copy-done.1, ...), custom_call_target="tpu_custom_call" | custom-call | tf_op jit(solution)/shard_map/project/pallas_call | solution.py:281
  96.6 0.0 collective-permute-done.21.refs_0_
  96.6 0.2 collective-permute-start.25
  96.8 1.4 %collective-permute-start.27 = (bf16[48,1536]{1,0:T(8,128)(2,1)S(1)}, bf16[48,1536]{1,0:T(8,128)(2,1)S(1)}, u32[]{:S(2)}, u32[]{:S(2)}) collective-permute-start(bf16[48,1536]{1,0:T(8,128)(2,1)S(1)} %project.15.refs_1_.refs_12_), channel_id=1, source_target_pairs={{0,8},{4,12},{8,0},{12,4},{1,9},{5,13},{9,1},{13,5},{2,10},{6,14},... | collective-permute-start | bytes 442376 | tf_op jit(solution)/shard_map/ppermute | solution.py:532
  98.3 0.0 collective-permute-done.13.refs_5_
  98.3 0.1 collective-permute-start.26
  98.4 0.0 collective-permute-done.20.refs_9_
  98.4 4.7 %attend.2 = (bf16[512,1024]{1,0:T(8,128)(2,1)}, bf16[2,512,256]{2,1,0:T(8,128)(2,1)}, f32[8,128]{1,0:T(8,128)S(1)}) custom-call(s32[4]{0:T(128)S(1)} %copy-done.5, s32[16]{0:T(128)S(1)} %copy-done.6, bf16[32,1536]{1,0:T(8,128)(2,1)S(1)} %project.9.refs_3_.refs_1_.refs_0_, bf16[32,1536]{1,0:T(8,128)(2,1)S(1)} %collective-permute-done.6.refs_2_.refs_1_, ...), custom_call_target="tpu_custom_call" | custom-call | tf_op jit(solution)/shard_map/attend/pallas_call | solution.py:503
  103.1 1.6 %collective-permute-start.28 = (bf16[48,1536]{1,0:T(8,128)(2,1)S(1)}, bf16[48,1536]{1,0:T(8,128)(2,1)S(1)}, u32[]{:S(2)}, u32[]{:S(2)}) collective-permute-start(bf16[48,1536]{1,0:T(8,128)(2,1)S(1)} %after.17.refs_14_), channel_id=1, source_target_pairs={{0,4},{4,0},{8,12},{12,8},{1,5},{5,1},{9,13},{13,9},{2,6},{6,2},{1... | collective-permute-start | bytes 442376 | tf_op jit(solution)/shard_map/ppermute | solution.py:536
  104.7 1.0 collective-permute-done.28.refs_15_
  105.7 5.0 %attend.3 = (bf16[512,1024]{1,0:T(8,128)(2,1)}, bf16[2,512,256]{2,1,0:T(8,128)(2,1)}, f32[8,128]{1,0:T(8,128)}) custom-call(s32[4]{0:T(128)S(1)} %copy-done.5, s32[16]{0:T(128)S(1)} %copy-done.6, bf16[32,1536]{1,0:T(8,128)(2,1)S(1)} %project.9.refs_3_.refs_1_.refs_0_, ...), custom_call_target="tpu_custom_call", output_to_operand_aliasing={{0}: (18, {}), {1}: (19, {})} | custom-call | tf_op jit(solution)/shard_map/attend/pallas_call | solution.py:503
  (41 shorter events, 0.2 us)
Async XLA Ops:
  0.6 4.5 %collective-permute-start = (bf16[512,2048]{1,0:T(8,128)(2,1)}, bf16[512,2048]{1,0:T(8,128)(2,1)S(1)}, u32[]{:S(2)}, u32[]{:S(2)}) collective-permute-start(bf16[512,2048]{1,0:T(8,128)(2,1)} %refs_0_.3), channel_id=1, source_target_pairs={{0,4},{4,0},{8,12},{12,8},{1,5},{5,1},{9,13},{13,9},{2,6},{6,2},{1... | collective-permute-start | bytes 6291464 | tf_op jit(solution)/shard_map/ppermute | solution.py:536
  1.1 1.6 %copy-start.2 = (bf16[512,2048]{1,0:T(8,128)(2,1)S(1)}, bf16[512,2048]{1,0:T(8,128)(2,1)}, u32[]{:S(2)}) copy-start(bf16[512,2048]{1,0:T(8,128)(2,1)} %refs_0_.3) | copy-start | bytes 6291460
  2.7 0.7 copy-start.4
  3.4 6.0 %copy-start.3 = (bf16[512,2048]{1,0:T(8,128)(2,1)S(1)}, bf16[512,2048]{1,0:T(8,128)(2,1)}, u32[]{:S(2)}) copy-start(bf16[512,2048]{1,0:T(8,128)(2,1)} %refs_0_.3) | copy-start | bytes 6291460
  6.4 6.7 %collective-permute-start.1 = (bf16[32,2048]{1,0:T(8,128)(2,1)S(1)}, bf16[32,2048]{1,0:T(8,128)(2,1)S(1)}, u32[]{:S(2)}, u32[]{:S(2)}) collective-permute-start(bf16[32,2048]{1,0:T(8,128)(2,1)S(1)} %bitcast.16), channel_id=1, source_target_pairs={{0,8},{4,12},{8,0},{12,4},{1,9},{5,13},{9,1},{13,5},{2,10},{6,14},... | collective-permute-start | bytes 393224 | tf_op jit(solution)/shard_map/ppermute | solution.py:532
  13.2 12.1 %collective-permute-start.3 = (bf16[96,2048]{1,0:T(8,128)(2,1)S(1)}, bf16[96,2048]{1,0:T(8,128)(2,1)S(1)}, u32[]{:S(2)}, u32[]{:S(2)}) collective-permute-start(bf16[96,2048]{1,0:T(8,128)(2,1)S(1)} %bitcast.13), channel_id=1, source_target_pairs={{0,8},{4,12},{8,0},{12,4},{1,9},{5,13},{9,1},{13,5},{2,10},{6,14},... | collective-permute-start | bytes 1179656 | tf_op jit(solution)/shard_map/ppermute | solution.py:532
  15.0 15.1 %copy-start.8 = (bf16[8192]{0:T(1024)(128)(2,1)S(1)}, bf16[8192]{0:T(1024)(128)(2,1)}, u32[]{:S(2)}) copy-start(bf16[8192]{0:T(1024)(128)(2,1)} %param.9) | copy-start | bytes 49156
  15.0 15.1 %copy-start.5 = (s32[4]{0:T(128)S(1)}, s32[4]{0:T(128)}, u32[]{:S(2)}) copy-start(s32[4]{0:T(128)} %lengths_ref.11) | copy-start | bytes 52
  15.0 15.1 %copy-start.7 = (f32[1,128]{1,0:T(1,128)S(1)}, f32[1,128]{1,0:T(1,128)}, u32[]{:S(2)}) copy-start(f32[1,128]{1,0:T(1,128)} %constant.2.clone.frequency_ref) | copy-start | bytes 1540
  15.0 10.3 %collective-permute-start.4 = (bf16[32,2048]{1,0:T(8,128)(2,1)S(1)}, bf16[32,2048]{1,0:T(8,128)(2,1)S(1)}, u32[]{:S(2)}, u32[]{:S(2)}) collective-permute-start(bf16[32,2048]{1,0:T(8,128)(2,1)S(1)} %get-tuple-element.52.anchor_ref.refs_0_), channel_id=1, source_target_pairs={{0,1},{1,0},{2,3},{3,2},{4,5},{5,4},{6,7},{7,6},{8,9},{9,8},{10,11... | collective-permute-start | bytes 393224 | tf_op jit(solution)/shard_map/ppermute | solution.py:587
  16.6 8.7 %collective-permute-start.2 = (bf16[32,2048]{1,0:T(8,128)(2,1)S(1)}, bf16[32,2048]{1,0:T(8,128)(2,1)S(1)}, u32[]{:S(2)}, u32[]{:S(2)}) collective-permute-start(bf16[32,2048]{1,0:T(8,128)(2,1)S(1)} %get-tuple-element.52.anchor_ref.refs_0_), channel_id=1, source_target_pairs={{0,2},{1,3},{2,0},{3,1},{4,6},{5,7},{6,4},{7,5},{8,10},{9,11},{10,... | collective-permute-start | bytes 393224 | tf_op jit(solution)/shard_map/ppermute | solution.py:587
  19.2 12.0 %copy-start = (bf16[8192,256]{1,0:T(8,128)(2,1)S(1)}, bf16[8192,256]{1,0:T(8,128)(2,1)}, u32[]{:S(2)}) copy-start(bf16[8192,256]{1,0:T(8,128)(2,1)} %refs_3_.7) | copy-start | bytes 12582916
  19.2 12.0 %copy-start.1 = (bf16[8192,256]{1,0:T(8,128)(2,1)S(1)}, bf16[8192,256]{1,0:T(8,128)(2,1)}, u32[]{:S(2)}) copy-start(bf16[8192,256]{1,0:T(8,128)(2,1)} %refs_4_.7) | copy-start | bytes 12582916
  25.3 22.3 %collective-permute-start.10 = (bf16[96,2048]{1,0:T(8,128)(2,1)S(1)}, bf16[96,2048]{1,0:T(8,128)(2,1)S(1)}, u32[]{:S(2)}, u32[]{:S(2)}) collective-permute-start(bf16[96,2048]{1,0:T(8,128)(2,1)S(1)} %get-tuple-element.62.anchor_ref.refs_0_), channel_id=1, source_target_pairs={{0,1},{1,0},{2,3},{3,2},{4,5},{5,4},{6,7},{7,6},{8,9},{9,8},{10,11... | collective-permute-start | bytes 1179656 | tf_op jit(solution)/shard_map/ppermute | solution.py:587
  25.8 21.8 %collective-permute-start.8 = (bf16[96,2048]{1,0:T(8,128)(2,1)S(1)}, bf16[96,2048]{1,0:T(8,128)(2,1)S(1)}, u32[]{:S(2)}, u32[]{:S(2)}) collective-permute-start(bf16[96,2048]{1,0:T(8,128)(2,1)S(1)} %get-tuple-element.62.anchor_ref.refs_0_), channel_id=1, source_target_pairs={{0,2},{1,3},{2,0},{3,1},{4,6},{5,7},{6,4},{7,5},{8,10},{9,11},{10,... | collective-permute-start | bytes 1179656 | tf_op jit(solution)/shard_map/ppermute | solution.py:587
  28.2 19.4 %collective-permute-start.9 = (bf16[80,2048]{1,0:T(8,128)(2,1)S(1)}, bf16[80,2048]{1,0:T(8,128)(2,1)S(1)}, u32[]{:S(2)}, u32[]{:S(2)}) collective-permute-start(bf16[80,2048]{1,0:T(8,128)(2,1)S(1)} %bitcast.14), channel_id=1, source_target_pairs={{0,8},{4,12},{8,0},{12,4},{1,9},{5,13},{9,1},{13,5},{2,10},{6,14},... | collective-permute-start | bytes 983048 | tf_op jit(solution)/shard_map/ppermute | solution.py:532
  29.6 16.5 %collective-permute-start.5 = (bf16[32,2048]{1,0:T(8,128)(2,1)S(1)}, bf16[32,2048]{1,0:T(8,128)(2,1)S(1)}, u32[]{:S(2)}, u32[]{:S(2)}) collective-permute-start(bf16[32,2048]{1,0:T(8,128)(2,1)S(1)} %get-tuple-element.58.refs_1_), channel_id=1, source_target_pairs={{0,1},{1,0},{2,3},{3,2},{4,5},{5,4},{6,7},{7,6},{8,9},{9,8},{10,11... | collective-permute-start | bytes 393224 | tf_op jit(solution)/shard_map/ppermute | solution.py:587
  47.7 18.1 %collective-permute-start.11 = (bf16[96,2048]{1,0:T(8,128)(2,1)S(1)}, bf16[96,2048]{1,0:T(8,128)(2,1)S(1)}, u32[]{:S(2)}, u32[]{:S(2)}) collective-permute-start(bf16[96,2048]{1,0:T(8,128)(2,1)S(1)} %get-tuple-element.69.refs_1_), channel_id=1, source_target_pairs={{0,1},{1,0},{2,3},{3,2},{4,5},{5,4},{6,7},{7,6},{8,9},{9,8},{10,11... | collective-permute-start | bytes 1179656 | tf_op jit(solution)/shard_map/ppermute | solution.py:587
  48.2 19.2 %collective-permute-start.15 = (bf16[80,2048]{1,0:T(8,128)(2,1)S(1)}, bf16[80,2048]{1,0:T(8,128)(2,1)S(1)}, u32[]{:S(2)}, u32[]{:S(2)}) collective-permute-start(bf16[80,2048]{1,0:T(8,128)(2,1)S(1)} %get-tuple-element.74.refs_0_), channel_id=1, source_target_pairs={{0,2},{1,3},{2,0},{3,1},{4,6},{5,7},{6,4},{7,5},{8,10},{9,11},{10,... | collective-permute-start | bytes 983048 | tf_op jit(solution)/shard_map/ppermute | solution.py:587
  50.4 21.3 %collective-permute-start.17 = (bf16[80,2048]{1,0:T(8,128)(2,1)S(1)}, bf16[80,2048]{1,0:T(8,128)(2,1)S(1)}, u32[]{:S(2)}, u32[]{:S(2)}) collective-permute-start(bf16[80,2048]{1,0:T(8,128)(2,1)S(1)} %get-tuple-element.74.refs_0_), channel_id=1, source_target_pairs={{0,1},{1,0},{2,3},{3,2},{4,5},{5,4},{6,7},{7,6},{8,9},{9,8},{10,11... | collective-permute-start | bytes 983048 | tf_op jit(solution)/shard_map/ppermute | solution.py:587
  50.9 6.0 %collective-permute-start.16 = (bf16[48,2048]{1,0:T(8,128)(2,1)S(1)}, bf16[48,2048]{1,0:T(8,128)(2,1)S(1)}, u32[]{:S(2)}, u32[]{:S(2)}) collective-permute-start(bf16[48,2048]{1,0:T(8,128)(2,1)S(1)} %bitcast.15), channel_id=1, source_target_pairs={{0,8},{4,12},{8,0},{12,4},{1,9},{5,13},{9,1},{13,5},{2,10},{6,14},... | collective-permute-start | bytes 589832 | tf_op jit(solution)/shard_map/ppermute | solution.py:532
  52.4 15.1 %collective-permute-start.7 = (bf16[32,1536]{1,0:T(8,128)(2,1)S(1)}, bf16[32,1536]{1,0:T(8,128)(2,1)S(1)}, u32[]{:S(2)}, u32[]{:S(2)}) collective-permute-start(bf16[32,1536]{1,0:T(8,128)(2,1)S(1)} %project.9.refs_3_.refs_1_.refs_0_), channel_id=1, source_target_pairs={{0,8},{4,12},{8,0},{12,4},{1,9},{5,13},{9,1},{13,5},{2,10},{6,14},... | collective-permute-start | bytes 294920 | tf_op jit(solution)/shard_map/ppermute | solution.py:532
  71.7 14.8 %collective-permute-start.18 = (bf16[80,2048]{1,0:T(8,128)(2,1)S(1)}, bf16[80,2048]{1,0:T(8,128)(2,1)S(1)}, u32[]{:S(2)}, u32[]{:S(2)}) collective-permute-start(bf16[80,2048]{1,0:T(8,128)(2,1)S(1)} %get-tuple-element.77.refs_1_), channel_id=1, source_target_pairs={{0,1},{1,0},{2,3},{3,2},{4,5},{5,4},{6,7},{7,6},{8,9},{9,8},{10,11... | collective-permute-start | bytes 983048 | tf_op jit(solution)/shard_map/ppermute | solution.py:587
  72.0 16.7 %collective-permute-start.14 = (bf16[96,1536]{1,0:T(8,128)(2,1)S(1)}, bf16[96,1536]{1,0:T(8,128)(2,1)S(1)}, u32[]{:S(2)}, u32[]{:S(2)}) collective-permute-start(bf16[96,1536]{1,0:T(8,128)(2,1)S(1)} %project.11.refs_1_.refs_3_.refs_4_), channel_id=1, source_target_pairs={{0,8},{4,12},{8,0},{12,4},{1,9},{5,13},{9,1},{13,5},{2,10},{6,14},... | collective-permute-start | bytes 884744 | tf_op jit(solution)/shard_map/ppermute | solution.py:532
  72.0 16.3 %collective-permute-start.22 = (bf16[48,2048]{1,0:T(8,128)(2,1)S(1)}, bf16[48,2048]{1,0:T(8,128)(2,1)S(1)}, u32[]{:S(2)}, u32[]{:S(2)}) collective-permute-start(bf16[48,2048]{1,0:T(8,128)(2,1)S(1)} %get-tuple-element.82.refs_0_), channel_id=1, source_target_pairs={{0,2},{1,3},{2,0},{3,1},{4,6},{5,7},{6,4},{7,5},{8,10},{9,11},{10,... | collective-permute-start | bytes 589832 | tf_op jit(solution)/shard_map/ppermute | solution.py:587
  75.8 12.9 %collective-permute-start.23 = (bf16[48,2048]{1,0:T(8,128)(2,1)S(1)}, bf16[48,2048]{1,0:T(8,128)(2,1)S(1)}, u32[]{:S(2)}, u32[]{:S(2)}) collective-permute-start(bf16[48,2048]{1,0:T(8,128)(2,1)S(1)} %get-tuple-element.82.refs_0_), channel_id=1, source_target_pairs={{0,1},{1,0},{2,3},{3,2},{4,5},{5,4},{6,7},{7,6},{8,9},{9,8},{10,11... | collective-permute-start | bytes 589832 | tf_op jit(solution)/shard_map/ppermute | solution.py:587
  88.2 8.5 %collective-permute-start.21 = (bf16[80,1536]{1,0:T(8,128)(2,1)S(1)}, bf16[80,1536]{1,0:T(8,128)(2,1)S(1)}, u32[]{:S(2)}, u32[]{:S(2)}) collective-permute-start(bf16[80,1536]{1,0:T(8,128)(2,1)S(1)} %project.13.refs_1_.refs_8_), channel_id=1, source_target_pairs={{0,8},{4,12},{8,0},{12,4},{1,9},{5,13},{9,1},{13,5},{2,10},{6,14},... | collective-permute-start | bytes 737288 | tf_op jit(solution)/shard_map/ppermute | solution.py:532
  88.7 6.2 %collective-permute-start.24 = (bf16[48,2048]{1,0:T(8,128)(2,1)S(1)}, bf16[48,2048]{1,0:T(8,128)(2,1)S(1)}, u32[]{:S(2)}, u32[]{:S(2)}) collective-permute-start(bf16[48,2048]{1,0:T(8,128)(2,1)S(1)} %after.14.refs_1_), channel_id=1, source_target_pairs={{0,1},{1,0},{2,3},{3,2},{4,5},{5,4},{6,7},{7,6},{8,9},{9,8},{10,11... | collective-permute-start | bytes 589832 | tf_op jit(solution)/shard_map/ppermute | solution.py:587
  89.0 1.3 %collective-permute-start.6 = (bf16[32,1536]{1,0:T(8,128)(2,1)S(1)}, bf16[32,1536]{1,0:T(8,128)(2,1)S(1)}, u32[]{:S(2)}, u32[]{:S(2)}) collective-permute-start(bf16[32,1536]{1,0:T(8,128)(2,1)S(1)} %project.9.refs_3_.refs_1_.refs_0_), channel_id=1, source_target_pairs={{0,4},{4,0},{8,12},{12,8},{1,5},{5,1},{9,13},{13,9},{2,6},{6,2},{1... | collective-permute-start | bytes 294920 | tf_op jit(solution)/shard_map/ppermute | solution.py:536
  89.0 5.5 %collective-permute-start.12 = (bf16[32,1536]{1,0:T(8,128)(2,1)S(1)}, bf16[32,1536]{1,0:T(8,128)(2,1)S(1)}, u32[]{:S(2)}, u32[]{:S(2)}) collective-permute-start(bf16[32,1536]{1,0:T(8,128)(2,1)S(1)} %after.11.refs_3_.refs_2_), channel_id=1, source_target_pairs={{0,4},{4,0},{8,12},{12,8},{1,5},{5,1},{9,13},{13,9},{2,6},{6,2},{1... | collective-permute-start | bytes 294920 | tf_op jit(solution)/shard_map/ppermute | solution.py:536
  89.5 8.8 %collective-permute-start.13 = (bf16[96,1536]{1,0:T(8,128)(2,1)S(1)}, bf16[96,1536]{1,0:T(8,128)(2,1)S(1)}, u32[]{:S(2)}, u32[]{:S(2)}) collective-permute-start(bf16[96,1536]{1,0:T(8,128)(2,1)S(1)} %project.11.refs_1_.refs_3_.refs_4_), channel_id=1, source_target_pairs={{0,4},{4,0},{8,12},{12,8},{1,5},{5,1},{9,13},{13,9},{2,6},{6,2},{1... | collective-permute-start | bytes 884744 | tf_op jit(solution)/shard_map/ppermute | solution.py:536
  90.3 8.1 %collective-permute-start.19 = (bf16[96,1536]{1,0:T(8,128)(2,1)S(1)}, bf16[96,1536]{1,0:T(8,128)(2,1)S(1)}, u32[]{:S(2)}, u32[]{:S(2)}) collective-permute-start(bf16[96,1536]{1,0:T(8,128)(2,1)S(1)} %after.13.refs_6_), channel_id=1, source_target_pairs={{0,4},{4,0},{8,12},{12,8},{1,5},{5,1},{9,13},{13,9},{2,6},{6,2},{1... | collective-permute-start | bytes 884744 | tf_op jit(solution)/shard_map/ppermute | solution.py:536
  94.5 3.9 %collective-permute-start.20 = (bf16[80,1536]{1,0:T(8,128)(2,1)S(1)}, bf16[80,1536]{1,0:T(8,128)(2,1)S(1)}, u32[]{:S(2)}, u32[]{:S(2)}) collective-permute-start(bf16[80,1536]{1,0:T(8,128)(2,1)S(1)} %project.13.refs_1_.refs_8_), channel_id=1, source_target_pairs={{0,4},{4,0},{8,12},{12,8},{1,5},{5,1},{9,13},{13,9},{2,6},{6,2},{1... | collective-permute-start | bytes 737288 | tf_op jit(solution)/shard_map/ppermute | solution.py:536
  94.9 3.4 %copy-start.6 = (s32[16]{0:T(128)S(1)}, s32[16]{0:T(128)}, u32[]{:S(2)}) copy-start(s32[16]{0:T(128)} %plan_ref.3) | copy-start | bytes 196
  96.6 1.7 %collective-permute-start.25 = (bf16[80,1536]{1,0:T(8,128)(2,1)S(1)}, bf16[80,1536]{1,0:T(8,128)(2,1)S(1)}, u32[]{:S(2)}, u32[]{:S(2)}) collective-permute-start(bf16[80,1536]{1,0:T(8,128)(2,1)S(1)} %after.16.refs_10_), channel_id=1, source_target_pairs={{0,4},{4,0},{8,12},{12,8},{1,5},{5,1},{9,13},{13,9},{2,6},{6,2},{1... | collective-permute-start | bytes 737288 | tf_op jit(solution)/shard_map/ppermute | solution.py:536
  96.8 6.3 %collective-permute-start.27 = (bf16[48,1536]{1,0:T(8,128)(2,1)S(1)}, bf16[48,1536]{1,0:T(8,128)(2,1)S(1)}, u32[]{:S(2)}, u32[]{:S(2)}) collective-permute-start(bf16[48,1536]{1,0:T(8,128)(2,1)S(1)} %project.15.refs_1_.refs_12_), channel_id=1, source_target_pairs={{0,8},{4,12},{8,0},{12,4},{1,9},{5,13},{9,1},{13,5},{2,10},{6,14},... | collective-permute-start | bytes 442376 | tf_op jit(solution)/shard_map/ppermute | solution.py:532
  98.3 6.4 %collective-permute-start.26 = (bf16[48,1536]{1,0:T(8,128)(2,1)S(1)}, bf16[48,1536]{1,0:T(8,128)(2,1)S(1)}, u32[]{:S(2)}, u32[]{:S(2)}) collective-permute-start(bf16[48,1536]{1,0:T(8,128)(2,1)S(1)} %project.15.refs_1_.refs_12_), channel_id=1, source_target_pairs={{0,4},{4,0},{8,12},{12,8},{1,5},{5,1},{9,13},{13,9},{2,6},{6,2},{1... | collective-permute-start | bytes 442376 | tf_op jit(solution)/shard_map/ppermute | solution.py:536
  103.1 2.6 %collective-permute-start.28 = (bf16[48,1536]{1,0:T(8,128)(2,1)S(1)}, bf16[48,1536]{1,0:T(8,128)(2,1)S(1)}, u32[]{:S(2)}, u32[]{:S(2)}) collective-permute-start(bf16[48,1536]{1,0:T(8,128)(2,1)S(1)} %after.17.refs_14_), channel_id=1, source_target_pairs={{0,4},{4,0},{8,12},{12,8},{1,5},{5,1},{9,13},{13,9},{2,6},{6,2},{1... | collective-permute-start | bytes 442376 | tf_op jit(solution)/shard_map/ppermute | solution.py:536

commit v6 on v5

--- a/solution.py
+++ b/solution.py
@@ -13,7 +13,7 @@
 SPAN = 128
 ALIGN = 16
 TILE = 2 * SPAN
-SHARES = (2, 6, 5, 3)
+SHARES = (3, 5, 5, 3)
 DEPTH = 1024
 MEBI = 1024 * 1024
 F32, BF16 = jnp.float32, jnp.bfloat16

time: 111 us -> 110 us (level)
  waiting for transfers between devices: 33.6 us -> 31.8 us
  starting transfers between devices: 28.6 us -> 30.3 us
    ppermute x12, waiting for transfers between devices: 30.7 us -> 24.3 us  [start(): line[index + 1] = lax.ppermute(line[source], 'tp', pairs)]
    ppermute x8, waiting for transfers between devices: 0.71 us -> 5.15 us  [shift_chips(): return lax.ppermute(value, 'req', pairs)]
    ppermute x8, starting transfers between devices: 9.75 us -> 11.4 us  [shift_chips(): return lax.ppermute(value, 'req', pairs)]
    pallas_call x2, Pallas kernels: 9.72 us -> 8.49 us  [attend(): pl.pallas_call(functools.partial(attend_kernel, chips, groups, known, pri...]
  transfers between devices with their start and end apart: 29 -> 29, of which waited for: 9 -> 12; matrix products, arithmetic and copies ran while one was open for 0% -> 0% of each run, Pallas kernels for 35% -> 34%
where the time goes in v6:
time: 110 us
  Pallas kernels  44.5 us (40%)
  waiting for transfers between devices  31.8 us (29%)
  starting transfers between devices  30.3 us (28%)
  local copies, waits for them, and re-layouts  2.27 us (2%)
  between operations  1.1 us (1%)
    ppermute x12, waiting for transfers between devices, start(): line[index + 1] = lax.ppermute(line[source], 'tp', pairs)  24.3 us
    pallas_call x8, Pallas kernels, project(): pl.pallas_call(functools.partial(project_kernel, masks, bool(carried), fi...  23.2 us
    ppermute x12, starting transfers between devices, start(): line[index + 1] = lax.ppermute(line[source], 'tp', pairs)  15.8 us
    ppermute x8, starting transfers between devices, shift_chips(): return lax.ppermute(value, 'req', pairs)  11.4 us
    pallas_call x2, Pallas kernels, attend(): pl.pallas_call(functools.partial(attend_kernel, chips, groups, known, pri...  8.49 us
    pallas_call x1, Pallas kernels, load(): pl.pallas_call(kernel, in_specs=[anywhere, anywhere], out_specs=[vmem, vm...  6.06 us
    pallas_call x3, Pallas kernels, deal(): pl.pallas_call(functools.partial(deal_kernel, chips, bases, sizes, twins)...  5.53 us
    ppermute x8, waiting for transfers between devices, shift_chips(): return lax.ppermute(value, 'req', pairs)  5.15 us
  transfers between devices with their start and end apart: 29, of which 12 were waited for; matrix products, arithmetic and copies ran while one was open for 0% of the time, Pallas kernels for 34%

profile of v6, /device:TPU:0, one launch (start us, length us, event | category | flops | bytes accessed | tf_op | source)
XLA Modules:
  0.0 110.0 jit_solution(8207039707142355338)
XLA Ops:
  0.6 0.5 collective-permute-start
  1.1 1.6 %copy-done.2 = bf16[512,2048]{1,0:T(8,128)(2,1)S(1)} copy-done((bf16[512,2048]{1,0:T(8,128)(2,1)S(1)}, bf16[512,2048]{1,0:T(8,128)(2,1)}, u32[]{:S(2)}) %copy-start.2) | copy-done | bytes 2097176
  2.7 0.7 copy-done.4
  3.4 1.3 %deal.3 = (bf16[48,2048]{1,0:T(8,128)(2,1)S(1)}, bf16[1,48,2048]{2,1,0:T(8,128)(2,1)S(1)}) custom-call(s32[4]{0:T(128)S(1)} %copy-done.4, bf16[512,2048]{1,0:T(8,128)(2,1)S(1)} %copy-done.2), custom_call_target="tpu_custom_call" | custom-call | tf_op jit(solution)/shard_map/deal/pallas_call | solution.py:86
  4.7 0.4 collective-permute-done.refs_0_.refs_1_
  5.1 1.3 %deal.4 = (bf16[48,2048]{1,0:T(8,128)(2,1)S(1)}, bf16[1,48,2048]{2,1,0:T(8,128)(2,1)S(1)}) custom-call(s32[4]{0:T(128)S(1)} %copy-done.4, bf16[512,2048]{1,0:T(8,128)(2,1)S(1)} %collective-permute-done.refs_0_.refs_1_, bf16[48,2048]{1,0:T(8,128)(2,1)S(1)} %get-tuple-element.47.refs_1_, bf16[1,48,2048]{2,1,0:T(8,128)(2,1)S(1)} %get-tuple-element.48.refs_2_), custom_call_target="tpu_custom_call" | custom-call | tf_op jit(solution)/shard_map/deal/pallas_call | solution.py:86
  6.5 2.9 %collective-permute-start.1 = (bf16[48,2048]{1,0:T(8,128)(2,1)S(1)}, bf16[48,2048]{1,0:T(8,128)(2,1)S(1)}, u32[]{:S(2)}, u32[]{:S(2)}) collective-permute-start(bf16[48,2048]{1,0:T(8,128)(2,1)S(1)} %bitcast.16), channel_id=1, source_target_pairs={{0,8},{4,12},{8,0},{12,4},{1,9},{5,13},{9,1},{13,5},{2,10},{6,14},... | collective-permute-start | bytes 589832 | tf_op jit(solution)/shard_map/ppermute | solution.py:532
  9.4 2.9 %deal.5 = (bf16[80,2048]{1,0:T(8,128)(2,1)S(1)}, bf16[1,80,2048]{2,1,0:T(8,128)(2,1)S(1)}, bf16[80,2048]{1,0:T(8,128)(2,1)S(1)}, bf16[1,80,2048]{2,1,0:T(8,128)(...) custom-call(s32[4]{0:T(128)S(1)} %copy-done.4, bf16[512,2048]{1,0:T(8,128)(2,1)S(1)} %copy-done.3, ...), custom_call_target="tpu_custom_call" | custom-call | tf_op jit(solution)/shard_map/deal/pallas_call | solution.py:86
  12.3 2.3 %collective-permute-done.1.refs_0_ = bf16[48,2048]{1,0:T(8,128)(2,1)S(1)} collective-permute-done((bf16[48,2048]{1,0:T(8,128)(2,1)S(1)}, bf16[48,2048]{1,0:T(8,128)(2,1)S(1)}, u32[]{:S(2)}, u32[]{:S(2)}) %collective-permute-start.1) | collective-permute-done | bytes 196640 | tf_op jit(solution)/shard_map/ppermute | solution.py:532
  14.6 1.8 %collective-permute-start.3 = (bf16[80,2048]{1,0:T(8,128)(2,1)S(1)}, bf16[80,2048]{1,0:T(8,128)(2,1)S(1)}, u32[]{:S(2)}, u32[]{:S(2)}) collective-permute-start(bf16[80,2048]{1,0:T(8,128)(2,1)S(1)} %bitcast.13), channel_id=1, source_target_pairs={{0,8},{4,12},{8,0},{12,4},{1,9},{5,13},{9,1},{13,5},{2,10},{6,14},... | collective-permute-start | bytes 983048 | tf_op jit(solution)/shard_map/ppermute | solution.py:532
  16.4 1.6 %collective-permute-start.4 = (bf16[48,2048]{1,0:T(8,128)(2,1)S(1)}, bf16[48,2048]{1,0:T(8,128)(2,1)S(1)}, u32[]{:S(2)}, u32[]{:S(2)}) collective-permute-start(bf16[48,2048]{1,0:T(8,128)(2,1)S(1)} %get-tuple-element.52.anchor_ref.refs_0_), channel_id=1, source_target_pairs={{0,1},{1,0},{2,3},{3,2},{4,5},{5,4},{6,7},{7,6},{8,9},{9,8},{10,11... | collective-permute-start | bytes 589832 | tf_op jit(solution)/shard_map/ppermute | solution.py:587
  18.0 2.6 %collective-permute-start.2 = (bf16[48,2048]{1,0:T(8,128)(2,1)S(1)}, bf16[48,2048]{1,0:T(8,128)(2,1)S(1)}, u32[]{:S(2)}, u32[]{:S(2)}) collective-permute-start(bf16[48,2048]{1,0:T(8,128)(2,1)S(1)} %get-tuple-element.52.anchor_ref.refs_0_), channel_id=1, source_target_pairs={{0,2},{1,3},{2,0},{3,1},{4,6},{5,7},{6,4},{7,5},{8,10},{9,11},{10,... | collective-permute-start | bytes 589832 | tf_op jit(solution)/shard_map/ppermute | solution.py:587
  20.6 6.1 %load.1 = (bf16[8192,1024]{1,0:T(8,128)(2,1)S(1)}, f32[8,128]{1,0:T(8,128)S(1)}) custom-call(bf16[8192,1024]{1,0:T(8,128)(2,1)} %weight_ref.1, bf16[48,2048]{1,0:T(8,128)(2,1)S(1)} %get-tuple-element.52.anchor_ref.refs_0_), custom_call_target="tpu_custom_call" | custom-call | tf_op jit(solution)/shard_map/load/pallas_call | solution.py:206
  26.7 0.0 collective-permute-done.3.refs_0_
  26.7 0.6 collective-permute-start.9
  27.3 1.5 %collective-permute-done.2.refs_0_ = bf16[48,2048]{1,0:T(8,128)(2,1)S(1)} collective-permute-done((bf16[48,2048]{1,0:T(8,128)(2,1)S(1)}, bf16[48,2048]{1,0:T(8,128)(2,1)S(1)}, u32[]{:S(2)}, u32[]{:S(2)}) %collective-permute-start.2) | collective-permute-done | bytes 196640 | tf_op jit(solution)/shard_map/ppermute | solution.py:587
  28.8 0.3 collective-permute-start.10
  29.2 2.7 %collective-permute-start.8 = (bf16[80,2048]{1,0:T(8,128)(2,1)S(1)}, bf16[80,2048]{1,0:T(8,128)(2,1)S(1)}, u32[]{:S(2)}, u32[]{:S(2)}) collective-permute-start(bf16[80,2048]{1,0:T(8,128)(2,1)S(1)} %get-tuple-element.62.anchor_ref.refs_0_), channel_id=1, source_target_pairs={{0,2},{1,3},{2,0},{3,1},{4,6},{5,7},{6,4},{7,5},{8,10},{9,11},{10,... | collective-permute-start | bytes 983048 | tf_op jit(solution)/shard_map/ppermute | solution.py:587
  31.9 0.0 collective-permute-start.5
  31.9 1.1 angles.1
  33.0 4.0 %project.8 = (f32[48,1536]{1,0:T(8,128)S(1)}, f32[48,128]{1,0:T(8,128)S(1)}) custom-call(bf16[48,2048]{1,0:T(8,128)(2,1)S(1)} %get-tuple-element.52.anchor_ref.refs_0_, bf16[48,2048]{1,0:T(8,128)(2,1)S(1)} %get-tuple-element.58.refs_1_, bf16[48,2048]{1,0:T(8,128)(2,1)S(1)} %collective-permute-done.4.refs_2_, f32[1,8192]{1,0:T(1,128)S(1)} %bitcast.5, ...), custom_call_target="tpu_custom_call" | custom-call | tf_op jit(solution)/shard_map/project/pallas_call | solution.py:281
  37.0 9.4 %collective-permute-done.5.refs_0_ = bf16[48,2048]{1,0:T(8,128)(2,1)S(1)} collective-permute-done((bf16[48,2048]{1,0:T(8,128)(2,1)S(1)}, bf16[48,2048]{1,0:T(8,128)(2,1)S(1)}, u32[]{:S(2)}, u32[]{:S(2)}) %collective-permute-start.5) | collective-permute-done | bytes 196640 | tf_op jit(solution)/shard_map/ppermute | solution.py:587
  46.5 1.6 %project.9.refs_3_.refs_1_.refs_0_ = bf16[48,1536]{1,0:T(8,128)(2,1)S(1)} custom-call(bf16[48,2048]{1,0:T(8,128)(2,1)S(1)} %collective-permute-done.5.refs_0_, f32[1,8192]{1,0:T(1,128)S(1)} %bitcast.6, bf16[8192,1024]{1,0:T(8,128)(2,1)S(1)} %get-tuple-element.59.refs_4_.refs_2_, bf16[8192,256]{1,0:T(8,128)(2,1)S(1)} %copy-done, ...), custom_call_target="tpu_custom_call" | custom-call | tf_op jit(solution)/shard_map/project/pallas_call | solution.py:281
  48.1 0.0 collective-permute-done.9.refs_0_
  48.1 0.0 collective-permute-done.10.refs_2_
  48.1 1.6 %collective-permute-start.11 = (bf16[80,2048]{1,0:T(8,128)(2,1)S(1)}, bf16[80,2048]{1,0:T(8,128)(2,1)S(1)}, u32[]{:S(2)}, u32[]{:S(2)}) collective-permute-start(bf16[80,2048]{1,0:T(8,128)(2,1)S(1)} %get-tuple-element.69.refs_1_), channel_id=1, source_target_pairs={{0,1},{1,0},{2,3},{3,2},{4,5},{5,4},{6,7},{7,6},{8,9},{9,8},{10,11... | collective-permute-start | bytes 983048 | tf_op jit(solution)/shard_map/ppermute | solution.py:587
  49.8 1.9 %collective-permute-start.15 = (bf16[80,2048]{1,0:T(8,128)(2,1)S(1)}, bf16[80,2048]{1,0:T(8,128)(2,1)S(1)}, u32[]{:S(2)}, u32[]{:S(2)}) collective-permute-start(bf16[80,2048]{1,0:T(8,128)(2,1)S(1)} %get-tuple-element.74.refs_0_), channel_id=1, source_target_pairs={{0,2},{1,3},{2,0},{3,1},{4,6},{5,7},{6,4},{7,5},{8,10},{9,11},{10,... | collective-permute-start | bytes 983048 | tf_op jit(solution)/shard_map/ppermute | solution.py:587
  51.7 0.1 collective-permute-start.17
  51.8 0.5 collective-permute-start.16
  52.3 1.5 %collective-permute-start.7 = (bf16[48,1536]{1,0:T(8,128)(2,1)S(1)}, bf16[48,1536]{1,0:T(8,128)(2,1)S(1)}, u32[]{:S(2)}, u32[]{:S(2)}) collective-permute-start(bf16[48,1536]{1,0:T(8,128)(2,1)S(1)} %project.9.refs_3_.refs_1_.refs_0_), channel_id=1, source_target_pairs={{0,8},{4,12},{8,0},{12,4},{1,9},{5,13},{9,1},{13,5},{2,10},{6,14},... | collective-permute-start | bytes 442376 | tf_op jit(solution)/shard_map/ppermute | solution.py:532
  53.8 4.3 %project.10 = (f32[80,1536]{1,0:T(8,128)S(1)}, f32[80,128]{1,0:T(8,128)S(1)}) custom-call(bf16[80,2048]{1,0:T(8,128)(2,1)S(1)} %get-tuple-element.62.anchor_ref.refs_0_, bf16[80,2048]{1,0:T(8,128)(2,1)S(1)} %get-tuple-element.69.refs_1_, bf16[80,2048]{1,0:T(8,128)(2,1)S(1)} %collective-permute-done.10.refs_2_, f32[1,8192]{1,0:T(1,128)S(1)} %bitcast.7, ...), custom_call_target="tpu_custom_call" | custom-call | tf_op jit(solution)/shard_map/project/pallas_call | solution.py:281
  58.1 0.9 collective-permute-done.16.refs_0_
  59.0 6.8 %collective-permute-done.11.refs_0_ = bf16[80,2048]{1,0:T(8,128)(2,1)S(1)} collective-permute-done((bf16[80,2048]{1,0:T(8,128)(2,1)S(1)}, bf16[80,2048]{1,0:T(8,128)(2,1)S(1)}, u32[]{:S(2)}, u32[]{:S(2)}) %collective-permute-start.11) | collective-permute-done | bytes 327712 | tf_op jit(solution)/shard_map/ppermute | solution.py:587
  65.8 1.7 %project.11.refs_1_.refs_3_.refs_4_ = bf16[80,1536]{1,0:T(8,128)(2,1)S(1)} custom-call(bf16[80,2048]{1,0:T(8,128)(2,1)S(1)} %collective-permute-done.11.refs_0_, f32[1,8192]{1,0:T(1,128)S(1)} %bitcast.8, bf16[8192,1024]{1,0:T(8,128)(2,1)S(1)} %get-tuple-element.59.refs_4_.refs_2_, bf16[8192,256]{1,0:T(8,128)(2,1)S(1)} %copy-done, ...), custom_call_target="tpu_custom_call" | custom-call | tf_op jit(solution)/shard_map/project/pallas_call | solution.py:281
  67.5 0.0 collective-permute-done.7.refs_0_.refs_4_
  67.5 0.0 collective-permute-done.15.refs_0_
  67.5 2.5 %collective-permute-done.17.refs_2_ = bf16[80,2048]{1,0:T(8,128)(2,1)S(1)} collective-permute-done((bf16[80,2048]{1,0:T(8,128)(2,1)S(1)}, bf16[80,2048]{1,0:T(8,128)(2,1)S(1)}, u32[]{:S(2)}, u32[]{:S(2)}) %collective-permute-start.17) | collective-permute-done | bytes 327712 | tf_op jit(solution)/shard_map/ppermute | solution.py:587
  70.1 1.6 %collective-permute-start.18 = (bf16[80,2048]{1,0:T(8,128)(2,1)S(1)}, bf16[80,2048]{1,0:T(8,128)(2,1)S(1)}, u32[]{:S(2)}, u32[]{:S(2)}) collective-permute-start(bf16[80,2048]{1,0:T(8,128)(2,1)S(1)} %get-tuple-element.77.refs_1_), channel_id=1, source_target_pairs={{0,1},{1,0},{2,3},{3,2},{4,5},{5,4},{6,7},{7,6},{8,9},{9,8},{10,11... | collective-permute-start | bytes 983048 | tf_op jit(solution)/shard_map/ppermute | solution.py:587
  71.6 0.6 collective-permute-start.14
  72.2 3.0 %collective-permute-start.22 = (bf16[48,2048]{1,0:T(8,128)(2,1)S(1)}, bf16[48,2048]{1,0:T(8,128)(2,1)S(1)}, u32[]{:S(2)}, u32[]{:S(2)}) collective-permute-start(bf16[48,2048]{1,0:T(8,128)(2,1)S(1)} %get-tuple-element.82.refs_0_), channel_id=1, source_target_pairs={{0,2},{1,3},{2,0},{3,1},{4,6},{5,7},{6,4},{7,5},{8,10},{9,11},{10,... | collective-permute-start | bytes 589832 | tf_op jit(solution)/shard_map/ppermute | solution.py:587
  75.2 0.3 collective-permute-start.23
  75.6 4.3 %project.12 = (f32[80,1536]{1,0:T(8,128)S(1)}, f32[80,128]{1,0:T(8,128)S(1)}) custom-call(bf16[80,2048]{1,0:T(8,128)(2,1)S(1)} %get-tuple-element.74.refs_0_, bf16[80,2048]{1,0:T(8,128)(2,1)S(1)} %get-tuple-element.77.refs_1_, bf16[80,2048]{1,0:T(8,128)(2,1)S(1)} %collective-permute-done.17.refs_2_, f32[1,8192]{1,0:T(1,128)S(1)} %bitcast.9, ...), custom_call_target="tpu_custom_call" | custom-call | tf_op jit(solution)/shard_map/project/pallas_call | solution.py:281
  79.8 3.7 %collective-permute-done.18.refs_0_ = bf16[80,2048]{1,0:T(8,128)(2,1)S(1)} collective-permute-done((bf16[80,2048]{1,0:T(8,128)(2,1)S(1)}, bf16[80,2048]{1,0:T(8,128)(2,1)S(1)}, u32[]{:S(2)}, u32[]{:S(2)}) %collective-permute-start.18) | collective-permute-done | bytes 327712 | tf_op jit(solution)/shard_map/ppermute | solution.py:587
  83.5 1.7 %project.13.refs_1_.refs_8_ = bf16[80,1536]{1,0:T(8,128)(2,1)S(1)} custom-call(bf16[80,2048]{1,0:T(8,128)(2,1)S(1)} %collective-permute-done.18.refs_0_, f32[1,8192]{1,0:T(1,128)S(1)} %bitcast.10, bf16[8192,1024]{1,0:T(8,128)(2,1)S(1)} %get-tuple-element.59.refs_4_.refs_2_, bf16[8192,256]{1,0:T(8,128)(2,1)S(1)} %copy-done, bf16[8192,256]{1,0:T(8,128)(2,1)S(1)} %copy-done.1, ...), custom_call_target="tpu_custom_call" | custom-call | tf_op jit(solution)/shard_map/project/pallas_call | solution.py:281
  85.2 3.0 %collective-permute-start.21 = (bf16[80,1536]{1,0:T(8,128)(2,1)S(1)}, bf16[80,1536]{1,0:T(8,128)(2,1)S(1)}, u32[]{:S(2)}, u32[]{:S(2)}) collective-permute-start(bf16[80,1536]{1,0:T(8,128)(2,1)S(1)} %project.13.refs_1_.refs_8_), channel_id=1, source_target_pairs={{0,8},{4,12},{8,0},{12,4},{1,9},{5,13},{9,1},{13,5},{2,10},{6,14},... | collective-permute-start | bytes 737288 | tf_op jit(solution)/shard_map/ppermute | solution.py:532
  88.2 0.0 collective-permute-done.22.refs_0_
  88.2 0.0 collective-permute-done.23.refs_1_.refs_2_
  88.2 0.1 collective-permute-start.24
  88.3 0.1 collective-permute-start.6
  88.4 0.5 collective-permute-start.12
  88.9 0.1 collective-permute-start.13
  89.0 4.1 %project.14 = (f32[48,1536]{1,0:T(8,128)S(1)}, f32[48,128]{1,0:T(8,128)S(1)}) custom-call(bf16[48,2048]{1,0:T(8,128)(2,1)S(1)} %get-tuple-element.82.refs_0_, bf16[48,2048]{1,0:T(8,128)(2,1)S(1)} %after.14.refs_1_, bf16[48,2048]{1,0:T(8,128)(2,1)S(1)} %collective-permute-done.23.refs_1_.refs_2_, f32[1,8192]{1,0:T(1,128)S(1)} %bitcast.11, ...), custom_call_target="tpu_custom_call" | custom-call | tf_op jit(solution)/shard_map/project/pallas_call | solution.py:281
  93.1 0.5 collective-permute-start.20
  93.5 0.1 collective-permute-start.19
  93.6 0.3 collective-permute-done.24.refs_0_
  94.0 1.7 %project.15.refs_1_.refs_12_ = bf16[48,1536]{1,0:T(8,128)(2,1)S(1)} custom-call(bf16[48,2048]{1,0:T(8,128)(2,1)S(1)} %collective-permute-done.24.refs_0_, f32[1,8192]{1,0:T(1,128)S(1)} %bitcast.12, bf16[8192,1024]{1,0:T(8,128)(2,1)S(1)} %get-tuple-element.59.refs_4_.refs_2_, bf16[8192,256]{1,0:T(8,128)(2,1)S(1)} %copy-done, bf16[8192,256]{1,0:T(8,128)(2,1)S(1)} %copy-done.1, ...), custom_call_target="tpu_custom_call" | custom-call | tf_op jit(solution)/shard_map/project/pallas_call | solution.py:281
  95.7 0.2 collective-permute-start.25
  95.8 0.5 collective-permute-start.27
  96.3 0.9 collective-permute-done.25.refs_11_
  97.2 2.7 %attend.2 = (bf16[512,1024]{1,0:T(8,128)(2,1)}, bf16[2,512,256]{2,1,0:T(8,128)(2,1)}, f32[8,128]{1,0:T(8,128)S(1)}) custom-call(s32[4]{0:T(128)S(1)} %copy-done.5, s32[16]{0:T(128)S(1)} %copy-done.6, bf16[48,1536]{1,0:T(8,128)(2,1)S(1)} %project.9.refs_3_.refs_1_.refs_0_, bf16[48,1536]{1,0:T(8,128)(2,1)S(1)} %collective-permute-done.6.refs_2_.refs_1_, ...), custom_call_target="tpu_custom_call" | custom-call | tf_op jit(solution)/shard_map/attend/pallas_call | solution.py:503
  100.0 2.0 %collective-permute-done.27.refs_0_ = bf16[48,1536]{1,0:T(8,128)(2,1)S(1)} collective-permute-done((bf16[48,1536]{1,0:T(8,128)(2,1)S(1)}, bf16[48,1536]{1,0:T(8,128)(2,1)S(1)}, u32[]{:S(2)}, u32[]{:S(2)}) %collective-permute-start.27) | collective-permute-done | bytes 147488 | tf_op jit(solution)/shard_map/ppermute | solution.py:532
  102.0 1.1 collective-permute-start.28
  103.1 1.0 collective-permute-done.28.refs_15_
  104.1 5.7 %attend.3 = (bf16[512,1024]{1,0:T(8,128)(2,1)}, bf16[2,512,256]{2,1,0:T(8,128)(2,1)}, f32[8,128]{1,0:T(8,128)}) custom-call(s32[4]{0:T(128)S(1)} %copy-done.5, s32[16]{0:T(128)S(1)} %copy-done.6, bf16[48,1536]{1,0:T(8,128)(2,1)S(1)} %project.9.refs_3_.refs_1_.refs_0_, ...), custom_call_target="tpu_custom_call", output_to_operand_aliasing={{0}: (18, {}), {1}: (19, {})} | custom-call | tf_op jit(solution)/shard_map/attend/pallas_call | solution.py:503
  (41 shorter events, 0.2 us)
Async XLA Ops:
  0.6 4.5 %collective-permute-start = (bf16[512,2048]{1,0:T(8,128)(2,1)}, bf16[512,2048]{1,0:T(8,128)(2,1)S(1)}, u32[]{:S(2)}, u32[]{:S(2)}) collective-permute-start(bf16[512,2048]{1,0:T(8,128)(2,1)} %refs_0_.3), channel_id=1, source_target_pairs={{0,4},{4,0},{8,12},{12,8},{1,5},{5,1},{9,13},{13,9},{2,6},{6,2},{1... | collective-permute-start | bytes 6291464 | tf_op jit(solution)/shard_map/ppermute | solution.py:536
  1.1 1.6 %copy-start.2 = (bf16[512,2048]{1,0:T(8,128)(2,1)S(1)}, bf16[512,2048]{1,0:T(8,128)(2,1)}, u32[]{:S(2)}) copy-start(bf16[512,2048]{1,0:T(8,128)(2,1)} %refs_0_.3) | copy-start | bytes 6291460
  2.7 0.7 copy-start.4
  3.4 6.0 %copy-start.3 = (bf16[512,2048]{1,0:T(8,128)(2,1)S(1)}, bf16[512,2048]{1,0:T(8,128)(2,1)}, u32[]{:S(2)}) copy-start(bf16[512,2048]{1,0:T(8,128)(2,1)} %refs_0_.3) | copy-start | bytes 6291460
  6.5 8.1 %collective-permute-start.1 = (bf16[48,2048]{1,0:T(8,128)(2,1)S(1)}, bf16[48,2048]{1,0:T(8,128)(2,1)S(1)}, u32[]{:S(2)}, u32[]{:S(2)}) collective-permute-start(bf16[48,2048]{1,0:T(8,128)(2,1)S(1)} %bitcast.16), channel_id=1, source_target_pairs={{0,8},{4,12},{8,0},{12,4},{1,9},{5,13},{9,1},{13,5},{2,10},{6,14},... | collective-permute-start | bytes 589832 | tf_op jit(solution)/shard_map/ppermute | solution.py:532
  14.6 12.1 %collective-permute-start.3 = (bf16[80,2048]{1,0:T(8,128)(2,1)S(1)}, bf16[80,2048]{1,0:T(8,128)(2,1)S(1)}, u32[]{:S(2)}, u32[]{:S(2)}) collective-permute-start(bf16[80,2048]{1,0:T(8,128)(2,1)S(1)} %bitcast.13), channel_id=1, source_target_pairs={{0,8},{4,12},{8,0},{12,4},{1,9},{5,13},{9,1},{13,5},{2,10},{6,14},... | collective-permute-start | bytes 983048 | tf_op jit(solution)/shard_map/ppermute | solution.py:532
  16.4 15.4 %copy-start.8 = (bf16[8192]{0:T(1024)(128)(2,1)S(1)}, bf16[8192]{0:T(1024)(128)(2,1)}, u32[]{:S(2)}) copy-start(bf16[8192]{0:T(1024)(128)(2,1)} %param.9) | copy-start | bytes 49156
  16.4 15.5 %copy-start.5 = (s32[4]{0:T(128)S(1)}, s32[4]{0:T(128)}, u32[]{:S(2)}) copy-start(s32[4]{0:T(128)} %lengths_ref.11) | copy-start | bytes 52
  16.4 15.5 %copy-start.7 = (f32[1,128]{1,0:T(1,128)S(1)}, f32[1,128]{1,0:T(1,128)}, u32[]{:S(2)}) copy-start(f32[1,128]{1,0:T(1,128)} %constant.2.clone.frequency_ref) | copy-start | bytes 1540
  16.4 10.9 %collective-permute-start.4 = (bf16[48,2048]{1,0:T(8,128)(2,1)S(1)}, bf16[48,2048]{1,0:T(8,128)(2,1)S(1)}, u32[]{:S(2)}, u32[]{:S(2)}) collective-permute-start(bf16[48,2048]{1,0:T(8,128)(2,1)S(1)} %get-tuple-element.52.anchor_ref.refs_0_), channel_id=1, source_target_pairs={{0,1},{1,0},{2,3},{3,2},{4,5},{5,4},{6,7},{7,6},{8,9},{9,8},{10,11... | collective-permute-start | bytes 589832 | tf_op jit(solution)/shard_map/ppermute | solution.py:587
  18.0 10.8 %collective-permute-start.2 = (bf16[48,2048]{1,0:T(8,128)(2,1)S(1)}, bf16[48,2048]{1,0:T(8,128)(2,1)S(1)}, u32[]{:S(2)}, u32[]{:S(2)}) collective-permute-start(bf16[48,2048]{1,0:T(8,128)(2,1)S(1)} %get-tuple-element.52.anchor_ref.refs_0_), channel_id=1, source_target_pairs={{0,2},{1,3},{2,0},{3,1},{4,6},{5,7},{6,4},{7,5},{8,10},{9,11},{10,... | collective-permute-start | bytes 589832 | tf_op jit(solution)/shard_map/ppermute | solution.py:587
  20.6 12.4 %copy-start = (bf16[8192,256]{1,0:T(8,128)(2,1)S(1)}, bf16[8192,256]{1,0:T(8,128)(2,1)}, u32[]{:S(2)}) copy-start(bf16[8192,256]{1,0:T(8,128)(2,1)} %refs_3_.7) | copy-start | bytes 12582916
  20.6 12.4 %copy-start.1 = (bf16[8192,256]{1,0:T(8,128)(2,1)S(1)}, bf16[8192,256]{1,0:T(8,128)(2,1)}, u32[]{:S(2)}) copy-start(bf16[8192,256]{1,0:T(8,128)(2,1)} %refs_4_.7) | copy-start | bytes 12582916
  26.7 21.3 %collective-permute-start.9 = (bf16[80,2048]{1,0:T(8,128)(2,1)S(1)}, bf16[80,2048]{1,0:T(8,128)(2,1)S(1)}, u32[]{:S(2)}, u32[]{:S(2)}) collective-permute-start(bf16[80,2048]{1,0:T(8,128)(2,1)S(1)} %bitcast.14), channel_id=1, source_target_pairs={{0,8},{4,12},{8,0},{12,4},{1,9},{5,13},{9,1},{13,5},{2,10},{6,14},... | collective-permute-start | bytes 983048 | tf_op jit(solution)/shard_map/ppermute | solution.py:532
  28.8 19.3 %collective-permute-start.10 = (bf16[80,2048]{1,0:T(8,128)(2,1)S(1)}, bf16[80,2048]{1,0:T(8,128)(2,1)S(1)}, u32[]{:S(2)}, u32[]{:S(2)}) collective-permute-start(bf16[80,2048]{1,0:T(8,128)(2,1)S(1)} %get-tuple-element.62.anchor_ref.refs_0_), channel_id=1, source_target_pairs={{0,1},{1,0},{2,3},{3,2},{4,5},{5,4},{6,7},{7,6},{8,9},{9,8},{10,11... | collective-permute-start | bytes 983048 | tf_op jit(solution)/shard_map/ppermute | solution.py:587
  29.2 18.9 %collective-permute-start.8 = (bf16[80,2048]{1,0:T(8,128)(2,1)S(1)}, bf16[80,2048]{1,0:T(8,128)(2,1)S(1)}, u32[]{:S(2)}, u32[]{:S(2)}) collective-permute-start(bf16[80,2048]{1,0:T(8,128)(2,1)S(1)} %get-tuple-element.62.anchor_ref.refs_0_), channel_id=1, source_target_pairs={{0,2},{1,3},{2,0},{3,1},{4,6},{5,7},{6,4},{7,5},{8,10},{9,11},{10,... | collective-permute-start | bytes 983048 | tf_op jit(solution)/shard_map/ppermute | solution.py:587
  31.9 14.6 %collective-permute-start.5 = (bf16[48,2048]{1,0:T(8,128)(2,1)S(1)}, bf16[48,2048]{1,0:T(8,128)(2,1)S(1)}, u32[]{:S(2)}, u32[]{:S(2)}) collective-permute-start(bf16[48,2048]{1,0:T(8,128)(2,1)S(1)} %get-tuple-element.58.refs_1_), channel_id=1, source_target_pairs={{0,1},{1,0},{2,3},{3,2},{4,5},{5,4},{6,7},{7,6},{8,9},{9,8},{10,11... | collective-permute-start | bytes 589832 | tf_op jit(solution)/shard_map/ppermute | solution.py:587
  48.1 17.7 %collective-permute-start.11 = (bf16[80,2048]{1,0:T(8,128)(2,1)S(1)}, bf16[80,2048]{1,0:T(8,128)(2,1)S(1)}, u32[]{:S(2)}, u32[]{:S(2)}) collective-permute-start(bf16[80,2048]{1,0:T(8,128)(2,1)S(1)} %get-tuple-element.69.refs_1_), channel_id=1, source_target_pairs={{0,1},{1,0},{2,3},{3,2},{4,5},{5,4},{6,7},{7,6},{8,9},{9,8},{10,11... | collective-permute-start | bytes 983048 | tf_op jit(solution)/shard_map/ppermute | solution.py:587
  49.8 17.7 %collective-permute-start.15 = (bf16[80,2048]{1,0:T(8,128)(2,1)S(1)}, bf16[80,2048]{1,0:T(8,128)(2,1)S(1)}, u32[]{:S(2)}, u32[]{:S(2)}) collective-permute-start(bf16[80,2048]{1,0:T(8,128)(2,1)S(1)} %get-tuple-element.74.refs_0_), channel_id=1, source_target_pairs={{0,2},{1,3},{2,0},{3,1},{4,6},{5,7},{6,4},{7,5},{8,10},{9,11},{10,... | collective-permute-start | bytes 983048 | tf_op jit(solution)/shard_map/ppermute | solution.py:587
  51.7 18.3 %collective-permute-start.17 = (bf16[80,2048]{1,0:T(8,128)(2,1)S(1)}, bf16[80,2048]{1,0:T(8,128)(2,1)S(1)}, u32[]{:S(2)}, u32[]{:S(2)}) collective-permute-start(bf16[80,2048]{1,0:T(8,128)(2,1)S(1)} %get-tuple-element.74.refs_0_), channel_id=1, source_target_pairs={{0,1},{1,0},{2,3},{3,2},{4,5},{5,4},{6,7},{7,6},{8,9},{9,8},{10,11... | collective-permute-start | bytes 983048 | tf_op jit(solution)/shard_map/ppermute | solution.py:587
  51.8 7.1 %collective-permute-start.16 = (bf16[48,2048]{1,0:T(8,128)(2,1)S(1)}, bf16[48,2048]{1,0:T(8,128)(2,1)S(1)}, u32[]{:S(2)}, u32[]{:S(2)}) collective-permute-start(bf16[48,2048]{1,0:T(8,128)(2,1)S(1)} %bitcast.15), channel_id=1, source_target_pairs={{0,8},{4,12},{8,0},{12,4},{1,9},{5,13},{9,1},{13,5},{2,10},{6,14},... | collective-permute-start | bytes 589832 | tf_op jit(solution)/shard_map/ppermute | solution.py:532
  52.3 15.2 %collective-permute-start.7 = (bf16[48,1536]{1,0:T(8,128)(2,1)S(1)}, bf16[48,1536]{1,0:T(8,128)(2,1)S(1)}, u32[]{:S(2)}, u32[]{:S(2)}) collective-permute-start(bf16[48,1536]{1,0:T(8,128)(2,1)S(1)} %project.9.refs_3_.refs_1_.refs_0_), channel_id=1, source_target_pairs={{0,8},{4,12},{8,0},{12,4},{1,9},{5,13},{9,1},{13,5},{2,10},{6,14},... | collective-permute-start | bytes 442376 | tf_op jit(solution)/shard_map/ppermute | solution.py:532
  70.1 13.4 %collective-permute-start.18 = (bf16[80,2048]{1,0:T(8,128)(2,1)S(1)}, bf16[80,2048]{1,0:T(8,128)(2,1)S(1)}, u32[]{:S(2)}, u32[]{:S(2)}) collective-permute-start(bf16[80,2048]{1,0:T(8,128)(2,1)S(1)} %get-tuple-element.77.refs_1_), channel_id=1, source_target_pairs={{0,1},{1,0},{2,3},{3,2},{4,5},{5,4},{6,7},{7,6},{8,9},{9,8},{10,11... | collective-permute-start | bytes 983048 | tf_op jit(solution)/shard_map/ppermute | solution.py:587
  71.6 16.6 %collective-permute-start.14 = (bf16[80,1536]{1,0:T(8,128)(2,1)S(1)}, bf16[80,1536]{1,0:T(8,128)(2,1)S(1)}, u32[]{:S(2)}, u32[]{:S(2)}) collective-permute-start(bf16[80,1536]{1,0:T(8,128)(2,1)S(1)} %project.11.refs_1_.refs_3_.refs_4_), channel_id=1, source_target_pairs={{0,8},{4,12},{8,0},{12,4},{1,9},{5,13},{9,1},{13,5},{2,10},{6,14},... | collective-permute-start | bytes 737288 | tf_op jit(solution)/shard_map/ppermute | solution.py:532
  72.2 16.0 %collective-permute-start.22 = (bf16[48,2048]{1,0:T(8,128)(2,1)S(1)}, bf16[48,2048]{1,0:T(8,128)(2,1)S(1)}, u32[]{:S(2)}, u32[]{:S(2)}) collective-permute-start(bf16[48,2048]{1,0:T(8,128)(2,1)S(1)} %get-tuple-element.82.refs_0_), channel_id=1, source_target_pairs={{0,2},{1,3},{2,0},{3,1},{4,6},{5,7},{6,4},{7,5},{8,10},{9,11},{10,... | collective-permute-start | bytes 589832 | tf_op jit(solution)/shard_map/ppermute | solution.py:587
  75.2 13.0 %collective-permute-start.23 = (bf16[48,2048]{1,0:T(8,128)(2,1)S(1)}, bf16[48,2048]{1,0:T(8,128)(2,1)S(1)}, u32[]{:S(2)}, u32[]{:S(2)}) collective-permute-start(bf16[48,2048]{1,0:T(8,128)(2,1)S(1)} %get-tuple-element.82.refs_0_), channel_id=1, source_target_pairs={{0,1},{1,0},{2,3},{3,2},{4,5},{5,4},{6,7},{7,6},{8,9},{9,8},{10,11... | collective-permute-start | bytes 589832 | tf_op jit(solution)/shard_map/ppermute | solution.py:587
  85.2 10.5 %collective-permute-start.21 = (bf16[80,1536]{1,0:T(8,128)(2,1)S(1)}, bf16[80,1536]{1,0:T(8,128)(2,1)S(1)}, u32[]{:S(2)}, u32[]{:S(2)}) collective-permute-start(bf16[80,1536]{1,0:T(8,128)(2,1)S(1)} %project.13.refs_1_.refs_8_), channel_id=1, source_target_pairs={{0,8},{4,12},{8,0},{12,4},{1,9},{5,13},{9,1},{13,5},{2,10},{6,14},... | collective-permute-start | bytes 737288 | tf_op jit(solution)/shard_map/ppermute | solution.py:532
  88.2 5.7 %collective-permute-start.24 = (bf16[48,2048]{1,0:T(8,128)(2,1)S(1)}, bf16[48,2048]{1,0:T(8,128)(2,1)S(1)}, u32[]{:S(2)}, u32[]{:S(2)}) collective-permute-start(bf16[48,2048]{1,0:T(8,128)(2,1)S(1)} %after.14.refs_1_), channel_id=1, source_target_pairs={{0,1},{1,0},{2,3},{3,2},{4,5},{5,4},{6,7},{7,6},{8,9},{9,8},{10,11... | collective-permute-start | bytes 589832 | tf_op jit(solution)/shard_map/ppermute | solution.py:587
  88.3 4.7 %collective-permute-start.6 = (bf16[48,1536]{1,0:T(8,128)(2,1)S(1)}, bf16[48,1536]{1,0:T(8,128)(2,1)S(1)}, u32[]{:S(2)}, u32[]{:S(2)}) collective-permute-start(bf16[48,1536]{1,0:T(8,128)(2,1)S(1)} %project.9.refs_3_.refs_1_.refs_0_), channel_id=1, source_target_pairs={{0,4},{4,0},{8,12},{12,8},{1,5},{5,1},{9,13},{13,9},{2,6},{6,2},{1... | collective-permute-start | bytes 442376 | tf_op jit(solution)/shard_map/ppermute | solution.py:536
  88.4 4.7 %collective-permute-start.12 = (bf16[48,1536]{1,0:T(8,128)(2,1)S(1)}, bf16[48,1536]{1,0:T(8,128)(2,1)S(1)}, u32[]{:S(2)}, u32[]{:S(2)}) collective-permute-start(bf16[48,1536]{1,0:T(8,128)(2,1)S(1)} %after.11.refs_3_.refs_2_), channel_id=1, source_target_pairs={{0,4},{4,0},{8,12},{12,8},{1,5},{5,1},{9,13},{13,9},{2,6},{6,2},{1... | collective-permute-start | bytes 442376 | tf_op jit(solution)/shard_map/ppermute | solution.py:536
  88.9 7.4 %collective-permute-start.13 = (bf16[80,1536]{1,0:T(8,128)(2,1)S(1)}, bf16[80,1536]{1,0:T(8,128)(2,1)S(1)}, u32[]{:S(2)}, u32[]{:S(2)}) collective-permute-start(bf16[80,1536]{1,0:T(8,128)(2,1)S(1)} %project.11.refs_1_.refs_3_.refs_4_), channel_id=1, source_target_pairs={{0,4},{4,0},{8,12},{12,8},{1,5},{5,1},{9,13},{13,9},{2,6},{6,2},{1... | collective-permute-start | bytes 737288 | tf_op jit(solution)/shard_map/ppermute | solution.py:536
  93.1 3.3 %collective-permute-start.20 = (bf16[80,1536]{1,0:T(8,128)(2,1)S(1)}, bf16[80,1536]{1,0:T(8,128)(2,1)S(1)}, u32[]{:S(2)}, u32[]{:S(2)}) collective-permute-start(bf16[80,1536]{1,0:T(8,128)(2,1)S(1)} %project.13.refs_1_.refs_8_), channel_id=1, source_target_pairs={{0,4},{4,0},{8,12},{12,8},{1,5},{5,1},{9,13},{13,9},{2,6},{6,2},{1... | collective-permute-start | bytes 737288 | tf_op jit(solution)/shard_map/ppermute | solution.py:536
  93.5 2.8 %collective-permute-start.19 = (bf16[80,1536]{1,0:T(8,128)(2,1)S(1)}, bf16[80,1536]{1,0:T(8,128)(2,1)S(1)}, u32[]{:S(2)}, u32[]{:S(2)}) collective-permute-start(bf16[80,1536]{1,0:T(8,128)(2,1)S(1)} %after.13.refs_6_), channel_id=1, source_target_pairs={{0,4},{4,0},{8,12},{12,8},{1,5},{5,1},{9,13},{13,9},{2,6},{6,2},{1... | collective-permute-start | bytes 737288 | tf_op jit(solution)/shard_map/ppermute | solution.py:536
  93.9 3.3 %copy-start.6 = (s32[16]{0:T(128)S(1)}, s32[16]{0:T(128)}, u32[]{:S(2)}) copy-start(s32[16]{0:T(128)} %plan_ref.3) | copy-start | bytes 196
  95.7 1.6 %collective-permute-start.25 = (bf16[80,1536]{1,0:T(8,128)(2,1)S(1)}, bf16[80,1536]{1,0:T(8,128)(2,1)S(1)}, u32[]{:S(2)}, u32[]{:S(2)}) collective-permute-start(bf16[80,1536]{1,0:T(8,128)(2,1)S(1)} %after.16.refs_10_), channel_id=1, source_target_pairs={{0,4},{4,0},{8,12},{12,8},{1,5},{5,1},{9,13},{13,9},{2,6},{6,2},{1... | collective-permute-start | bytes 737288 | tf_op jit(solution)/shard_map/ppermute | solution.py:536
  95.8 6.2 %collective-permute-start.27 = (bf16[48,1536]{1,0:T(8,128)(2,1)S(1)}, bf16[48,1536]{1,0:T(8,128)(2,1)S(1)}, u32[]{:S(2)}, u32[]{:S(2)}) collective-permute-start(bf16[48,1536]{1,0:T(8,128)(2,1)S(1)} %project.15.refs_1_.refs_12_), channel_id=1, source_target_pairs={{0,8},{4,12},{8,0},{12,4},{1,9},{5,13},{9,1},{13,5},{2,10},{6,14},... | collective-permute-start | bytes 442376 | tf_op jit(solution)/shard_map/ppermute | solution.py:532
  96.3 6.8 %collective-permute-start.26 = (bf16[48,1536]{1,0:T(8,128)(2,1)S(1)}, bf16[48,1536]{1,0:T(8,128)(2,1)S(1)}, u32[]{:S(2)}, u32[]{:S(2)}) collective-permute-start(bf16[48,1536]{1,0:T(8,128)(2,1)S(1)} %project.15.refs_1_.refs_12_), channel_id=1, source_target_pairs={{0,4},{4,0},{8,12},{12,8},{1,5},{5,1},{9,13},{13,9},{2,6},{6,2},{1... | collective-permute-start | bytes 442376 | tf_op jit(solution)/shard_map/ppermute | solution.py:536
  102.0 2.1 %collective-permute-start.28 = (bf16[48,1536]{1,0:T(8,128)(2,1)S(1)}, bf16[48,1536]{1,0:T(8,128)(2,1)S(1)}, u32[]{:S(2)}, u32[]{:S(2)}) collective-permute-start(bf16[48,1536]{1,0:T(8,128)(2,1)S(1)} %after.17.refs_14_), channel_id=1, source_target_pairs={{0,4},{4,0},{8,12},{12,8},{1,5},{5,1},{9,13},{13,9},{2,6},{6,2},{1... | collective-permute-start | bytes 442376 | tf_op jit(solution)/shard_map/ppermute | solution.py:536

commit v7 on v3

--- a/solution.py
+++ b/solution.py
@@ -443,7 +443,8 @@
                     )
                     scores = scores + bias
                     scores_ref[head, tile] = scores
-                    top_ref[head] = jnp.maximum(top_ref[head], scores)
+                    halves = jnp.maximum(scores[:, :SPAN], scores[:, SPAN:])
+                    top_ref[head] = jnp.maximum(top_ref[head], halves)
                 return carry
 
             lax.fori_loop(0, tiles, score, 0)
@@ -518,7 +519,7 @@
             pltpu.VMEM((total + TILE + ALIGN, width), BF16),
             pltpu.VMEM((key_heads, tall, HEAD_SIZE), BF16),
             pltpu.VMEM((key_heads, slots // TILE + 1, tall, TILE), F32),
-            pltpu.VMEM((key_heads, tall, TILE), F32),
+            pltpu.VMEM((key_heads, tall, SPAN), F32),
             pltpu.SemaphoreType.DMA((copies,)),
             pltpu.SemaphoreType.DMA((slots // SPAN + 1,)),
         ],

time: 110 us -> 110 us (level)
  no operation moved by 1% of the time
where the time goes in v7:
time: 110 us
  Pallas kernels  48.5 us (44%)
  waiting for transfers between devices  29.7 us (27%)
  starting transfers between devices  28.1 us (26%)
  local copies, waits for them, and re-layouts  2.27 us (2%)
    pallas_call x8, Pallas kernels, project(): pl.pallas_call(functools.partial(project_kernel, masks, bool(carried), fi...  22.9 us
    ppermute x12, waiting for transfers between devices, start(): line[index + 1] = lax.ppermute(line[source], 'tp', pairs)  22.6 us
    ppermute x12, starting transfers between devices, start(): line[index + 1] = lax.ppermute(line[source], 'tp', pairs)  16.4 us
    pallas_call x3, Pallas kernels, attend(): pl.pallas_call(functools.partial(attend_kernel, chips, groups, known, pri...  12.8 us
    ppermute x8, starting transfers between devices, shift_chips(): return lax.ppermute(value, 'req', pairs)  8.95 us
    pallas_call x1, Pallas kernels, load(): pl.pallas_call(kernel, in_specs=[anywhere, anywhere], out_specs=[vmem, vm...  6.06 us
    pallas_call x3, Pallas kernels, deal(): pl.pallas_call(functools.partial(deal_kernel, chips, bases, sizes, twins)...  5.53 us
    ppermute x8, waiting for transfers between devices, shift_chips(): return lax.ppermute(value, 'req', pairs)  3.54 us
  transfers between devices with their start and end apart: 29, of which 13 were waited for; matrix products, arithmetic and copies ran while one was open for 0% of the time, Pallas kernels for 39%

profile of v7, /device:TPU:0, one launch (start us, length us, event | category | flops | bytes accessed | tf_op | source)
XLA Modules:
  0.0 109.6 jit_solution(15758283316149616370)
XLA Ops:
  0.6 0.5 collective-permute-start
  1.1 1.6 %copy-done.2 = bf16[512,2048]{1,0:T(8,128)(2,1)S(1)} copy-done((bf16[512,2048]{1,0:T(8,128)(2,1)S(1)}, bf16[512,2048]{1,0:T(8,128)(2,1)}, u32[]{:S(2)}) %copy-start.2) | copy-done | bytes 2097176
  2.7 0.7 copy-done.4
  3.4 1.3 %deal.3 = (bf16[48,2048]{1,0:T(8,128)(2,1)S(1)}, bf16[1,48,2048]{2,1,0:T(8,128)(2,1)S(1)}) custom-call(s32[4]{0:T(128)S(1)} %copy-done.4, bf16[512,2048]{1,0:T(8,128)(2,1)S(1)} %copy-done.2), custom_call_target="tpu_custom_call" | custom-call | tf_op jit(solution)/shard_map/deal/pallas_call | solution.py:86
  4.7 0.4 collective-permute-done.refs_0_.refs_1_
  5.1 1.3 %deal.4 = (bf16[48,2048]{1,0:T(8,128)(2,1)S(1)}, bf16[1,48,2048]{2,1,0:T(8,128)(2,1)S(1)}) custom-call(s32[4]{0:T(128)S(1)} %copy-done.4, bf16[512,2048]{1,0:T(8,128)(2,1)S(1)} %collective-permute-done.refs_0_.refs_1_, bf16[48,2048]{1,0:T(8,128)(2,1)S(1)} %get-tuple-element.50.refs_1_, bf16[1,48,2048]{2,1,0:T(8,128)(2,1)S(1)} %get-tuple-element.51.refs_2_), custom_call_target="tpu_custom_call" | custom-call | tf_op jit(solution)/shard_map/deal/pallas_call | solution.py:86
  6.5 2.9 %collective-permute-start.1 = (bf16[48,2048]{1,0:T(8,128)(2,1)S(1)}, bf16[48,2048]{1,0:T(8,128)(2,1)S(1)}, u32[]{:S(2)}, u32[]{:S(2)}) collective-permute-start(bf16[48,2048]{1,0:T(8,128)(2,1)S(1)} %bitcast.16), channel_id=1, source_target_pairs={{0,8},{4,12},{8,0},{12,4},{1,9},{5,13},{9,1},{13,5},{2,10},{6,14},... | collective-permute-start | bytes 589832 | tf_op jit(solution)/shard_map/ppermute | solution.py:533
  9.4 2.9 %deal.5 = (bf16[80,2048]{1,0:T(8,128)(2,1)S(1)}, bf16[1,80,2048]{2,1,0:T(8,128)(2,1)S(1)}, bf16[80,2048]{1,0:T(8,128)(2,1)S(1)}, bf16[1,80,2048]{2,1,0:T(8,128)(...) custom-call(s32[4]{0:T(128)S(1)} %copy-done.4, bf16[512,2048]{1,0:T(8,128)(2,1)S(1)} %copy-done.3, ...), custom_call_target="tpu_custom_call" | custom-call | tf_op jit(solution)/shard_map/deal/pallas_call | solution.py:86
  12.3 2.3 %collective-permute-done.1.refs_0_ = bf16[48,2048]{1,0:T(8,128)(2,1)S(1)} collective-permute-done((bf16[48,2048]{1,0:T(8,128)(2,1)S(1)}, bf16[48,2048]{1,0:T(8,128)(2,1)S(1)}, u32[]{:S(2)}, u32[]{:S(2)}) %collective-permute-start.1) | collective-permute-done | bytes 196640 | tf_op jit(solution)/shard_map/ppermute | solution.py:533
  14.6 1.8 %collective-permute-start.3 = (bf16[80,2048]{1,0:T(8,128)(2,1)S(1)}, bf16[80,2048]{1,0:T(8,128)(2,1)S(1)}, u32[]{:S(2)}, u32[]{:S(2)}) collective-permute-start(bf16[80,2048]{1,0:T(8,128)(2,1)S(1)} %bitcast.13), channel_id=1, source_target_pairs={{0,8},{4,12},{8,0},{12,4},{1,9},{5,13},{9,1},{13,5},{2,10},{6,14},... | collective-permute-start | bytes 983048 | tf_op jit(solution)/shard_map/ppermute | solution.py:533
  16.4 1.6 %collective-permute-start.4 = (bf16[48,2048]{1,0:T(8,128)(2,1)S(1)}, bf16[48,2048]{1,0:T(8,128)(2,1)S(1)}, u32[]{:S(2)}, u32[]{:S(2)}) collective-permute-start(bf16[48,2048]{1,0:T(8,128)(2,1)S(1)} %get-tuple-element.55.anchor_ref.refs_0_), channel_id=1, source_target_pairs={{0,1},{1,0},{2,3},{3,2},{4,5},{5,4},{6,7},{7,6},{8,9},{9,8},{10,11... | collective-permute-start | bytes 589832 | tf_op jit(solution)/shard_map/ppermute | solution.py:588
  18.0 2.6 %collective-permute-start.2 = (bf16[48,2048]{1,0:T(8,128)(2,1)S(1)}, bf16[48,2048]{1,0:T(8,128)(2,1)S(1)}, u32[]{:S(2)}, u32[]{:S(2)}) collective-permute-start(bf16[48,2048]{1,0:T(8,128)(2,1)S(1)} %get-tuple-element.55.anchor_ref.refs_0_), channel_id=1, source_target_pairs={{0,2},{1,3},{2,0},{3,1},{4,6},{5,7},{6,4},{7,5},{8,10},{9,11},{10,... | collective-permute-start | bytes 589832 | tf_op jit(solution)/shard_map/ppermute | solution.py:588
  20.6 6.1 %load.1 = (bf16[8192,1024]{1,0:T(8,128)(2,1)S(1)}, f32[8,128]{1,0:T(8,128)S(1)}) custom-call(bf16[8192,1024]{1,0:T(8,128)(2,1)} %weight_ref.1, bf16[48,2048]{1,0:T(8,128)(2,1)S(1)} %get-tuple-element.55.anchor_ref.refs_0_), custom_call_target="tpu_custom_call" | custom-call | tf_op jit(solution)/shard_map/load/pallas_call | solution.py:206
  26.7 0.6 collective-permute-start.9
  27.3 1.5 %collective-permute-done.2.refs_0_ = bf16[48,2048]{1,0:T(8,128)(2,1)S(1)} collective-permute-done((bf16[48,2048]{1,0:T(8,128)(2,1)S(1)}, bf16[48,2048]{1,0:T(8,128)(2,1)S(1)}, u32[]{:S(2)}, u32[]{:S(2)}) %collective-permute-start.2) | collective-permute-done | bytes 196640 | tf_op jit(solution)/shard_map/ppermute | solution.py:588
  28.8 0.3 collective-permute-start.10
  29.2 2.7 %collective-permute-start.8 = (bf16[80,2048]{1,0:T(8,128)(2,1)S(1)}, bf16[80,2048]{1,0:T(8,128)(2,1)S(1)}, u32[]{:S(2)}, u32[]{:S(2)}) collective-permute-start(bf16[80,2048]{1,0:T(8,128)(2,1)S(1)} %get-tuple-element.65.anchor_ref.refs_0_), channel_id=1, source_target_pairs={{0,2},{1,3},{2,0},{3,1},{4,6},{5,7},{6,4},{7,5},{8,10},{9,11},{10,... | collective-permute-start | bytes 983048 | tf_op jit(solution)/shard_map/ppermute | solution.py:588
  31.9 0.0 collective-permute-start.5
  31.9 1.1 angles.1
  33.0 4.0 %project.8 = (f32[48,1536]{1,0:T(8,128)S(1)}, f32[48,128]{1,0:T(8,128)S(1)}) custom-call(bf16[48,2048]{1,0:T(8,128)(2,1)S(1)} %get-tuple-element.55.anchor_ref.refs_0_, bf16[48,2048]{1,0:T(8,128)(2,1)S(1)} %get-tuple-element.61.refs_1_, bf16[48,2048]{1,0:T(8,128)(2,1)S(1)} %collective-permute-done.4.refs_2_, f32[1,8192]{1,0:T(1,128)S(1)} %bitcast.5, ...), custom_call_target="tpu_custom_call" | custom-call | tf_op jit(solution)/shard_map/project/pallas_call | solution.py:281
  37.0 9.5 %collective-permute-done.5.refs_0_ = bf16[48,2048]{1,0:T(8,128)(2,1)S(1)} collective-permute-done((bf16[48,2048]{1,0:T(8,128)(2,1)S(1)}, bf16[48,2048]{1,0:T(8,128)(2,1)S(1)}, u32[]{:S(2)}, u32[]{:S(2)}) %collective-permute-start.5) | collective-permute-done | bytes 196640 | tf_op jit(solution)/shard_map/ppermute | solution.py:588
  46.5 1.6 %project.9.refs_3_.refs_4_.refs_0_ = bf16[48,1536]{1,0:T(8,128)(2,1)S(1)} custom-call(bf16[48,2048]{1,0:T(8,128)(2,1)S(1)} %collective-permute-done.5.refs_0_, f32[1,8192]{1,0:T(1,128)S(1)} %bitcast.6, bf16[8192,1024]{1,0:T(8,128)(2,1)S(1)} %get-tuple-element.62.refs_4_.refs_2_, bf16[8192,256]{1,0:T(8,128)(2,1)S(1)} %copy-done, ...), custom_call_target="tpu_custom_call" | custom-call | tf_op jit(solution)/shard_map/project/pallas_call | solution.py:281
  48.1 0.0 collective-permute-done.9.refs_0_
  48.1 0.0 collective-permute-done.10.refs_2_
  48.1 1.6 %collective-permute-start.11 = (bf16[80,2048]{1,0:T(8,128)(2,1)S(1)}, bf16[80,2048]{1,0:T(8,128)(2,1)S(1)}, u32[]{:S(2)}, u32[]{:S(2)}) collective-permute-start(bf16[80,2048]{1,0:T(8,128)(2,1)S(1)} %get-tuple-element.72.refs_1_), channel_id=1, source_target_pairs={{0,1},{1,0},{2,3},{3,2},{4,5},{5,4},{6,7},{7,6},{8,9},{9,8},{10,11... | collective-permute-start | bytes 983048 | tf_op jit(solution)/shard_map/ppermute | solution.py:588
  49.8 0.5 collective-permute-start.16
  50.3 2.0 %collective-permute-start.15 = (bf16[80,2048]{1,0:T(8,128)(2,1)S(1)}, bf16[80,2048]{1,0:T(8,128)(2,1)S(1)}, u32[]{:S(2)}, u32[]{:S(2)}) collective-permute-start(bf16[80,2048]{1,0:T(8,128)(2,1)S(1)} %get-tuple-element.77.refs_0_), channel_id=1, source_target_pairs={{0,2},{1,3},{2,0},{3,1},{4,6},{5,7},{6,4},{7,5},{8,10},{9,11},{10,... | collective-permute-start | bytes 983048 | tf_op jit(solution)/shard_map/ppermute | solution.py:588
  52.3 0.1 collective-permute-start.17
  52.3 1.5 %collective-permute-start.7 = (bf16[48,1536]{1,0:T(8,128)(2,1)S(1)}, bf16[48,1536]{1,0:T(8,128)(2,1)S(1)}, u32[]{:S(2)}, u32[]{:S(2)}) collective-permute-start(bf16[48,1536]{1,0:T(8,128)(2,1)S(1)} %project.9.refs_3_.refs_4_.refs_0_), channel_id=1, source_target_pairs={{0,8},{4,12},{8,0},{12,4},{1,9},{5,13},{9,1},{13,5},{2,10},{6,14},... | collective-permute-start | bytes 442376 | tf_op jit(solution)/shard_map/ppermute | solution.py:533
  53.8 4.2 %project.10 = (f32[80,1536]{1,0:T(8,128)S(1)}, f32[80,128]{1,0:T(8,128)S(1)}) custom-call(bf16[80,2048]{1,0:T(8,128)(2,1)S(1)} %get-tuple-element.65.anchor_ref.refs_0_, bf16[80,2048]{1,0:T(8,128)(2,1)S(1)} %get-tuple-element.72.refs_1_, bf16[80,2048]{1,0:T(8,128)(2,1)S(1)} %collective-permute-done.10.refs_2_, f32[1,8192]{1,0:T(1,128)S(1)} %bitcast.7, ...), custom_call_target="tpu_custom_call" | custom-call | tf_op jit(solution)/shard_map/project/pallas_call | solution.py:281
  58.1 7.8 %collective-permute-done.11.refs_0_ = bf16[80,2048]{1,0:T(8,128)(2,1)S(1)} collective-permute-done((bf16[80,2048]{1,0:T(8,128)(2,1)S(1)}, bf16[80,2048]{1,0:T(8,128)(2,1)S(1)}, u32[]{:S(2)}, u32[]{:S(2)}) %collective-permute-start.11) | collective-permute-done | bytes 327712 | tf_op jit(solution)/shard_map/ppermute | solution.py:588
  65.9 1.7 %project.11.refs_1_.refs_3_.refs_4_ = bf16[80,1536]{1,0:T(8,128)(2,1)S(1)} custom-call(bf16[80,2048]{1,0:T(8,128)(2,1)S(1)} %collective-permute-done.11.refs_0_, f32[1,8192]{1,0:T(1,128)S(1)} %bitcast.8, bf16[8192,1024]{1,0:T(8,128)(2,1)S(1)} %get-tuple-element.62.refs_4_.refs_2_, bf16[8192,256]{1,0:T(8,128)(2,1)S(1)} %copy-done, ...), custom_call_target="tpu_custom_call" | custom-call | tf_op jit(solution)/shard_map/project/pallas_call | solution.py:281
  67.6 1.2 %collective-permute-start.14 = (bf16[80,1536]{1,0:T(8,128)(2,1)S(1)}, bf16[80,1536]{1,0:T(8,128)(2,1)S(1)}, u32[]{:S(2)}, u32[]{:S(2)}) collective-permute-start(bf16[80,1536]{1,0:T(8,128)(2,1)S(1)} %project.11.refs_1_.refs_3_.refs_4_), channel_id=1, source_target_pairs={{0,8},{4,12},{8,0},{12,4},{1,9},{5,13},{9,1},{13,5},{2,10},{6,14},... | collective-permute-start | bytes 737288 | tf_op jit(solution)/shard_map/ppermute | solution.py:533
  68.7 0.0 collective-permute-done.7.refs_0_
  68.7 0.0 collective-permute-start.6
  68.8 0.5 collective-permute-start.12
  69.3 0.8 collective-permute-done.6.refs_5_.refs_1_
  70.1 0.2 collective-permute-done.12.refs_7_.refs_3_
  70.3 0.6 collective-permute-start.19
  70.9 4.2 %project.12 = (f32[80,1536]{1,0:T(8,128)S(1)}, f32[80,128]{1,0:T(8,128)S(1)}) custom-call(bf16[80,2048]{1,0:T(8,128)(2,1)S(1)} %get-tuple-element.77.refs_0_, bf16[80,2048]{1,0:T(8,128)(2,1)S(1)} %get-tuple-element.80.refs_1_, bf16[80,2048]{1,0:T(8,128)(2,1)S(1)} %collective-permute-done.17.refs_2_, f32[1,8192]{1,0:T(1,128)S(1)} %bitcast.9, ...), custom_call_target="tpu_custom_call" | custom-call | tf_op jit(solution)/shard_map/project/pallas_call | solution.py:281
  75.1 0.6 collective-permute-start.18
  75.7 3.8 %collective-permute-start.22 = (bf16[48,2048]{1,0:T(8,128)(2,1)S(1)}, bf16[48,2048]{1,0:T(8,128)(2,1)S(1)}, u32[]{:S(2)}, u32[]{:S(2)}) collective-permute-start(bf16[48,2048]{1,0:T(8,128)(2,1)S(1)} %get-tuple-element.86.refs_0_), channel_id=1, source_target_pairs={{0,2},{1,3},{2,0},{3,1},{4,6},{5,7},{6,4},{7,5},{8,10},{9,11},{10,... | collective-permute-start | bytes 589832 | tf_op jit(solution)/shard_map/ppermute | solution.py:588
  79.5 0.3 collective-permute-start.23
  79.9 5.1 %attend.3 = (bf16[512,1024]{1,0:T(8,128)(2,1)}, bf16[2,512,256]{2,1,0:T(8,128)(2,1)}, f32[8,128]{1,0:T(8,128)S(1)}) custom-call(s32[4]{0:T(128)S(1)} %copy-done.5, s32[16]{0:T(128)S(1)} %copy-done.6, bf16[48,1536]{1,0:T(8,128)(2,1)S(1)} %project.9.refs_3_.refs_4_.refs_0_, bf16[48,1536]{1,0:T(8,128)(2,1)S(1)} %collective-permute-done.6.refs_5_.refs_1_, ...), custom_call_target="tpu_custom_call" | custom-call | tf_op jit(solution)/shard_map/attend/pallas_call | solution.py:504
  85.0 0.0 collective-permute-done.19.refs_0_
  85.0 1.7 %project.13.refs_8_ = bf16[80,1536]{1,0:T(8,128)(2,1)S(1)} custom-call(bf16[80,2048]{1,0:T(8,128)(2,1)S(1)} %collective-permute-done.19.refs_0_, f32[1,8192]{1,0:T(1,128)S(1)} %bitcast.10, bf16[8192,1024]{1,0:T(8,128)(2,1)S(1)} %get-tuple-element.62.refs_4_.refs_2_, bf16[8192,256]{1,0:T(8,128)(2,1)S(1)} %copy-done, bf16[8192,256]{1,0:T(8,128)(2,1)S(1)} %copy-done.1, ...), custom_call_target="tpu_custom_call" | custom-call | tf_op jit(solution)/shard_map/project/pallas_call | solution.py:281
  86.7 0.1 collective-permute-start.21
  86.8 2.1 %collective-permute-done.22.refs_0_ = bf16[48,2048]{1,0:T(8,128)(2,1)S(1)} collective-permute-done((bf16[48,2048]{1,0:T(8,128)(2,1)S(1)}, bf16[48,2048]{1,0:T(8,128)(2,1)S(1)}, u32[]{:S(2)}, u32[]{:S(2)}) %collective-permute-start.22) | collective-permute-done | bytes 196640 | tf_op jit(solution)/shard_map/ppermute | solution.py:588
  88.9 1.0 collective-permute-done.23.refs_1_.refs_2_
  89.9 0.8 collective-permute-start.24
  90.7 4.0 %project.14 = (f32[48,1536]{1,0:T(8,128)S(1)}, f32[48,128]{1,0:T(8,128)S(1)}) custom-call(bf16[48,2048]{1,0:T(8,128)(2,1)S(1)} %get-tuple-element.86.refs_0_, bf16[48,2048]{1,0:T(8,128)(2,1)S(1)} %after.15.refs_1_, bf16[48,2048]{1,0:T(8,128)(2,1)S(1)} %collective-permute-done.23.refs_1_.refs_2_, f32[1,8192]{1,0:T(1,128)S(1)} %bitcast.11, ...), custom_call_target="tpu_custom_call" | custom-call | tf_op jit(solution)/shard_map/project/pallas_call | solution.py:281
  94.7 0.1 collective-permute-start.20
  94.8 0.8 collective-permute-done.24.refs_0_
  95.5 1.6 %project.15.refs_1_.refs_12_ = bf16[48,1536]{1,0:T(8,128)(2,1)S(1)} custom-call(bf16[48,2048]{1,0:T(8,128)(2,1)S(1)} %collective-permute-done.24.refs_0_, f32[1,8192]{1,0:T(1,128)S(1)} %bitcast.12, bf16[8192,1024]{1,0:T(8,128)(2,1)S(1)} %get-tuple-element.62.refs_4_.refs_2_, bf16[8192,256]{1,0:T(8,128)(2,1)S(1)} %copy-done, bf16[8192,256]{1,0:T(8,128)(2,1)S(1)} %copy-done.1, ...), custom_call_target="tpu_custom_call" | custom-call | tf_op jit(solution)/shard_map/project/pallas_call | solution.py:281
  97.1 0.0 collective-permute-done.21.refs_0_
  97.1 0.1 collective-permute-start.25
  97.2 0.3 collective-permute-start.27
  97.5 0.2 collective-permute-start.26
  97.7 1.0 collective-permute-done.25.refs_11_
  98.7 3.5 %attend.4 = (bf16[512,1024]{1,0:T(8,128)(2,1)}, bf16[2,512,256]{2,1,0:T(8,128)(2,1)}, f32[8,128]{1,0:T(8,128)S(1)}) custom-call(s32[4]{0:T(128)S(1)} %copy-done.5, s32[16]{0:T(128)S(1)} %copy-done.6, bf16[48,1536]{1,0:T(8,128)(2,1)S(1)} %project.9.refs_3_.refs_4_.refs_0_, ...), custom_call_target="tpu_custom_call", output_to_operand_aliasing={{0}: (14, {}), {1}: (15, {})} | custom-call | tf_op jit(solution)/shard_map/attend/pallas_call | solution.py:504
  102.2 1.3 %collective-permute-done.27.refs_0_ = bf16[48,1536]{1,0:T(8,128)(2,1)S(1)} collective-permute-done((bf16[48,1536]{1,0:T(8,128)(2,1)S(1)}, bf16[48,1536]{1,0:T(8,128)(2,1)S(1)}, u32[]{:S(2)}, u32[]{:S(2)}) %collective-permute-start.27) | collective-permute-done | bytes 147488 | tf_op jit(solution)/shard_map/ppermute | solution.py:533
  103.5 0.8 collective-permute-start.28
  104.3 1.0 collective-permute-done.28.refs_15_
  105.3 4.2 %attend.5 = (bf16[512,1024]{1,0:T(8,128)(2,1)}, bf16[2,512,256]{2,1,0:T(8,128)(2,1)}, f32[8,128]{1,0:T(8,128)}) custom-call(s32[4]{0:T(128)S(1)} %copy-done.5, s32[16]{0:T(128)S(1)} %copy-done.6, bf16[48,1536]{1,0:T(8,128)(2,1)S(1)} %project.9.refs_3_.refs_4_.refs_0_, ...), custom_call_target="tpu_custom_call", output_to_operand_aliasing={{0}: (18, {}), {1}: (19, {})} | custom-call | tf_op jit(solution)/shard_map/attend/pallas_call | solution.py:504
  (42 shorter events, 0.2 us)
Async XLA Ops:
  0.6 4.5 %collective-permute-start = (bf16[512,2048]{1,0:T(8,128)(2,1)}, bf16[512,2048]{1,0:T(8,128)(2,1)S(1)}, u32[]{:S(2)}, u32[]{:S(2)}) collective-permute-start(bf16[512,2048]{1,0:T(8,128)(2,1)} %refs_0_.3), channel_id=1, source_target_pairs={{0,4},{4,0},{8,12},{12,8},{1,5},{5,1},{9,13},{13,9},{2,6},{6,2},{1... | collective-permute-start | bytes 6291464 | tf_op jit(solution)/shard_map/ppermute | solution.py:537
  1.1 1.6 %copy-start.2 = (bf16[512,2048]{1,0:T(8,128)(2,1)S(1)}, bf16[512,2048]{1,0:T(8,128)(2,1)}, u32[]{:S(2)}) copy-start(bf16[512,2048]{1,0:T(8,128)(2,1)} %refs_0_.3) | copy-start | bytes 6291460
  2.7 0.7 copy-start.4
  3.4 6.0 %copy-start.3 = (bf16[512,2048]{1,0:T(8,128)(2,1)S(1)}, bf16[512,2048]{1,0:T(8,128)(2,1)}, u32[]{:S(2)}) copy-start(bf16[512,2048]{1,0:T(8,128)(2,1)} %refs_0_.3) | copy-start | bytes 6291460
  6.5 8.1 %collective-permute-start.1 = (bf16[48,2048]{1,0:T(8,128)(2,1)S(1)}, bf16[48,2048]{1,0:T(8,128)(2,1)S(1)}, u32[]{:S(2)}, u32[]{:S(2)}) collective-permute-start(bf16[48,2048]{1,0:T(8,128)(2,1)S(1)} %bitcast.16), channel_id=1, source_target_pairs={{0,8},{4,12},{8,0},{12,4},{1,9},{5,13},{9,1},{13,5},{2,10},{6,14},... | collective-permute-start | bytes 589832 | tf_op jit(solution)/shard_map/ppermute | solution.py:533
  14.6 12.1 %collective-permute-start.3 = (bf16[80,2048]{1,0:T(8,128)(2,1)S(1)}, bf16[80,2048]{1,0:T(8,128)(2,1)S(1)}, u32[]{:S(2)}, u32[]{:S(2)}) collective-permute-start(bf16[80,2048]{1,0:T(8,128)(2,1)S(1)} %bitcast.13), channel_id=1, source_target_pairs={{0,8},{4,12},{8,0},{12,4},{1,9},{5,13},{9,1},{13,5},{2,10},{6,14},... | collective-permute-start | bytes 983048 | tf_op jit(solution)/shard_map/ppermute | solution.py:533
  16.4 15.4 %copy-start.8 = (bf16[8192]{0:T(1024)(128)(2,1)S(1)}, bf16[8192]{0:T(1024)(128)(2,1)}, u32[]{:S(2)}) copy-start(bf16[8192]{0:T(1024)(128)(2,1)} %param.9) | copy-start | bytes 49156
  16.4 15.5 %copy-start.5 = (s32[4]{0:T(128)S(1)}, s32[4]{0:T(128)}, u32[]{:S(2)}) copy-start(s32[4]{0:T(128)} %lengths_ref.13) | copy-start | bytes 52
  16.4 15.5 %copy-start.7 = (f32[1,128]{1,0:T(1,128)S(1)}, f32[1,128]{1,0:T(1,128)}, u32[]{:S(2)}) copy-start(f32[1,128]{1,0:T(1,128)} %constant.2.clone.frequency_ref) | copy-start | bytes 1540
  16.4 10.9 %collective-permute-start.4 = (bf16[48,2048]{1,0:T(8,128)(2,1)S(1)}, bf16[48,2048]{1,0:T(8,128)(2,1)S(1)}, u32[]{:S(2)}, u32[]{:S(2)}) collective-permute-start(bf16[48,2048]{1,0:T(8,128)(2,1)S(1)} %get-tuple-element.55.anchor_ref.refs_0_), channel_id=1, source_target_pairs={{0,1},{1,0},{2,3},{3,2},{4,5},{5,4},{6,7},{7,6},{8,9},{9,8},{10,11... | collective-permute-start | bytes 589832 | tf_op jit(solution)/shard_map/ppermute | solution.py:588
  18.0 10.8 %collective-permute-start.2 = (bf16[48,2048]{1,0:T(8,128)(2,1)S(1)}, bf16[48,2048]{1,0:T(8,128)(2,1)S(1)}, u32[]{:S(2)}, u32[]{:S(2)}) collective-permute-start(bf16[48,2048]{1,0:T(8,128)(2,1)S(1)} %get-tuple-element.55.anchor_ref.refs_0_), channel_id=1, source_target_pairs={{0,2},{1,3},{2,0},{3,1},{4,6},{5,7},{6,4},{7,5},{8,10},{9,11},{10,... | collective-permute-start | bytes 589832 | tf_op jit(solution)/shard_map/ppermute | solution.py:588
  20.6 12.4 %copy-start = (bf16[8192,256]{1,0:T(8,128)(2,1)S(1)}, bf16[8192,256]{1,0:T(8,128)(2,1)}, u32[]{:S(2)}) copy-start(bf16[8192,256]{1,0:T(8,128)(2,1)} %refs_3_.7) | copy-start | bytes 12582916
  20.6 12.4 %copy-start.1 = (bf16[8192,256]{1,0:T(8,128)(2,1)S(1)}, bf16[8192,256]{1,0:T(8,128)(2,1)}, u32[]{:S(2)}) copy-start(bf16[8192,256]{1,0:T(8,128)(2,1)} %refs_4_.7) | copy-start | bytes 12582916
  26.7 21.3 %collective-permute-start.9 = (bf16[80,2048]{1,0:T(8,128)(2,1)S(1)}, bf16[80,2048]{1,0:T(8,128)(2,1)S(1)}, u32[]{:S(2)}, u32[]{:S(2)}) collective-permute-start(bf16[80,2048]{1,0:T(8,128)(2,1)S(1)} %bitcast.14), channel_id=1, source_target_pairs={{0,8},{4,12},{8,0},{12,4},{1,9},{5,13},{9,1},{13,5},{2,10},{6,14},... | collective-permute-start | bytes 983048 | tf_op jit(solution)/shard_map/ppermute | solution.py:533
  28.8 19.3 %collective-permute-start.10 = (bf16[80,2048]{1,0:T(8,128)(2,1)S(1)}, bf16[80,2048]{1,0:T(8,128)(2,1)S(1)}, u32[]{:S(2)}, u32[]{:S(2)}) collective-permute-start(bf16[80,2048]{1,0:T(8,128)(2,1)S(1)} %get-tuple-element.65.anchor_ref.refs_0_), channel_id=1, source_target_pairs={{0,1},{1,0},{2,3},{3,2},{4,5},{5,4},{6,7},{7,6},{8,9},{9,8},{10,11... | collective-permute-start | bytes 983048 | tf_op jit(solution)/shard_map/ppermute | solution.py:588
  29.2 19.0 %collective-permute-start.8 = (bf16[80,2048]{1,0:T(8,128)(2,1)S(1)}, bf16[80,2048]{1,0:T(8,128)(2,1)S(1)}, u32[]{:S(2)}, u32[]{:S(2)}) collective-permute-start(bf16[80,2048]{1,0:T(8,128)(2,1)S(1)} %get-tuple-element.65.anchor_ref.refs_0_), channel_id=1, source_target_pairs={{0,2},{1,3},{2,0},{3,1},{4,6},{5,7},{6,4},{7,5},{8,10},{9,11},{10,... | collective-permute-start | bytes 983048 | tf_op jit(solution)/shard_map/ppermute | solution.py:588
  31.9 14.6 %collective-permute-start.5 = (bf16[48,2048]{1,0:T(8,128)(2,1)S(1)}, bf16[48,2048]{1,0:T(8,128)(2,1)S(1)}, u32[]{:S(2)}, u32[]{:S(2)}) collective-permute-start(bf16[48,2048]{1,0:T(8,128)(2,1)S(1)} %get-tuple-element.61.refs_1_), channel_id=1, source_target_pairs={{0,1},{1,0},{2,3},{3,2},{4,5},{5,4},{6,7},{7,6},{8,9},{9,8},{10,11... | collective-permute-start | bytes 589832 | tf_op jit(solution)/shard_map/ppermute | solution.py:588
  48.1 17.7 %collective-permute-start.11 = (bf16[80,2048]{1,0:T(8,128)(2,1)S(1)}, bf16[80,2048]{1,0:T(8,128)(2,1)S(1)}, u32[]{:S(2)}, u32[]{:S(2)}) collective-permute-start(bf16[80,2048]{1,0:T(8,128)(2,1)S(1)} %get-tuple-element.72.refs_1_), channel_id=1, source_target_pairs={{0,1},{1,0},{2,3},{3,2},{4,5},{5,4},{6,7},{7,6},{8,9},{9,8},{10,11... | collective-permute-start | bytes 983048 | tf_op jit(solution)/shard_map/ppermute | solution.py:588
  49.8 19.0 %collective-permute-start.16 = (bf16[48,2048]{1,0:T(8,128)(2,1)S(1)}, bf16[48,2048]{1,0:T(8,128)(2,1)S(1)}, u32[]{:S(2)}, u32[]{:S(2)}) collective-permute-start(bf16[48,2048]{1,0:T(8,128)(2,1)S(1)} %bitcast.15), channel_id=1, source_target_pairs={{0,8},{4,12},{8,0},{12,4},{1,9},{5,13},{9,1},{13,5},{2,10},{6,14},... | collective-permute-start | bytes 589832 | tf_op jit(solution)/shard_map/ppermute | solution.py:533
  50.3 19.8 %collective-permute-start.15 = (bf16[80,2048]{1,0:T(8,128)(2,1)S(1)}, bf16[80,2048]{1,0:T(8,128)(2,1)S(1)}, u32[]{:S(2)}, u32[]{:S(2)}) collective-permute-start(bf16[80,2048]{1,0:T(8,128)(2,1)S(1)} %get-tuple-element.77.refs_0_), channel_id=1, source_target_pairs={{0,2},{1,3},{2,0},{3,1},{4,6},{5,7},{6,4},{7,5},{8,10},{9,11},{10,... | collective-permute-start | bytes 983048 | tf_op jit(solution)/shard_map/ppermute | solution.py:588
  52.3 17.9 %collective-permute-start.17 = (bf16[80,2048]{1,0:T(8,128)(2,1)S(1)}, bf16[80,2048]{1,0:T(8,128)(2,1)S(1)}, u32[]{:S(2)}, u32[]{:S(2)}) collective-permute-start(bf16[80,2048]{1,0:T(8,128)(2,1)S(1)} %get-tuple-element.77.refs_0_), channel_id=1, source_target_pairs={{0,1},{1,0},{2,3},{3,2},{4,5},{5,4},{6,7},{7,6},{8,9},{9,8},{10,11... | collective-permute-start | bytes 983048 | tf_op jit(solution)/shard_map/ppermute | solution.py:588
  52.3 16.4 %collective-permute-start.7 = (bf16[48,1536]{1,0:T(8,128)(2,1)S(1)}, bf16[48,1536]{1,0:T(8,128)(2,1)S(1)}, u32[]{:S(2)}, u32[]{:S(2)}) collective-permute-start(bf16[48,1536]{1,0:T(8,128)(2,1)S(1)} %project.9.refs_3_.refs_4_.refs_0_), channel_id=1, source_target_pairs={{0,8},{4,12},{8,0},{12,4},{1,9},{5,13},{9,1},{13,5},{2,10},{6,14},... | collective-permute-start | bytes 442376 | tf_op jit(solution)/shard_map/ppermute | solution.py:533
  67.6 7.6 %collective-permute-start.14 = (bf16[80,1536]{1,0:T(8,128)(2,1)S(1)}, bf16[80,1536]{1,0:T(8,128)(2,1)S(1)}, u32[]{:S(2)}, u32[]{:S(2)}) collective-permute-start(bf16[80,1536]{1,0:T(8,128)(2,1)S(1)} %project.11.refs_1_.refs_3_.refs_4_), channel_id=1, source_target_pairs={{0,8},{4,12},{8,0},{12,4},{1,9},{5,13},{9,1},{13,5},{2,10},{6,14},... | collective-permute-start | bytes 737288 | tf_op jit(solution)/shard_map/ppermute | solution.py:533
  68.7 1.4 %collective-permute-start.6 = (bf16[48,1536]{1,0:T(8,128)(2,1)S(1)}, bf16[48,1536]{1,0:T(8,128)(2,1)S(1)}, u32[]{:S(2)}, u32[]{:S(2)}) collective-permute-start(bf16[48,1536]{1,0:T(8,128)(2,1)S(1)} %project.9.refs_3_.refs_4_.refs_0_), channel_id=1, source_target_pairs={{0,4},{4,0},{8,12},{12,8},{1,5},{5,1},{9,13},{13,9},{2,6},{6,2},{1... | collective-permute-start | bytes 442376 | tf_op jit(solution)/shard_map/ppermute | solution.py:537
  68.8 1.6 %collective-permute-start.12 = (bf16[48,1536]{1,0:T(8,128)(2,1)S(1)}, bf16[48,1536]{1,0:T(8,128)(2,1)S(1)}, u32[]{:S(2)}, u32[]{:S(2)}) collective-permute-start(bf16[48,1536]{1,0:T(8,128)(2,1)S(1)} %after.11.refs_6_.refs_2_), channel_id=1, source_target_pairs={{0,4},{4,0},{8,12},{12,8},{1,5},{5,1},{9,13},{13,9},{2,6},{6,2},{1... | collective-permute-start | bytes 442376 | tf_op jit(solution)/shard_map/ppermute | solution.py:537
  70.3 9.5 %copy-start.6 = (s32[16]{0:T(128)S(1)}, s32[16]{0:T(128)}, u32[]{:S(2)}) copy-start(s32[16]{0:T(128)} %plan_ref.5) | copy-start | bytes 196
  70.3 14.7 %collective-permute-start.19 = (bf16[80,2048]{1,0:T(8,128)(2,1)S(1)}, bf16[80,2048]{1,0:T(8,128)(2,1)S(1)}, u32[]{:S(2)}, u32[]{:S(2)}) collective-permute-start(bf16[80,2048]{1,0:T(8,128)(2,1)S(1)} %get-tuple-element.80.refs_1_), channel_id=1, source_target_pairs={{0,1},{1,0},{2,3},{3,2},{4,5},{5,4},{6,7},{7,6},{8,9},{9,8},{10,11... | collective-permute-start | bytes 983048 | tf_op jit(solution)/shard_map/ppermute | solution.py:588
  70.9 8.9 %collective-permute-start.13 = (bf16[80,1536]{1,0:T(8,128)(2,1)S(1)}, bf16[80,1536]{1,0:T(8,128)(2,1)S(1)}, u32[]{:S(2)}, u32[]{:S(2)}) collective-permute-start(bf16[80,1536]{1,0:T(8,128)(2,1)S(1)} %project.11.refs_1_.refs_3_.refs_4_), channel_id=1, source_target_pairs={{0,4},{4,0},{8,12},{12,8},{1,5},{5,1},{9,13},{13,9},{2,6},{6,2},{1... | collective-permute-start | bytes 737288 | tf_op jit(solution)/shard_map/ppermute | solution.py:537
  75.1 4.7 %collective-permute-start.18 = (bf16[80,1536]{1,0:T(8,128)(2,1)S(1)}, bf16[80,1536]{1,0:T(8,128)(2,1)S(1)}, u32[]{:S(2)}, u32[]{:S(2)}) collective-permute-start(bf16[80,1536]{1,0:T(8,128)(2,1)S(1)} %after.13.refs_6_), channel_id=1, source_target_pairs={{0,4},{4,0},{8,12},{12,8},{1,5},{5,1},{9,13},{13,9},{2,6},{6,2},{1... | collective-permute-start | bytes 737288 | tf_op jit(solution)/shard_map/ppermute | solution.py:537
  75.7 13.2 %collective-permute-start.22 = (bf16[48,2048]{1,0:T(8,128)(2,1)S(1)}, bf16[48,2048]{1,0:T(8,128)(2,1)S(1)}, u32[]{:S(2)}, u32[]{:S(2)}) collective-permute-start(bf16[48,2048]{1,0:T(8,128)(2,1)S(1)} %get-tuple-element.86.refs_0_), channel_id=1, source_target_pairs={{0,2},{1,3},{2,0},{3,1},{4,6},{5,7},{6,4},{7,5},{8,10},{9,11},{10,... | collective-permute-start | bytes 589832 | tf_op jit(solution)/shard_map/ppermute | solution.py:588
  79.5 10.3 %collective-permute-start.23 = (bf16[48,2048]{1,0:T(8,128)(2,1)S(1)}, bf16[48,2048]{1,0:T(8,128)(2,1)S(1)}, u32[]{:S(2)}, u32[]{:S(2)}) collective-permute-start(bf16[48,2048]{1,0:T(8,128)(2,1)S(1)} %get-tuple-element.86.refs_0_), channel_id=1, source_target_pairs={{0,1},{1,0},{2,3},{3,2},{4,5},{5,4},{6,7},{7,6},{8,9},{9,8},{10,11... | collective-permute-start | bytes 589832 | tf_op jit(solution)/shard_map/ppermute | solution.py:588
  86.7 10.4 %collective-permute-start.21 = (bf16[80,1536]{1,0:T(8,128)(2,1)S(1)}, bf16[80,1536]{1,0:T(8,128)(2,1)S(1)}, u32[]{:S(2)}, u32[]{:S(2)}) collective-permute-start(bf16[80,1536]{1,0:T(8,128)(2,1)S(1)} %project.13.refs_8_), channel_id=1, source_target_pairs={{0,8},{4,12},{8,0},{12,4},{1,9},{5,13},{9,1},{13,5},{2,10},{6,14},... | collective-permute-start | bytes 737288 | tf_op jit(solution)/shard_map/ppermute | solution.py:533
  89.9 5.7 %collective-permute-start.24 = (bf16[48,2048]{1,0:T(8,128)(2,1)S(1)}, bf16[48,2048]{1,0:T(8,128)(2,1)S(1)}, u32[]{:S(2)}, u32[]{:S(2)}) collective-permute-start(bf16[48,2048]{1,0:T(8,128)(2,1)S(1)} %after.15.refs_1_), channel_id=1, source_target_pairs={{0,1},{1,0},{2,3},{3,2},{4,5},{5,4},{6,7},{7,6},{8,9},{9,8},{10,11... | collective-permute-start | bytes 589832 | tf_op jit(solution)/shard_map/ppermute | solution.py:588
  94.7 3.0 %collective-permute-start.20 = (bf16[80,1536]{1,0:T(8,128)(2,1)S(1)}, bf16[80,1536]{1,0:T(8,128)(2,1)S(1)}, u32[]{:S(2)}, u32[]{:S(2)}) collective-permute-start(bf16[80,1536]{1,0:T(8,128)(2,1)S(1)} %project.13.refs_8_), channel_id=1, source_target_pairs={{0,4},{4,0},{8,12},{12,8},{1,5},{5,1},{9,13},{13,9},{2,6},{6,2},{1... | collective-permute-start | bytes 737288 | tf_op jit(solution)/shard_map/ppermute | solution.py:537
  97.1 1.6 %collective-permute-start.25 = (bf16[80,1536]{1,0:T(8,128)(2,1)S(1)}, bf16[80,1536]{1,0:T(8,128)(2,1)S(1)}, u32[]{:S(2)}, u32[]{:S(2)}) collective-permute-start(bf16[80,1536]{1,0:T(8,128)(2,1)S(1)} %after.16.refs_10_), channel_id=1, source_target_pairs={{0,4},{4,0},{8,12},{12,8},{1,5},{5,1},{9,13},{13,9},{2,6},{6,2},{1... | collective-permute-start | bytes 737288 | tf_op jit(solution)/shard_map/ppermute | solution.py:537
  97.2 6.3 %collective-permute-start.27 = (bf16[48,1536]{1,0:T(8,128)(2,1)S(1)}, bf16[48,1536]{1,0:T(8,128)(2,1)S(1)}, u32[]{:S(2)}, u32[]{:S(2)}) collective-permute-start(bf16[48,1536]{1,0:T(8,128)(2,1)S(1)} %project.15.refs_1_.refs_12_), channel_id=1, source_target_pairs={{0,8},{4,12},{8,0},{12,4},{1,9},{5,13},{9,1},{13,5},{2,10},{6,14},... | collective-permute-start | bytes 442376 | tf_op jit(solution)/shard_map/ppermute | solution.py:533
  97.5 6.8 %collective-permute-start.26 = (bf16[48,1536]{1,0:T(8,128)(2,1)S(1)}, bf16[48,1536]{1,0:T(8,128)(2,1)S(1)}, u32[]{:S(2)}, u32[]{:S(2)}) collective-permute-start(bf16[48,1536]{1,0:T(8,128)(2,1)S(1)} %project.15.refs_1_.refs_12_), channel_id=1, source_target_pairs={{0,4},{4,0},{8,12},{12,8},{1,5},{5,1},{9,13},{13,9},{2,6},{6,2},{1... | collective-permute-start | bytes 442376 | tf_op jit(solution)/shard_map/ppermute | solution.py:537
  103.5 1.9 %collective-permute-start.28 = (bf16[48,1536]{1,0:T(8,128)(2,1)S(1)}, bf16[48,1536]{1,0:T(8,128)(2,1)S(1)}, u32[]{:S(2)}, u32[]{:S(2)}) collective-permute-start(bf16[48,1536]{1,0:T(8,128)(2,1)S(1)} %after.17.refs_14_), channel_id=1, source_target_pairs={{0,4},{4,0},{8,12},{12,8},{1,5},{5,1},{9,13},{13,9},{2,6},{6,2},{1... | collective-permute-start | bytes 442376 | tf_op jit(solution)/shard_map/ppermute | solution.py:537
